TPU v7x, 32 devices: a whole 2x2x4 slice. The times are simulated.
32 devices in a mesh: ctx: 8 (over y, x, core), tp: 4 (over z).
Axes of the slice: x: 2, y: 2, z: 4, core: 2. Of those that a mesh axis runs over, the one named last changes fastest.
Arguments:
- query_proj: bfloat16 [1024, 4096], P('ctx', 'tp'), may hold values from -6 to 6
- key_proj: bfloat16 [1024, 4096], P('ctx', 'tp'), may hold values from -6 to 6
- value_proj: bfloat16 [1024, 4096], P('ctx', 'tp'), may hold values from -6 to 6
- cotangent: bfloat16 [1024, 4096], P('ctx', 'tp'), may hold values from -6 to 6
- filter_taps: float32 [1024, 4096], P('ctx', 'tp'), may hold values from -1 to 1
- short_weights: float32 [3, 3, 4096], P(None, None, 'tp'), may hold values from -3.5 to 3.5
Outputs:
- gated_out: bfloat16 [1024, 4096], P('ctx', 'tp')
- query_grad: bfloat16 [1024, 4096], P('ctx', 'tp')
- key_grad: bfloat16 [1024, 4096], P('ctx', 'tp')
- value_grad: bfloat16 [1024, 4096], P('ctx', 'tp')
- filter_grad: float32 [1024, 4096], P('ctx', 'tp')
- short_grad: float32 [3, 3, 4096], P(None, None, 'tp')
All inputs are finite; a program needn't handle non-finite values.
Results may differ from a plain program's by a relative error of at most 0.0065.
Values may be sent and summed in bfloat16 or wider, within the bound.
No kernel may reach another device: no remote copies, remote signals or barrier semaphores. Data moves between devices by JAX's collectives and lax.ppermute only.
A program may use at most 64 MiB of HBM per device.

v0:
```python
import functools
import math

import jax
import jax.numpy as jnp
import numpy as np
from jax import lax
from jax.experimental import pallas as pl
from jax.experimental.pallas import tpu as pltpu
from jax.sharding import PartitionSpec as P

F32 = jnp.float32
BF16 = jnp.bfloat16
LANES = 128
PHASES = 4
TILE = 16
PAD = 8
RIM = 2
PIECES = 3
VMEM_LIMIT = 24 * 1024 * 1024


def partners(peers):
    return [0] + list(range(peers - 1, 0, -1))


def exchange(blocks):
    peers = len(blocks)
    got = [blocks[0]]
    for step, block in list(zip(partners(peers), blocks))[1:]:
        got.append(lax.ppermute(block, "ctx", [(i, i ^ step) for i in range(peers)]))
    return got


def in_vmem(count):
    return [pl.BlockSpec(memory_space=pltpu.VMEM)] * count


def lanes_of(place):
    return pl.ds(pl.multiple_of(place * LANES, LANES), LANES)


def pack_kernel(count, *refs):
    sources, packed = refs[:count], refs[count:]
    tokens = sources[0].shape[0]
    me = lax.axis_index("ctx")
    for step, target in zip(partners(len(packed)), packed):
        for at, source in enumerate(sources):
            target[at * tokens : (at + 1) * tokens, :] = source[:, lanes_of(me ^ step)].astype(BF16)


def pack(name, arrays, peers):
    tokens = arrays[0].shape[0]
    return pl.pallas_call(
        functools.partial(pack_kernel, len(arrays)),
        in_specs=in_vmem(len(arrays)),
        out_specs=in_vmem(peers),
        out_shape=[jax.ShapeDtypeStruct((len(arrays) * tokens, LANES), BF16)] * peers,
        name=name,
    )(*arrays)


@functools.lru_cache(maxsize=None)
def dft_tables(seq_len):
    size = seq_len // PHASES
    k = np.arange(size, dtype=np.int64)[:, None]
    m = np.arange(size, dtype=np.int64)[None, :]
    forward = []
    for phase in range(PHASES):
        turns = ((4 * k + 1) * (PHASES * m + phase)) % (4 * seq_len)
        angle = 2.0 * np.pi / (4 * seq_len) * turns
        forward.append(np.concatenate([np.cos(angle), -np.sin(angle)], axis=0))
    forward = np.stack(forward)
    backward = np.swapaxes(forward, 1, 2) / seq_len

    def pieces(table):
        high = table.astype(BF16)
        low = (table - high.astype(np.float64)).astype(BF16)
        return np.stack([high, low], axis=1)

    return pieces(forward), pieces(backward)


def forward_mix(parts):
    (r0, i0), (r1, i1), (r2, i2), (r3, i3) = parts
    ar, ai, br, bi = r0 + r2, i0 + i2, r0 - r2, i0 - i2
    cr, ci, dr, di = r1 + r3, i1 + i3, r1 - r3, i1 - i3
    return ((ar + cr, ai + ci), (br + di, bi - dr), (ar - cr, ai - ci), (br - di, bi + dr))


def inverse_mix(parts):
    (r0, i0), (r1, i1), (r2, i2), (r3, i3) = parts
    ar, ai, br, bi = r0 + r2, i0 + i2, r0 - r2, i0 - i2
    cr, ci, dr, di = r1 + r3, i1 + i3, r1 - r3, i1 - i3
    return ((ar + cr, ai + ci), (br - di, bi + dr), (ar - cr, ai - ci), (br + di, bi - dr))


def times(left, right):
    return tuple(
        (lr * rr - li * ri, lr * ri + li * rr) for (lr, li), (rr, ri) in zip(left, right)
    )


def conj_times(left, right):
    return tuple(
        (lr * rr + li * ri, lr * ri - li * rr) for (lr, li), (rr, ri) in zip(left, right)
    )


def split_store(ref, r, rows, lanes, values):
    half = ref.shape[-1] // 2
    rounded = values.astype(BF16)
    ref[r, rows, lanes] = rounded
    ref[r, rows, slice(lanes.start + half, lanes.stop + half)] = (
        values - rounded.astype(F32)
    ).astype(BF16)


def forward_transform(forward, signal):
    return jnp.dot(forward[0], signal, preferred_element_type=F32) + jnp.dot(
        forward[1], signal, preferred_element_type=F32
    )


def inverse_transform(backward, pieces):
    half = pieces.shape[-1] // 2
    both = jnp.dot(backward[0], pieces, preferred_element_type=F32)
    rest = jnp.dot(backward[1], pieces[:, :half], preferred_element_type=F32)
    return both[:, :half] + both[:, half:] + rest


def phase(ref, r, size):
    return ref[pl.ds(r, size, stride=PHASES), :]


def short_phases(ref, weights, array, lanes, r, size):
    summed = weights[array, 0:1, lanes] * phase(ref, PAD + r, size)
    for tap in range(1, weights.shape[1]):
        summed = summed + weights[array, tap : tap + 1, lanes] * phase(ref, PAD + r - tap, size)
    return summed


def clear_ends(ref):
    ref[:PAD, :] = jnp.zeros((PAD, LANES), F32)
    ref[ref.shape[0] - PAD :, :] = jnp.zeros((PAD, LANES), F32)


def key_value_kernel(tokens, peers, *refs):
    arrived = refs[:peers]
    weights, forward_far, backward_far = refs[peers : peers + 3]
    key, value, key_short, value_short, prod_spec, filt_spec, conv = refs[peers + 3 : peers + 10]
    taps, forward, backward, signals, spectra, pieces, sems = refs[peers + 10 :]
    size = peers * tokens // PHASES
    me = lax.axis_index("ctx")
    own = lanes_of(me)
    get_forward = pltpu.make_async_copy(forward_far, forward, sems.at[0])
    get_backward = pltpu.make_async_copy(backward_far, backward, sems.at[1])
    get_forward.start()
    get_backward.start()
    for ref in (key, value, conv):
        clear_ends(ref)
    for step, source in zip(partners(peers), arrived):
        start = (me ^ step) * tokens
        inner = pl.ds(pl.multiple_of(PAD + start, PAD), tokens)
        key[inner, :] = source[:tokens, :].astype(F32)
        value[inner, :] = source[tokens : 2 * tokens, :].astype(F32)
        taps[pl.ds(pl.multiple_of(start, PAD), tokens), :] = source[2 * tokens :, :].astype(F32)
    for r in range(PHASES):
        key_short[r] = short_phases(key, weights, 1, own, r, size)
        value_short[r] = short_phases(value, weights, 2, own, r, size)
        signals[r, :, :LANES] = (key_short[r] * value_short[r]).astype(BF16)
        signals[r, :, LANES:] = phase(taps, r, size).astype(BF16)
    get_forward.wait()
    for r in range(PHASES):
        spectra[r] = forward_transform(forward[r], signals[r])
    for chunk in range(size // TILE):
        real = slice(chunk * TILE, (chunk + 1) * TILE)
        imag = slice(size + chunk * TILE, size + (chunk + 1) * TILE)
        mixed = []
        for at, target in enumerate((prod_spec, filt_spec)):
            lanes = slice(at * LANES, (at + 1) * LANES)
            spectrum = forward_mix(
                [(spectra[r, real, lanes], spectra[r, imag, lanes]) for r in range(PHASES)]
            )
            for q, pair in enumerate(spectrum):
                target[q, real, :], target[q, imag, :] = pair
            mixed.append(spectrum)
        for r, pair in enumerate(inverse_mix(times(*mixed))):
            for rows, part in zip((real, imag), pair):
                split_store(pieces, r, rows, slice(0, LANES), part)
    get_backward.wait()
    for r in range(PHASES):
        result = inverse_transform(backward[r], pieces[r])
        conv[pl.ds(PAD + r, size, stride=PHASES), :] = result.astype(BF16).astype(F32)


def key_value_step(arrived, short_weights, tables, tokens):
    peers = len(arrived)
    seq_len = peers * tokens
    size = seq_len // PHASES
    padded = jax.ShapeDtypeStruct((seq_len + 2 * PAD, LANES), F32)
    phases = jax.ShapeDtypeStruct((PHASES, size, LANES), F32)
    spectrum = jax.ShapeDtypeStruct((PHASES, 2 * size, LANES), F32)
    return pl.pallas_call(
        functools.partial(key_value_kernel, tokens, peers),
        in_specs=in_vmem(peers + 1) + [pl.BlockSpec(memory_space=pltpu.HBM)] * 2,
        out_specs=in_vmem(7),
        out_shape=[padded, padded, phases, phases, spectrum, spectrum, padded],
        scratch_shapes=[
            pltpu.VMEM((seq_len, LANES), F32),
            pltpu.VMEM(tables[0].shape, BF16),
            pltpu.VMEM(tables[1].shape, BF16),
            pltpu.VMEM((PHASES, size, 2 * LANES), BF16),
            pltpu.VMEM((PHASES, 2 * size, 2 * LANES), F32),
            pltpu.VMEM((PHASES, 2 * size, 2 * LANES), BF16),
            pltpu.SemaphoreType.DMA((2,)),
        ],
        compiler_params=pltpu.CompilerParams(vmem_limit_bytes=VMEM_LIMIT),
        cost_estimate=pl.CostEstimate(
            flops=2 * 24 * PHASES * size * size * LANES,
            bytes_accessed=8 * 1024 * 1024,
            transcendentals=0,
        ),
        name="key_value_channels",
    )(*arrived, short_weights, *tables)


def extra_rows(short_weights):
    sums = PIECES * short_weights.shape[0] * short_weights.shape[1]
    return sums, -(-(sums + 8 * RIM) // TILE) * TILE


def gradient_kernel(tokens, peers, grad_scale, *refs):
    arrived = refs[:peers]
    weights, forward_far, backward_far = refs[peers : peers + 3]
    key, value, key_short, value_short, prod_spec, filt_spec, conv = refs[peers + 3 : peers + 10]
    out = refs[peers + 10 : 2 * peers + 10]
    (
        query,
        cot,
        conv_grad,
        filter_grad,
        forward,
        backward,
        signals,
        spectra,
        pieces,
        extra,
        sems,
    ) = refs[2 * peers + 10 :]
    size = peers * tokens // PHASES
    tap_count = weights.shape[1]
    me = lax.axis_index("ctx")
    own = lanes_of(me)
    get_forward = pltpu.make_async_copy(forward_far, forward, sems.at[0])
    get_backward = pltpu.make_async_copy(backward_far, backward, sems.at[1])
    get_forward.start()
    get_backward.start()
    for ref in (query, cot, conv_grad):
        clear_ends(ref)
    for step, source in zip(partners(peers), arrived):
        inner = pl.ds(pl.multiple_of(PAD + (me ^ step) * tokens, PAD), tokens)
        query[inner, :] = source[:tokens, :].astype(F32)
        cot[inner, :] = source[tokens:, :].astype(F32)
    for r in range(PHASES):
        query_short = short_phases(query, weights, 0, own, r, size)
        signals[r] = (phase(cot, PAD + r, size) * query_short).astype(BF16)
    get_forward.wait()
    for r in range(PHASES):
        spectra[r] = forward_transform(forward[r], signals[r])
    for chunk in range(size // TILE):
        real = slice(chunk * TILE, (chunk + 1) * TILE)
        imag = slice(size + chunk * TILE, size + (chunk + 1) * TILE)
        grad = forward_mix([(spectra[r, real, :], spectra[r, imag, :]) for r in range(PHASES)])
        for at, other in enumerate((filt_spec, prod_spec)):
            known = [(other[q, real, :], other[q, imag, :]) for q in range(PHASES)]
            for r, pair in enumerate(inverse_mix(conj_times(known, grad))):
                for rows, part in zip((real, imag), pair):
                    split_store(pieces, r, rows, slice(at * LANES, (at + 1) * LANES), part)
    get_backward.wait()
    for r in range(PHASES):
        result = inverse_transform(backward[r], pieces[r])
        conv_grad[pl.ds(PAD + r, size, stride=PHASES), :] = (
            result[:, :LANES].astype(BF16).astype(F32)
        )
        filter_grad[pl.ds(r, size, stride=PHASES), :] = result[:, LANES:] * grad_scale

    sums = []
    for array, signal in enumerate((query, key, value)):
        totals = [None] * tap_count
        for r in range(PHASES):
            if array == 0:
                pre = phase(cot, PAD + r, size) * phase(conv, PAD + r, size)
            else:
                pre = phase(conv_grad, PAD + r, size) * (value_short, key_short)[array - 1][r]
            for tap in range(tap_count):
                term = pre * phase(signal, PAD + r - tap, size)
                term = jnp.sum(term.reshape(size // 8, 8, LANES), axis=0)
                totals[tap] = term if r == 0 else totals[tap] + term
        sums.extend(jnp.sum(total, axis=0, keepdims=True) for total in totals)
    rest = jnp.concatenate(sums, axis=0) * grad_scale
    extra[...] = jnp.zeros_like(extra)
    for piece in range(PIECES):
        rounded = rest.astype(BF16).astype(F32)
        extra[piece * len(sums) : (piece + 1) * len(sums), :] = rounded
        rest = rest - rounded
    for step, target in zip(partners(peers), out):
        start = (me ^ step) * tokens
        inner = pl.ds(pl.multiple_of(PAD + start, PAD), tokens)
        target[:tokens, :] = conv[inner, :].astype(BF16)
        target[tokens : 2 * tokens, :] = conv_grad[inner, :].astype(BF16)
        target[2 * tokens : 3 * tokens, :] = filter_grad[
            pl.ds(pl.multiple_of(start, PAD), tokens), :
        ].astype(BF16)
        before = pl.ds(pl.multiple_of(start, PAD), PAD)
        after = pl.ds(pl.multiple_of(PAD + start + tokens, PAD), PAD)
        at = PIECES * len(sums)
        for ref in (query, key, value):
            extra[at : at + RIM, :] = ref[before, :][PAD - RIM :]
            at += RIM
        for ref in (cot, conv, conv_grad, key, value):
            extra[at : at + RIM, :] = ref[after, :][:RIM]
            at += RIM
        target[3 * tokens :, :] = extra[...].astype(BF16)


def gradient_step(arrived, short_weights, tables, known, tokens):
    peers = len(arrived)
    seq_len = peers * tokens
    size = seq_len // PHASES
    extra = extra_rows(short_weights)[1]
    return pl.pallas_call(
        functools.partial(gradient_kernel, tokens, peers, 1.0 / math.sqrt(seq_len)),
        in_specs=in_vmem(peers + 1) + [pl.BlockSpec(memory_space=pltpu.HBM)] * 2 + in_vmem(7),
        out_specs=in_vmem(peers),
        out_shape=[jax.ShapeDtypeStruct((3 * tokens + extra, LANES), BF16)] * peers,
        scratch_shapes=[
            pltpu.VMEM((seq_len + 2 * PAD, LANES), F32),
            pltpu.VMEM((seq_len + 2 * PAD, LANES), F32),
            pltpu.VMEM((seq_len + 2 * PAD, LANES), F32),
            pltpu.VMEM((seq_len, LANES), F32),
            pltpu.VMEM(tables[0].shape, BF16),
            pltpu.VMEM(tables[1].shape, BF16),
            pltpu.VMEM((PHASES, size, LANES), BF16),
            pltpu.VMEM((PHASES, 2 * size, LANES), F32),
            pltpu.VMEM((PHASES, 2 * size, 4 * LANES), BF16),
            pltpu.VMEM((extra, LANES), F32),
            pltpu.SemaphoreType.DMA((2,)),
        ],
        compiler_params=pltpu.CompilerParams(vmem_limit_bytes=VMEM_LIMIT),
        name="gradient_channels",
    )(*arrived, short_weights, *tables, *known)


def token_kernel(peers, sum_rows, *refs):
    arrived = refs[:peers]
    query, key, value, cot, weights = refs[peers : peers + 5]
    gated, query_grad, key_grad, value_grad, filter_grad, short_grad = refs[peers + 5 : peers + 11]
    longer, pre = refs[peers + 11 :]
    tokens = query.shape[0]
    tap_count = weights.shape[1]
    count = sum_rows // PIECES
    me = lax.axis_index("ctx")
    for step, source in zip(partners(peers), arrived):
        lanes = lanes_of(me ^ step)
        extra = source[3 * tokens :, :].astype(F32)

        def rim(at):
            return extra[sum_rows + at * RIM : sum_rows + (at + 1) * RIM]

        def short(array, signal, after, rows):
            longer[array, PAD - RIM : PAD, :] = rim(array)
            longer[array, PAD : PAD + tokens, :] = signal[:, lanes].astype(F32)
            if after is not None:
                longer[array, PAD + tokens : PAD + tokens + RIM, :] = rim(after)
            summed = weights[array, 0:1, lanes] * longer[array, PAD : PAD + rows, :]
            for tap in range(1, tap_count):
                summed = (
                    summed
                    + weights[array, tap : tap + 1, lanes]
                    * longer[array, PAD - tap : PAD - tap + rows, :]
                )
            return summed

        def taps_back(array, target):
            summed = weights[array, 0:1, lanes] * pre[array, :tokens, :]
            for tap in range(1, tap_count):
                summed = (
                    summed
                    + weights[array, tap : tap + 1, lanes] * pre[array, tap : tap + tokens, :]
                )
            target[:, lanes] = summed.astype(BF16)

        conv = source[:tokens, :].astype(F32)
        gated[:, lanes] = (short(0, query, None, tokens) * conv).astype(BF16)
        pre[0, :tokens, :] = cot[:, lanes].astype(F32) * conv
        pre[0, tokens : tokens + RIM, :] = rim(3) * rim(4)
        taps_back(0, query_grad)
        key_short = short(1, key, 6, tokens + PAD)
        value_short = short(2, value, 7, tokens + PAD)
        conv_grad = source[tokens : 2 * tokens, :].astype(F32)
        for array, other in ((1, value_short), (2, key_short)):
            pre[array, :tokens, :] = conv_grad * other[:tokens]
            pre[array, tokens : tokens + RIM, :] = rim(5) * other[tokens : tokens + RIM]
        taps_back(1, key_grad)
        taps_back(2, value_grad)
        filter_grad[:, lanes] = source[2 * tokens : 3 * tokens, :].astype(F32)
        whole = extra[:count]
        for piece in range(1, PIECES):
            whole = whole + extra[piece * count : (piece + 1) * count]
        for row in range(count):
            which, tap = divmod(row, tap_count)
            short_grad[which, tap : tap + 1, lanes] = whole[row : row + 1]


def token_step(arrived, query, key, value, cot, short_weights):
    peers = len(arrived)
    tokens, width = query.shape
    wide = jax.ShapeDtypeStruct((tokens, width), BF16)
    return pl.pallas_call(
        functools.partial(token_kernel, peers, extra_rows(short_weights)[0]),
        in_specs=in_vmem(peers + 5),
        out_specs=in_vmem(6),
        out_shape=[wide] * 4
        + [
            jax.ShapeDtypeStruct((tokens, width), F32),
            jax.ShapeDtypeStruct(short_weights.shape, F32),
        ],
        scratch_shapes=[
            pltpu.VMEM((3, tokens + 2 * PAD, LANES), F32),
            pltpu.VMEM((3, tokens + PAD, LANES), F32),
        ],
        compiler_params=pltpu.CompilerParams(vmem_limit_bytes=VMEM_LIMIT),
        name="token_outputs",
    )(*arrived, query, key, value, cot, short_weights)


def channel_shards(query_proj, key_proj, value_proj, cotangent, filter_taps, short_weights):
    peers = lax.axis_size("ctx")
    tokens = query_proj.shape[0]
    tables = [jnp.asarray(table) for table in dft_tables(peers * tokens)]
    first = exchange(pack("pack_key_value_taps", (key_proj, value_proj, filter_taps), peers))
    second = exchange(pack("pack_query_cot", (query_proj, cotangent), peers))
    known = key_value_step(first, short_weights, tables, tokens)
    back = exchange(gradient_step(second, short_weights, tables, known, tokens))
    return tuple(token_step(back, query_proj, key_proj, value_proj, cotangent, short_weights))


def from_behind(array, axis, by):
    peers = lax.axis_size(axis)
    pairs = [(i, i + by) for i in range(peers) if 0 <= i + by < peers]
    return lax.ppermute(array, axis, pairs)


def contract(form, left, right):
    return jnp.einsum(
        form, left, right, precision=lax.Precision.HIGHEST, preferred_element_type=jnp.float32
    )


def table_pair(rows, cols, period):
    row_ids = lax.broadcasted_iota(jnp.int32, (rows, cols), 0)
    col_ids = lax.broadcasted_iota(jnp.int32, (rows, cols), 1)
    angle = 2.0 * math.pi / period * (row_ids * col_ids % period).astype(jnp.float32)
    return (jnp.cos(angle), jnp.sin(angle))


def make_plan(seq_len):
    small_len = int(math.isqrt(2 * seq_len))
    while seq_len % small_len:
        small_len -= 1
    large_len = 2 * seq_len // small_len
    large_cos, large_sin = table_pair(large_len // 2, large_len, large_len)
    small_cos, small_sin = table_pair(small_len, small_len, small_len)
    twist_cos, twist_sin = table_pair(large_len, small_len, small_len * large_len)
    fwd_large = jnp.stack([large_cos, -large_sin], axis=1)
    fwd_small = jnp.stack([jnp.stack([small_cos, -small_sin]), jnp.stack([small_sin, small_cos])])
    inv_small = jnp.stack([jnp.stack([small_cos, small_sin]), jnp.stack([-small_sin, small_cos])])
    inv_large = jnp.stack([large_cos, -large_sin])
    return (small_len, large_len, fwd_large, fwd_small, inv_small, inv_large, twist_cos, twist_sin)


def forward_spec(signal, dft_plan):
    small_len, large_len, fwd_large, fwd_small, inv_small, inv_large, twist_cos, twist_sin = (
        dft_plan
    )
    cube = signal.reshape(signal.shape[0], large_len // 2, small_len)
    section_one = contract("cba,bpk->cpka", cube, fwd_large)
    real_one = section_one[:, 0]
    imag_one = section_one[:, 1]
    section_two = jnp.stack(
        [real_one * twist_cos + imag_one * twist_sin, imag_one * twist_cos - real_one * twist_sin],
        axis=1,
    )
    return contract("cpka,pqaj->cqkj", section_two, fwd_small)


def inverse_half(spec, dft_plan):
    small_len, large_len, fwd_large, fwd_small, inv_small, inv_large, twist_cos, twist_sin = (
        dft_plan
    )
    section_one = contract("cqkj,qpja->cpka", spec, inv_small)
    real_one = section_one[:, 0]
    imag_one = section_one[:, 1]
    section_two = jnp.stack(
        [real_one * twist_cos - imag_one * twist_sin, imag_one * twist_cos + real_one * twist_sin],
        axis=1,
    )
    signal = contract("cpka,pbk->cba", section_two, inv_large)
    return signal.reshape(signal.shape[0], -1) / float(small_len * large_len)


def complex_mul(left, right):
    left_real, left_imag = (left[:, 0], left[:, 1])
    right_real, right_imag = (right[:, 0], right[:, 1])
    return jnp.stack(
        [
            left_real * right_real - left_imag * right_imag,
            left_real * right_imag + left_imag * right_real,
        ],
        axis=1,
    )


def conj_mul(left, right):
    left_real, left_imag = (left[:, 0], left[:, 1])
    right_real, right_imag = (right[:, 0], right[:, 1])
    return jnp.stack(
        [
            left_real * right_real + left_imag * right_imag,
            left_real * right_imag - left_imag * right_real,
        ],
        axis=1,
    )


def conv_forward(prod_chan, filter_spec, dft_plan):
    prod_spec = forward_spec(prod_chan.astype(jnp.float32), dft_plan)
    conv_chan = inverse_half(complex_mul(prod_spec, filter_spec), dft_plan).astype(jnp.bfloat16)
    return (conv_chan, prod_spec)


def conv_backward(grad_chan, filter_spec, prod_spec, dft_plan, grad_scale):
    grad_spec = forward_spec(grad_chan.astype(jnp.float32), dft_plan)
    dconv_chan = inverse_half(conj_mul(filter_spec, grad_spec), dft_plan).astype(jnp.bfloat16)
    dfilter_chan = inverse_half(conj_mul(prod_spec, grad_spec), dft_plan) * grad_scale
    return (dconv_chan, dfilter_chan)


def receive_filter(filter_taps, dft_plan):
    filter_chan = lax.all_to_all(filter_taps.T, "ctx", split_axis=0, concat_axis=1, tiled=True)
    return forward_spec(filter_chan, dft_plan)


def return_filter(dfilter_chan):
    return (
        lax.all_to_all(
            dfilter_chan.astype(jnp.bfloat16), "ctx", split_axis=1, concat_axis=0, tiled=True
        )
        .astype(dfilter_chan.dtype)
        .T
    )


def causal_taps(extended, weights, length, axis):
    rim_rows = len(weights) - 1
    summed = weights[0] * lax.slice_in_dim(extended, rim_rows, rim_rows + length, axis=axis)
    for offset in range(1, len(weights)):
        summed = summed + weights[offset] * lax.slice_in_dim(
            extended, rim_rows - offset, rim_rows - offset + length, axis=axis
        )
    return summed


def reverse_taps(extended, weights, length, axis):
    summed = weights[0] * lax.slice_in_dim(extended, 0, length, axis=axis)
    for offset in range(1, len(weights)):
        summed = summed + weights[offset] * lax.slice_in_dim(
            extended, offset, offset + length, axis=axis
        )
    return summed


def tap_grads(grad_in, extended, tap_count, length, axis):
    rim_rows = tap_count - 1
    rows = [
        jnp.sum(
            grad_in
            * lax.slice_in_dim(extended, rim_rows - offset, rim_rows - offset + length, axis=axis),
            axis=axis,
        )
        for offset in range(tap_count)
    ]
    return jnp.stack(rows, axis=1)


def spread_shards(query_proj, key_proj, value_proj, cotangent, filter_taps, short_weights):
    tokens = query_proj.shape[0]
    tap_count = short_weights.shape[1]
    rim_rows = tap_count - 1
    seq_len = tokens * lax.axis_size("ctx")
    grad_scale = 1.0 / math.sqrt(seq_len)
    dft_plan = make_plan(seq_len)
    stacked = jnp.stack([query_proj, key_proj, value_proj])
    prev_rim = from_behind(stacked[:, tokens - rim_rows :], "ctx", 1)
    extended = jnp.concatenate([prev_rim, stacked], axis=1).astype(jnp.float32)
    weights = [short_weights[:, offset, None, :] for offset in range(tap_count)]
    short_out = causal_taps(extended, weights, tokens, 1)
    product = (short_out[1] * short_out[2]).astype(jnp.bfloat16)
    cot_wide = cotangent.astype(jnp.float32)
    gate_grad = (cot_wide * short_out[0]).astype(jnp.bfloat16)
    filter_spec = receive_filter(filter_taps, dft_plan)
    prod_chan = lax.all_to_all(product.T, "ctx", split_axis=0, concat_axis=1, tiled=True)
    conv_chan, prod_spec = conv_forward(prod_chan, filter_spec, dft_plan)
    conv_tok = lax.all_to_all(conv_chan, "ctx", split_axis=1, concat_axis=0, tiled=True)
    grad_chan = lax.all_to_all(gate_grad.T, "ctx", split_axis=0, concat_axis=1, tiled=True)
    dconv_chan, dfilter_chan = conv_backward(
        grad_chan, filter_spec, prod_spec, dft_plan, grad_scale
    )
    dconv_tok = lax.all_to_all(dconv_chan, "ctx", split_axis=1, concat_axis=0, tiled=True)
    filter_grad = return_filter(dfilter_chan)
    conv_wide = conv_tok.T.astype(jnp.float32)
    dconv_wide = dconv_tok.T.astype(jnp.float32)
    gated = (short_out[0] * conv_wide).astype(jnp.bfloat16)
    token_grads = jnp.stack(
        [cot_wide * conv_wide, dconv_wide * short_out[2], dconv_wide * short_out[1]]
    )
    next_rim = from_behind(token_grads[:, :rim_rows], "ctx", -1)
    grad_ext = jnp.concatenate([token_grads, next_rim], axis=1)
    inputs_grad = reverse_taps(grad_ext, weights, tokens, 1).astype(jnp.bfloat16)
    weight_part = tap_grads(token_grads, extended, tap_count, tokens, 1)
    short_grad = lax.psum(weight_part, "ctx") * grad_scale
    results = (gated, inputs_grad[0], inputs_grad[1], inputs_grad[2])
    return (results[0], results[1], results[2], results[3], filter_grad, short_grad)


def fits(query_proj, short_weights):
    peers = lax.axis_size("ctx")
    tokens, width = query_proj.shape
    tap_count = short_weights.shape[1]
    return (
        width == peers * LANES
        and peers.bit_count() == 1
        and tokens % (PHASES * TILE) == 0
        and tap_count == RIM + 1
        and peers * tokens <= 2048
    )


def shards(*arrays):
    return channel_shards(*arrays) if fits(arrays[0], arrays[5]) else spread_shards(*arrays)


def solution(mesh):
    placed = (
        P("ctx", "tp"),
        P("ctx", "tp"),
        P("ctx", "tp"),
        P("ctx", "tp"),
        P("ctx", "tp"),
        P(None, None, "tp"),
    )
    return jax.shard_map(
        shards,
        mesh=mesh,
        in_specs=placed,
        out_specs=(
            P("ctx", "tp"),
            P("ctx", "tp"),
            P("ctx", "tp"),
            P("ctx", "tp"),
            P("ctx", "tp"),
            P(None, None, "tp"),
        ),
        check_vma=False,
    )
```

profile of v0, /device:TPU:0, one launch (start us, length us, event | category | flops | bytes accessed | tf_op | source)
XLA Modules:
  0.0 51.4 jit_solution(206818249889446317)
XLA Ops:
  0.6 2.3 %pack_key_value_taps.1 = (bf16[384,128]{1,0:T(8,128)(2,1)}, bf16[384,128]{1,0:T(8,128)(2,1)}, bf16[384,128]{1,0:T(8,128)(2,1)}, bf16[384,128]{1,0:T(8,128)(2,1)}...) custom-call(bf16[128,1024]{1,0:T(8,128)(2,1)} %refs_9_.3, ...), custom_call_target="tpu_custom_call" | custom-call | tf_op jit(solution)/shard_map/pack_key_value_taps/pallas_call | solution.py:54
  2.9 3.3 %collective-permute-start.7 = (bf16[384,128]{1,0:T(8,128)(2,1)}, bf16[384,128]{1,0:T(8,128)(2,1)S(1)}, u32[]{:S(2)}, u32[]{:S(2)}) collective-permute-start(bf16[384,128]{1,0:T(8,128)(2,1)} %get-tuple-element.46), channel_id=1, source_target_pairs={{0,28},{4,24},{8,20},{12,16},{16,12},{20,8},{24,4},{28,0},{1,29},{... | collective-permute-start | bytes 294920 | tf_op jit(solution)/shard_map/ppermute | solution.py:31
  6.2 0.6 %collective-permute-start.8 = (bf16[384,128]{1,0:T(8,128)(2,1)}, bf16[384,128]{1,0:T(8,128)(2,1)S(1)}, u32[]{:S(2)}, u32[]{:S(2)}) collective-permute-start(bf16[384,128]{1,0:T(8,128)(2,1)} %get-tuple-element.47), channel_id=1, source_target_pairs={{0,24},{4,28},{8,16},{12,20},{16,8},{20,12},{24,0},{28,4},{1,25},{... | collective-permute-start | bytes 294920 | tf_op jit(solution)/shard_map/ppermute | solution.py:31
  6.8 2.0 %pack_query_cot.1 = (bf16[256,128]{1,0:T(8,128)(2,1)}, bf16[256,128]{1,0:T(8,128)(2,1)}, bf16[256,128]{1,0:T(8,128)(2,1)}, bf16[256,128]{1,0:T(8,128)(2,1)}, bf1...) custom-call(bf16[128,1024]{1,0:T(8,128)(2,1)} %refs_8_.5, ...), custom_call_target="tpu_custom_call" | custom-call | tf_op jit(solution)/shard_map/pack_query_cot/pallas_call | solution.py:54
  8.8 2.4 %collective-permute-start = (bf16[256,128]{1,0:T(8,128)(2,1)}, bf16[256,128]{1,0:T(8,128)(2,1)S(1)}, u32[]{:S(2)}, u32[]{:S(2)}) collective-permute-start(bf16[256,128]{1,0:T(8,128)(2,1)} %get-tuple-element.38), channel_id=1, source_target_pairs={{0,28},{4,24},{8,20},{12,16},{16,12},{20,8},{24,4},{28,0},{1,29},{... | collective-permute-start | bytes 196616 | tf_op jit(solution)/shard_map/ppermute | solution.py:31
  11.4 1.2 %collective-permute-start.9 = (bf16[384,128]{1,0:T(8,128)(2,1)}, bf16[384,128]{1,0:T(8,128)(2,1)S(1)}, u32[]{:S(2)}, u32[]{:S(2)}) collective-permute-start(bf16[384,128]{1,0:T(8,128)(2,1)} %get-tuple-element.48), channel_id=1, source_target_pairs={{0,20},{4,16},{8,28},{12,24},{16,4},{20,0},{24,12},{28,8},{1,21},{... | collective-permute-start | bytes 294920 | tf_op jit(solution)/shard_map/ppermute | solution.py:31
  12.6 1.5 %collective-permute-done.refs_1_ = bf16[256,128]{1,0:T(8,128)(2,1)S(1)} collective-permute-done((bf16[256,128]{1,0:T(8,128)(2,1)}, bf16[256,128]{1,0:T(8,128)(2,1)S(1)}, u32[]{:S(2)}, u32[]{:S(2)}) %collective-permute-start) | collective-permute-done | bytes 65568 | tf_op jit(solution)/shard_map/ppermute | solution.py:31
  14.1 1.1 %collective-permute-start.10 = (bf16[384,128]{1,0:T(8,128)(2,1)}, bf16[384,128]{1,0:T(8,128)(2,1)S(1)}, u32[]{:S(2)}, u32[]{:S(2)}) collective-permute-start(bf16[384,128]{1,0:T(8,128)(2,1)} %get-tuple-element.49), channel_id=1, source_target_pairs={{0,16},{4,20},{8,24},{12,28},{16,0},{20,4},{24,8},{28,12},{1,17},{... | collective-permute-start | bytes 294920 | tf_op jit(solution)/shard_map/ppermute | solution.py:31
  15.2 1.4 %collective-permute-done.1.refs_2_ = bf16[256,128]{1,0:T(8,128)(2,1)S(1)} collective-permute-done((bf16[256,128]{1,0:T(8,128)(2,1)}, bf16[256,128]{1,0:T(8,128)(2,1)S(1)}, u32[]{:S(2)}, u32[]{:S(2)}) %collective-permute-start.1) | collective-permute-done | bytes 65568 | tf_op jit(solution)/shard_map/ppermute | solution.py:31
  16.9 0.3 collective-permute-start.12
  17.2 1.2 %collective-permute-start.13 = (bf16[384,128]{1,0:T(8,128)(2,1)}, bf16[384,128]{1,0:T(8,128)(2,1)S(1)}, u32[]{:S(2)}, u32[]{:S(2)}) collective-permute-start(bf16[384,128]{1,0:T(8,128)(2,1)} %get-tuple-element.52), channel_id=1, source_target_pairs={{0,4},{4,0},{8,12},{12,8},{16,20},{20,16},{24,28},{28,24},{1,5},{5... | collective-permute-start | bytes 294920 | tf_op jit(solution)/shard_map/ppermute | solution.py:31
  18.5 0.5 collective-permute-start.2
  18.9 1.3 %collective-permute-done.10.refs_4_ = bf16[384,128]{1,0:T(8,128)(2,1)S(1)} collective-permute-done((bf16[384,128]{1,0:T(8,128)(2,1)}, bf16[384,128]{1,0:T(8,128)(2,1)S(1)}, u32[]{:S(2)}, u32[]{:S(2)}) %collective-permute-start.10) | collective-permute-done | bytes 98336 | tf_op jit(solution)/shard_map/ppermute | solution.py:31
  20.2 1.1 %collective-permute-start.3 = (bf16[256,128]{1,0:T(8,128)(2,1)}, bf16[256,128]{1,0:T(8,128)(2,1)S(1)}, u32[]{:S(2)}, u32[]{:S(2)}) collective-permute-start(bf16[256,128]{1,0:T(8,128)(2,1)} %get-tuple-element.41), channel_id=1, source_target_pairs={{0,16},{4,20},{8,24},{12,28},{16,0},{20,4},{24,8},{28,12},{1,17},{... | collective-permute-start | bytes 196616 | tf_op jit(solution)/shard_map/ppermute | solution.py:31
  21.5 1.0 %collective-permute-start.4 = (bf16[256,128]{1,0:T(8,128)(2,1)}, bf16[256,128]{1,0:T(8,128)(2,1)S(1)}, u32[]{:S(2)}, u32[]{:S(2)}) collective-permute-start(bf16[256,128]{1,0:T(8,128)(2,1)} %get-tuple-element.42), channel_id=1, source_target_pairs={{0,12},{4,8},{8,4},{12,0},{16,28},{20,24},{24,20},{28,16},{1,13},{... | collective-permute-start | bytes 196616 | tf_op jit(solution)/shard_map/ppermute | solution.py:31
  22.8 1.8 %collective-permute-start.5 = (bf16[256,128]{1,0:T(8,128)(2,1)}, bf16[256,128]{1,0:T(8,128)(2,1)S(1)}, u32[]{:S(2)}, u32[]{:S(2)}) collective-permute-start(bf16[256,128]{1,0:T(8,128)(2,1)} %get-tuple-element.43), channel_id=1, source_target_pairs={{0,8},{4,12},{8,0},{12,4},{16,24},{20,28},{24,16},{28,20},{1,9},{5... | collective-permute-start | bytes 196616 | tf_op jit(solution)/shard_map/ppermute | solution.py:31
  24.6 1.6 %copy-done = bf16[4,2,256,512]{3,2,1,0:T(8,128)(2,1)S(1)} copy-done((bf16[4,2,256,512]{3,2,1,0:T(8,128)(2,1)S(1)}, bf16[4,2,256,512]{3,2,1,0:T(8,128)(2,1)}, u32[]{:S(2)}) %copy-start) | copy-done | bytes 2097176
  26.2 1.6 %copy-done.2 = bf16[4,2,512,256]{3,2,1,0:T(8,128)(2,1)S(1)} copy-done((bf16[4,2,512,256]{3,2,1,0:T(8,128)(2,1)S(1)}, bf16[4,2,512,256]{3,2,1,0:T(8,128)(2,1)}, u32[]{:S(2)}) %copy-start.2) | copy-done | bytes 2097176
  27.8 0.8 %copy-done.7 = f32[3,3,1024]{2,1,0:T(4,128)S(1)} copy-done((f32[3,3,1024]{2,1,0:T(4,128)S(1)}, f32[3,3,1024]{2,1,0:T(4,128)}, u32[]{:S(2)}) %copy-start.7) | copy-done | bytes 36888
  28.6 0.9 %copy-done.9 = bf16[384,128]{1,0:T(8,128)(2,1)S(1)} copy-done((bf16[384,128]{1,0:T(8,128)(2,1)S(1)}, bf16[384,128]{1,0:T(8,128)(2,1)}, u32[]{:S(2)}) %copy-start.9) | copy-done | bytes 98328
  29.5 2.6 %key_value_channels.1 = (f32[1040,128]{1,0:T(8,128)S(1)}, f32[1040,128]{1,0:T(8,128)S(1)}, f32[4,256,128]{2,1,0:T(8,128)S(1)}, f32[4,256,128]{2,1,0:T(8,128)S(1)...) custom-call(bf16[384,128]{1,0:T(8,128)(2,1)S(1)} %copy-done.9, ...), custom_call_target="tpu_custom_call" | custom-call | flops 1610612736 | bytes 8388608 | tf_op jit(solution)/shard_map/key_value_channels/pallas_call | solution.py:204
  32.2 3.5 %gradient_channels.1 = (bf16[432,128]{1,0:T(8,128)(2,1)S(1)}, bf16[432,128]{1,0:T(8,128)(2,1)S(1)}, bf16[432,128]{1,0:T(8,128)(2,1)S(1)}, bf16[432,128]{1,0:T(8,...) custom-call(bf16[256,128]{1,0:T(8,128)(2,1)S(1)} %copy-done.8, ...), custom_call_target="tpu_custom_call" | custom-call | tf_op jit(solution)/shard_map/gradient_channels/pallas_call | solution.py:332
  35.7 1.7 %collective-permute-start.14 = (bf16[432,128]{1,0:T(8,128)(2,1)S(1)}, bf16[432,128]{1,0:T(8,128)(2,1)S(1)}, u32[]{:S(2)}, u32[]{:S(2)}) collective-permute-start(bf16[432,128]{1,0:T(8,128)(2,1)S(1)} %get-tuple-element.61), channel_id=1, source_target_pairs={{0,28},{4,24},{8,20},{12,16},{16,12},{20,8},{24,4},{28,0},{1,29},{... | collective-permute-start | bytes 331784 | tf_op jit(solution)/shard_map/ppermute | solution.py:31
  37.4 1.4 %collective-permute-start.15 = (bf16[432,128]{1,0:T(8,128)(2,1)S(1)}, bf16[432,128]{1,0:T(8,128)(2,1)S(1)}, u32[]{:S(2)}, u32[]{:S(2)}) collective-permute-start(bf16[432,128]{1,0:T(8,128)(2,1)S(1)} %get-tuple-element.62), channel_id=1, source_target_pairs={{0,24},{4,28},{8,16},{12,20},{16,8},{20,12},{24,0},{28,4},{1,25},{... | collective-permute-start | bytes 331784 | tf_op jit(solution)/shard_map/ppermute | solution.py:31
  39.0 1.2 %collective-permute-start.17 = (bf16[432,128]{1,0:T(8,128)(2,1)S(1)}, bf16[432,128]{1,0:T(8,128)(2,1)S(1)}, u32[]{:S(2)}, u32[]{:S(2)}) collective-permute-start(bf16[432,128]{1,0:T(8,128)(2,1)S(1)} %get-tuple-element.64), channel_id=1, source_target_pairs={{0,16},{4,20},{8,24},{12,28},{16,0},{20,4},{24,8},{28,12},{1,17},{... | collective-permute-start | bytes 331784 | tf_op jit(solution)/shard_map/ppermute | solution.py:31
  40.2 0.4 collective-permute-start.18
  40.6 0.8 %collective-permute-done.14.refs_1_ = bf16[432,128]{1,0:T(8,128)(2,1)S(1)} collective-permute-done((bf16[432,128]{1,0:T(8,128)(2,1)S(1)}, bf16[432,128]{1,0:T(8,128)(2,1)S(1)}, u32[]{:S(2)}, u32[]{:S(2)}) %collective-permute-start.14) | collective-permute-done | bytes 110624 | tf_op jit(solution)/shard_map/ppermute | solution.py:31
  41.4 0.9 %collective-permute-start.19 = (bf16[432,128]{1,0:T(8,128)(2,1)S(1)}, bf16[432,128]{1,0:T(8,128)(2,1)S(1)}, u32[]{:S(2)}, u32[]{:S(2)}) collective-permute-start(bf16[432,128]{1,0:T(8,128)(2,1)S(1)} %get-tuple-element.66), channel_id=1, source_target_pairs={{0,8},{4,12},{8,0},{12,4},{16,24},{20,28},{24,16},{28,20},{1,9},{5... | collective-permute-start | bytes 331784 | tf_op jit(solution)/shard_map/ppermute | solution.py:31
  42.3 2.8 %collective-permute-done.15.refs_2_ = bf16[432,128]{1,0:T(8,128)(2,1)S(1)} collective-permute-done((bf16[432,128]{1,0:T(8,128)(2,1)S(1)}, bf16[432,128]{1,0:T(8,128)(2,1)S(1)}, u32[]{:S(2)}, u32[]{:S(2)}) %collective-permute-start.15) | collective-permute-done | bytes 110624 | tf_op jit(solution)/shard_map/ppermute | solution.py:31
  45.1 1.7 %collective-permute-done.16.refs_3_ = bf16[432,128]{1,0:T(8,128)(2,1)S(1)} collective-permute-done((bf16[432,128]{1,0:T(8,128)(2,1)S(1)}, bf16[432,128]{1,0:T(8,128)(2,1)S(1)}, u32[]{:S(2)}, u32[]{:S(2)}) %collective-permute-start.16) | collective-permute-done | bytes 110624 | tf_op jit(solution)/shard_map/ppermute | solution.py:31
  46.8 2.4 %collective-permute-done.17.refs_4_ = bf16[432,128]{1,0:T(8,128)(2,1)S(1)} collective-permute-done((bf16[432,128]{1,0:T(8,128)(2,1)S(1)}, bf16[432,128]{1,0:T(8,128)(2,1)S(1)}, u32[]{:S(2)}, u32[]{:S(2)}) %collective-permute-start.17) | collective-permute-done | bytes 110624 | tf_op jit(solution)/shard_map/ppermute | solution.py:31
  49.2 2.1 %token_outputs.1 = (bf16[128,1024]{1,0:T(8,128)(2,1)}, bf16[128,1024]{1,0:T(8,128)(2,1)}, bf16[128,1024]{1,0:T(8,128)(2,1)}, bf16[128,1024]{1,0:T(8,128)(2,1)}, ...) custom-call(bf16[432,128]{1,0:T(8,128)(2,1)S(1)} %get-tuple-element.60.refs_0_, ...), custom_call_target="tpu_custom_call" | custom-call | tf_op jit(solution)/shard_map/token_outputs/pallas_call | solution.py:420
  (35 shorter events, 1.2 us)
Async XLA Ops:
  2.9 14.0 %collective-permute-start.7 = (bf16[384,128]{1,0:T(8,128)(2,1)}, bf16[384,128]{1,0:T(8,128)(2,1)S(1)}, u32[]{:S(2)}, u32[]{:S(2)}) collective-permute-start(bf16[384,128]{1,0:T(8,128)(2,1)} %get-tuple-element.46), channel_id=1, source_target_pairs={{0,28},{4,24},{8,20},{12,16},{16,12},{20,8},{24,4},{28,0},{1,29},{... | collective-permute-start | bytes 294920 | tf_op jit(solution)/shard_map/ppermute | solution.py:31
  6.2 11.0 %collective-permute-start.8 = (bf16[384,128]{1,0:T(8,128)(2,1)}, bf16[384,128]{1,0:T(8,128)(2,1)S(1)}, u32[]{:S(2)}, u32[]{:S(2)}) collective-permute-start(bf16[384,128]{1,0:T(8,128)(2,1)} %get-tuple-element.47), channel_id=1, source_target_pairs={{0,24},{4,28},{8,16},{12,20},{16,8},{20,12},{24,0},{28,4},{1,25},{... | collective-permute-start | bytes 294920 | tf_op jit(solution)/shard_map/ppermute | solution.py:31
  8.8 5.2 %collective-permute-start = (bf16[256,128]{1,0:T(8,128)(2,1)}, bf16[256,128]{1,0:T(8,128)(2,1)S(1)}, u32[]{:S(2)}, u32[]{:S(2)}) collective-permute-start(bf16[256,128]{1,0:T(8,128)(2,1)} %get-tuple-element.38), channel_id=1, source_target_pairs={{0,28},{4,24},{8,20},{12,16},{16,12},{20,8},{24,4},{28,0},{1,29},{... | collective-permute-start | bytes 196616 | tf_op jit(solution)/shard_map/ppermute | solution.py:31
  11.2 5.4 %collective-permute-start.1 = (bf16[256,128]{1,0:T(8,128)(2,1)}, bf16[256,128]{1,0:T(8,128)(2,1)S(1)}, u32[]{:S(2)}, u32[]{:S(2)}) collective-permute-start(bf16[256,128]{1,0:T(8,128)(2,1)} %get-tuple-element.39), channel_id=1, source_target_pairs={{0,24},{4,28},{8,16},{12,20},{16,8},{20,12},{24,0},{28,4},{1,25},{... | collective-permute-start | bytes 196616 | tf_op jit(solution)/shard_map/ppermute | solution.py:31
  11.4 7.1 %collective-permute-start.9 = (bf16[384,128]{1,0:T(8,128)(2,1)}, bf16[384,128]{1,0:T(8,128)(2,1)S(1)}, u32[]{:S(2)}, u32[]{:S(2)}) collective-permute-start(bf16[384,128]{1,0:T(8,128)(2,1)} %get-tuple-element.48), channel_id=1, source_target_pairs={{0,20},{4,16},{8,28},{12,24},{16,4},{20,0},{24,12},{28,8},{1,21},{... | collective-permute-start | bytes 294920 | tf_op jit(solution)/shard_map/ppermute | solution.py:31
  14.1 6.2 %collective-permute-start.10 = (bf16[384,128]{1,0:T(8,128)(2,1)}, bf16[384,128]{1,0:T(8,128)(2,1)S(1)}, u32[]{:S(2)}, u32[]{:S(2)}) collective-permute-start(bf16[384,128]{1,0:T(8,128)(2,1)} %get-tuple-element.49), channel_id=1, source_target_pairs={{0,16},{4,20},{8,24},{12,28},{16,0},{20,4},{24,8},{28,12},{1,17},{... | collective-permute-start | bytes 294920 | tf_op jit(solution)/shard_map/ppermute | solution.py:31
  16.6 4.9 %collective-permute-start.11 = (bf16[384,128]{1,0:T(8,128)(2,1)}, bf16[384,128]{1,0:T(8,128)(2,1)S(1)}, u32[]{:S(2)}, u32[]{:S(2)}) collective-permute-start(bf16[384,128]{1,0:T(8,128)(2,1)} %get-tuple-element.50), channel_id=1, source_target_pairs={{0,12},{4,8},{8,4},{12,0},{16,28},{20,24},{24,20},{28,16},{1,13},{... | collective-permute-start | bytes 294920 | tf_op jit(solution)/shard_map/ppermute | solution.py:31
  16.9 5.9 %collective-permute-start.12 = (bf16[384,128]{1,0:T(8,128)(2,1)}, bf16[384,128]{1,0:T(8,128)(2,1)S(1)}, u32[]{:S(2)}, u32[]{:S(2)}) collective-permute-start(bf16[384,128]{1,0:T(8,128)(2,1)} %get-tuple-element.51), channel_id=1, source_target_pairs={{0,8},{4,12},{8,0},{12,4},{16,24},{20,28},{24,16},{28,20},{1,9},{5... | collective-permute-start | bytes 294920 | tf_op jit(solution)/shard_map/ppermute | solution.py:31
  17.2 7.4 %collective-permute-start.13 = (bf16[384,128]{1,0:T(8,128)(2,1)}, bf16[384,128]{1,0:T(8,128)(2,1)S(1)}, u32[]{:S(2)}, u32[]{:S(2)}) collective-permute-start(bf16[384,128]{1,0:T(8,128)(2,1)} %get-tuple-element.52), channel_id=1, source_target_pairs={{0,4},{4,0},{8,12},{12,8},{16,20},{20,16},{24,28},{28,24},{1,5},{5... | collective-permute-start | bytes 294920 | tf_op jit(solution)/shard_map/ppermute | solution.py:31
  18.5 13.6 %collective-permute-start.2 = (bf16[256,128]{1,0:T(8,128)(2,1)}, bf16[256,128]{1,0:T(8,128)(2,1)S(1)}, u32[]{:S(2)}, u32[]{:S(2)}) collective-permute-start(bf16[256,128]{1,0:T(8,128)(2,1)} %get-tuple-element.40), channel_id=1, source_target_pairs={{0,20},{4,16},{8,28},{12,24},{16,4},{20,0},{24,12},{28,8},{1,21},{... | collective-permute-start | bytes 196616 | tf_op jit(solution)/shard_map/ppermute | solution.py:31
  20.2 11.9 %collective-permute-start.3 = (bf16[256,128]{1,0:T(8,128)(2,1)}, bf16[256,128]{1,0:T(8,128)(2,1)S(1)}, u32[]{:S(2)}, u32[]{:S(2)}) collective-permute-start(bf16[256,128]{1,0:T(8,128)(2,1)} %get-tuple-element.41), channel_id=1, source_target_pairs={{0,16},{4,20},{8,24},{12,28},{16,0},{20,4},{24,8},{28,12},{1,17},{... | collective-permute-start | bytes 196616 | tf_op jit(solution)/shard_map/ppermute | solution.py:31
  21.5 10.7 %collective-permute-start.4 = (bf16[256,128]{1,0:T(8,128)(2,1)}, bf16[256,128]{1,0:T(8,128)(2,1)S(1)}, u32[]{:S(2)}, u32[]{:S(2)}) collective-permute-start(bf16[256,128]{1,0:T(8,128)(2,1)} %get-tuple-element.42), channel_id=1, source_target_pairs={{0,12},{4,8},{8,4},{12,0},{16,28},{20,24},{24,20},{28,16},{1,13},{... | collective-permute-start | bytes 196616 | tf_op jit(solution)/shard_map/ppermute | solution.py:31
  22.8 9.4 %collective-permute-start.5 = (bf16[256,128]{1,0:T(8,128)(2,1)}, bf16[256,128]{1,0:T(8,128)(2,1)S(1)}, u32[]{:S(2)}, u32[]{:S(2)}) collective-permute-start(bf16[256,128]{1,0:T(8,128)(2,1)} %get-tuple-element.43), channel_id=1, source_target_pairs={{0,8},{4,12},{8,0},{12,4},{16,24},{20,28},{24,16},{28,20},{1,9},{5... | collective-permute-start | bytes 196616 | tf_op jit(solution)/shard_map/ppermute | solution.py:31
  24.6 7.6 %collective-permute-start.6 = (bf16[256,128]{1,0:T(8,128)(2,1)}, bf16[256,128]{1,0:T(8,128)(2,1)S(1)}, u32[]{:S(2)}, u32[]{:S(2)}) collective-permute-start(bf16[256,128]{1,0:T(8,128)(2,1)} %get-tuple-element.44), channel_id=1, source_target_pairs={{0,4},{4,0},{8,12},{12,8},{16,20},{20,16},{24,28},{28,24},{1,5},{5... | collective-permute-start | bytes 196616 | tf_op jit(solution)/shard_map/ppermute | solution.py:31
  24.6 1.6 %copy-start = (bf16[4,2,256,512]{3,2,1,0:T(8,128)(2,1)S(1)}, bf16[4,2,256,512]{3,2,1,0:T(8,128)(2,1)}, u32[]{:S(2)}) copy-start(bf16[4,2,256,512]{3,2,1,0:T(8,128)(2,1)} %constant.5.clone.refs_10_) | copy-start | bytes 6291460
  26.2 1.6 %copy-start.2 = (bf16[4,2,512,256]{3,2,1,0:T(8,128)(2,1)S(1)}, bf16[4,2,512,256]{3,2,1,0:T(8,128)(2,1)}, u32[]{:S(2)}) copy-start(bf16[4,2,512,256]{3,2,1,0:T(8,128)(2,1)} %constant.4.clone.refs_9_) | copy-start | bytes 6291460
  27.8 0.8 %copy-start.7 = (f32[3,3,1024]{2,1,0:T(4,128)S(1)}, f32[3,3,1024]{2,1,0:T(4,128)}, u32[]{:S(2)}) copy-start(f32[3,3,1024]{2,1,0:T(4,128)} %refs_12_.1) | copy-start | bytes 110596
  28.6 0.9 %copy-start.9 = (bf16[384,128]{1,0:T(8,128)(2,1)S(1)}, bf16[384,128]{1,0:T(8,128)(2,1)}, u32[]{:S(2)}) copy-start(bf16[384,128]{1,0:T(8,128)(2,1)} %get-tuple-element.45.refs_0_) | copy-start | bytes 294916
  29.5 2.7 %copy-start.1 = (bf16[4,2,256,512]{3,2,1,0:T(8,128)(2,1)S(1)}, bf16[4,2,256,512]{3,2,1,0:T(8,128)(2,1)}, u32[]{:S(2)}) copy-start(bf16[4,2,256,512]{3,2,1,0:T(8,128)(2,1)} %constant.5.clone.refs_10_) | copy-start | bytes 6291460
  29.5 2.7 %copy-start.8 = (bf16[256,128]{1,0:T(8,128)(2,1)S(1)}, bf16[256,128]{1,0:T(8,128)(2,1)}, u32[]{:S(2)}) copy-start(bf16[256,128]{1,0:T(8,128)(2,1)} %get-tuple-element.37.refs_0_) | copy-start | bytes 196612
  32.2 17.0 %copy-start.3 = (bf16[128,1024]{1,0:T(8,128)(2,1)S(1)}, bf16[128,1024]{1,0:T(8,128)(2,1)}, u32[]{:S(2)}) copy-start(bf16[128,1024]{1,0:T(8,128)(2,1)} %refs_8_.5) | copy-start | bytes 786436
  32.2 17.0 %copy-start.4 = (bf16[128,1024]{1,0:T(8,128)(2,1)S(1)}, bf16[128,1024]{1,0:T(8,128)(2,1)}, u32[]{:S(2)}) copy-start(bf16[128,1024]{1,0:T(8,128)(2,1)} %refs_11_.1) | copy-start | bytes 786436
  32.2 17.0 %copy-start.5 = (bf16[128,1024]{1,0:T(8,128)(2,1)S(1)}, bf16[128,1024]{1,0:T(8,128)(2,1)}, u32[]{:S(2)}) copy-start(bf16[128,1024]{1,0:T(8,128)(2,1)} %refs_9_.3) | copy-start | bytes 786436
  32.2 17.0 %copy-start.6 = (bf16[128,1024]{1,0:T(8,128)(2,1)S(1)}, bf16[128,1024]{1,0:T(8,128)(2,1)}, u32[]{:S(2)}) copy-start(bf16[128,1024]{1,0:T(8,128)(2,1)} %refs_10_.3) | copy-start | bytes 786436
  35.7 5.7 %collective-permute-start.14 = (bf16[432,128]{1,0:T(8,128)(2,1)S(1)}, bf16[432,128]{1,0:T(8,128)(2,1)S(1)}, u32[]{:S(2)}, u32[]{:S(2)}) collective-permute-start(bf16[432,128]{1,0:T(8,128)(2,1)S(1)} %get-tuple-element.61), channel_id=1, source_target_pairs={{0,28},{4,24},{8,20},{12,16},{16,12},{20,8},{24,4},{28,0},{1,29},{... | collective-permute-start | bytes 331784 | tf_op jit(solution)/shard_map/ppermute | solution.py:31
  37.4 7.7 %collective-permute-start.15 = (bf16[432,128]{1,0:T(8,128)(2,1)S(1)}, bf16[432,128]{1,0:T(8,128)(2,1)S(1)}, u32[]{:S(2)}, u32[]{:S(2)}) collective-permute-start(bf16[432,128]{1,0:T(8,128)(2,1)S(1)} %get-tuple-element.62), channel_id=1, source_target_pairs={{0,24},{4,28},{8,16},{12,20},{16,8},{20,12},{24,0},{28,4},{1,25},{... | collective-permute-start | bytes 331784 | tf_op jit(solution)/shard_map/ppermute | solution.py:31
  38.8 8.0 %collective-permute-start.16 = (bf16[432,128]{1,0:T(8,128)(2,1)S(1)}, bf16[432,128]{1,0:T(8,128)(2,1)S(1)}, u32[]{:S(2)}, u32[]{:S(2)}) collective-permute-start(bf16[432,128]{1,0:T(8,128)(2,1)S(1)} %get-tuple-element.63), channel_id=1, source_target_pairs={{0,20},{4,16},{8,28},{12,24},{16,4},{20,0},{24,12},{28,8},{1,21},{... | collective-permute-start | bytes 331784 | tf_op jit(solution)/shard_map/ppermute | solution.py:31
  39.0 10.2 %collective-permute-start.17 = (bf16[432,128]{1,0:T(8,128)(2,1)S(1)}, bf16[432,128]{1,0:T(8,128)(2,1)S(1)}, u32[]{:S(2)}, u32[]{:S(2)}) collective-permute-start(bf16[432,128]{1,0:T(8,128)(2,1)S(1)} %get-tuple-element.64), channel_id=1, source_target_pairs={{0,16},{4,20},{8,24},{12,28},{16,0},{20,4},{24,8},{28,12},{1,17},{... | collective-permute-start | bytes 331784 | tf_op jit(solution)/shard_map/ppermute | solution.py:31
  40.2 9.0 %collective-permute-start.18 = (bf16[432,128]{1,0:T(8,128)(2,1)S(1)}, bf16[432,128]{1,0:T(8,128)(2,1)S(1)}, u32[]{:S(2)}, u32[]{:S(2)}) collective-permute-start(bf16[432,128]{1,0:T(8,128)(2,1)S(1)} %get-tuple-element.65), channel_id=1, source_target_pairs={{0,12},{4,8},{8,4},{12,0},{16,28},{20,24},{24,20},{28,16},{1,13},{... | collective-permute-start | bytes 331784 | tf_op jit(solution)/shard_map/ppermute | solution.py:31
  41.4 7.8 %collective-permute-start.19 = (bf16[432,128]{1,0:T(8,128)(2,1)S(1)}, bf16[432,128]{1,0:T(8,128)(2,1)S(1)}, u32[]{:S(2)}, u32[]{:S(2)}) collective-permute-start(bf16[432,128]{1,0:T(8,128)(2,1)S(1)} %get-tuple-element.66), channel_id=1, source_target_pairs={{0,8},{4,12},{8,0},{12,4},{16,24},{20,28},{24,16},{28,20},{1,9},{5... | collective-permute-start | bytes 331784 | tf_op jit(solution)/shard_map/ppermute | solution.py:31
  45.1 4.1 %collective-permute-start.20 = (bf16[432,128]{1,0:T(8,128)(2,1)S(1)}, bf16[432,128]{1,0:T(8,128)(2,1)S(1)}, u32[]{:S(2)}, u32[]{:S(2)}) collective-permute-start(bf16[432,128]{1,0:T(8,128)(2,1)S(1)} %get-tuple-element.67), channel_id=1, source_target_pairs={{0,4},{4,0},{8,12},{12,8},{16,20},{20,16},{24,28},{28,24},{1,5},{5... | collective-permute-start | bytes 331784 | tf_op jit(solution)/shard_map/ppermute | solution.py:31
where the time goes:
time: 51.7 us; the launch traced here: 51.4 us
  starting transfers between devices  20.8 us (40%)
  Pallas kernels  12.5 us (24%)
  waiting for transfers between devices  12.3 us (24%)
  local copies, waits for them, and re-layouts  4.9 us (9%)
  between operations  0.8 us (2%)
    ppermute x21, starting transfers between devices, exchange(): lax.ppermute(block, 'ctx', [(i, i ^ step) for i in range(peers)])  20.8 us
    ppermute x21, waiting for transfers between devices, exchange(): lax.ppermute(block, 'ctx', [(i, i ^ step) for i in range(peers)])  12.3 us
    unnamed x20, local copies, waits for them, and re-layouts  4.9 us
    pallas_call x2, Pallas kernels, pack(): pl.pallas_call(functools.partial(pack_kernel, len(arrays)), in_specs=in_v...  4.24 us
    pallas_call x1, Pallas kernels, gradient_step(): pl.pallas_call(functools.partial(gradient_kernel, tokens, peers, 1.0 / ma...  3.51 us
    pallas_call x1, Pallas kernels, key_value_step(): pl.pallas_call(functools.partial(key_value_kernel, tokens, peers), in_spe...  2.63 us
    pallas_call x1, Pallas kernels, token_step(): pl.pallas_call(functools.partial(token_kernel, peers, extra_rows(short_we...  2.13 us
  transfers between devices with their start and end apart: 21, of which 9 were waited for; matrix products, arithmetic and copies ran while one was open for 0% of the time, Pallas kernels for 9%

commit v1 on v0

--- a/solution.py
+++ b/solution.py
@@ -17,7 +17,8 @@
 PAD = 8
 RIM = 2
 PIECES = 3
-VMEM_LIMIT = 24 * 1024 * 1024
+MIB = 1024 * 1024
+VMEM_LIMIT = 24 * MIB
 
 
 def partners(peers):
@@ -40,8 +41,8 @@
     return pl.ds(pl.multiple_of(place * LANES, LANES), LANES)
 
 
-def pack_kernel(count, *refs):
-    sources, packed = refs[:count], refs[count:]
+def pack_kernel(count, waits, *refs):
+    sources, packed = refs[:count], refs[count + waits :]
     tokens = sources[0].shape[0]
     me = lax.axis_index("ctx")
     for step, target in zip(partners(len(packed)), packed):
@@ -49,15 +50,16 @@
             target[at * tokens : (at + 1) * tokens, :] = source[:, lanes_of(me ^ step)].astype(BF16)
 
 
-def pack(name, arrays, peers):
+def pack(name, arrays, peers, after=()):
     tokens = arrays[0].shape[0]
     return pl.pallas_call(
-        functools.partial(pack_kernel, len(arrays)),
-        in_specs=in_vmem(len(arrays)),
+        functools.partial(pack_kernel, len(arrays), len(after)),
+        in_specs=in_vmem(len(arrays)) + [pl.BlockSpec(memory_space=pl.ANY)] * len(after),
         out_specs=in_vmem(peers),
         out_shape=[jax.ShapeDtypeStruct((len(arrays) * tokens, LANES), BF16)] * peers,
+        cost_estimate=pl.CostEstimate(flops=0, bytes_accessed=8 * MIB, transcendentals=0),
         name=name,
-    )(*arrays)
+    )(*arrays, *after)
 
 
 @functools.lru_cache(maxsize=None)
@@ -147,16 +149,12 @@
 
 def key_value_kernel(tokens, peers, *refs):
     arrived = refs[:peers]
-    weights, forward_far, backward_far = refs[peers : peers + 3]
+    weights, forward, backward = refs[peers : peers + 3]
     key, value, key_short, value_short, prod_spec, filt_spec, conv = refs[peers + 3 : peers + 10]
-    taps, forward, backward, signals, spectra, pieces, sems = refs[peers + 10 :]
+    taps, signals, spectra, pieces = refs[peers + 10 :]
     size = peers * tokens // PHASES
     me = lax.axis_index("ctx")
     own = lanes_of(me)
-    get_forward = pltpu.make_async_copy(forward_far, forward, sems.at[0])
-    get_backward = pltpu.make_async_copy(backward_far, backward, sems.at[1])
-    get_forward.start()
-    get_backward.start()
     for ref in (key, value, conv):
         clear_ends(ref)
     for step, source in zip(partners(peers), arrived):
@@ -170,7 +168,6 @@
         value_short[r] = short_phases(value, weights, 2, own, r, size)
         signals[r, :, :LANES] = (key_short[r] * value_short[r]).astype(BF16)
         signals[r, :, LANES:] = phase(taps, r, size).astype(BF16)
-    get_forward.wait()
     for r in range(PHASES):
         spectra[r] = forward_transform(forward[r], signals[r])
     for chunk in range(size // TILE):
@@ -188,7 +185,6 @@
         for r, pair in enumerate(inverse_mix(times(*mixed))):
             for rows, part in zip((real, imag), pair):
                 split_store(pieces, r, rows, slice(0, LANES), part)
-    get_backward.wait()
     for r in range(PHASES):
         result = inverse_transform(backward[r], pieces[r])
         conv[pl.ds(PAD + r, size, stride=PHASES), :] = result.astype(BF16).astype(F32)
@@ -203,22 +199,19 @@
     spectrum = jax.ShapeDtypeStruct((PHASES, 2 * size, LANES), F32)
     return pl.pallas_call(
         functools.partial(key_value_kernel, tokens, peers),
-        in_specs=in_vmem(peers + 1) + [pl.BlockSpec(memory_space=pltpu.HBM)] * 2,
+        in_specs=in_vmem(peers + 3),
         out_specs=in_vmem(7),
         out_shape=[padded, padded, phases, phases, spectrum, spectrum, padded],
         scratch_shapes=[
             pltpu.VMEM((seq_len, LANES), F32),
-            pltpu.VMEM(tables[0].shape, BF16),
-            pltpu.VMEM(tables[1].shape, BF16),
             pltpu.VMEM((PHASES, size, 2 * LANES), BF16),
             pltpu.VMEM((PHASES, 2 * size, 2 * LANES), F32),
             pltpu.VMEM((PHASES, 2 * size, 2 * LANES), BF16),
-            pltpu.SemaphoreType.DMA((2,)),
         ],
         compiler_params=pltpu.CompilerParams(vmem_limit_bytes=VMEM_LIMIT),
         cost_estimate=pl.CostEstimate(
             flops=2 * 24 * PHASES * size * size * LANES,
-            bytes_accessed=8 * 1024 * 1024,
+            bytes_accessed=8 * MIB,
             transcendentals=0,
         ),
         name="key_value_channels",
@@ -232,7 +225,7 @@
 
 def gradient_kernel(tokens, peers, grad_scale, *refs):
     arrived = refs[:peers]
-    weights, forward_far, backward_far = refs[peers : peers + 3]
+    weights, forward, backward = refs[peers : peers + 3]
     key, value, key_short, value_short, prod_spec, filt_spec, conv = refs[peers + 3 : peers + 10]
     out = refs[peers + 10 : 2 * peers + 10]
     (
@@ -240,22 +233,15 @@
         cot,
         conv_grad,
         filter_grad,
-        forward,
-        backward,
         signals,
         spectra,
         pieces,
         extra,
-        sems,
     ) = refs[2 * peers + 10 :]
     size = peers * tokens // PHASES
     tap_count = weights.shape[1]
     me = lax.axis_index("ctx")
     own = lanes_of(me)
-    get_forward = pltpu.make_async_copy(forward_far, forward, sems.at[0])
-    get_backward = pltpu.make_async_copy(backward_far, backward, sems.at[1])
-    get_forward.start()
-    get_backward.start()
     for ref in (query, cot, conv_grad):
         clear_ends(ref)
     for step, source in zip(partners(peers), arrived):
@@ -265,7 +251,6 @@
     for r in range(PHASES):
         query_short = short_phases(query, weights, 0, own, r, size)
         signals[r] = (phase(cot, PAD + r, size) * query_short).astype(BF16)
-    get_forward.wait()
     for r in range(PHASES):
         spectra[r] = forward_transform(forward[r], signals[r])
     for chunk in range(size // TILE):
@@ -277,7 +262,6 @@
             for r, pair in enumerate(inverse_mix(conj_times(known, grad))):
                 for rows, part in zip((real, imag), pair):
                     split_store(pieces, r, rows, slice(at * LANES, (at + 1) * LANES), part)
-    get_backward.wait()
     for r in range(PHASES):
         result = inverse_transform(backward[r], pieces[r])
         conv_grad[pl.ds(PAD + r, size, stride=PHASES), :] = (
@@ -331,7 +315,7 @@
     extra = extra_rows(short_weights)[1]
     return pl.pallas_call(
         functools.partial(gradient_kernel, tokens, peers, 1.0 / math.sqrt(seq_len)),
-        in_specs=in_vmem(peers + 1) + [pl.BlockSpec(memory_space=pltpu.HBM)] * 2 + in_vmem(7),
+        in_specs=in_vmem(peers + 10),
         out_specs=in_vmem(peers),
         out_shape=[jax.ShapeDtypeStruct((3 * tokens + extra, LANES), BF16)] * peers,
         scratch_shapes=[
@@ -339,13 +323,10 @@
             pltpu.VMEM((seq_len + 2 * PAD, LANES), F32),
             pltpu.VMEM((seq_len + 2 * PAD, LANES), F32),
             pltpu.VMEM((seq_len, LANES), F32),
-            pltpu.VMEM(tables[0].shape, BF16),
-            pltpu.VMEM(tables[1].shape, BF16),
             pltpu.VMEM((PHASES, size, LANES), BF16),
             pltpu.VMEM((PHASES, 2 * size, LANES), F32),
             pltpu.VMEM((PHASES, 2 * size, 4 * LANES), BF16),
             pltpu.VMEM((extra, LANES), F32),
-            pltpu.SemaphoreType.DMA((2,)),
         ],
         compiler_params=pltpu.CompilerParams(vmem_limit_bytes=VMEM_LIMIT),
         name="gradient_channels",
@@ -440,7 +421,7 @@
     tokens = query_proj.shape[0]
     tables = [jnp.asarray(table) for table in dft_tables(peers * tokens)]
     first = exchange(pack("pack_key_value_taps", (key_proj, value_proj, filter_taps), peers))
-    second = exchange(pack("pack_query_cot", (query_proj, cotangent), peers))
+    second = exchange(pack("pack_query_cot", (query_proj, cotangent), peers, first[2:3]))
     known = key_value_step(first, short_weights, tables, tokens)
     back = exchange(gradient_step(second, short_weights, tables, known, tokens))
     return tuple(token_step(back, query_proj, key_proj, value_proj, cotangent, short_weights))

time: 51.7 us -> 49.3 us (0.954)
  waiting for transfers between devices: 12.3 us -> 8.29 us
  starting transfers between devices: 20.8 us -> 22.6 us
  Pallas kernels: 12.5 us -> 11.5 us
  local copies, waits for them, and re-layouts: 4.9 us -> 5.8 us
    ppermute x21, waiting for transfers between devices: 12.3 us -> 8.29 us  [exchange(): lax.ppermute(block, 'ctx', [(i, i ^ step) for i in range(peers)])]
    ppermute x21, starting transfers between devices: 20.8 us -> 22.6 us  [exchange(): lax.ppermute(block, 'ctx', [(i, i ^ step) for i in range(peers)])]
    unnamed x20 -> x24, local copies, waits for them, and re-layouts: 4.9 us -> 5.8 us
  transfers between devices with their start and end apart: 21 -> 21, of which waited for: 9 -> 5; matrix products, arithmetic and copies ran while one was open for 0% -> 0% of each run, Pallas kernels for 9% -> 8%
where the time goes in v1:
time: 49.3 us; the launch traced here: 49 us
  starting transfers between devices  22.6 us (46%)
  Pallas kernels  11.5 us (23%)
  waiting for transfers between devices  8.29 us (17%)
  local copies, waits for them, and re-layouts  5.8 us (12%)
  between operations  0.79 us (2%)
    ppermute x21, starting transfers between devices, exchange(): lax.ppermute(block, 'ctx', [(i, i ^ step) for i in range(peers)])  22.6 us
    ppermute x21, waiting for transfers between devices, exchange(): lax.ppermute(block, 'ctx', [(i, i ^ step) for i in range(peers)])  8.29 us
    unnamed x24, local copies, waits for them, and re-layouts  5.8 us
    pallas_call x2, Pallas kernels, pack(): pl.pallas_call(functools.partial(pack_kernel, len(arrays), len(after)), i...  4.21 us
    pallas_call x1, Pallas kernels, gradient_step(): pl.pallas_call(functools.partial(gradient_kernel, tokens, peers, 1.0 / ma...  3.07 us
    pallas_call x1, Pallas kernels, token_step(): pl.pallas_call(functools.partial(token_kernel, peers, extra_rows(short_we...  2.13 us
    pallas_call x1, Pallas kernels, key_value_step(): pl.pallas_call(functools.partial(key_value_kernel, tokens, peers), in_spe...  2.12 us
  transfers between devices with their start and end apart: 21, of which 5 were waited for; matrix products, arithmetic and copies ran while one was open for 0% of the time, Pallas kernels for 8%

profile of v1, /device:TPU:0, one launch (start us, length us, event | category | flops | bytes accessed | tf_op | source)
XLA Modules:
  0.0 49.0 jit_solution(397072240160690593)
XLA Ops:
  0.6 2.3 %pack_key_value_taps.1 = (bf16[384,128]{1,0:T(8,128)(2,1)}, bf16[384,128]{1,0:T(8,128)(2,1)}, bf16[384,128]{1,0:T(8,128)(2,1)}, bf16[384,128]{1,0:T(8,128)(2,1)}...) custom-call(bf16[128,1024]{1,0:T(8,128)(2,1)} %refs_9_.3, ...), custom_call_target="tpu_custom_call" | custom-call | bytes 8388608 | tf_op jit(solution)/shard_map/pack_key_value_taps/pallas_call | solution.py:55
  2.9 3.9 %collective-permute-start = (bf16[384,128]{1,0:T(8,128)(2,1)}, bf16[384,128]{1,0:T(8,128)(2,1)S(1)}, u32[]{:S(2)}, u32[]{:S(2)}) collective-permute-start(bf16[384,128]{1,0:T(8,128)(2,1)} %get-tuple-element.37), channel_id=1, source_target_pairs={{0,24},{4,28},{8,16},{12,20},{16,8},{20,12},{24,0},{28,4},{1,25},{... | collective-permute-start | bytes 294920 | tf_op jit(solution)/shard_map/ppermute | solution.py:32
  6.8 1.7 %collective-permute-start.9 = (bf16[384,128]{1,0:T(8,128)(2,1)}, bf16[384,128]{1,0:T(8,128)(2,1)S(1)}, u32[]{:S(2)}, u32[]{:S(2)}) collective-permute-start(bf16[384,128]{1,0:T(8,128)(2,1)} %get-tuple-element.48), channel_id=1, source_target_pairs={{0,20},{4,16},{8,28},{12,24},{16,4},{20,0},{24,12},{28,8},{1,21},{... | collective-permute-start | bytes 294920 | tf_op jit(solution)/shard_map/ppermute | solution.py:32
  8.5 0.1 collective-permute-start.10
  8.6 1.2 %collective-permute-start.11 = (bf16[384,128]{1,0:T(8,128)(2,1)}, bf16[384,128]{1,0:T(8,128)(2,1)S(1)}, u32[]{:S(2)}, u32[]{:S(2)}) collective-permute-start(bf16[384,128]{1,0:T(8,128)(2,1)} %get-tuple-element.50), channel_id=1, source_target_pairs={{0,12},{4,8},{8,4},{12,0},{16,28},{20,24},{24,20},{28,16},{1,13},{... | collective-permute-start | bytes 294920 | tf_op jit(solution)/shard_map/ppermute | solution.py:32
  9.8 0.5 collective-permute-done.refs_2_
  10.2 1.5 %collective-permute-start.12 = (bf16[384,128]{1,0:T(8,128)(2,1)}, bf16[384,128]{1,0:T(8,128)(2,1)S(1)}, u32[]{:S(2)}, u32[]{:S(2)}) collective-permute-start(bf16[384,128]{1,0:T(8,128)(2,1)} %get-tuple-element.51), channel_id=1, source_target_pairs={{0,8},{4,12},{8,0},{12,4},{16,24},{20,28},{24,16},{28,20},{1,9},{5... | collective-permute-start | bytes 294920 | tf_op jit(solution)/shard_map/ppermute | solution.py:32
  11.7 1.1 %collective-permute-done.8.refs_1_ = bf16[384,128]{1,0:T(8,128)(2,1)S(1)} collective-permute-done((bf16[384,128]{1,0:T(8,128)(2,1)}, bf16[384,128]{1,0:T(8,128)(2,1)S(1)}, u32[]{:S(2)}, u32[]{:S(2)}) %collective-permute-start.8) | collective-permute-done | bytes 98336 | tf_op jit(solution)/shard_map/ppermute | solution.py:32
  12.9 1.9 %pack_query_cot.1 = (bf16[256,128]{1,0:T(8,128)(2,1)}, bf16[256,128]{1,0:T(8,128)(2,1)}, bf16[256,128]{1,0:T(8,128)(2,1)}, bf16[256,128]{1,0:T(8,128)(2,1)}, bf1...) custom-call(bf16[128,1024]{1,0:T(8,128)(2,1)} %refs_8_.5, ...), custom_call_target="tpu_custom_call" | custom-call | bytes 8388608 | tf_op jit(solution)/shard_map/pack_query_cot/pallas_call | solution.py:55
  14.8 1.5 %collective-permute-start.1 = (bf16[256,128]{1,0:T(8,128)(2,1)}, bf16[256,128]{1,0:T(8,128)(2,1)S(1)}, u32[]{:S(2)}, u32[]{:S(2)}) collective-permute-start(bf16[256,128]{1,0:T(8,128)(2,1)} %get-tuple-element.39), channel_id=1, source_target_pairs={{0,28},{4,24},{8,20},{12,16},{16,12},{20,8},{24,4},{28,0},{1,29},{... | collective-permute-start | bytes 196616 | tf_op jit(solution)/shard_map/ppermute | solution.py:32
  16.3 0.0 collective-permute-done.10.refs_4_
  16.3 2.4 %collective-permute-start.2 = (bf16[256,128]{1,0:T(8,128)(2,1)}, bf16[256,128]{1,0:T(8,128)(2,1)S(1)}, u32[]{:S(2)}, u32[]{:S(2)}) collective-permute-start(bf16[256,128]{1,0:T(8,128)(2,1)} %get-tuple-element.40), channel_id=1, source_target_pairs={{0,24},{4,28},{8,16},{12,20},{16,8},{20,12},{24,0},{28,4},{1,25},{... | collective-permute-start | bytes 196616 | tf_op jit(solution)/shard_map/ppermute | solution.py:32
  18.8 1.4 %collective-permute-start.4 = (bf16[256,128]{1,0:T(8,128)(2,1)}, bf16[256,128]{1,0:T(8,128)(2,1)S(1)}, u32[]{:S(2)}, u32[]{:S(2)}) collective-permute-start(bf16[256,128]{1,0:T(8,128)(2,1)} %get-tuple-element.42), channel_id=1, source_target_pairs={{0,16},{4,20},{8,24},{12,28},{16,0},{20,4},{24,8},{28,12},{1,17},{... | collective-permute-start | bytes 196616 | tf_op jit(solution)/shard_map/ppermute | solution.py:32
  20.1 0.7 %collective-permute-start.5 = (bf16[256,128]{1,0:T(8,128)(2,1)}, bf16[256,128]{1,0:T(8,128)(2,1)S(1)}, u32[]{:S(2)}, u32[]{:S(2)}) collective-permute-start(bf16[256,128]{1,0:T(8,128)(2,1)} %get-tuple-element.43), channel_id=1, source_target_pairs={{0,12},{4,8},{8,4},{12,0},{16,28},{20,24},{24,20},{28,16},{1,13},{... | collective-permute-start | bytes 196616 | tf_op jit(solution)/shard_map/ppermute | solution.py:32
  20.9 1.4 %collective-permute-start.6 = (bf16[256,128]{1,0:T(8,128)(2,1)}, bf16[256,128]{1,0:T(8,128)(2,1)S(1)}, u32[]{:S(2)}, u32[]{:S(2)}) collective-permute-start(bf16[256,128]{1,0:T(8,128)(2,1)} %get-tuple-element.44), channel_id=1, source_target_pairs={{0,8},{4,12},{8,0},{12,4},{16,24},{20,28},{24,16},{28,20},{1,9},{5... | collective-permute-start | bytes 196616 | tf_op jit(solution)/shard_map/ppermute | solution.py:32
  22.3 1.6 %copy-done = bf16[4,2,256,512]{3,2,1,0:T(8,128)(2,1)S(1)} copy-done((bf16[4,2,256,512]{3,2,1,0:T(8,128)(2,1)S(1)}, bf16[4,2,256,512]{3,2,1,0:T(8,128)(2,1)}, u32[]{:S(2)}) %copy-start) | copy-done | bytes 2097176
  23.9 1.6 %copy-done.2 = bf16[4,2,512,256]{3,2,1,0:T(8,128)(2,1)S(1)} copy-done((bf16[4,2,512,256]{3,2,1,0:T(8,128)(2,1)S(1)}, bf16[4,2,512,256]{3,2,1,0:T(8,128)(2,1)}, u32[]{:S(2)}) %copy-start.2) | copy-done | bytes 2097176
  25.5 0.8 %copy-done.7 = f32[3,3,1024]{2,1,0:T(4,128)S(1)} copy-done((f32[3,3,1024]{2,1,0:T(4,128)S(1)}, f32[3,3,1024]{2,1,0:T(4,128)}, u32[]{:S(2)}) %copy-start.7) | copy-done | bytes 36888
  26.3 0.9 %copy-done.9 = bf16[384,128]{1,0:T(8,128)(2,1)S(1)} copy-done((bf16[384,128]{1,0:T(8,128)(2,1)S(1)}, bf16[384,128]{1,0:T(8,128)(2,1)}, u32[]{:S(2)}) %copy-start.9) | copy-done | bytes 98328
  27.2 0.9 %copy-done.11 = bf16[384,128]{1,0:T(8,128)(2,1)S(1)} copy-done((bf16[384,128]{1,0:T(8,128)(2,1)S(1)}, bf16[384,128]{1,0:T(8,128)(2,1)}, u32[]{:S(2)}) %copy-start.11) | copy-done | bytes 98328
  28.1 2.1 %key_value_channels.1 = (f32[1040,128]{1,0:T(8,128)S(1)}, f32[1040,128]{1,0:T(8,128)S(1)}, f32[4,256,128]{2,1,0:T(8,128)S(1)}, f32[4,256,128]{2,1,0:T(8,128)S(1)...) custom-call(bf16[384,128]{1,0:T(8,128)(2,1)S(1)} %copy-done.11, ...), custom_call_target="tpu_custom_call" | custom-call | flops 1610612736 | bytes 8388608 | tf_op jit(solution)/shard_map/key_value_channels/pallas_call | solution.py:200
  30.3 3.1 %gradient_channels.1 = (bf16[432,128]{1,0:T(8,128)(2,1)S(1)}, bf16[432,128]{1,0:T(8,128)(2,1)S(1)}, bf16[432,128]{1,0:T(8,128)(2,1)S(1)}, bf16[432,128]{1,0:T(8,...) custom-call(bf16[256,128]{1,0:T(8,128)(2,1)S(1)} %copy-done.10, ...), custom_call_target="tpu_custom_call" | custom-call | tf_op jit(solution)/shard_map/gradient_channels/pallas_call | solution.py:316
  33.4 2.1 %collective-permute-start.14 = (bf16[432,128]{1,0:T(8,128)(2,1)S(1)}, bf16[432,128]{1,0:T(8,128)(2,1)S(1)}, u32[]{:S(2)}, u32[]{:S(2)}) collective-permute-start(bf16[432,128]{1,0:T(8,128)(2,1)S(1)} %get-tuple-element.61), channel_id=1, source_target_pairs={{0,28},{4,24},{8,20},{12,16},{16,12},{20,8},{24,4},{28,0},{1,29},{... | collective-permute-start | bytes 331784 | tf_op jit(solution)/shard_map/ppermute | solution.py:32
  35.5 1.0 %collective-permute-start.15 = (bf16[432,128]{1,0:T(8,128)(2,1)S(1)}, bf16[432,128]{1,0:T(8,128)(2,1)S(1)}, u32[]{:S(2)}, u32[]{:S(2)}) collective-permute-start(bf16[432,128]{1,0:T(8,128)(2,1)S(1)} %get-tuple-element.62), channel_id=1, source_target_pairs={{0,24},{4,28},{8,16},{12,20},{16,8},{20,12},{24,0},{28,4},{1,25},{... | collective-permute-start | bytes 331784 | tf_op jit(solution)/shard_map/ppermute | solution.py:32
  36.5 0.5 collective-permute-start.16
  36.9 0.9 %collective-permute-start.17 = (bf16[432,128]{1,0:T(8,128)(2,1)S(1)}, bf16[432,128]{1,0:T(8,128)(2,1)S(1)}, u32[]{:S(2)}, u32[]{:S(2)}) collective-permute-start(bf16[432,128]{1,0:T(8,128)(2,1)S(1)} %get-tuple-element.64), channel_id=1, source_target_pairs={{0,16},{4,20},{8,24},{12,28},{16,0},{20,4},{24,8},{28,12},{1,17},{... | collective-permute-start | bytes 331784 | tf_op jit(solution)/shard_map/ppermute | solution.py:32
  37.8 1.2 %collective-permute-start.18 = (bf16[432,128]{1,0:T(8,128)(2,1)S(1)}, bf16[432,128]{1,0:T(8,128)(2,1)S(1)}, u32[]{:S(2)}, u32[]{:S(2)}) collective-permute-start(bf16[432,128]{1,0:T(8,128)(2,1)S(1)} %get-tuple-element.65), channel_id=1, source_target_pairs={{0,12},{4,8},{8,4},{12,0},{16,28},{20,24},{24,20},{28,16},{1,13},{... | collective-permute-start | bytes 331784 | tf_op jit(solution)/shard_map/ppermute | solution.py:32
  39.1 1.1 %collective-permute-start.19 = (bf16[432,128]{1,0:T(8,128)(2,1)S(1)}, bf16[432,128]{1,0:T(8,128)(2,1)S(1)}, u32[]{:S(2)}, u32[]{:S(2)}) collective-permute-start(bf16[432,128]{1,0:T(8,128)(2,1)S(1)} %get-tuple-element.66), channel_id=1, source_target_pairs={{0,8},{4,12},{8,0},{12,4},{16,24},{20,28},{24,16},{28,20},{1,9},{5... | collective-permute-start | bytes 331784 | tf_op jit(solution)/shard_map/ppermute | solution.py:32
  40.1 2.6 %collective-permute-done.15.refs_2_ = bf16[432,128]{1,0:T(8,128)(2,1)S(1)} collective-permute-done((bf16[432,128]{1,0:T(8,128)(2,1)S(1)}, bf16[432,128]{1,0:T(8,128)(2,1)S(1)}, u32[]{:S(2)}, u32[]{:S(2)}) %collective-permute-start.15) | collective-permute-done | bytes 110624 | tf_op jit(solution)/shard_map/ppermute | solution.py:32
  42.8 1.7 %collective-permute-done.16.refs_3_ = bf16[432,128]{1,0:T(8,128)(2,1)S(1)} collective-permute-done((bf16[432,128]{1,0:T(8,128)(2,1)S(1)}, bf16[432,128]{1,0:T(8,128)(2,1)S(1)}, u32[]{:S(2)}, u32[]{:S(2)}) %collective-permute-start.16) | collective-permute-done | bytes 110624 | tf_op jit(solution)/shard_map/ppermute | solution.py:32
  44.4 2.4 %collective-permute-done.17.refs_4_ = bf16[432,128]{1,0:T(8,128)(2,1)S(1)} collective-permute-done((bf16[432,128]{1,0:T(8,128)(2,1)S(1)}, bf16[432,128]{1,0:T(8,128)(2,1)S(1)}, u32[]{:S(2)}, u32[]{:S(2)}) %collective-permute-start.17) | collective-permute-done | bytes 110624 | tf_op jit(solution)/shard_map/ppermute | solution.py:32
  46.8 2.1 %token_outputs.1 = (bf16[128,1024]{1,0:T(8,128)(2,1)}, bf16[128,1024]{1,0:T(8,128)(2,1)}, bf16[128,1024]{1,0:T(8,128)(2,1)}, bf16[128,1024]{1,0:T(8,128)(2,1)}, ...) custom-call(bf16[432,128]{1,0:T(8,128)(2,1)S(1)} %get-tuple-element.60.refs_0_, ...), custom_call_target="tpu_custom_call" | custom-call | tf_op jit(solution)/shard_map/token_outputs/pallas_call | solution.py:401
  (39 shorter events, 0.1 us)
Async XLA Ops:
  2.9 7.3 %collective-permute-start = (bf16[384,128]{1,0:T(8,128)(2,1)}, bf16[384,128]{1,0:T(8,128)(2,1)S(1)}, u32[]{:S(2)}, u32[]{:S(2)}) collective-permute-start(bf16[384,128]{1,0:T(8,128)(2,1)} %get-tuple-element.37), channel_id=1, source_target_pairs={{0,24},{4,28},{8,16},{12,20},{16,8},{20,12},{24,0},{28,4},{1,25},{... | collective-permute-start | bytes 294920 | tf_op jit(solution)/shard_map/ppermute | solution.py:32
  6.8 6.0 %collective-permute-start.8 = (bf16[384,128]{1,0:T(8,128)(2,1)}, bf16[384,128]{1,0:T(8,128)(2,1)S(1)}, u32[]{:S(2)}, u32[]{:S(2)}) collective-permute-start(bf16[384,128]{1,0:T(8,128)(2,1)} %get-tuple-element.47), channel_id=1, source_target_pairs={{0,28},{4,24},{8,20},{12,16},{16,12},{20,8},{24,4},{28,0},{1,29},{... | collective-permute-start | bytes 294920 | tf_op jit(solution)/shard_map/ppermute | solution.py:32
  6.8 8.0 %collective-permute-start.9 = (bf16[384,128]{1,0:T(8,128)(2,1)}, bf16[384,128]{1,0:T(8,128)(2,1)S(1)}, u32[]{:S(2)}, u32[]{:S(2)}) collective-permute-start(bf16[384,128]{1,0:T(8,128)(2,1)} %get-tuple-element.48), channel_id=1, source_target_pairs={{0,20},{4,16},{8,28},{12,24},{16,4},{20,0},{24,12},{28,8},{1,21},{... | collective-permute-start | bytes 294920 | tf_op jit(solution)/shard_map/ppermute | solution.py:32
  8.5 7.8 %collective-permute-start.10 = (bf16[384,128]{1,0:T(8,128)(2,1)}, bf16[384,128]{1,0:T(8,128)(2,1)S(1)}, u32[]{:S(2)}, u32[]{:S(2)}) collective-permute-start(bf16[384,128]{1,0:T(8,128)(2,1)} %get-tuple-element.49), channel_id=1, source_target_pairs={{0,16},{4,20},{8,24},{12,28},{16,0},{20,4},{24,8},{28,12},{1,17},{... | collective-permute-start | bytes 294920 | tf_op jit(solution)/shard_map/ppermute | solution.py:32
  8.6 10.2 %collective-permute-start.11 = (bf16[384,128]{1,0:T(8,128)(2,1)}, bf16[384,128]{1,0:T(8,128)(2,1)S(1)}, u32[]{:S(2)}, u32[]{:S(2)}) collective-permute-start(bf16[384,128]{1,0:T(8,128)(2,1)} %get-tuple-element.50), channel_id=1, source_target_pairs={{0,12},{4,8},{8,4},{12,0},{16,28},{20,24},{24,20},{28,16},{1,13},{... | collective-permute-start | bytes 294920 | tf_op jit(solution)/shard_map/ppermute | solution.py:32
  10.2 2.6 %copy-start.8 = (bf16[384,128]{1,0:T(8,128)(2,1)}, bf16[384,128]{1,0:T(8,128)(2,1)S(1)}, u32[]{:S(2)}) copy-start(bf16[384,128]{1,0:T(8,128)(2,1)S(1)} %collective-permute-done.refs_2_) | copy-start | bytes 294916
  10.2 8.5 %collective-permute-start.12 = (bf16[384,128]{1,0:T(8,128)(2,1)}, bf16[384,128]{1,0:T(8,128)(2,1)S(1)}, u32[]{:S(2)}, u32[]{:S(2)}) collective-permute-start(bf16[384,128]{1,0:T(8,128)(2,1)} %get-tuple-element.51), channel_id=1, source_target_pairs={{0,8},{4,12},{8,0},{12,4},{16,24},{20,28},{24,16},{28,20},{1,9},{5... | collective-permute-start | bytes 294920 | tf_op jit(solution)/shard_map/ppermute | solution.py:32
  12.8 7.3 %collective-permute-start.13 = (bf16[384,128]{1,0:T(8,128)(2,1)}, bf16[384,128]{1,0:T(8,128)(2,1)S(1)}, u32[]{:S(2)}, u32[]{:S(2)}) collective-permute-start(bf16[384,128]{1,0:T(8,128)(2,1)} %get-tuple-element.52), channel_id=1, source_target_pairs={{0,4},{4,0},{8,12},{12,8},{16,20},{20,16},{24,28},{28,24},{1,5},{5... | collective-permute-start | bytes 294920 | tf_op jit(solution)/shard_map/ppermute | solution.py:32
  14.8 6.1 %collective-permute-start.1 = (bf16[256,128]{1,0:T(8,128)(2,1)}, bf16[256,128]{1,0:T(8,128)(2,1)S(1)}, u32[]{:S(2)}, u32[]{:S(2)}) collective-permute-start(bf16[256,128]{1,0:T(8,128)(2,1)} %get-tuple-element.39), channel_id=1, source_target_pairs={{0,28},{4,24},{8,20},{12,16},{16,12},{20,8},{24,4},{28,0},{1,29},{... | collective-permute-start | bytes 196616 | tf_op jit(solution)/shard_map/ppermute | solution.py:32
  16.3 6.0 %collective-permute-start.2 = (bf16[256,128]{1,0:T(8,128)(2,1)}, bf16[256,128]{1,0:T(8,128)(2,1)S(1)}, u32[]{:S(2)}, u32[]{:S(2)}) collective-permute-start(bf16[256,128]{1,0:T(8,128)(2,1)} %get-tuple-element.40), channel_id=1, source_target_pairs={{0,24},{4,28},{8,16},{12,20},{16,8},{20,12},{24,0},{28,4},{1,25},{... | collective-permute-start | bytes 196616 | tf_op jit(solution)/shard_map/ppermute | solution.py:32
  18.8 11.4 %collective-permute-start.3 = (bf16[256,128]{1,0:T(8,128)(2,1)}, bf16[256,128]{1,0:T(8,128)(2,1)S(1)}, u32[]{:S(2)}, u32[]{:S(2)}) collective-permute-start(bf16[256,128]{1,0:T(8,128)(2,1)} %get-tuple-element.41), channel_id=1, source_target_pairs={{0,20},{4,16},{8,28},{12,24},{16,4},{20,0},{24,12},{28,8},{1,21},{... | collective-permute-start | bytes 196616 | tf_op jit(solution)/shard_map/ppermute | solution.py:32
  18.8 11.4 %collective-permute-start.4 = (bf16[256,128]{1,0:T(8,128)(2,1)}, bf16[256,128]{1,0:T(8,128)(2,1)S(1)}, u32[]{:S(2)}, u32[]{:S(2)}) collective-permute-start(bf16[256,128]{1,0:T(8,128)(2,1)} %get-tuple-element.42), channel_id=1, source_target_pairs={{0,16},{4,20},{8,24},{12,28},{16,0},{20,4},{24,8},{28,12},{1,17},{... | collective-permute-start | bytes 196616 | tf_op jit(solution)/shard_map/ppermute | solution.py:32
  20.1 10.1 %collective-permute-start.5 = (bf16[256,128]{1,0:T(8,128)(2,1)}, bf16[256,128]{1,0:T(8,128)(2,1)S(1)}, u32[]{:S(2)}, u32[]{:S(2)}) collective-permute-start(bf16[256,128]{1,0:T(8,128)(2,1)} %get-tuple-element.43), channel_id=1, source_target_pairs={{0,12},{4,8},{8,4},{12,0},{16,28},{20,24},{24,20},{28,16},{1,13},{... | collective-permute-start | bytes 196616 | tf_op jit(solution)/shard_map/ppermute | solution.py:32
  20.9 9.3 %collective-permute-start.6 = (bf16[256,128]{1,0:T(8,128)(2,1)}, bf16[256,128]{1,0:T(8,128)(2,1)S(1)}, u32[]{:S(2)}, u32[]{:S(2)}) collective-permute-start(bf16[256,128]{1,0:T(8,128)(2,1)} %get-tuple-element.44), channel_id=1, source_target_pairs={{0,8},{4,12},{8,0},{12,4},{16,24},{20,28},{24,16},{28,20},{1,9},{5... | collective-permute-start | bytes 196616 | tf_op jit(solution)/shard_map/ppermute | solution.py:32
  22.3 7.9 %collective-permute-start.7 = (bf16[256,128]{1,0:T(8,128)(2,1)}, bf16[256,128]{1,0:T(8,128)(2,1)S(1)}, u32[]{:S(2)}, u32[]{:S(2)}) collective-permute-start(bf16[256,128]{1,0:T(8,128)(2,1)} %get-tuple-element.45), channel_id=1, source_target_pairs={{0,4},{4,0},{8,12},{12,8},{16,20},{20,16},{24,28},{28,24},{1,5},{5... | collective-permute-start | bytes 196616 | tf_op jit(solution)/shard_map/ppermute | solution.py:32
  22.3 1.6 %copy-start = (bf16[4,2,256,512]{3,2,1,0:T(8,128)(2,1)S(1)}, bf16[4,2,256,512]{3,2,1,0:T(8,128)(2,1)}, u32[]{:S(2)}) copy-start(bf16[4,2,256,512]{3,2,1,0:T(8,128)(2,1)} %constant.5.clone.refs_10_) | copy-start | bytes 6291460
  23.9 1.6 %copy-start.2 = (bf16[4,2,512,256]{3,2,1,0:T(8,128)(2,1)S(1)}, bf16[4,2,512,256]{3,2,1,0:T(8,128)(2,1)}, u32[]{:S(2)}) copy-start(bf16[4,2,512,256]{3,2,1,0:T(8,128)(2,1)} %constant.4.clone.refs_9_) | copy-start | bytes 6291460
  26.3 0.9 %copy-start.9 = (bf16[384,128]{1,0:T(8,128)(2,1)S(1)}, bf16[384,128]{1,0:T(8,128)(2,1)}, u32[]{:S(2)}) copy-start(bf16[384,128]{1,0:T(8,128)(2,1)} %copy-done.8) | copy-start | bytes 294916
  27.2 0.9 %copy-start.11 = (bf16[384,128]{1,0:T(8,128)(2,1)S(1)}, bf16[384,128]{1,0:T(8,128)(2,1)}, u32[]{:S(2)}) copy-start(bf16[384,128]{1,0:T(8,128)(2,1)} %get-tuple-element.46.refs_0_) | copy-start | bytes 294916
  28.1 2.2 %copy-start.1 = (bf16[4,2,256,512]{3,2,1,0:T(8,128)(2,1)S(1)}, bf16[4,2,256,512]{3,2,1,0:T(8,128)(2,1)}, u32[]{:S(2)}) copy-start(bf16[4,2,256,512]{3,2,1,0:T(8,128)(2,1)} %constant.5.clone.refs_10_) | copy-start | bytes 6291460
  28.1 2.2 %copy-start.10 = (bf16[256,128]{1,0:T(8,128)(2,1)S(1)}, bf16[256,128]{1,0:T(8,128)(2,1)}, u32[]{:S(2)}) copy-start(bf16[256,128]{1,0:T(8,128)(2,1)} %get-tuple-element.38.refs_0_) | copy-start | bytes 196612
  30.3 16.6 %copy-start.3 = (bf16[128,1024]{1,0:T(8,128)(2,1)S(1)}, bf16[128,1024]{1,0:T(8,128)(2,1)}, u32[]{:S(2)}) copy-start(bf16[128,1024]{1,0:T(8,128)(2,1)} %refs_8_.5) | copy-start | bytes 786436
  30.3 16.6 %copy-start.4 = (bf16[128,1024]{1,0:T(8,128)(2,1)S(1)}, bf16[128,1024]{1,0:T(8,128)(2,1)}, u32[]{:S(2)}) copy-start(bf16[128,1024]{1,0:T(8,128)(2,1)} %refs_11_.1) | copy-start | bytes 786436
  30.3 16.6 %copy-start.5 = (bf16[128,1024]{1,0:T(8,128)(2,1)S(1)}, bf16[128,1024]{1,0:T(8,128)(2,1)}, u32[]{:S(2)}) copy-start(bf16[128,1024]{1,0:T(8,128)(2,1)} %refs_9_.3) | copy-start | bytes 786436
  30.3 16.6 %copy-start.6 = (bf16[128,1024]{1,0:T(8,128)(2,1)S(1)}, bf16[128,1024]{1,0:T(8,128)(2,1)}, u32[]{:S(2)}) copy-start(bf16[128,1024]{1,0:T(8,128)(2,1)} %refs_10_.3) | copy-start | bytes 786436
  33.4 5.7 %collective-permute-start.14 = (bf16[432,128]{1,0:T(8,128)(2,1)S(1)}, bf16[432,128]{1,0:T(8,128)(2,1)S(1)}, u32[]{:S(2)}, u32[]{:S(2)}) collective-permute-start(bf16[432,128]{1,0:T(8,128)(2,1)S(1)} %get-tuple-element.61), channel_id=1, source_target_pairs={{0,28},{4,24},{8,20},{12,16},{16,12},{20,8},{24,4},{28,0},{1,29},{... | collective-permute-start | bytes 331784 | tf_op jit(solution)/shard_map/ppermute | solution.py:32
  35.5 7.3 %collective-permute-start.15 = (bf16[432,128]{1,0:T(8,128)(2,1)S(1)}, bf16[432,128]{1,0:T(8,128)(2,1)S(1)}, u32[]{:S(2)}, u32[]{:S(2)}) collective-permute-start(bf16[432,128]{1,0:T(8,128)(2,1)S(1)} %get-tuple-element.62), channel_id=1, source_target_pairs={{0,24},{4,28},{8,16},{12,20},{16,8},{20,12},{24,0},{28,4},{1,25},{... | collective-permute-start | bytes 331784 | tf_op jit(solution)/shard_map/ppermute | solution.py:32
  36.5 7.9 %collective-permute-start.16 = (bf16[432,128]{1,0:T(8,128)(2,1)S(1)}, bf16[432,128]{1,0:T(8,128)(2,1)S(1)}, u32[]{:S(2)}, u32[]{:S(2)}) collective-permute-start(bf16[432,128]{1,0:T(8,128)(2,1)S(1)} %get-tuple-element.63), channel_id=1, source_target_pairs={{0,20},{4,16},{8,28},{12,24},{16,4},{20,0},{24,12},{28,8},{1,21},{... | collective-permute-start | bytes 331784 | tf_op jit(solution)/shard_map/ppermute | solution.py:32
  36.9 9.9 %collective-permute-start.17 = (bf16[432,128]{1,0:T(8,128)(2,1)S(1)}, bf16[432,128]{1,0:T(8,128)(2,1)S(1)}, u32[]{:S(2)}, u32[]{:S(2)}) collective-permute-start(bf16[432,128]{1,0:T(8,128)(2,1)S(1)} %get-tuple-element.64), channel_id=1, source_target_pairs={{0,16},{4,20},{8,24},{12,28},{16,0},{20,4},{24,8},{28,12},{1,17},{... | collective-permute-start | bytes 331784 | tf_op jit(solution)/shard_map/ppermute | solution.py:32
  37.8 9.0 %collective-permute-start.18 = (bf16[432,128]{1,0:T(8,128)(2,1)S(1)}, bf16[432,128]{1,0:T(8,128)(2,1)S(1)}, u32[]{:S(2)}, u32[]{:S(2)}) collective-permute-start(bf16[432,128]{1,0:T(8,128)(2,1)S(1)} %get-tuple-element.65), channel_id=1, source_target_pairs={{0,12},{4,8},{8,4},{12,0},{16,28},{20,24},{24,20},{28,16},{1,13},{... | collective-permute-start | bytes 331784 | tf_op jit(solution)/shard_map/ppermute | solution.py:32
  39.1 7.7 %collective-permute-start.19 = (bf16[432,128]{1,0:T(8,128)(2,1)S(1)}, bf16[432,128]{1,0:T(8,128)(2,1)S(1)}, u32[]{:S(2)}, u32[]{:S(2)}) collective-permute-start(bf16[432,128]{1,0:T(8,128)(2,1)S(1)} %get-tuple-element.66), channel_id=1, source_target_pairs={{0,8},{4,12},{8,0},{12,4},{16,24},{20,28},{24,16},{28,20},{1,9},{5... | collective-permute-start | bytes 331784 | tf_op jit(solution)/shard_map/ppermute | solution.py:32
  42.8 4.0 %collective-permute-start.20 = (bf16[432,128]{1,0:T(8,128)(2,1)S(1)}, bf16[432,128]{1,0:T(8,128)(2,1)S(1)}, u32[]{:S(2)}, u32[]{:S(2)}) collective-permute-start(bf16[432,128]{1,0:T(8,128)(2,1)S(1)} %get-tuple-element.67), channel_id=1, source_target_pairs={{0,4},{4,0},{8,12},{12,8},{16,20},{20,16},{24,28},{28,24},{1,5},{5... | collective-permute-start | bytes 331784 | tf_op jit(solution)/shard_map/ppermute | solution.py:32
  (1 other events, 0.8 us)

commit v2 on v1

--- a/solution.py
+++ b/solution.py
@@ -41,8 +41,8 @@
     return pl.ds(pl.multiple_of(place * LANES, LANES), LANES)
 
 
-def pack_kernel(count, waits, *refs):
-    sources, packed = refs[:count], refs[count + waits :]
+def pack_kernel(count, *refs):
+    sources, packed = refs[:count], refs[count:]
     tokens = sources[0].shape[0]
     me = lax.axis_index("ctx")
     for step, target in zip(partners(len(packed)), packed):
@@ -50,16 +50,16 @@
             target[at * tokens : (at + 1) * tokens, :] = source[:, lanes_of(me ^ step)].astype(BF16)
 
 
-def pack(name, arrays, peers, after=()):
+def pack(arrays, peers):
     tokens = arrays[0].shape[0]
     return pl.pallas_call(
-        functools.partial(pack_kernel, len(arrays), len(after)),
-        in_specs=in_vmem(len(arrays)) + [pl.BlockSpec(memory_space=pl.ANY)] * len(after),
+        functools.partial(pack_kernel, len(arrays)),
+        in_specs=in_vmem(len(arrays)),
         out_specs=in_vmem(peers),
         out_shape=[jax.ShapeDtypeStruct((len(arrays) * tokens, LANES), BF16)] * peers,
         cost_estimate=pl.CostEstimate(flops=0, bytes_accessed=8 * MIB, transcendentals=0),
-        name=name,
-    )(*arrays, *after)
+        name="pack_inputs",
+    )(*arrays)
 
 
 @functools.lru_cache(maxsize=None)
@@ -147,127 +147,106 @@
     ref[ref.shape[0] - PAD :, :] = jnp.zeros((PAD, LANES), F32)
 
 
-def key_value_kernel(tokens, peers, *refs):
+def stage_kernel(count, *refs):
+    sources, targets, sems = refs[:count], refs[count + 1 : 2 * count + 1], refs[2 * count + 1]
+    copies = [
+        pltpu.make_async_copy(source, target, sems.at[at])
+        for at, (source, target) in enumerate(zip(sources, targets))
+    ]
+    for copy in copies:
+        copy.start()
+    for copy in copies:
+        copy.wait()
+
+
+def stage(arrays, after):
+    count = len(arrays)
+    return pl.pallas_call(
+        functools.partial(stage_kernel, count),
+        in_specs=[pl.BlockSpec(memory_space=pl.ANY)] * (count + 1),
+        out_specs=in_vmem(count),
+        out_shape=[jax.ShapeDtypeStruct(array.shape, array.dtype) for array in arrays],
+        scratch_shapes=[pltpu.SemaphoreType.DMA((count,))],
+        compiler_params=pltpu.CompilerParams(vmem_limit_bytes=8 * MIB),
+        cost_estimate=pl.CostEstimate(flops=0, bytes_accessed=8 * MIB, transcendentals=0),
+        name="stage_tables",
+    )(*arrays, after)
+
+
+def extra_rows(short_weights):
+    sums = PIECES * short_weights.shape[0] * short_weights.shape[1]
+    return sums, -(-(sums + 8 * RIM) // TILE) * TILE
+
+
+def channel_kernel(tokens, peers, grad_scale, *refs):
     arrived = refs[:peers]
     weights, forward, backward = refs[peers : peers + 3]
-    key, value, key_short, value_short, prod_spec, filt_spec, conv = refs[peers + 3 : peers + 10]
-    taps, signals, spectra, pieces = refs[peers + 10 :]
+    out = refs[peers + 3 : 2 * peers + 3]
+    (
+        query,
+        key,
+        value,
+        cot,
+        conv,
+        conv_grad,
+        filter_grad,
+        taps,
+        key_short,
+        value_short,
+        signals,
+        spectra,
+        pieces,
+        extra,
+    ) = refs[2 * peers + 3 :]
     size = peers * tokens // PHASES
+    tap_count = weights.shape[1]
     me = lax.axis_index("ctx")
     own = lanes_of(me)
-    for ref in (key, value, conv):
+    for ref in (query, key, value, cot, conv, conv_grad):
         clear_ends(ref)
     for step, source in zip(partners(peers), arrived):
         start = (me ^ step) * tokens
         inner = pl.ds(pl.multiple_of(PAD + start, PAD), tokens)
-        key[inner, :] = source[:tokens, :].astype(F32)
-        value[inner, :] = source[tokens : 2 * tokens, :].astype(F32)
-        taps[pl.ds(pl.multiple_of(start, PAD), tokens), :] = source[2 * tokens :, :].astype(F32)
+        for at, ref in enumerate((query, key, value, cot)):
+            ref[inner, :] = source[at * tokens : (at + 1) * tokens, :].astype(F32)
+        taps[pl.ds(pl.multiple_of(start, PAD), tokens), :] = source[4 * tokens :, :].astype(F32)
     for r in range(PHASES):
         key_short[r] = short_phases(key, weights, 1, own, r, size)
         value_short[r] = short_phases(value, weights, 2, own, r, size)
+        query_short = short_phases(query, weights, 0, own, r, size)
         signals[r, :, :LANES] = (key_short[r] * value_short[r]).astype(BF16)
-        signals[r, :, LANES:] = phase(taps, r, size).astype(BF16)
+        signals[r, :, LANES : 2 * LANES] = phase(taps, r, size).astype(BF16)
+        signals[r, :, 2 * LANES :] = (phase(cot, PAD + r, size) * query_short).astype(BF16)
     for r in range(PHASES):
         spectra[r] = forward_transform(forward[r], signals[r])
     for chunk in range(size // TILE):
         real = slice(chunk * TILE, (chunk + 1) * TILE)
         imag = slice(size + chunk * TILE, size + (chunk + 1) * TILE)
-        mixed = []
-        for at, target in enumerate((prod_spec, filt_spec)):
-            lanes = slice(at * LANES, (at + 1) * LANES)
-            spectrum = forward_mix(
-                [(spectra[r, real, lanes], spectra[r, imag, lanes]) for r in range(PHASES)]
+        prod, filt, grad = (
+            forward_mix(
+                [
+                    (
+                        spectra[r, real, at * LANES : (at + 1) * LANES],
+                        spectra[r, imag, at * LANES : (at + 1) * LANES],
+                    )
+                    for r in range(PHASES)
+                ]
             )
-            for q, pair in enumerate(spectrum):
-                target[q, real, :], target[q, imag, :] = pair
-            mixed.append(spectrum)
-        for r, pair in enumerate(inverse_mix(times(*mixed))):
-            for rows, part in zip((real, imag), pair):
-                split_store(pieces, r, rows, slice(0, LANES), part)
-    for r in range(PHASES):
-        result = inverse_transform(backward[r], pieces[r])
-        conv[pl.ds(PAD + r, size, stride=PHASES), :] = result.astype(BF16).astype(F32)
-
-
-def key_value_step(arrived, short_weights, tables, tokens):
-    peers = len(arrived)
-    seq_len = peers * tokens
-    size = seq_len // PHASES
-    padded = jax.ShapeDtypeStruct((seq_len + 2 * PAD, LANES), F32)
-    phases = jax.ShapeDtypeStruct((PHASES, size, LANES), F32)
-    spectrum = jax.ShapeDtypeStruct((PHASES, 2 * size, LANES), F32)
-    return pl.pallas_call(
-        functools.partial(key_value_kernel, tokens, peers),
-        in_specs=in_vmem(peers + 3),
-        out_specs=in_vmem(7),
-        out_shape=[padded, padded, phases, phases, spectrum, spectrum, padded],
-        scratch_shapes=[
-            pltpu.VMEM((seq_len, LANES), F32),
-            pltpu.VMEM((PHASES, size, 2 * LANES), BF16),
-            pltpu.VMEM((PHASES, 2 * size, 2 * LANES), F32),
-            pltpu.VMEM((PHASES, 2 * size, 2 * LANES), BF16),
-        ],
-        compiler_params=pltpu.CompilerParams(vmem_limit_bytes=VMEM_LIMIT),
-        cost_estimate=pl.CostEstimate(
-            flops=2 * 24 * PHASES * size * size * LANES,
-            bytes_accessed=8 * MIB,
-            transcendentals=0,
-        ),
-        name="key_value_channels",
-    )(*arrived, short_weights, *tables)
-
-
-def extra_rows(short_weights):
-    sums = PIECES * short_weights.shape[0] * short_weights.shape[1]
-    return sums, -(-(sums + 8 * RIM) // TILE) * TILE
-
-
-def gradient_kernel(tokens, peers, grad_scale, *refs):
-    arrived = refs[:peers]
-    weights, forward, backward = refs[peers : peers + 3]
-    key, value, key_short, value_short, prod_spec, filt_spec, conv = refs[peers + 3 : peers + 10]
-    out = refs[peers + 10 : 2 * peers + 10]
-    (
-        query,
-        cot,
-        conv_grad,
-        filter_grad,
-        signals,
-        spectra,
-        pieces,
-        extra,
-    ) = refs[2 * peers + 10 :]
-    size = peers * tokens // PHASES
-    tap_count = weights.shape[1]
-    me = lax.axis_index("ctx")
-    own = lanes_of(me)
-    for ref in (query, cot, conv_grad):
-        clear_ends(ref)
-    for step, source in zip(partners(peers), arrived):
-        inner = pl.ds(pl.multiple_of(PAD + (me ^ step) * tokens, PAD), tokens)
-        query[inner, :] = source[:tokens, :].astype(F32)
-        cot[inner, :] = source[tokens:, :].astype(F32)
-    for r in range(PHASES):
-        query_short = short_phases(query, weights, 0, own, r, size)
-        signals[r] = (phase(cot, PAD + r, size) * query_short).astype(BF16)
-    for r in range(PHASES):
-        spectra[r] = forward_transform(forward[r], signals[r])
-    for chunk in range(size // TILE):
-        real = slice(chunk * TILE, (chunk + 1) * TILE)
-        imag = slice(size + chunk * TILE, size + (chunk + 1) * TILE)
-        grad = forward_mix([(spectra[r, real, :], spectra[r, imag, :]) for r in range(PHASES)])
-        for at, other in enumerate((filt_spec, prod_spec)):
-            known = [(other[q, real, :], other[q, imag, :]) for q in range(PHASES)]
-            for r, pair in enumerate(inverse_mix(conj_times(known, grad))):
+            for at in range(3)
+        )
+        for at, mixed in enumerate(
+            (times(prod, filt), conj_times(filt, grad), conj_times(prod, grad))
+        ):
+            for r, pair in enumerate(inverse_mix(mixed)):
                 for rows, part in zip((real, imag), pair):
                     split_store(pieces, r, rows, slice(at * LANES, (at + 1) * LANES), part)
     for r in range(PHASES):
         result = inverse_transform(backward[r], pieces[r])
-        conv_grad[pl.ds(PAD + r, size, stride=PHASES), :] = (
-            result[:, :LANES].astype(BF16).astype(F32)
-        )
-        filter_grad[pl.ds(r, size, stride=PHASES), :] = result[:, LANES:] * grad_scale
+        for at, ref in enumerate((conv, conv_grad)):
+            ref[pl.ds(PAD + r, size, stride=PHASES), :] = (
+                result[:, at * LANES : (at + 1) * LANES].astype(BF16).astype(F32)
+            )
+        filter_grad[pl.ds(r, size, stride=PHASES), :] = result[:, 2 * LANES :] * grad_scale
 
     sums = []
     for array, signal in enumerate((query, key, value)):
@@ -308,29 +287,33 @@
         target[3 * tokens :, :] = extra[...].astype(BF16)
 
 
-def gradient_step(arrived, short_weights, tables, known, tokens):
+def channel_step(arrived, short_weights, tables, tokens):
     peers = len(arrived)
     seq_len = peers * tokens
     size = seq_len // PHASES
     extra = extra_rows(short_weights)[1]
+    padded = pltpu.VMEM((seq_len + 2 * PAD, LANES), F32)
+    plain = pltpu.VMEM((seq_len, LANES), F32)
+    phases = pltpu.VMEM((PHASES, size, LANES), F32)
     return pl.pallas_call(
-        functools.partial(gradient_kernel, tokens, peers, 1.0 / math.sqrt(seq_len)),
-        in_specs=in_vmem(peers + 10),
+        functools.partial(channel_kernel, tokens, peers, 1.0 / math.sqrt(seq_len)),
+        in_specs=in_vmem(peers + 3),
         out_specs=in_vmem(peers),
         out_shape=[jax.ShapeDtypeStruct((3 * tokens + extra, LANES), BF16)] * peers,
         scratch_shapes=[
-            pltpu.VMEM((seq_len + 2 * PAD, LANES), F32),
-            pltpu.VMEM((seq_len + 2 * PAD, LANES), F32),
-            pltpu.VMEM((seq_len + 2 * PAD, LANES), F32),
-            pltpu.VMEM((seq_len, LANES), F32),
-            pltpu.VMEM((PHASES, size, LANES), BF16),
-            pltpu.VMEM((PHASES, 2 * size, LANES), F32),
-            pltpu.VMEM((PHASES, 2 * size, 4 * LANES), BF16),
+            *[padded] * 6,
+            plain,
+            plain,
+            phases,
+            phases,
+            pltpu.VMEM((PHASES, size, 3 * LANES), BF16),
+            pltpu.VMEM((PHASES, 2 * size, 3 * LANES), F32),
+            pltpu.VMEM((PHASES, 2 * size, 6 * LANES), BF16),
             pltpu.VMEM((extra, LANES), F32),
         ],
         compiler_params=pltpu.CompilerParams(vmem_limit_bytes=VMEM_LIMIT),
-        name="gradient_channels",
-    )(*arrived, short_weights, *tables, *known)
+        name="channel_operator",
+    )(*arrived, short_weights, *tables)
 
 
 def token_kernel(peers, sum_rows, *refs):
@@ -420,10 +403,12 @@
     peers = lax.axis_size("ctx")
     tokens = query_proj.shape[0]
     tables = [jnp.asarray(table) for table in dft_tables(peers * tokens)]
-    first = exchange(pack("pack_key_value_taps", (key_proj, value_proj, filter_taps), peers))
-    second = exchange(pack("pack_query_cot", (query_proj, cotangent), peers, first[2:3]))
-    known = key_value_step(first, short_weights, tables, tokens)
-    back = exchange(gradient_step(second, short_weights, tables, known, tokens))
+    sent = pack((query_proj, key_proj, value_proj, cotangent, filter_taps), peers)
+    arrived = exchange(sent)
+    staged = stage((sent[0], short_weights, *tables), arrived[1])
+    back = exchange(
+        channel_step((staged[0], *arrived[1:]), staged[1], staged[2:], tokens)
+    )
     return tuple(token_step(back, query_proj, key_proj, value_proj, cotangent, short_weights))
 
 

time: 49.3 us -> 43.7 us (0.89)
  starting transfers between devices: 22.6 us -> 16.3 us
  waiting for transfers between devices: 8.29 us -> 11.4 us
  Pallas kernels: 11.5 us -> 10.1 us
  local copies, waits for them, and re-layouts: 5.8 us -> 4.92 us
    ppermute x21 -> x14, starting transfers between devices: 22.6 us -> 16.3 us  [exchange(): lax.ppermute(block, 'ctx', [(i, i ^ step) for i in range(peers)])]
    ppermute x21 -> x14, waiting for transfers between devices: 8.29 us -> 11.4 us  [exchange(): lax.ppermute(block, 'ctx', [(i, i ^ step) for i in range(peers)])]
    pallas_call x4 -> x3, Pallas kernels: 9.39 us -> 7.95 us  [the longest x1 4.65 us: channel_step(): pl.pallas_call(functools.partial(channel_kernel, tokens, peers, 1.0 / mat...]
    unnamed x24 -> x18, local copies, waits for them, and re-layouts: 5.8 us -> 4.92 us
  transfers between devices with their start and end apart: 21 -> 14, of which waited for: 5 -> 8; matrix products, arithmetic and copies ran while one was open for 0% -> 0% of each run, Pallas kernels for 8% -> 1%
where the time goes in v2:
time: 43.7 us; the launch traced here: 43.4 us
  starting transfers between devices  16.3 us (37%)
  waiting for transfers between devices  11.4 us (26%)
  Pallas kernels  10.1 us (23%)
  local copies, waits for them, and re-layouts  4.92 us (11%)
  between operations  0.72 us (2%)
    ppermute x14, starting transfers between devices, exchange(): lax.ppermute(block, 'ctx', [(i, i ^ step) for i in range(peers)])  16.3 us
    ppermute x14, waiting for transfers between devices, exchange(): lax.ppermute(block, 'ctx', [(i, i ^ step) for i in range(peers)])  11.4 us
    unnamed x18, local copies, waits for them, and re-layouts  4.92 us
    pallas_call x1, Pallas kernels, channel_step(): pl.pallas_call(functools.partial(channel_kernel, tokens, peers, 1.0 / mat...  4.65 us
    pallas_call x1, Pallas kernels, pack(): pl.pallas_call(functools.partial(pack_kernel, len(arrays)), in_specs=in_v...  2.74 us
    pallas_call x1, Pallas kernels, token_step(): pl.pallas_call(functools.partial(token_kernel, peers, extra_rows(short_we...  2.14 us
  transfers between devices with their start and end apart: 14, of which 8 were waited for; matrix products, arithmetic and copies ran while one was open for 0% of the time, Pallas kernels for 1%

profile of v2, /device:TPU:0, one launch (start us, length us, event | category | flops | bytes accessed | tf_op | source)
XLA Modules:
  0.0 43.4 jit_solution(2273909704644891065)
XLA Ops:
  0.6 2.7 %pack_inputs.1 = (bf16[640,128]{1,0:T(8,128)(2,1)}, bf16[640,128]{1,0:T(8,128)(2,1)}, bf16[640,128]{1,0:T(8,128)(2,1)}, bf16[640,128]{1,0:T(8,128)(2,1)}, bf16[6...) custom-call(bf16[128,1024]{1,0:T(8,128)(2,1)} %refs_8_.1, ...), custom_call_target="tpu_custom_call" | custom-call | bytes 8388608 | tf_op jit(solution)/shard_map/pack_inputs/pallas_call | solution.py:55
  3.4 3.3 %collective-permute-start = (bf16[640,128]{1,0:T(8,128)(2,1)}, bf16[640,128]{1,0:T(8,128)(2,1)S(1)}, u32[]{:S(2)}, u32[]{:S(2)}) collective-permute-start(bf16[640,128]{1,0:T(8,128)(2,1)} %get-tuple-element.27), channel_id=1, source_target_pairs={{0,28},{4,24},{8,20},{12,16},{16,12},{20,8},{24,4},{28,0},{1,29},{... | collective-permute-start | bytes 491528 | tf_op jit(solution)/shard_map/ppermute | solution.py:32
  6.7 0.6 %collective-permute-start.1 = (bf16[640,128]{1,0:T(8,128)(2,1)}, bf16[640,128]{1,0:T(8,128)(2,1)S(1)}, u32[]{:S(2)}, u32[]{:S(2)}) collective-permute-start(bf16[640,128]{1,0:T(8,128)(2,1)} %get-tuple-element.29), channel_id=1, source_target_pairs={{0,24},{4,28},{8,16},{12,20},{16,8},{20,12},{24,0},{28,4},{1,25},{... | collective-permute-start | bytes 491528 | tf_op jit(solution)/shard_map/ppermute | solution.py:32
  7.3 1.4 %collective-permute-start.2 = (bf16[640,128]{1,0:T(8,128)(2,1)}, bf16[640,128]{1,0:T(8,128)(2,1)S(1)}, u32[]{:S(2)}, u32[]{:S(2)}) collective-permute-start(bf16[640,128]{1,0:T(8,128)(2,1)} %get-tuple-element.30), channel_id=1, source_target_pairs={{0,20},{4,16},{8,28},{12,24},{16,4},{20,0},{24,12},{28,8},{1,21},{... | collective-permute-start | bytes 491528 | tf_op jit(solution)/shard_map/ppermute | solution.py:32
  8.7 0.3 collective-permute-start.3
  9.0 1.1 %collective-permute-start.4 = (bf16[640,128]{1,0:T(8,128)(2,1)}, bf16[640,128]{1,0:T(8,128)(2,1)S(1)}, u32[]{:S(2)}, u32[]{:S(2)}) collective-permute-start(bf16[640,128]{1,0:T(8,128)(2,1)} %get-tuple-element.32), channel_id=1, source_target_pairs={{0,12},{4,8},{8,4},{12,0},{16,28},{20,24},{24,20},{28,16},{1,13},{... | collective-permute-start | bytes 491528 | tf_op jit(solution)/shard_map/ppermute | solution.py:32
  10.1 1.5 %collective-permute-done.refs_4_.refs_1_ = bf16[640,128]{1,0:T(8,128)(2,1)S(1)} collective-permute-done((bf16[640,128]{1,0:T(8,128)(2,1)}, bf16[640,128]{1,0:T(8,128)(2,1)S(1)}, u32[]{:S(2)}, u32[]{:S(2)}) %collective-permute-start) | collective-permute-done | bytes 163872 | tf_op jit(solution)/shard_map/ppermute | solution.py:32
  11.7 2.3 %collective-permute-start.5 = (bf16[640,128]{1,0:T(8,128)(2,1)}, bf16[640,128]{1,0:T(8,128)(2,1)S(1)}, u32[]{:S(2)}, u32[]{:S(2)}) collective-permute-start(bf16[640,128]{1,0:T(8,128)(2,1)} %get-tuple-element.33), channel_id=1, source_target_pairs={{0,8},{4,12},{8,0},{12,4},{16,24},{20,28},{24,16},{28,20},{1,9},{5... | collective-permute-start | bytes 491528 | tf_op jit(solution)/shard_map/ppermute | solution.py:32
  14.0 1.7 %collective-permute-done.1.refs_2_ = bf16[640,128]{1,0:T(8,128)(2,1)S(1)} collective-permute-done((bf16[640,128]{1,0:T(8,128)(2,1)}, bf16[640,128]{1,0:T(8,128)(2,1)S(1)}, u32[]{:S(2)}, u32[]{:S(2)}) %collective-permute-start.1) | collective-permute-done | bytes 163872 | tf_op jit(solution)/shard_map/ppermute | solution.py:32
  15.8 0.0 collective-permute-start.6
  15.8 1.6 %copy-done = bf16[4,2,256,512]{3,2,1,0:T(8,128)(2,1)S(1)} copy-done((bf16[4,2,256,512]{3,2,1,0:T(8,128)(2,1)S(1)}, bf16[4,2,256,512]{3,2,1,0:T(8,128)(2,1)}, u32[]{:S(2)}) %copy-start) | copy-done | bytes 2097176
  17.3 1.6 %copy-done.1 = bf16[4,2,512,256]{3,2,1,0:T(8,128)(2,1)S(1)} copy-done((bf16[4,2,512,256]{3,2,1,0:T(8,128)(2,1)S(1)}, bf16[4,2,512,256]{3,2,1,0:T(8,128)(2,1)}, u32[]{:S(2)}) %copy-start.1) | copy-done | bytes 2097176
  18.9 0.8 %copy-done.6 = f32[3,3,1024]{2,1,0:T(4,128)S(1)} copy-done((f32[3,3,1024]{2,1,0:T(4,128)S(1)}, f32[3,3,1024]{2,1,0:T(4,128)}, u32[]{:S(2)}) %copy-start.6) | copy-done | bytes 36888
  19.7 0.9 %copy-done.8 = bf16[640,128]{1,0:T(8,128)(2,1)S(1)} copy-done((bf16[640,128]{1,0:T(8,128)(2,1)S(1)}, bf16[640,128]{1,0:T(8,128)(2,1)}, u32[]{:S(2)}) %copy-start.8) | copy-done | bytes 163864
  20.7 0.6 %stage_tables.1 = (bf16[640,128]{1,0:T(8,128)(2,1)S(1)}, f32[3,3,1024]{2,1,0:T(4,128)S(1)}, bf16[4,2,512,256]{3,2,1,0:T(8,128)(2,1)S(1)}, bf16[4,2,256,512]{3,2,1,0:T(8,128)(2,1)S(1)}) custom-call(bf16[640,128]{1,0:T(8,128)(2,1)S(1)} %copy-done.8, f32[3,3,1024]{2,1,0:T(4,128)S(1)} %copy-done.6, bf16[4,2,512,256]{3,2,1,0:T(8,128)(2,1)S(1)} %copy-done.1, ...), custom_call_target="tpu_custom_call" | custom-call | bytes 8388608 | tf_op jit(solution)/shard_map/stage_tables/pallas_call | solution.py:164
  21.2 1.0 %collective-permute-done.3.refs_4_ = bf16[640,128]{1,0:T(8,128)(2,1)S(1)} collective-permute-done((bf16[640,128]{1,0:T(8,128)(2,1)}, bf16[640,128]{1,0:T(8,128)(2,1)S(1)}, u32[]{:S(2)}, u32[]{:S(2)}) %collective-permute-start.3) | collective-permute-done | bytes 163872 | tf_op jit(solution)/shard_map/ppermute | solution.py:32
  22.2 0.9 %collective-permute-done.5.refs_6_ = bf16[640,128]{1,0:T(8,128)(2,1)S(1)} collective-permute-done((bf16[640,128]{1,0:T(8,128)(2,1)}, bf16[640,128]{1,0:T(8,128)(2,1)S(1)}, u32[]{:S(2)}, u32[]{:S(2)}) %collective-permute-start.5) | collective-permute-done | bytes 163872 | tf_op jit(solution)/shard_map/ppermute | solution.py:32
  23.1 0.0 copy-start.5
  23.1 0.0 copy-start.7
  23.1 4.6 %channel_operator.1 = (bf16[432,128]{1,0:T(8,128)(2,1)S(1)}, bf16[432,128]{1,0:T(8,128)(2,1)S(1)}, bf16[432,128]{1,0:T(8,128)(2,1)S(1)}, bf16[432,128]{1,0:T(8,1...) custom-call(bf16[640,128]{1,0:T(8,128)(2,1)S(1)} %get-tuple-element., ...), custom_call_target="tpu_custom_call" | custom-call | tf_op jit(solution)/shard_map/channel_operator/pallas_call | solution.py:298
  27.8 2.1 %collective-permute-start.7 = (bf16[432,128]{1,0:T(8,128)(2,1)S(1)}, bf16[432,128]{1,0:T(8,128)(2,1)S(1)}, u32[]{:S(2)}, u32[]{:S(2)}) collective-permute-start(bf16[432,128]{1,0:T(8,128)(2,1)S(1)} %get-tuple-element.39), channel_id=1, source_target_pairs={{0,28},{4,24},{8,20},{12,16},{16,12},{20,8},{24,4},{28,0},{1,29},{... | collective-permute-start | bytes 331784 | tf_op jit(solution)/shard_map/ppermute | solution.py:32
  29.9 0.6 %collective-permute-start.8 = (bf16[432,128]{1,0:T(8,128)(2,1)S(1)}, bf16[432,128]{1,0:T(8,128)(2,1)S(1)}, u32[]{:S(2)}, u32[]{:S(2)}) collective-permute-start(bf16[432,128]{1,0:T(8,128)(2,1)S(1)} %get-tuple-element.40), channel_id=1, source_target_pairs={{0,24},{4,28},{8,16},{12,20},{16,8},{20,12},{24,0},{28,4},{1,25},{... | collective-permute-start | bytes 331784 | tf_op jit(solution)/shard_map/ppermute | solution.py:32
  30.5 1.2 %collective-permute-start.9 = (bf16[432,128]{1,0:T(8,128)(2,1)S(1)}, bf16[432,128]{1,0:T(8,128)(2,1)S(1)}, u32[]{:S(2)}, u32[]{:S(2)}) collective-permute-start(bf16[432,128]{1,0:T(8,128)(2,1)S(1)} %get-tuple-element.41), channel_id=1, source_target_pairs={{0,20},{4,16},{8,28},{12,24},{16,4},{20,0},{24,12},{28,8},{1,21},{... | collective-permute-start | bytes 331784 | tf_op jit(solution)/shard_map/ppermute | solution.py:32
  31.6 0.6 %collective-permute-start.10 = (bf16[432,128]{1,0:T(8,128)(2,1)S(1)}, bf16[432,128]{1,0:T(8,128)(2,1)S(1)}, u32[]{:S(2)}, u32[]{:S(2)}) collective-permute-start(bf16[432,128]{1,0:T(8,128)(2,1)S(1)} %get-tuple-element.42), channel_id=1, source_target_pairs={{0,16},{4,20},{8,24},{12,28},{16,0},{20,4},{24,8},{28,12},{1,17},{... | collective-permute-start | bytes 331784 | tf_op jit(solution)/shard_map/ppermute | solution.py:32
  32.3 1.2 %collective-permute-start.11 = (bf16[432,128]{1,0:T(8,128)(2,1)S(1)}, bf16[432,128]{1,0:T(8,128)(2,1)S(1)}, u32[]{:S(2)}, u32[]{:S(2)}) collective-permute-start(bf16[432,128]{1,0:T(8,128)(2,1)S(1)} %get-tuple-element.43), channel_id=1, source_target_pairs={{0,12},{4,8},{8,4},{12,0},{16,28},{20,24},{24,20},{28,16},{1,13},{... | collective-permute-start | bytes 331784 | tf_op jit(solution)/shard_map/ppermute | solution.py:32
  33.4 0.4 collective-permute-done.7.refs_1_
  33.8 1.5 %collective-permute-start.12 = (bf16[432,128]{1,0:T(8,128)(2,1)S(1)}, bf16[432,128]{1,0:T(8,128)(2,1)S(1)}, u32[]{:S(2)}, u32[]{:S(2)}) collective-permute-start(bf16[432,128]{1,0:T(8,128)(2,1)S(1)} %get-tuple-element.44), channel_id=1, source_target_pairs={{0,8},{4,12},{8,0},{12,4},{16,24},{20,28},{24,16},{28,20},{1,9},{5... | collective-permute-start | bytes 331784 | tf_op jit(solution)/shard_map/ppermute | solution.py:32
  35.3 1.4 %collective-permute-done.8.refs_2_ = bf16[432,128]{1,0:T(8,128)(2,1)S(1)} collective-permute-done((bf16[432,128]{1,0:T(8,128)(2,1)S(1)}, bf16[432,128]{1,0:T(8,128)(2,1)S(1)}, u32[]{:S(2)}, u32[]{:S(2)}) %collective-permute-start.8) | collective-permute-done | bytes 110624 | tf_op jit(solution)/shard_map/ppermute | solution.py:32
  36.7 2.0 %collective-permute-done.9.refs_3_ = bf16[432,128]{1,0:T(8,128)(2,1)S(1)} collective-permute-done((bf16[432,128]{1,0:T(8,128)(2,1)S(1)}, bf16[432,128]{1,0:T(8,128)(2,1)S(1)}, u32[]{:S(2)}, u32[]{:S(2)}) %collective-permute-start.9) | collective-permute-done | bytes 110624 | tf_op jit(solution)/shard_map/ppermute | solution.py:32
  38.8 2.4 %collective-permute-done.10.refs_4_ = bf16[432,128]{1,0:T(8,128)(2,1)S(1)} collective-permute-done((bf16[432,128]{1,0:T(8,128)(2,1)S(1)}, bf16[432,128]{1,0:T(8,128)(2,1)S(1)}, u32[]{:S(2)}, u32[]{:S(2)}) %collective-permute-start.10) | collective-permute-done | bytes 110624 | tf_op jit(solution)/shard_map/ppermute | solution.py:32
  41.2 0.0 collective-permute-done.12.refs_6_
  41.3 2.1 %token_outputs.1 = (bf16[128,1024]{1,0:T(8,128)(2,1)}, bf16[128,1024]{1,0:T(8,128)(2,1)}, bf16[128,1024]{1,0:T(8,128)(2,1)}, bf16[128,1024]{1,0:T(8,128)(2,1)}, ...) custom-call(bf16[432,128]{1,0:T(8,128)(2,1)S(1)} %get-tuple-element.38.refs_0_, ...), custom_call_target="tpu_custom_call" | custom-call | tf_op jit(solution)/shard_map/token_outputs/pallas_call | solution.py:384
  (18 shorter events, 0.0 us)
Async XLA Ops:
  3.4 8.3 %collective-permute-start = (bf16[640,128]{1,0:T(8,128)(2,1)}, bf16[640,128]{1,0:T(8,128)(2,1)S(1)}, u32[]{:S(2)}, u32[]{:S(2)}) collective-permute-start(bf16[640,128]{1,0:T(8,128)(2,1)} %get-tuple-element.27), channel_id=1, source_target_pairs={{0,28},{4,24},{8,20},{12,16},{16,12},{20,8},{24,4},{28,0},{1,29},{... | collective-permute-start | bytes 491528 | tf_op jit(solution)/shard_map/ppermute | solution.py:32
  6.7 9.0 %collective-permute-start.1 = (bf16[640,128]{1,0:T(8,128)(2,1)}, bf16[640,128]{1,0:T(8,128)(2,1)S(1)}, u32[]{:S(2)}, u32[]{:S(2)}) collective-permute-start(bf16[640,128]{1,0:T(8,128)(2,1)} %get-tuple-element.29), channel_id=1, source_target_pairs={{0,24},{4,28},{8,16},{12,20},{16,8},{20,12},{24,0},{28,4},{1,25},{... | collective-permute-start | bytes 491528 | tf_op jit(solution)/shard_map/ppermute | solution.py:32
  7.3 13.9 %collective-permute-start.2 = (bf16[640,128]{1,0:T(8,128)(2,1)}, bf16[640,128]{1,0:T(8,128)(2,1)S(1)}, u32[]{:S(2)}, u32[]{:S(2)}) collective-permute-start(bf16[640,128]{1,0:T(8,128)(2,1)} %get-tuple-element.30), channel_id=1, source_target_pairs={{0,20},{4,16},{8,28},{12,24},{16,4},{20,0},{24,12},{28,8},{1,21},{... | collective-permute-start | bytes 491528 | tf_op jit(solution)/shard_map/ppermute | solution.py:32
  8.7 13.5 %collective-permute-start.3 = (bf16[640,128]{1,0:T(8,128)(2,1)}, bf16[640,128]{1,0:T(8,128)(2,1)S(1)}, u32[]{:S(2)}, u32[]{:S(2)}) collective-permute-start(bf16[640,128]{1,0:T(8,128)(2,1)} %get-tuple-element.31), channel_id=1, source_target_pairs={{0,16},{4,20},{8,24},{12,28},{16,0},{20,4},{24,8},{28,12},{1,17},{... | collective-permute-start | bytes 491528 | tf_op jit(solution)/shard_map/ppermute | solution.py:32
  9.0 13.2 %collective-permute-start.4 = (bf16[640,128]{1,0:T(8,128)(2,1)}, bf16[640,128]{1,0:T(8,128)(2,1)S(1)}, u32[]{:S(2)}, u32[]{:S(2)}) collective-permute-start(bf16[640,128]{1,0:T(8,128)(2,1)} %get-tuple-element.32), channel_id=1, source_target_pairs={{0,12},{4,8},{8,4},{12,0},{16,28},{20,24},{24,20},{28,16},{1,13},{... | collective-permute-start | bytes 491528 | tf_op jit(solution)/shard_map/ppermute | solution.py:32
  11.7 11.4 %collective-permute-start.5 = (bf16[640,128]{1,0:T(8,128)(2,1)}, bf16[640,128]{1,0:T(8,128)(2,1)S(1)}, u32[]{:S(2)}, u32[]{:S(2)}) collective-permute-start(bf16[640,128]{1,0:T(8,128)(2,1)} %get-tuple-element.33), channel_id=1, source_target_pairs={{0,8},{4,12},{8,0},{12,4},{16,24},{20,28},{24,16},{28,20},{1,9},{5... | collective-permute-start | bytes 491528 | tf_op jit(solution)/shard_map/ppermute | solution.py:32
  15.8 7.3 %collective-permute-start.6 = (bf16[640,128]{1,0:T(8,128)(2,1)}, bf16[640,128]{1,0:T(8,128)(2,1)S(1)}, u32[]{:S(2)}, u32[]{:S(2)}) collective-permute-start(bf16[640,128]{1,0:T(8,128)(2,1)} %get-tuple-element.34), channel_id=1, source_target_pairs={{0,4},{4,0},{8,12},{12,8},{16,20},{20,16},{24,28},{28,24},{1,5},{5... | collective-permute-start | bytes 491528 | tf_op jit(solution)/shard_map/ppermute | solution.py:32
  15.8 1.6 %copy-start = (bf16[4,2,256,512]{3,2,1,0:T(8,128)(2,1)S(1)}, bf16[4,2,256,512]{3,2,1,0:T(8,128)(2,1)}, u32[]{:S(2)}) copy-start(bf16[4,2,256,512]{3,2,1,0:T(8,128)(2,1)} %constant.5.clone.refs_3_) | copy-start | bytes 6291460
  17.3 1.6 %copy-start.1 = (bf16[4,2,512,256]{3,2,1,0:T(8,128)(2,1)S(1)}, bf16[4,2,512,256]{3,2,1,0:T(8,128)(2,1)}, u32[]{:S(2)}) copy-start(bf16[4,2,512,256]{3,2,1,0:T(8,128)(2,1)} %constant.4.clone.refs_2_) | copy-start | bytes 6291460
  18.9 0.8 %copy-start.6 = (f32[3,3,1024]{2,1,0:T(4,128)S(1)}, f32[3,3,1024]{2,1,0:T(4,128)}, u32[]{:S(2)}) copy-start(f32[3,3,1024]{2,1,0:T(4,128)} %refs_12_.1) | copy-start | bytes 110596
  19.7 0.9 %copy-start.8 = (bf16[640,128]{1,0:T(8,128)(2,1)S(1)}, bf16[640,128]{1,0:T(8,128)(2,1)}, u32[]{:S(2)}) copy-start(bf16[640,128]{1,0:T(8,128)(2,1)} %get-tuple-element.26.refs_0_) | copy-start | bytes 491524
  23.1 18.2 %copy-start.2 = (bf16[128,1024]{1,0:T(8,128)(2,1)S(1)}, bf16[128,1024]{1,0:T(8,128)(2,1)}, u32[]{:S(2)}) copy-start(bf16[128,1024]{1,0:T(8,128)(2,1)} %refs_8_.1) | copy-start | bytes 786436
  23.1 18.2 %copy-start.3 = (bf16[128,1024]{1,0:T(8,128)(2,1)S(1)}, bf16[128,1024]{1,0:T(8,128)(2,1)}, u32[]{:S(2)}) copy-start(bf16[128,1024]{1,0:T(8,128)(2,1)} %refs_9_.1) | copy-start | bytes 786436
  23.1 18.2 %copy-start.4 = (bf16[128,1024]{1,0:T(8,128)(2,1)S(1)}, bf16[128,1024]{1,0:T(8,128)(2,1)}, u32[]{:S(2)}) copy-start(bf16[128,1024]{1,0:T(8,128)(2,1)} %refs_10_.1) | copy-start | bytes 786436
  23.1 18.2 %copy-start.5 = (bf16[128,1024]{1,0:T(8,128)(2,1)S(1)}, bf16[128,1024]{1,0:T(8,128)(2,1)}, u32[]{:S(2)}) copy-start(bf16[128,1024]{1,0:T(8,128)(2,1)} %refs_11_.1) | copy-start | bytes 786436
  23.1 18.2 %copy-start.7 = (f32[3,3,1024]{2,1,0:T(4,128)S(1)}, f32[3,3,1024]{2,1,0:T(4,128)}, u32[]{:S(2)}) copy-start(f32[3,3,1024]{2,1,0:T(4,128)} %refs_12_.1) | copy-start | bytes 110596
  27.8 6.1 %collective-permute-start.7 = (bf16[432,128]{1,0:T(8,128)(2,1)S(1)}, bf16[432,128]{1,0:T(8,128)(2,1)S(1)}, u32[]{:S(2)}, u32[]{:S(2)}) collective-permute-start(bf16[432,128]{1,0:T(8,128)(2,1)S(1)} %get-tuple-element.39), channel_id=1, source_target_pairs={{0,28},{4,24},{8,20},{12,16},{16,12},{20,8},{24,4},{28,0},{1,29},{... | collective-permute-start | bytes 331784 | tf_op jit(solution)/shard_map/ppermute | solution.py:32
  29.9 6.9 %collective-permute-start.8 = (bf16[432,128]{1,0:T(8,128)(2,1)S(1)}, bf16[432,128]{1,0:T(8,128)(2,1)S(1)}, u32[]{:S(2)}, u32[]{:S(2)}) collective-permute-start(bf16[432,128]{1,0:T(8,128)(2,1)S(1)} %get-tuple-element.40), channel_id=1, source_target_pairs={{0,24},{4,28},{8,16},{12,20},{16,8},{20,12},{24,0},{28,4},{1,25},{... | collective-permute-start | bytes 331784 | tf_op jit(solution)/shard_map/ppermute | solution.py:32
  30.5 8.3 %collective-permute-start.9 = (bf16[432,128]{1,0:T(8,128)(2,1)S(1)}, bf16[432,128]{1,0:T(8,128)(2,1)S(1)}, u32[]{:S(2)}, u32[]{:S(2)}) collective-permute-start(bf16[432,128]{1,0:T(8,128)(2,1)S(1)} %get-tuple-element.41), channel_id=1, source_target_pairs={{0,20},{4,16},{8,28},{12,24},{16,4},{20,0},{24,12},{28,8},{1,21},{... | collective-permute-start | bytes 331784 | tf_op jit(solution)/shard_map/ppermute | solution.py:32
  31.6 9.5 %collective-permute-start.10 = (bf16[432,128]{1,0:T(8,128)(2,1)S(1)}, bf16[432,128]{1,0:T(8,128)(2,1)S(1)}, u32[]{:S(2)}, u32[]{:S(2)}) collective-permute-start(bf16[432,128]{1,0:T(8,128)(2,1)S(1)} %get-tuple-element.42), channel_id=1, source_target_pairs={{0,16},{4,20},{8,24},{12,28},{16,0},{20,4},{24,8},{28,12},{1,17},{... | collective-permute-start | bytes 331784 | tf_op jit(solution)/shard_map/ppermute | solution.py:32
  32.3 8.9 %collective-permute-start.11 = (bf16[432,128]{1,0:T(8,128)(2,1)S(1)}, bf16[432,128]{1,0:T(8,128)(2,1)S(1)}, u32[]{:S(2)}, u32[]{:S(2)}) collective-permute-start(bf16[432,128]{1,0:T(8,128)(2,1)S(1)} %get-tuple-element.43), channel_id=1, source_target_pairs={{0,12},{4,8},{8,4},{12,0},{16,28},{20,24},{24,20},{28,16},{1,13},{... | collective-permute-start | bytes 331784 | tf_op jit(solution)/shard_map/ppermute | solution.py:32
  33.8 7.4 %collective-permute-start.12 = (bf16[432,128]{1,0:T(8,128)(2,1)S(1)}, bf16[432,128]{1,0:T(8,128)(2,1)S(1)}, u32[]{:S(2)}, u32[]{:S(2)}) collective-permute-start(bf16[432,128]{1,0:T(8,128)(2,1)S(1)} %get-tuple-element.44), channel_id=1, source_target_pairs={{0,8},{4,12},{8,0},{12,4},{16,24},{20,28},{24,16},{28,20},{1,9},{5... | collective-permute-start | bytes 331784 | tf_op jit(solution)/shard_map/ppermute | solution.py:32
  36.7 4.5 %collective-permute-start.13 = (bf16[432,128]{1,0:T(8,128)(2,1)S(1)}, bf16[432,128]{1,0:T(8,128)(2,1)S(1)}, u32[]{:S(2)}, u32[]{:S(2)}) collective-permute-start(bf16[432,128]{1,0:T(8,128)(2,1)S(1)} %get-tuple-element.45), channel_id=1, source_target_pairs={{0,4},{4,0},{8,12},{12,8},{16,20},{20,16},{24,28},{28,24},{1,5},{5... | collective-permute-start | bytes 331784 | tf_op jit(solution)/shard_map/ppermute | solution.py:32

commit v3 on v2

--- a/solution.py
+++ b/solution.py
@@ -22,7 +22,11 @@
 
 
 def partners(peers):
-    return [0] + list(range(peers - 1, 0, -1))
+    def rank(step):
+        links = (step >> 1).bit_count()
+        return (links == 0, links, step & 1, -step)
+
+    return [0] + sorted(range(1, peers), key=rank)
 
 
 def exchange(blocks):

time: 43.7 us -> 43.3 us (level)
  waiting for transfers between devices: 11.4 us -> 9.55 us
  starting transfers between devices: 16.3 us -> 17.7 us
    ppermute x14, waiting for transfers between devices: 11.4 us -> 9.55 us  [exchange(): lax.ppermute(block, 'ctx', [(i, i ^ step) for i in range(peers)])]
    ppermute x14, starting transfers between devices: 16.3 us -> 17.7 us  [exchange(): lax.ppermute(block, 'ctx', [(i, i ^ step) for i in range(peers)])]
  transfers between devices with their start and end apart: 14 -> 14, of which waited for: 8 -> 5; matrix products, arithmetic and copies ran while one was open for 0% -> 0% of each run, Pallas kernels for 1% -> 1%
where the time goes in v3:
time: 43.3 us; the launch traced here: 43 us
  starting transfers between devices  17.7 us (41%)
  Pallas kernels  10.1 us (23%)
  waiting for transfers between devices  9.55 us (22%)
  local copies, waits for them, and re-layouts  4.92 us (11%)
  between operations  0.74 us (2%)
    ppermute x14, starting transfers between devices, exchange(): lax.ppermute(block, 'ctx', [(i, i ^ step) for i in range(peers)])  17.7 us
    ppermute x14, waiting for transfers between devices, exchange(): lax.ppermute(block, 'ctx', [(i, i ^ step) for i in range(peers)])  9.55 us
    unnamed x18, local copies, waits for them, and re-layouts  4.92 us
    pallas_call x1, Pallas kernels, channel_step(): pl.pallas_call(functools.partial(channel_kernel, tokens, peers, 1.0 / mat...  4.65 us
    pallas_call x1, Pallas kernels, pack(): pl.pallas_call(functools.partial(pack_kernel, len(arrays)), in_specs=in_v...  2.74 us
    pallas_call x1, Pallas kernels, token_step(): pl.pallas_call(functools.partial(token_kernel, peers, extra_rows(short_we...  2.13 us
  transfers between devices with their start and end apart: 14, of which 5 were waited for; matrix products, arithmetic and copies ran while one was open for 0% of the time, Pallas kernels for 1%

profile of v3, /device:TPU:0, one launch (start us, length us, event | category | flops | bytes accessed | tf_op | source)
XLA Modules:
  0.0 43.0 jit_solution(6290580839619666794)
XLA Ops:
  0.6 2.7 %pack_inputs.1 = (bf16[640,128]{1,0:T(8,128)(2,1)}, bf16[640,128]{1,0:T(8,128)(2,1)}, bf16[640,128]{1,0:T(8,128)(2,1)}, bf16[640,128]{1,0:T(8,128)(2,1)}, bf16[6...) custom-call(bf16[128,1024]{1,0:T(8,128)(2,1)} %refs_8_.1, ...), custom_call_target="tpu_custom_call" | custom-call | bytes 8388608 | tf_op jit(solution)/shard_map/pack_inputs/pallas_call | solution.py:59
  3.4 3.0 %collective-permute-start = (bf16[640,128]{1,0:T(8,128)(2,1)}, bf16[640,128]{1,0:T(8,128)(2,1)S(1)}, u32[]{:S(2)}, u32[]{:S(2)}) collective-permute-start(bf16[640,128]{1,0:T(8,128)(2,1)} %get-tuple-element.27), channel_id=1, source_target_pairs={{0,16},{4,20},{8,24},{12,28},{16,0},{20,4},{24,8},{28,12},{1,17},{... | collective-permute-start | bytes 491528 | tf_op jit(solution)/shard_map/ppermute | solution.py:36
  6.3 1.5 %collective-permute-start.1 = (bf16[640,128]{1,0:T(8,128)(2,1)}, bf16[640,128]{1,0:T(8,128)(2,1)S(1)}, u32[]{:S(2)}, u32[]{:S(2)}) collective-permute-start(bf16[640,128]{1,0:T(8,128)(2,1)} %get-tuple-element.29), channel_id=1, source_target_pairs={{0,8},{4,12},{8,0},{12,4},{16,24},{20,28},{24,16},{28,20},{1,9},{5... | collective-permute-start | bytes 491528 | tf_op jit(solution)/shard_map/ppermute | solution.py:36
  7.8 0.0 collective-permute-start.2
  7.8 0.3 collective-permute-start.3
  8.1 2.9 %collective-permute-start.4 = (bf16[640,128]{1,0:T(8,128)(2,1)}, bf16[640,128]{1,0:T(8,128)(2,1)S(1)}, u32[]{:S(2)}, u32[]{:S(2)}) collective-permute-start(bf16[640,128]{1,0:T(8,128)(2,1)} %get-tuple-element.32), channel_id=1, source_target_pairs={{0,24},{4,28},{8,16},{12,20},{16,8},{20,12},{24,0},{28,4},{1,25},{... | collective-permute-start | bytes 491528 | tf_op jit(solution)/shard_map/ppermute | solution.py:36
  11.0 0.9 %collective-permute-start.5 = (bf16[640,128]{1,0:T(8,128)(2,1)}, bf16[640,128]{1,0:T(8,128)(2,1)S(1)}, u32[]{:S(2)}, u32[]{:S(2)}) collective-permute-start(bf16[640,128]{1,0:T(8,128)(2,1)} %get-tuple-element.33), channel_id=1, source_target_pairs={{0,28},{4,24},{8,20},{12,16},{16,12},{20,8},{24,4},{28,0},{1,29},{... | collective-permute-start | bytes 491528 | tf_op jit(solution)/shard_map/ppermute | solution.py:36
  12.0 1.4 %collective-permute-done.1.refs_2_ = bf16[640,128]{1,0:T(8,128)(2,1)S(1)} collective-permute-done((bf16[640,128]{1,0:T(8,128)(2,1)}, bf16[640,128]{1,0:T(8,128)(2,1)S(1)}, u32[]{:S(2)}, u32[]{:S(2)}) %collective-permute-start.1) | collective-permute-done | bytes 163872 | tf_op jit(solution)/shard_map/ppermute | solution.py:36
  13.4 1.3 %collective-permute-start.6 = (bf16[640,128]{1,0:T(8,128)(2,1)}, bf16[640,128]{1,0:T(8,128)(2,1)S(1)}, u32[]{:S(2)}, u32[]{:S(2)}) collective-permute-start(bf16[640,128]{1,0:T(8,128)(2,1)} %get-tuple-element.34), channel_id=1, source_target_pairs={{0,4},{4,0},{8,12},{12,8},{16,20},{20,16},{24,28},{28,24},{1,5},{5... | collective-permute-start | bytes 491528 | tf_op jit(solution)/shard_map/ppermute | solution.py:36
  14.7 1.6 %copy-done = bf16[4,2,256,512]{3,2,1,0:T(8,128)(2,1)S(1)} copy-done((bf16[4,2,256,512]{3,2,1,0:T(8,128)(2,1)S(1)}, bf16[4,2,256,512]{3,2,1,0:T(8,128)(2,1)}, u32[]{:S(2)}) %copy-start) | copy-done | bytes 2097176
  16.3 1.6 %copy-done.1 = bf16[4,2,512,256]{3,2,1,0:T(8,128)(2,1)S(1)} copy-done((bf16[4,2,512,256]{3,2,1,0:T(8,128)(2,1)S(1)}, bf16[4,2,512,256]{3,2,1,0:T(8,128)(2,1)}, u32[]{:S(2)}) %copy-start.1) | copy-done | bytes 2097176
  17.9 0.8 %copy-done.6 = f32[3,3,1024]{2,1,0:T(4,128)S(1)} copy-done((f32[3,3,1024]{2,1,0:T(4,128)S(1)}, f32[3,3,1024]{2,1,0:T(4,128)}, u32[]{:S(2)}) %copy-start.6) | copy-done | bytes 36888
  18.7 0.9 %copy-done.8 = bf16[640,128]{1,0:T(8,128)(2,1)S(1)} copy-done((bf16[640,128]{1,0:T(8,128)(2,1)S(1)}, bf16[640,128]{1,0:T(8,128)(2,1)}, u32[]{:S(2)}) %copy-start.8) | copy-done | bytes 163864
  19.6 0.6 %stage_tables.1 = (bf16[640,128]{1,0:T(8,128)(2,1)S(1)}, f32[3,3,1024]{2,1,0:T(4,128)S(1)}, bf16[4,2,512,256]{3,2,1,0:T(8,128)(2,1)S(1)}, bf16[4,2,256,512]{3,2,1,0:T(8,128)(2,1)S(1)}) custom-call(bf16[640,128]{1,0:T(8,128)(2,1)S(1)} %copy-done.8, f32[3,3,1024]{2,1,0:T(4,128)S(1)} %copy-done.6, bf16[4,2,512,256]{3,2,1,0:T(8,128)(2,1)S(1)} %copy-done.1, ...), custom_call_target="tpu_custom_call" | custom-call | bytes 8388608 | tf_op jit(solution)/shard_map/stage_tables/pallas_call | solution.py:168
  20.2 0.0 collective-permute-done.2.refs_3_
  20.2 0.0 collective-permute-done.4.refs_5_
  20.2 1.7 %collective-permute-done.5.refs_6_ = bf16[640,128]{1,0:T(8,128)(2,1)S(1)} collective-permute-done((bf16[640,128]{1,0:T(8,128)(2,1)}, bf16[640,128]{1,0:T(8,128)(2,1)S(1)}, u32[]{:S(2)}, u32[]{:S(2)}) %collective-permute-start.5) | collective-permute-done | bytes 163872 | tf_op jit(solution)/shard_map/ppermute | solution.py:36
  21.9 0.0 collective-permute-done.6.refs_7_
  21.9 0.0 copy-start.5
  21.9 0.0 copy-start.7
  21.9 4.7 %channel_operator.1 = (bf16[432,128]{1,0:T(8,128)(2,1)S(1)}, bf16[432,128]{1,0:T(8,128)(2,1)S(1)}, bf16[432,128]{1,0:T(8,128)(2,1)S(1)}, bf16[432,128]{1,0:T(8,1...) custom-call(bf16[640,128]{1,0:T(8,128)(2,1)S(1)} %get-tuple-element., ...), custom_call_target="tpu_custom_call" | custom-call | tf_op jit(solution)/shard_map/channel_operator/pallas_call | solution.py:302
  26.6 1.2 %collective-permute-start.7 = (bf16[432,128]{1,0:T(8,128)(2,1)S(1)}, bf16[432,128]{1,0:T(8,128)(2,1)S(1)}, u32[]{:S(2)}, u32[]{:S(2)}) collective-permute-start(bf16[432,128]{1,0:T(8,128)(2,1)S(1)} %get-tuple-element.39), channel_id=1, source_target_pairs={{0,16},{4,20},{8,24},{12,28},{16,0},{20,4},{24,8},{28,12},{1,17},{... | collective-permute-start | bytes 331784 | tf_op jit(solution)/shard_map/ppermute | solution.py:36
  27.8 1.2 %collective-permute-start.8 = (bf16[432,128]{1,0:T(8,128)(2,1)S(1)}, bf16[432,128]{1,0:T(8,128)(2,1)S(1)}, u32[]{:S(2)}, u32[]{:S(2)}) collective-permute-start(bf16[432,128]{1,0:T(8,128)(2,1)S(1)} %get-tuple-element.40), channel_id=1, source_target_pairs={{0,8},{4,12},{8,0},{12,4},{16,24},{20,28},{24,16},{28,20},{1,9},{5... | collective-permute-start | bytes 331784 | tf_op jit(solution)/shard_map/ppermute | solution.py:36
  29.0 0.9 %collective-permute-start.9 = (bf16[432,128]{1,0:T(8,128)(2,1)S(1)}, bf16[432,128]{1,0:T(8,128)(2,1)S(1)}, u32[]{:S(2)}, u32[]{:S(2)}) collective-permute-start(bf16[432,128]{1,0:T(8,128)(2,1)S(1)} %get-tuple-element.41), channel_id=1, source_target_pairs={{0,20},{4,16},{8,28},{12,24},{16,4},{20,0},{24,12},{28,8},{1,21},{... | collective-permute-start | bytes 331784 | tf_op jit(solution)/shard_map/ppermute | solution.py:36
  29.9 0.5 %collective-permute-start.10 = (bf16[432,128]{1,0:T(8,128)(2,1)S(1)}, bf16[432,128]{1,0:T(8,128)(2,1)S(1)}, u32[]{:S(2)}, u32[]{:S(2)}) collective-permute-start(bf16[432,128]{1,0:T(8,128)(2,1)S(1)} %get-tuple-element.42), channel_id=1, source_target_pairs={{0,12},{4,8},{8,4},{12,0},{16,28},{20,24},{24,20},{28,16},{1,13},{... | collective-permute-start | bytes 331784 | tf_op jit(solution)/shard_map/ppermute | solution.py:36
  30.4 1.8 %collective-permute-start.11 = (bf16[432,128]{1,0:T(8,128)(2,1)S(1)}, bf16[432,128]{1,0:T(8,128)(2,1)S(1)}, u32[]{:S(2)}, u32[]{:S(2)}) collective-permute-start(bf16[432,128]{1,0:T(8,128)(2,1)S(1)} %get-tuple-element.43), channel_id=1, source_target_pairs={{0,24},{4,28},{8,16},{12,20},{16,8},{20,12},{24,0},{28,4},{1,25},{... | collective-permute-start | bytes 331784 | tf_op jit(solution)/shard_map/ppermute | solution.py:36
  32.2 0.0 collective-permute-done.7.refs_1_
  32.2 2.2 %collective-permute-start.12 = (bf16[432,128]{1,0:T(8,128)(2,1)S(1)}, bf16[432,128]{1,0:T(8,128)(2,1)S(1)}, u32[]{:S(2)}, u32[]{:S(2)}) collective-permute-start(bf16[432,128]{1,0:T(8,128)(2,1)S(1)} %get-tuple-element.44), channel_id=1, source_target_pairs={{0,28},{4,24},{8,20},{12,16},{16,12},{20,8},{24,4},{28,0},{1,29},{... | collective-permute-start | bytes 331784 | tf_op jit(solution)/shard_map/ppermute | solution.py:36
  34.4 1.2 %collective-permute-done.10.refs_4_ = bf16[432,128]{1,0:T(8,128)(2,1)S(1)} collective-permute-done((bf16[432,128]{1,0:T(8,128)(2,1)S(1)}, bf16[432,128]{1,0:T(8,128)(2,1)S(1)}, u32[]{:S(2)}, u32[]{:S(2)}) %collective-permute-start.10) | collective-permute-done | bytes 110624 | tf_op jit(solution)/shard_map/ppermute | solution.py:36
  35.6 2.8 %collective-permute-done.11.refs_5_ = bf16[432,128]{1,0:T(8,128)(2,1)S(1)} collective-permute-done((bf16[432,128]{1,0:T(8,128)(2,1)S(1)}, bf16[432,128]{1,0:T(8,128)(2,1)S(1)}, u32[]{:S(2)}, u32[]{:S(2)}) %collective-permute-start.11) | collective-permute-done | bytes 110624 | tf_op jit(solution)/shard_map/ppermute | solution.py:36
  38.4 2.4 %collective-permute-done.12.refs_6_ = bf16[432,128]{1,0:T(8,128)(2,1)S(1)} collective-permute-done((bf16[432,128]{1,0:T(8,128)(2,1)S(1)}, bf16[432,128]{1,0:T(8,128)(2,1)S(1)}, u32[]{:S(2)}, u32[]{:S(2)}) %collective-permute-start.12) | collective-permute-done | bytes 110624 | tf_op jit(solution)/shard_map/ppermute | solution.py:36
  40.9 2.1 %token_outputs.1 = (bf16[128,1024]{1,0:T(8,128)(2,1)}, bf16[128,1024]{1,0:T(8,128)(2,1)}, bf16[128,1024]{1,0:T(8,128)(2,1)}, bf16[128,1024]{1,0:T(8,128)(2,1)}, ...) custom-call(bf16[432,128]{1,0:T(8,128)(2,1)S(1)} %get-tuple-element.38.refs_0_, ...), custom_call_target="tpu_custom_call" | custom-call | tf_op jit(solution)/shard_map/token_outputs/pallas_call | solution.py:388
  (18 shorter events, 0.0 us)
Async XLA Ops:
  3.4 7.7 %collective-permute-start = (bf16[640,128]{1,0:T(8,128)(2,1)}, bf16[640,128]{1,0:T(8,128)(2,1)S(1)}, u32[]{:S(2)}, u32[]{:S(2)}) collective-permute-start(bf16[640,128]{1,0:T(8,128)(2,1)} %get-tuple-element.27), channel_id=1, source_target_pairs={{0,16},{4,20},{8,24},{12,28},{16,0},{20,4},{24,8},{28,12},{1,17},{... | collective-permute-start | bytes 491528 | tf_op jit(solution)/shard_map/ppermute | solution.py:36
  6.3 7.1 %collective-permute-start.1 = (bf16[640,128]{1,0:T(8,128)(2,1)}, bf16[640,128]{1,0:T(8,128)(2,1)S(1)}, u32[]{:S(2)}, u32[]{:S(2)}) collective-permute-start(bf16[640,128]{1,0:T(8,128)(2,1)} %get-tuple-element.29), channel_id=1, source_target_pairs={{0,8},{4,12},{8,0},{12,4},{16,24},{20,28},{24,16},{28,20},{1,9},{5... | collective-permute-start | bytes 491528 | tf_op jit(solution)/shard_map/ppermute | solution.py:36
  7.8 12.3 %collective-permute-start.2 = (bf16[640,128]{1,0:T(8,128)(2,1)}, bf16[640,128]{1,0:T(8,128)(2,1)S(1)}, u32[]{:S(2)}, u32[]{:S(2)}) collective-permute-start(bf16[640,128]{1,0:T(8,128)(2,1)} %get-tuple-element.30), channel_id=1, source_target_pairs={{0,20},{4,16},{8,28},{12,24},{16,4},{20,0},{24,12},{28,8},{1,21},{... | collective-permute-start | bytes 491528 | tf_op jit(solution)/shard_map/ppermute | solution.py:36
  7.8 12.3 %collective-permute-start.3 = (bf16[640,128]{1,0:T(8,128)(2,1)}, bf16[640,128]{1,0:T(8,128)(2,1)S(1)}, u32[]{:S(2)}, u32[]{:S(2)}) collective-permute-start(bf16[640,128]{1,0:T(8,128)(2,1)} %get-tuple-element.31), channel_id=1, source_target_pairs={{0,12},{4,8},{8,4},{12,0},{16,28},{20,24},{24,20},{28,16},{1,13},{... | collective-permute-start | bytes 491528 | tf_op jit(solution)/shard_map/ppermute | solution.py:36
  8.1 12.1 %collective-permute-start.4 = (bf16[640,128]{1,0:T(8,128)(2,1)}, bf16[640,128]{1,0:T(8,128)(2,1)S(1)}, u32[]{:S(2)}, u32[]{:S(2)}) collective-permute-start(bf16[640,128]{1,0:T(8,128)(2,1)} %get-tuple-element.32), channel_id=1, source_target_pairs={{0,24},{4,28},{8,16},{12,20},{16,8},{20,12},{24,0},{28,4},{1,25},{... | collective-permute-start | bytes 491528 | tf_op jit(solution)/shard_map/ppermute | solution.py:36
  11.0 10.8 %collective-permute-start.5 = (bf16[640,128]{1,0:T(8,128)(2,1)}, bf16[640,128]{1,0:T(8,128)(2,1)S(1)}, u32[]{:S(2)}, u32[]{:S(2)}) collective-permute-start(bf16[640,128]{1,0:T(8,128)(2,1)} %get-tuple-element.33), channel_id=1, source_target_pairs={{0,28},{4,24},{8,20},{12,16},{16,12},{20,8},{24,4},{28,0},{1,29},{... | collective-permute-start | bytes 491528 | tf_op jit(solution)/shard_map/ppermute | solution.py:36
  13.4 8.5 %collective-permute-start.6 = (bf16[640,128]{1,0:T(8,128)(2,1)}, bf16[640,128]{1,0:T(8,128)(2,1)S(1)}, u32[]{:S(2)}, u32[]{:S(2)}) collective-permute-start(bf16[640,128]{1,0:T(8,128)(2,1)} %get-tuple-element.34), channel_id=1, source_target_pairs={{0,4},{4,0},{8,12},{12,8},{16,20},{20,16},{24,28},{28,24},{1,5},{5... | collective-permute-start | bytes 491528 | tf_op jit(solution)/shard_map/ppermute | solution.py:36
  14.7 1.6 %copy-start = (bf16[4,2,256,512]{3,2,1,0:T(8,128)(2,1)S(1)}, bf16[4,2,256,512]{3,2,1,0:T(8,128)(2,1)}, u32[]{:S(2)}) copy-start(bf16[4,2,256,512]{3,2,1,0:T(8,128)(2,1)} %constant.5.clone.refs_3_) | copy-start | bytes 6291460
  16.3 1.6 %copy-start.1 = (bf16[4,2,512,256]{3,2,1,0:T(8,128)(2,1)S(1)}, bf16[4,2,512,256]{3,2,1,0:T(8,128)(2,1)}, u32[]{:S(2)}) copy-start(bf16[4,2,512,256]{3,2,1,0:T(8,128)(2,1)} %constant.4.clone.refs_2_) | copy-start | bytes 6291460
  17.9 0.8 %copy-start.6 = (f32[3,3,1024]{2,1,0:T(4,128)S(1)}, f32[3,3,1024]{2,1,0:T(4,128)}, u32[]{:S(2)}) copy-start(f32[3,3,1024]{2,1,0:T(4,128)} %refs_12_.1) | copy-start | bytes 110596
  18.7 0.9 %copy-start.8 = (bf16[640,128]{1,0:T(8,128)(2,1)S(1)}, bf16[640,128]{1,0:T(8,128)(2,1)}, u32[]{:S(2)}) copy-start(bf16[640,128]{1,0:T(8,128)(2,1)} %get-tuple-element.26.refs_0_) | copy-start | bytes 491524
  21.9 19.0 %copy-start.2 = (bf16[128,1024]{1,0:T(8,128)(2,1)S(1)}, bf16[128,1024]{1,0:T(8,128)(2,1)}, u32[]{:S(2)}) copy-start(bf16[128,1024]{1,0:T(8,128)(2,1)} %refs_8_.1) | copy-start | bytes 786436
  21.9 19.0 %copy-start.3 = (bf16[128,1024]{1,0:T(8,128)(2,1)S(1)}, bf16[128,1024]{1,0:T(8,128)(2,1)}, u32[]{:S(2)}) copy-start(bf16[128,1024]{1,0:T(8,128)(2,1)} %refs_9_.1) | copy-start | bytes 786436
  21.9 19.0 %copy-start.4 = (bf16[128,1024]{1,0:T(8,128)(2,1)S(1)}, bf16[128,1024]{1,0:T(8,128)(2,1)}, u32[]{:S(2)}) copy-start(bf16[128,1024]{1,0:T(8,128)(2,1)} %refs_10_.1) | copy-start | bytes 786436
  21.9 19.0 %copy-start.5 = (bf16[128,1024]{1,0:T(8,128)(2,1)S(1)}, bf16[128,1024]{1,0:T(8,128)(2,1)}, u32[]{:S(2)}) copy-start(bf16[128,1024]{1,0:T(8,128)(2,1)} %refs_11_.1) | copy-start | bytes 786436
  21.9 19.0 %copy-start.7 = (f32[3,3,1024]{2,1,0:T(4,128)S(1)}, f32[3,3,1024]{2,1,0:T(4,128)}, u32[]{:S(2)}) copy-start(f32[3,3,1024]{2,1,0:T(4,128)} %refs_12_.1) | copy-start | bytes 110596
  26.6 5.7 %collective-permute-start.7 = (bf16[432,128]{1,0:T(8,128)(2,1)S(1)}, bf16[432,128]{1,0:T(8,128)(2,1)S(1)}, u32[]{:S(2)}, u32[]{:S(2)}) collective-permute-start(bf16[432,128]{1,0:T(8,128)(2,1)S(1)} %get-tuple-element.39), channel_id=1, source_target_pairs={{0,16},{4,20},{8,24},{12,28},{16,0},{20,4},{24,8},{28,12},{1,17},{... | collective-permute-start | bytes 331784 | tf_op jit(solution)/shard_map/ppermute | solution.py:36
  27.8 6.6 %collective-permute-start.8 = (bf16[432,128]{1,0:T(8,128)(2,1)S(1)}, bf16[432,128]{1,0:T(8,128)(2,1)S(1)}, u32[]{:S(2)}, u32[]{:S(2)}) collective-permute-start(bf16[432,128]{1,0:T(8,128)(2,1)S(1)} %get-tuple-element.40), channel_id=1, source_target_pairs={{0,8},{4,12},{8,0},{12,4},{16,24},{20,28},{24,16},{28,20},{1,9},{5... | collective-permute-start | bytes 331784 | tf_op jit(solution)/shard_map/ppermute | solution.py:36
  29.0 5.4 %collective-permute-start.9 = (bf16[432,128]{1,0:T(8,128)(2,1)S(1)}, bf16[432,128]{1,0:T(8,128)(2,1)S(1)}, u32[]{:S(2)}, u32[]{:S(2)}) collective-permute-start(bf16[432,128]{1,0:T(8,128)(2,1)S(1)} %get-tuple-element.41), channel_id=1, source_target_pairs={{0,20},{4,16},{8,28},{12,24},{16,4},{20,0},{24,12},{28,8},{1,21},{... | collective-permute-start | bytes 331784 | tf_op jit(solution)/shard_map/ppermute | solution.py:36
  29.9 5.7 %collective-permute-start.10 = (bf16[432,128]{1,0:T(8,128)(2,1)S(1)}, bf16[432,128]{1,0:T(8,128)(2,1)S(1)}, u32[]{:S(2)}, u32[]{:S(2)}) collective-permute-start(bf16[432,128]{1,0:T(8,128)(2,1)S(1)} %get-tuple-element.42), channel_id=1, source_target_pairs={{0,12},{4,8},{8,4},{12,0},{16,28},{20,24},{24,20},{28,16},{1,13},{... | collective-permute-start | bytes 331784 | tf_op jit(solution)/shard_map/ppermute | solution.py:36
  30.4 8.0 %collective-permute-start.11 = (bf16[432,128]{1,0:T(8,128)(2,1)S(1)}, bf16[432,128]{1,0:T(8,128)(2,1)S(1)}, u32[]{:S(2)}, u32[]{:S(2)}) collective-permute-start(bf16[432,128]{1,0:T(8,128)(2,1)S(1)} %get-tuple-element.43), channel_id=1, source_target_pairs={{0,24},{4,28},{8,16},{12,20},{16,8},{20,12},{24,0},{28,4},{1,25},{... | collective-permute-start | bytes 331784 | tf_op jit(solution)/shard_map/ppermute | solution.py:36
  32.2 8.6 %collective-permute-start.12 = (bf16[432,128]{1,0:T(8,128)(2,1)S(1)}, bf16[432,128]{1,0:T(8,128)(2,1)S(1)}, u32[]{:S(2)}, u32[]{:S(2)}) collective-permute-start(bf16[432,128]{1,0:T(8,128)(2,1)S(1)} %get-tuple-element.44), channel_id=1, source_target_pairs={{0,28},{4,24},{8,20},{12,16},{16,12},{20,8},{24,4},{28,0},{1,29},{... | collective-permute-start | bytes 331784 | tf_op jit(solution)/shard_map/ppermute | solution.py:36
  34.4 6.5 %collective-permute-start.13 = (bf16[432,128]{1,0:T(8,128)(2,1)S(1)}, bf16[432,128]{1,0:T(8,128)(2,1)S(1)}, u32[]{:S(2)}, u32[]{:S(2)}) collective-permute-start(bf16[432,128]{1,0:T(8,128)(2,1)S(1)} %get-tuple-element.45), channel_id=1, source_target_pairs={{0,4},{4,0},{8,12},{12,8},{16,20},{20,16},{24,28},{28,24},{1,5},{5... | collective-permute-start | bytes 331784 | tf_op jit(solution)/shard_map/ppermute | solution.py:36

commit v4 on v3

--- a/solution.py
+++ b/solution.py
@@ -24,7 +24,7 @@
 def partners(peers):
     def rank(step):
         links = (step >> 1).bit_count()
-        return (links == 0, links, step & 1, -step)
+        return (links == 0, links == 1 and step & 1, links, step & 1, -step)
 
     return [0] + sorted(range(1, peers), key=rank)
 
@@ -61,6 +61,7 @@
         in_specs=in_vmem(len(arrays)),
         out_specs=in_vmem(peers),
         out_shape=[jax.ShapeDtypeStruct((len(arrays) * tokens, LANES), BF16)] * peers,
+        compiler_params=pltpu.CompilerParams(vmem_limit_bytes=VMEM_LIMIT),
         cost_estimate=pl.CostEstimate(flops=0, bytes_accessed=8 * MIB, transcendentals=0),
         name="pack_inputs",
     )(*arrays)

time: 43.3 us -> 45.4 us (1.048)
  local copies, waits for them, and re-layouts: 4.92 us -> 8.84 us
  waiting for transfers between devices: 9.55 us -> 13.4 us
  starting transfers between devices: 17.7 us -> 14.4 us
  Pallas kernels: 10.1 us -> 7.69 us
    unnamed x18 -> x26, local copies, waits for them, and re-layouts: 4.92 us -> 8.84 us
    ppermute x14, waiting for transfers between devices: 9.55 us -> 13.4 us  [exchange(): lax.ppermute(block, 'ctx', [(i, i ^ step) for i in range(peers)])]
    ppermute x14, starting transfers between devices: 17.7 us -> 14.4 us  [exchange(): lax.ppermute(block, 'ctx', [(i, i ^ step) for i in range(peers)])]
    pallas_call x1, Pallas kernels: 2.74 us -> 0.34 us  [pack(): pl.pallas_call(functools.partial(pack_kernel, len(arrays)), in_specs=in_v...]
  transfers between devices with their start and end apart: 14 -> 14, of which waited for: 5 -> 8; matrix products, arithmetic and copies ran while one was open for 0% -> 0% of each run, Pallas kernels for 1% -> 1%
where the time goes in v4:
time: 45.4 us; the launch traced here: 45 us
  starting transfers between devices  14.4 us (32%)
  waiting for transfers between devices  13.4 us (30%)
  local copies, waits for them, and re-layouts  8.84 us (19%)
  Pallas kernels  7.69 us (17%)
  between operations  0.74 us (2%)
    ppermute x14, starting transfers between devices, exchange(): lax.ppermute(block, 'ctx', [(i, i ^ step) for i in range(peers)])  14.4 us
    ppermute x14, waiting for transfers between devices, exchange(): lax.ppermute(block, 'ctx', [(i, i ^ step) for i in range(peers)])  13.4 us
    unnamed x26, local copies, waits for them, and re-layouts  8.84 us
    pallas_call x1, Pallas kernels, channel_step(): pl.pallas_call(functools.partial(channel_kernel, tokens, peers, 1.0 / mat...  4.65 us
    pallas_call x1, Pallas kernels, token_step(): pl.pallas_call(functools.partial(token_kernel, peers, extra_rows(short_we...  2.14 us
  transfers between devices with their start and end apart: 14, of which 8 were waited for; matrix products, arithmetic and copies ran while one was open for 0% of the time, Pallas kernels for 1%

profile of v4, /device:TPU:0, one launch (start us, length us, event | category | flops | bytes accessed | tf_op | source)
XLA Modules:
  0.0 45.0 jit_solution(3222496944494104104)
XLA Ops:
  0.6 0.9 %copy-done.2 = bf16[128,1024]{1,0:T(8,128)(2,1)S(1)} copy-done((bf16[128,1024]{1,0:T(8,128)(2,1)S(1)}, bf16[128,1024]{1,0:T(8,128)(2,1)}, u32[]{:S(2)}) %copy-start.2) | copy-done | bytes 262168
  1.6 0.9 %copy-done.4 = bf16[128,1024]{1,0:T(8,128)(2,1)S(1)} copy-done((bf16[128,1024]{1,0:T(8,128)(2,1)S(1)}, bf16[128,1024]{1,0:T(8,128)(2,1)}, u32[]{:S(2)}) %copy-start.4) | copy-done | bytes 262168
  2.5 0.9 %copy-done.6 = bf16[128,1024]{1,0:T(8,128)(2,1)S(1)} copy-done((bf16[128,1024]{1,0:T(8,128)(2,1)S(1)}, bf16[128,1024]{1,0:T(8,128)(2,1)}, u32[]{:S(2)}) %copy-start.6) | copy-done | bytes 262168
  3.5 0.9 %copy-done.8 = bf16[128,1024]{1,0:T(8,128)(2,1)S(1)} copy-done((bf16[128,1024]{1,0:T(8,128)(2,1)S(1)}, bf16[128,1024]{1,0:T(8,128)(2,1)}, u32[]{:S(2)}) %copy-start.8) | copy-done | bytes 262168
  4.4 1.0 %copy-done.10 = f32[128,1024]{1,0:T(8,128)S(1)} copy-done((f32[128,1024]{1,0:T(8,128)S(1)}, f32[128,1024]{1,0:T(8,128)}, u32[]{:S(2)}) %copy-start.10) | copy-done | bytes 524312
  5.5 0.3 pack_inputs.1
  5.8 3.0 %collective-permute-start = (bf16[640,128]{1,0:T(8,128)(2,1)S(1)}, bf16[640,128]{1,0:T(8,128)(2,1)S(1)}, u32[]{:S(2)}, u32[]{:S(2)}) collective-permute-start(bf16[640,128]{1,0:T(8,128)(2,1)S(1)} %get-tuple-element.27), channel_id=1, source_target_pairs={{0,16},{4,20},{8,24},{12,28},{16,0},{20,4},{24,8},{28,12},{1,17},{... | collective-permute-start | bytes 491528 | tf_op jit(solution)/shard_map/ppermute | solution.py:36
  8.9 1.5 %collective-permute-start.1 = (bf16[640,128]{1,0:T(8,128)(2,1)S(1)}, bf16[640,128]{1,0:T(8,128)(2,1)S(1)}, u32[]{:S(2)}, u32[]{:S(2)}) collective-permute-start(bf16[640,128]{1,0:T(8,128)(2,1)S(1)} %get-tuple-element.29), channel_id=1, source_target_pairs={{0,8},{4,12},{8,0},{12,4},{16,24},{20,28},{24,16},{28,20},{1,9},{5... | collective-permute-start | bytes 491528 | tf_op jit(solution)/shard_map/ppermute | solution.py:36
  10.3 0.0 collective-permute-start.2
  10.4 1.5 %collective-permute-start.3 = (bf16[640,128]{1,0:T(8,128)(2,1)S(1)}, bf16[640,128]{1,0:T(8,128)(2,1)S(1)}, u32[]{:S(2)}, u32[]{:S(2)}) collective-permute-start(bf16[640,128]{1,0:T(8,128)(2,1)S(1)} %get-tuple-element.31), channel_id=1, source_target_pairs={{0,28},{4,24},{8,20},{12,16},{16,12},{20,8},{24,4},{28,0},{1,29},{... | collective-permute-start | bytes 491528 | tf_op jit(solution)/shard_map/ppermute | solution.py:36
  11.9 1.6 %collective-permute-start.4 = (bf16[640,128]{1,0:T(8,128)(2,1)S(1)}, bf16[640,128]{1,0:T(8,128)(2,1)S(1)}, u32[]{:S(2)}, u32[]{:S(2)}) collective-permute-start(bf16[640,128]{1,0:T(8,128)(2,1)S(1)} %get-tuple-element.32), channel_id=1, source_target_pairs={{0,20},{4,16},{8,28},{12,24},{16,4},{20,0},{24,12},{28,8},{1,21},{... | collective-permute-start | bytes 491528 | tf_op jit(solution)/shard_map/ppermute | solution.py:36
  13.5 0.1 collective-permute-start.5
  13.6 2.4 %collective-permute-done.1.refs_2_ = bf16[640,128]{1,0:T(8,128)(2,1)S(1)} collective-permute-done((bf16[640,128]{1,0:T(8,128)(2,1)S(1)}, bf16[640,128]{1,0:T(8,128)(2,1)S(1)}, u32[]{:S(2)}, u32[]{:S(2)}) %collective-permute-start.1) | collective-permute-done | bytes 163872 | tf_op jit(solution)/shard_map/ppermute | solution.py:36
  16.0 1.6 %copy-done = bf16[4,2,256,512]{3,2,1,0:T(8,128)(2,1)S(1)} copy-done((bf16[4,2,256,512]{3,2,1,0:T(8,128)(2,1)S(1)}, bf16[4,2,256,512]{3,2,1,0:T(8,128)(2,1)}, u32[]{:S(2)}) %copy-start) | copy-done | bytes 2097176
  17.6 1.6 %copy-done.1 = bf16[4,2,512,256]{3,2,1,0:T(8,128)(2,1)S(1)} copy-done((bf16[4,2,512,256]{3,2,1,0:T(8,128)(2,1)S(1)}, bf16[4,2,512,256]{3,2,1,0:T(8,128)(2,1)}, u32[]{:S(2)}) %copy-start.1) | copy-done | bytes 2097176
  19.2 0.8 %copy-done.11 = f32[3,3,1024]{2,1,0:T(4,128)S(1)} copy-done((f32[3,3,1024]{2,1,0:T(4,128)S(1)}, f32[3,3,1024]{2,1,0:T(4,128)}, u32[]{:S(2)}) %copy-start.11) | copy-done | bytes 36888
  20.0 0.6 %stage_tables.1 = (bf16[640,128]{1,0:T(8,128)(2,1)S(1)}, f32[3,3,1024]{2,1,0:T(4,128)S(1)}, bf16[4,2,512,256]{3,2,1,0:T(8,128)(2,1)S(1)}, bf16[4,2,256,512]{3,2,1,0:T(8,128)(2,1)S(1)}) custom-call(bf16[640,128]{1,0:T(8,128)(2,1)S(1)} %get-tuple-element.26.refs_0_, f32[3,3,1024]{2,1,0:T(4,128)S(1)} %copy-done.11, bf16[4,2,512,256]{3,2,1,0:T(8,128)(2,1)S(1)} %copy-done.1, ...), custom_call_target="tpu_custom_call" | custom-call | bytes 8388608 | tf_op jit(solution)/shard_map/stage_tables/pallas_call | solution.py:169
  20.5 1.5 %collective-permute-done.3.refs_4_ = bf16[640,128]{1,0:T(8,128)(2,1)S(1)} collective-permute-done((bf16[640,128]{1,0:T(8,128)(2,1)S(1)}, bf16[640,128]{1,0:T(8,128)(2,1)S(1)}, u32[]{:S(2)}, u32[]{:S(2)}) %collective-permute-start.3) | collective-permute-done | bytes 163872 | tf_op jit(solution)/shard_map/ppermute | solution.py:36
  22.1 2.0 %collective-permute-done.4.refs_5_ = bf16[640,128]{1,0:T(8,128)(2,1)S(1)} collective-permute-done((bf16[640,128]{1,0:T(8,128)(2,1)S(1)}, bf16[640,128]{1,0:T(8,128)(2,1)S(1)}, u32[]{:S(2)}, u32[]{:S(2)}) %collective-permute-start.4) | collective-permute-done | bytes 163872 | tf_op jit(solution)/shard_map/ppermute | solution.py:36
  24.1 4.7 %channel_operator.1 = (bf16[432,128]{1,0:T(8,128)(2,1)S(1)}, bf16[432,128]{1,0:T(8,128)(2,1)S(1)}, bf16[432,128]{1,0:T(8,128)(2,1)S(1)}, bf16[432,128]{1,0:T(8,1...) custom-call(bf16[640,128]{1,0:T(8,128)(2,1)S(1)} %get-tuple-element., ...), custom_call_target="tpu_custom_call" | custom-call | tf_op jit(solution)/shard_map/channel_operator/pallas_call | solution.py:303
  28.8 1.5 %collective-permute-start.7 = (bf16[432,128]{1,0:T(8,128)(2,1)S(1)}, bf16[432,128]{1,0:T(8,128)(2,1)S(1)}, u32[]{:S(2)}, u32[]{:S(2)}) collective-permute-start(bf16[432,128]{1,0:T(8,128)(2,1)S(1)} %get-tuple-element.39), channel_id=1, source_target_pairs={{0,16},{4,20},{8,24},{12,28},{16,0},{20,4},{24,8},{28,12},{1,17},{... | collective-permute-start | bytes 331784 | tf_op jit(solution)/shard_map/ppermute | solution.py:36
  30.3 1.2 %collective-permute-start.8 = (bf16[432,128]{1,0:T(8,128)(2,1)S(1)}, bf16[432,128]{1,0:T(8,128)(2,1)S(1)}, u32[]{:S(2)}, u32[]{:S(2)}) collective-permute-start(bf16[432,128]{1,0:T(8,128)(2,1)S(1)} %get-tuple-element.40), channel_id=1, source_target_pairs={{0,8},{4,12},{8,0},{12,4},{16,24},{20,28},{24,16},{28,20},{1,9},{5... | collective-permute-start | bytes 331784 | tf_op jit(solution)/shard_map/ppermute | solution.py:36
  31.6 0.8 %collective-permute-start.9 = (bf16[432,128]{1,0:T(8,128)(2,1)S(1)}, bf16[432,128]{1,0:T(8,128)(2,1)S(1)}, u32[]{:S(2)}, u32[]{:S(2)}) collective-permute-start(bf16[432,128]{1,0:T(8,128)(2,1)S(1)} %get-tuple-element.41), channel_id=1, source_target_pairs={{0,24},{4,28},{8,16},{12,20},{16,8},{20,12},{24,0},{28,4},{1,25},{... | collective-permute-start | bytes 331784 | tf_op jit(solution)/shard_map/ppermute | solution.py:36
  32.3 1.0 %collective-permute-start.10 = (bf16[432,128]{1,0:T(8,128)(2,1)S(1)}, bf16[432,128]{1,0:T(8,128)(2,1)S(1)}, u32[]{:S(2)}, u32[]{:S(2)}) collective-permute-start(bf16[432,128]{1,0:T(8,128)(2,1)S(1)} %get-tuple-element.42), channel_id=1, source_target_pairs={{0,28},{4,24},{8,20},{12,16},{16,12},{20,8},{24,4},{28,0},{1,29},{... | collective-permute-start | bytes 331784 | tf_op jit(solution)/shard_map/ppermute | solution.py:36
  33.4 1.2 %collective-permute-start.11 = (bf16[432,128]{1,0:T(8,128)(2,1)S(1)}, bf16[432,128]{1,0:T(8,128)(2,1)S(1)}, u32[]{:S(2)}, u32[]{:S(2)}) collective-permute-start(bf16[432,128]{1,0:T(8,128)(2,1)S(1)} %get-tuple-element.43), channel_id=1, source_target_pairs={{0,20},{4,16},{8,28},{12,24},{16,4},{20,0},{24,12},{28,8},{1,21},{... | collective-permute-start | bytes 331784 | tf_op jit(solution)/shard_map/ppermute | solution.py:36
  34.6 0.1 collective-permute-done.7.refs_1_
  34.6 0.9 %collective-permute-start.12 = (bf16[432,128]{1,0:T(8,128)(2,1)S(1)}, bf16[432,128]{1,0:T(8,128)(2,1)S(1)}, u32[]{:S(2)}, u32[]{:S(2)}) collective-permute-start(bf16[432,128]{1,0:T(8,128)(2,1)S(1)} %get-tuple-element.44), channel_id=1, source_target_pairs={{0,12},{4,8},{8,4},{12,0},{16,28},{20,24},{24,20},{28,16},{1,13},{... | collective-permute-start | bytes 331784 | tf_op jit(solution)/shard_map/ppermute | solution.py:36
  35.5 0.3 collective-permute-done.8.refs_2_
  35.8 2.8 %collective-permute-done.9.refs_3_ = bf16[432,128]{1,0:T(8,128)(2,1)S(1)} collective-permute-done((bf16[432,128]{1,0:T(8,128)(2,1)S(1)}, bf16[432,128]{1,0:T(8,128)(2,1)S(1)}, u32[]{:S(2)}, u32[]{:S(2)}) %collective-permute-start.9) | collective-permute-done | bytes 110624 | tf_op jit(solution)/shard_map/ppermute | solution.py:36
  38.6 1.7 %collective-permute-done.10.refs_4_ = bf16[432,128]{1,0:T(8,128)(2,1)S(1)} collective-permute-done((bf16[432,128]{1,0:T(8,128)(2,1)S(1)}, bf16[432,128]{1,0:T(8,128)(2,1)S(1)}, u32[]{:S(2)}, u32[]{:S(2)}) %collective-permute-start.10) | collective-permute-done | bytes 110624 | tf_op jit(solution)/shard_map/ppermute | solution.py:36
  40.3 2.5 %collective-permute-done.11.refs_5_ = bf16[432,128]{1,0:T(8,128)(2,1)S(1)} collective-permute-done((bf16[432,128]{1,0:T(8,128)(2,1)S(1)}, bf16[432,128]{1,0:T(8,128)(2,1)S(1)}, u32[]{:S(2)}, u32[]{:S(2)}) %collective-permute-start.11) | collective-permute-done | bytes 110624 | tf_op jit(solution)/shard_map/ppermute | solution.py:36
  42.9 2.1 %token_outputs.1 = (bf16[128,1024]{1,0:T(8,128)(2,1)}, bf16[128,1024]{1,0:T(8,128)(2,1)}, bf16[128,1024]{1,0:T(8,128)(2,1)}, bf16[128,1024]{1,0:T(8,128)(2,1)}, ...) custom-call(bf16[432,128]{1,0:T(8,128)(2,1)S(1)} %get-tuple-element.38.refs_0_, ...), custom_call_target="tpu_custom_call" | custom-call | tf_op jit(solution)/shard_map/token_outputs/pallas_call | solution.py:389
  (26 shorter events, 0.1 us)
Async XLA Ops:
  0.6 1.0 %copy-start.2 = (bf16[128,1024]{1,0:T(8,128)(2,1)S(1)}, bf16[128,1024]{1,0:T(8,128)(2,1)}, u32[]{:S(2)}) copy-start(bf16[128,1024]{1,0:T(8,128)(2,1)} %refs_8_.1) | copy-start | bytes 786436
  1.6 0.9 %copy-start.4 = (bf16[128,1024]{1,0:T(8,128)(2,1)S(1)}, bf16[128,1024]{1,0:T(8,128)(2,1)}, u32[]{:S(2)}) copy-start(bf16[128,1024]{1,0:T(8,128)(2,1)} %refs_9_.1) | copy-start | bytes 786436
  2.5 0.9 %copy-start.6 = (bf16[128,1024]{1,0:T(8,128)(2,1)S(1)}, bf16[128,1024]{1,0:T(8,128)(2,1)}, u32[]{:S(2)}) copy-start(bf16[128,1024]{1,0:T(8,128)(2,1)} %refs_10_.1) | copy-start | bytes 786436
  3.5 0.9 %copy-start.8 = (bf16[128,1024]{1,0:T(8,128)(2,1)S(1)}, bf16[128,1024]{1,0:T(8,128)(2,1)}, u32[]{:S(2)}) copy-start(bf16[128,1024]{1,0:T(8,128)(2,1)} %refs_11_.1) | copy-start | bytes 786436
  4.4 1.0 %copy-start.10 = (f32[128,1024]{1,0:T(8,128)S(1)}, f32[128,1024]{1,0:T(8,128)}, u32[]{:S(2)}) copy-start(f32[128,1024]{1,0:T(8,128)} %refs_4_.1) | copy-start | bytes 1572868
  5.8 7.7 %collective-permute-start = (bf16[640,128]{1,0:T(8,128)(2,1)S(1)}, bf16[640,128]{1,0:T(8,128)(2,1)S(1)}, u32[]{:S(2)}, u32[]{:S(2)}) collective-permute-start(bf16[640,128]{1,0:T(8,128)(2,1)S(1)} %get-tuple-element.27), channel_id=1, source_target_pairs={{0,16},{4,20},{8,24},{12,28},{16,0},{20,4},{24,8},{28,12},{1,17},{... | collective-permute-start | bytes 491528 | tf_op jit(solution)/shard_map/ppermute | solution.py:36
  8.9 7.1 %collective-permute-start.1 = (bf16[640,128]{1,0:T(8,128)(2,1)S(1)}, bf16[640,128]{1,0:T(8,128)(2,1)S(1)}, u32[]{:S(2)}, u32[]{:S(2)}) collective-permute-start(bf16[640,128]{1,0:T(8,128)(2,1)S(1)} %get-tuple-element.29), channel_id=1, source_target_pairs={{0,8},{4,12},{8,0},{12,4},{16,24},{20,28},{24,16},{28,20},{1,9},{5... | collective-permute-start | bytes 491528 | tf_op jit(solution)/shard_map/ppermute | solution.py:36
  10.3 10.2 %collective-permute-start.2 = (bf16[640,128]{1,0:T(8,128)(2,1)S(1)}, bf16[640,128]{1,0:T(8,128)(2,1)S(1)}, u32[]{:S(2)}, u32[]{:S(2)}) collective-permute-start(bf16[640,128]{1,0:T(8,128)(2,1)S(1)} %get-tuple-element.30), channel_id=1, source_target_pairs={{0,24},{4,28},{8,16},{12,20},{16,8},{20,12},{24,0},{28,4},{1,25},{... | collective-permute-start | bytes 491528 | tf_op jit(solution)/shard_map/ppermute | solution.py:36
  10.4 11.7 %collective-permute-start.3 = (bf16[640,128]{1,0:T(8,128)(2,1)S(1)}, bf16[640,128]{1,0:T(8,128)(2,1)S(1)}, u32[]{:S(2)}, u32[]{:S(2)}) collective-permute-start(bf16[640,128]{1,0:T(8,128)(2,1)S(1)} %get-tuple-element.31), channel_id=1, source_target_pairs={{0,28},{4,24},{8,20},{12,16},{16,12},{20,8},{24,4},{28,0},{1,29},{... | collective-permute-start | bytes 491528 | tf_op jit(solution)/shard_map/ppermute | solution.py:36
  11.9 12.2 %collective-permute-start.4 = (bf16[640,128]{1,0:T(8,128)(2,1)S(1)}, bf16[640,128]{1,0:T(8,128)(2,1)S(1)}, u32[]{:S(2)}, u32[]{:S(2)}) collective-permute-start(bf16[640,128]{1,0:T(8,128)(2,1)S(1)} %get-tuple-element.32), channel_id=1, source_target_pairs={{0,20},{4,16},{8,28},{12,24},{16,4},{20,0},{24,12},{28,8},{1,21},{... | collective-permute-start | bytes 491528 | tf_op jit(solution)/shard_map/ppermute | solution.py:36
  13.5 10.6 %collective-permute-start.5 = (bf16[640,128]{1,0:T(8,128)(2,1)S(1)}, bf16[640,128]{1,0:T(8,128)(2,1)S(1)}, u32[]{:S(2)}, u32[]{:S(2)}) collective-permute-start(bf16[640,128]{1,0:T(8,128)(2,1)S(1)} %get-tuple-element.33), channel_id=1, source_target_pairs={{0,12},{4,8},{8,4},{12,0},{16,28},{20,24},{24,20},{28,16},{1,13},{... | collective-permute-start | bytes 491528 | tf_op jit(solution)/shard_map/ppermute | solution.py:36
  16.0 8.1 %collective-permute-start.6 = (bf16[640,128]{1,0:T(8,128)(2,1)S(1)}, bf16[640,128]{1,0:T(8,128)(2,1)S(1)}, u32[]{:S(2)}, u32[]{:S(2)}) collective-permute-start(bf16[640,128]{1,0:T(8,128)(2,1)S(1)} %get-tuple-element.34), channel_id=1, source_target_pairs={{0,4},{4,0},{8,12},{12,8},{16,20},{20,16},{24,28},{28,24},{1,5},{5... | collective-permute-start | bytes 491528 | tf_op jit(solution)/shard_map/ppermute | solution.py:36
  16.0 1.6 %copy-start = (bf16[4,2,256,512]{3,2,1,0:T(8,128)(2,1)S(1)}, bf16[4,2,256,512]{3,2,1,0:T(8,128)(2,1)}, u32[]{:S(2)}) copy-start(bf16[4,2,256,512]{3,2,1,0:T(8,128)(2,1)} %constant.5.clone.refs_3_) | copy-start | bytes 6291460
  17.6 1.6 %copy-start.1 = (bf16[4,2,512,256]{3,2,1,0:T(8,128)(2,1)S(1)}, bf16[4,2,512,256]{3,2,1,0:T(8,128)(2,1)}, u32[]{:S(2)}) copy-start(bf16[4,2,512,256]{3,2,1,0:T(8,128)(2,1)} %constant.4.clone.refs_2_) | copy-start | bytes 6291460
  19.2 0.8 %copy-start.11 = (f32[3,3,1024]{2,1,0:T(4,128)S(1)}, f32[3,3,1024]{2,1,0:T(4,128)}, u32[]{:S(2)}) copy-start(f32[3,3,1024]{2,1,0:T(4,128)} %refs_12_.1) | copy-start | bytes 110596
  24.1 18.7 %copy-start.3 = (bf16[128,1024]{1,0:T(8,128)(2,1)S(1)}, bf16[128,1024]{1,0:T(8,128)(2,1)}, u32[]{:S(2)}) copy-start(bf16[128,1024]{1,0:T(8,128)(2,1)} %refs_8_.1) | copy-start | bytes 786436
  24.1 18.7 %copy-start.5 = (bf16[128,1024]{1,0:T(8,128)(2,1)S(1)}, bf16[128,1024]{1,0:T(8,128)(2,1)}, u32[]{:S(2)}) copy-start(bf16[128,1024]{1,0:T(8,128)(2,1)} %refs_9_.1) | copy-start | bytes 786436
  24.1 18.8 %copy-start.7 = (bf16[128,1024]{1,0:T(8,128)(2,1)S(1)}, bf16[128,1024]{1,0:T(8,128)(2,1)}, u32[]{:S(2)}) copy-start(bf16[128,1024]{1,0:T(8,128)(2,1)} %refs_10_.1) | copy-start | bytes 786436
  24.1 18.8 %copy-start.9 = (bf16[128,1024]{1,0:T(8,128)(2,1)S(1)}, bf16[128,1024]{1,0:T(8,128)(2,1)}, u32[]{:S(2)}) copy-start(bf16[128,1024]{1,0:T(8,128)(2,1)} %refs_11_.1) | copy-start | bytes 786436
  24.1 18.8 %copy-start.12 = (f32[3,3,1024]{2,1,0:T(4,128)S(1)}, f32[3,3,1024]{2,1,0:T(4,128)}, u32[]{:S(2)}) copy-start(f32[3,3,1024]{2,1,0:T(4,128)} %refs_12_.1) | copy-start | bytes 110596
  28.8 5.8 %collective-permute-start.7 = (bf16[432,128]{1,0:T(8,128)(2,1)S(1)}, bf16[432,128]{1,0:T(8,128)(2,1)S(1)}, u32[]{:S(2)}, u32[]{:S(2)}) collective-permute-start(bf16[432,128]{1,0:T(8,128)(2,1)S(1)} %get-tuple-element.39), channel_id=1, source_target_pairs={{0,16},{4,20},{8,24},{12,28},{16,0},{20,4},{24,8},{28,12},{1,17},{... | collective-permute-start | bytes 331784 | tf_op jit(solution)/shard_map/ppermute | solution.py:36
  30.3 5.5 %collective-permute-start.8 = (bf16[432,128]{1,0:T(8,128)(2,1)S(1)}, bf16[432,128]{1,0:T(8,128)(2,1)S(1)}, u32[]{:S(2)}, u32[]{:S(2)}) collective-permute-start(bf16[432,128]{1,0:T(8,128)(2,1)S(1)} %get-tuple-element.40), channel_id=1, source_target_pairs={{0,8},{4,12},{8,0},{12,4},{16,24},{20,28},{24,16},{28,20},{1,9},{5... | collective-permute-start | bytes 331784 | tf_op jit(solution)/shard_map/ppermute | solution.py:36
  31.6 7.1 %collective-permute-start.9 = (bf16[432,128]{1,0:T(8,128)(2,1)S(1)}, bf16[432,128]{1,0:T(8,128)(2,1)S(1)}, u32[]{:S(2)}, u32[]{:S(2)}) collective-permute-start(bf16[432,128]{1,0:T(8,128)(2,1)S(1)} %get-tuple-element.41), channel_id=1, source_target_pairs={{0,24},{4,28},{8,16},{12,20},{16,8},{20,12},{24,0},{28,4},{1,25},{... | collective-permute-start | bytes 331784 | tf_op jit(solution)/shard_map/ppermute | solution.py:36
  32.3 8.0 %collective-permute-start.10 = (bf16[432,128]{1,0:T(8,128)(2,1)S(1)}, bf16[432,128]{1,0:T(8,128)(2,1)S(1)}, u32[]{:S(2)}, u32[]{:S(2)}) collective-permute-start(bf16[432,128]{1,0:T(8,128)(2,1)S(1)} %get-tuple-element.42), channel_id=1, source_target_pairs={{0,28},{4,24},{8,20},{12,16},{16,12},{20,8},{24,4},{28,0},{1,29},{... | collective-permute-start | bytes 331784 | tf_op jit(solution)/shard_map/ppermute | solution.py:36
  33.4 9.5 %collective-permute-start.11 = (bf16[432,128]{1,0:T(8,128)(2,1)S(1)}, bf16[432,128]{1,0:T(8,128)(2,1)S(1)}, u32[]{:S(2)}, u32[]{:S(2)}) collective-permute-start(bf16[432,128]{1,0:T(8,128)(2,1)S(1)} %get-tuple-element.43), channel_id=1, source_target_pairs={{0,20},{4,16},{8,28},{12,24},{16,4},{20,0},{24,12},{28,8},{1,21},{... | collective-permute-start | bytes 331784 | tf_op jit(solution)/shard_map/ppermute | solution.py:36
  34.6 8.2 %collective-permute-start.12 = (bf16[432,128]{1,0:T(8,128)(2,1)S(1)}, bf16[432,128]{1,0:T(8,128)(2,1)S(1)}, u32[]{:S(2)}, u32[]{:S(2)}) collective-permute-start(bf16[432,128]{1,0:T(8,128)(2,1)S(1)} %get-tuple-element.44), channel_id=1, source_target_pairs={{0,12},{4,8},{8,4},{12,0},{16,28},{20,24},{24,20},{28,16},{1,13},{... | collective-permute-start | bytes 331784 | tf_op jit(solution)/shard_map/ppermute | solution.py:36
  35.8 7.1 %collective-permute-start.13 = (bf16[432,128]{1,0:T(8,128)(2,1)S(1)}, bf16[432,128]{1,0:T(8,128)(2,1)S(1)}, u32[]{:S(2)}, u32[]{:S(2)}) collective-permute-start(bf16[432,128]{1,0:T(8,128)(2,1)S(1)} %get-tuple-element.45), channel_id=1, source_target_pairs={{0,4},{4,0},{8,12},{12,8},{16,20},{20,16},{24,28},{28,24},{1,5},{5... | collective-permute-start | bytes 331784 | tf_op jit(solution)/shard_map/ppermute | solution.py:36

commit v5 on v4

--- a/solution.py
+++ b/solution.py
@@ -15,6 +15,7 @@
 PHASES = 4
 TILE = 16
 PAD = 8
+CHUNK = 32
 RIM = 2
 PIECES = 3
 MIB = 1024 * 1024
@@ -61,7 +62,6 @@
         in_specs=in_vmem(len(arrays)),
         out_specs=in_vmem(peers),
         out_shape=[jax.ShapeDtypeStruct((len(arrays) * tokens, LANES), BF16)] * peers,
-        compiler_params=pltpu.CompilerParams(vmem_limit_bytes=VMEM_LIMIT),
         cost_estimate=pl.CostEstimate(flops=0, bytes_accessed=8 * MIB, transcendentals=0),
         name="pack_inputs",
     )(*arrays)
@@ -114,37 +114,35 @@
     )
 
 
-def split_store(ref, r, rows, lanes, values):
-    half = ref.shape[-1] // 2
-    rounded = values.astype(BF16)
-    ref[r, rows, lanes] = rounded
-    ref[r, rows, slice(lanes.start + half, lanes.stop + half)] = (
-        values - rounded.astype(F32)
-    ).astype(BF16)
-
-
-def forward_transform(forward, signal):
-    return jnp.dot(forward[0], signal, preferred_element_type=F32) + jnp.dot(
-        forward[1], signal, preferred_element_type=F32
-    )
-
-
-def inverse_transform(backward, pieces):
-    half = pieces.shape[-1] // 2
-    both = jnp.dot(backward[0], pieces, preferred_element_type=F32)
-    rest = jnp.dot(backward[1], pieces[:, :half], preferred_element_type=F32)
-    return both[:, :half] + both[:, half:] + rest
-
-
-def phase(ref, r, size):
-    return ref[pl.ds(r, size, stride=PHASES), :]
-
-
-def short_phases(ref, weights, array, lanes, r, size):
-    summed = weights[array, 0:1, lanes] * phase(ref, PAD + r, size)
-    for tap in range(1, weights.shape[1]):
-        summed = summed + weights[array, tap : tap + 1, lanes] * phase(ref, PAD + r - tap, size)
-    return summed
+def transform(tables, signal):
+    return jnp.dot(tables[0], signal, preferred_element_type=F32) + jnp.dot(
+        tables[1], signal, preferred_element_type=F32
+    )
+
+
+def phases_near(ref, chunk, tap_count):
+    start = PAD + chunk * CHUNK * PHASES
+    return {
+        offset: ref[pl.ds(start + offset, CHUNK, stride=PHASES), :]
+        for offset in range(1 - tap_count, PHASES)
+    }
+
+
+def short_conv(near, taps):
+    results = []
+    for r in range(PHASES):
+        summed = taps[0] * near[r]
+        for at in range(1, len(taps)):
+            summed = summed + taps[at] * near[r - at]
+        results.append(summed)
+    return results
+
+
+def add_rows(total, terms):
+    for term in terms:
+        folded = jnp.sum(term.reshape(CHUNK // 8, 8, LANES), axis=0)
+        total = folded if total is None else total + folded
+    return total
 
 
 def clear_ends(ref):
@@ -200,7 +198,7 @@
         value_short,
         signals,
         spectra,
-        pieces,
+        products,
         extra,
     ) = refs[2 * peers + 3 :]
     size = peers * tokens // PHASES
@@ -215,57 +213,91 @@
         for at, ref in enumerate((query, key, value, cot)):
             ref[inner, :] = source[at * tokens : (at + 1) * tokens, :].astype(F32)
         taps[pl.ds(pl.multiple_of(start, PAD), tokens), :] = source[4 * tokens :, :].astype(F32)
+    chunks = range(size // CHUNK)
+    taps_of = [
+        [weights[array, tap : tap + 1, own] for tap in range(tap_count)] for array in range(3)
+    ]
+
+    def rows_of(chunk):
+        return slice(chunk * CHUNK, (chunk + 1) * CHUNK)
+
+    def spectrum(at, real, imag):
+        lanes = slice(at * LANES, (at + 1) * LANES)
+        return forward_mix(
+            [(spectra[r, real, lanes], spectra[r, imag, lanes]) for r in range(PHASES)]
+        )
+
+    def keep(at, real, imag, mixed):
+        lanes = slice(at * LANES, (at + 1) * LANES)
+        for r, pair in enumerate(inverse_mix(mixed)):
+            for rows, part in zip((real, imag), pair):
+                products[r, rows, lanes] = part.astype(BF16)
+
+    for chunk in chunks:
+        rows = rows_of(chunk)
+        key_now = short_conv(phases_near(key, chunk, tap_count), taps_of[1])
+        value_now = short_conv(phases_near(value, chunk, tap_count), taps_of[2])
+        for r in range(PHASES):
+            key_short[r, rows, :] = key_now[r]
+            value_short[r, rows, :] = value_now[r]
+            signals[r, rows, :LANES] = (key_now[r] * value_now[r]).astype(BF16)
+            filt = taps[pl.ds(chunk * CHUNK * PHASES + r, CHUNK, stride=PHASES), :]
+            signals[r, rows, LANES : 2 * LANES] = filt.astype(BF16)
     for r in range(PHASES):
-        key_short[r] = short_phases(key, weights, 1, own, r, size)
-        value_short[r] = short_phases(value, weights, 2, own, r, size)
-        query_short = short_phases(query, weights, 0, own, r, size)
-        signals[r, :, :LANES] = (key_short[r] * value_short[r]).astype(BF16)
-        signals[r, :, LANES : 2 * LANES] = phase(taps, r, size).astype(BF16)
-        signals[r, :, 2 * LANES :] = (phase(cot, PAD + r, size) * query_short).astype(BF16)
+        spectra[r, :, : 2 * LANES] = transform(forward[r], signals[r, :, : 2 * LANES])
+    for chunk in chunks:
+        rows = rows_of(chunk)
+        query_now = short_conv(phases_near(query, chunk, tap_count), taps_of[0])
+        cot_now = phases_near(cot, chunk, 1)
+        for r in range(PHASES):
+            signals[r, rows, 2 * LANES :] = (cot_now[r] * query_now[r]).astype(BF16)
     for r in range(PHASES):
-        spectra[r] = forward_transform(forward[r], signals[r])
-    for chunk in range(size // TILE):
-        real = slice(chunk * TILE, (chunk + 1) * TILE)
-        imag = slice(size + chunk * TILE, size + (chunk + 1) * TILE)
-        prod, filt, grad = (
-            forward_mix(
-                [
-                    (
-                        spectra[r, real, at * LANES : (at + 1) * LANES],
-                        spectra[r, imag, at * LANES : (at + 1) * LANES],
-                    )
-                    for r in range(PHASES)
-                ]
+        spectra[r, :, 2 * LANES :] = transform(forward[r], signals[r, :, 2 * LANES :])
+    for step in range(size // TILE):
+        real = slice(step * TILE, (step + 1) * TILE)
+        imag = slice(size + step * TILE, size + (step + 1) * TILE)
+        prod, filt = spectrum(0, real, imag), spectrum(1, real, imag)
+        for at, mixed in enumerate((prod, filt)):
+            lanes = slice(at * LANES, (at + 1) * LANES)
+            for q, pair in enumerate(mixed):
+                spectra[q, real, lanes], spectra[q, imag, lanes] = pair
+        keep(0, real, imag, times(prod, filt))
+    for r in range(PHASES):
+        result = transform(backward[r], products[r, :, :LANES])
+        conv[pl.ds(PAD + r, size, stride=PHASES), :] = result.astype(BF16).astype(F32)
+    for step in range(size // TILE):
+        real = slice(step * TILE, (step + 1) * TILE)
+        imag = slice(size + step * TILE, size + (step + 1) * TILE)
+        grad = spectrum(2, real, imag)
+        for at in range(2):
+            lanes = slice(at * LANES, (at + 1) * LANES)
+            known = [(spectra[q, real, lanes], spectra[q, imag, lanes]) for q in range(PHASES)]
+            keep(2 - at, real, imag, conj_times(known, grad))
+    for r in range(PHASES):
+        result = transform(backward[r], products[r, :, LANES:])
+        conv_grad[pl.ds(PAD + r, size, stride=PHASES), :] = (
+            result[:, :LANES].astype(BF16).astype(F32)
+        )
+        filter_grad[pl.ds(r, size, stride=PHASES), :] = result[:, LANES:] * grad_scale
+
+    totals = [[None] * tap_count for _ in range(3)]
+
+    def add_sums(array, signal, chunk, pre):
+        near = phases_near(signal, chunk, tap_count)
+        for tap in range(tap_count):
+            totals[array][tap] = add_rows(
+                totals[array][tap], [pre[r] * near[r - tap] for r in range(PHASES)]
             )
-            for at in range(3)
-        )
-        for at, mixed in enumerate(
-            (times(prod, filt), conj_times(filt, grad), conj_times(prod, grad))
-        ):
-            for r, pair in enumerate(inverse_mix(mixed)):
-                for rows, part in zip((real, imag), pair):
-                    split_store(pieces, r, rows, slice(at * LANES, (at + 1) * LANES), part)
-    for r in range(PHASES):
-        result = inverse_transform(backward[r], pieces[r])
-        for at, ref in enumerate((conv, conv_grad)):
-            ref[pl.ds(PAD + r, size, stride=PHASES), :] = (
-                result[:, at * LANES : (at + 1) * LANES].astype(BF16).astype(F32)
-            )
-        filter_grad[pl.ds(r, size, stride=PHASES), :] = result[:, 2 * LANES :] * grad_scale
-
-    sums = []
-    for array, signal in enumerate((query, key, value)):
-        totals = [None] * tap_count
-        for r in range(PHASES):
-            if array == 0:
-                pre = phase(cot, PAD + r, size) * phase(conv, PAD + r, size)
-            else:
-                pre = phase(conv_grad, PAD + r, size) * (value_short, key_short)[array - 1][r]
-            for tap in range(tap_count):
-                term = pre * phase(signal, PAD + r - tap, size)
-                term = jnp.sum(term.reshape(size // 8, 8, LANES), axis=0)
-                totals[tap] = term if r == 0 else totals[tap] + term
-        sums.extend(jnp.sum(total, axis=0, keepdims=True) for total in totals)
+
+    for chunk in chunks:
+        cot_now, conv_now = phases_near(cot, chunk, 1), phases_near(conv, chunk, 1)
+        add_sums(0, query, chunk, [cot_now[r] * conv_now[r] for r in range(PHASES)])
+    for chunk in chunks:
+        rows = rows_of(chunk)
+        grad_now = phases_near(conv_grad, chunk, 1)
+        add_sums(1, key, chunk, [grad_now[r] * value_short[r, rows, :] for r in range(PHASES)])
+        add_sums(2, value, chunk, [grad_now[r] * key_short[r, rows, :] for r in range(PHASES)])
+    sums = [jnp.sum(total, axis=0, keepdims=True) for row in totals for total in row]
     rest = jnp.concatenate(sums, axis=0) * grad_scale
     extra[...] = jnp.zeros_like(extra)
     for piece in range(PIECES):
@@ -313,7 +345,7 @@
             phases,
             pltpu.VMEM((PHASES, size, 3 * LANES), BF16),
             pltpu.VMEM((PHASES, 2 * size, 3 * LANES), F32),
-            pltpu.VMEM((PHASES, 2 * size, 6 * LANES), BF16),
+            pltpu.VMEM((PHASES, 2 * size, 3 * LANES), BF16),
             pltpu.VMEM((extra, LANES), F32),
         ],
         compiler_params=pltpu.CompilerParams(vmem_limit_bytes=VMEM_LIMIT),
@@ -612,7 +644,7 @@
     return (
         width == peers * LANES
         and peers.bit_count() == 1
-        and tokens % (PHASES * TILE) == 0
+        and tokens % (PHASES * CHUNK) == 0
         and tap_count == RIM + 1
         and peers * tokens <= 2048
     )

time: 45.4 us -> 42 us (0.925)
  local copies, waits for them, and re-layouts: 8.84 us -> 4.92 us
  Pallas kernels: 7.69 us -> 9.12 us
  waiting for transfers between devices: 13.4 us -> 12.8 us
    unnamed x26 -> x18, local copies, waits for them, and re-layouts: 8.84 us -> 4.92 us
    pallas_call x1, Pallas kernels: 0.34 us -> 2.74 us  [pack(): pl.pallas_call(functools.partial(pack_kernel, len(arrays)), in_specs=in_v...]
    pallas_call x1, Pallas kernels: 4.65 us -> 3.68 us  [channel_step(): pl.pallas_call(functools.partial(channel_kernel, tokens, peers, 1.0 / mat...]
    ppermute x14, waiting for transfers between devices: 13.4 us -> 12.8 us  [exchange(): lax.ppermute(block, 'ctx', [(i, i ^ step) for i in range(peers)])]
  transfers between devices with their start and end apart: 14 -> 14, of which waited for: 8 -> 9; matrix products, arithmetic and copies ran while one was open for 0% -> 0% of each run, Pallas kernels for 1% -> 1%
where the time goes in v5:
time: 42 us; the launch traced here: 41.8 us
  starting transfers between devices  14.2 us (34%)
  waiting for transfers between devices  12.8 us (30%)
  Pallas kernels  9.12 us (22%)
  local copies, waits for them, and re-layouts  4.92 us (12%)
  between operations  0.72 us (2%)
    ppermute x14, starting transfers between devices, exchange(): lax.ppermute(block, 'ctx', [(i, i ^ step) for i in range(peers)])  14.2 us
    ppermute x14, waiting for transfers between devices, exchange(): lax.ppermute(block, 'ctx', [(i, i ^ step) for i in range(peers)])  12.8 us
    unnamed x18, local copies, waits for them, and re-layouts  4.92 us
    pallas_call x1, Pallas kernels, channel_step(): pl.pallas_call(functools.partial(channel_kernel, tokens, peers, 1.0 / mat...  3.68 us
    pallas_call x1, Pallas kernels, pack(): pl.pallas_call(functools.partial(pack_kernel, len(arrays)), in_specs=in_v...  2.74 us
    pallas_call x1, Pallas kernels, token_step(): pl.pallas_call(functools.partial(token_kernel, peers, extra_rows(short_we...  2.14 us
  transfers between devices with their start and end apart: 14, of which 9 were waited for; matrix products, arithmetic and copies ran while one was open for 0% of the time, Pallas kernels for 1%

profile of v5, /device:TPU:0, one launch (start us, length us, event | category | flops | bytes accessed | tf_op | source)
XLA Modules:
  0.0 41.8 jit_solution(6607418162413807552)
XLA Ops:
  0.6 2.7 %pack_inputs.1 = (bf16[640,128]{1,0:T(8,128)(2,1)}, bf16[640,128]{1,0:T(8,128)(2,1)}, bf16[640,128]{1,0:T(8,128)(2,1)}, bf16[640,128]{1,0:T(8,128)(2,1)}, bf16[6...) custom-call(bf16[128,1024]{1,0:T(8,128)(2,1)} %refs_8_.1, ...), custom_call_target="tpu_custom_call" | custom-call | bytes 8388608 | tf_op jit(solution)/shard_map/pack_inputs/pallas_call | solution.py:60
  3.4 3.0 %collective-permute-start = (bf16[640,128]{1,0:T(8,128)(2,1)}, bf16[640,128]{1,0:T(8,128)(2,1)S(1)}, u32[]{:S(2)}, u32[]{:S(2)}) collective-permute-start(bf16[640,128]{1,0:T(8,128)(2,1)} %get-tuple-element.27), channel_id=1, source_target_pairs={{0,16},{4,20},{8,24},{12,28},{16,0},{20,4},{24,8},{28,12},{1,17},{... | collective-permute-start | bytes 491528 | tf_op jit(solution)/shard_map/ppermute | solution.py:37
  6.3 1.5 %collective-permute-start.1 = (bf16[640,128]{1,0:T(8,128)(2,1)}, bf16[640,128]{1,0:T(8,128)(2,1)S(1)}, u32[]{:S(2)}, u32[]{:S(2)}) collective-permute-start(bf16[640,128]{1,0:T(8,128)(2,1)} %get-tuple-element.29), channel_id=1, source_target_pairs={{0,8},{4,12},{8,0},{12,4},{16,24},{20,28},{24,16},{28,20},{1,9},{5... | collective-permute-start | bytes 491528 | tf_op jit(solution)/shard_map/ppermute | solution.py:37
  7.8 0.0 collective-permute-start.2
  7.8 1.5 %collective-permute-start.3 = (bf16[640,128]{1,0:T(8,128)(2,1)}, bf16[640,128]{1,0:T(8,128)(2,1)S(1)}, u32[]{:S(2)}, u32[]{:S(2)}) collective-permute-start(bf16[640,128]{1,0:T(8,128)(2,1)} %get-tuple-element.31), channel_id=1, source_target_pairs={{0,28},{4,24},{8,20},{12,16},{16,12},{20,8},{24,4},{28,0},{1,29},{... | collective-permute-start | bytes 491528 | tf_op jit(solution)/shard_map/ppermute | solution.py:37
  9.4 1.6 %collective-permute-start.4 = (bf16[640,128]{1,0:T(8,128)(2,1)}, bf16[640,128]{1,0:T(8,128)(2,1)S(1)}, u32[]{:S(2)}, u32[]{:S(2)}) collective-permute-start(bf16[640,128]{1,0:T(8,128)(2,1)} %get-tuple-element.32), channel_id=1, source_target_pairs={{0,20},{4,16},{8,28},{12,24},{16,4},{20,0},{24,12},{28,8},{1,21},{... | collective-permute-start | bytes 491528 | tf_op jit(solution)/shard_map/ppermute | solution.py:37
  11.0 0.1 collective-permute-start.5
  11.0 2.6 %collective-permute-done.1.refs_2_ = bf16[640,128]{1,0:T(8,128)(2,1)S(1)} collective-permute-done((bf16[640,128]{1,0:T(8,128)(2,1)}, bf16[640,128]{1,0:T(8,128)(2,1)S(1)}, u32[]{:S(2)}, u32[]{:S(2)}) %collective-permute-start.1) | collective-permute-done | bytes 163872 | tf_op jit(solution)/shard_map/ppermute | solution.py:37
  13.7 1.6 %copy-done = bf16[4,2,256,512]{3,2,1,0:T(8,128)(2,1)S(1)} copy-done((bf16[4,2,256,512]{3,2,1,0:T(8,128)(2,1)S(1)}, bf16[4,2,256,512]{3,2,1,0:T(8,128)(2,1)}, u32[]{:S(2)}) %copy-start) | copy-done | bytes 2097176
  15.3 1.6 %copy-done.1 = bf16[4,2,512,256]{3,2,1,0:T(8,128)(2,1)S(1)} copy-done((bf16[4,2,512,256]{3,2,1,0:T(8,128)(2,1)S(1)}, bf16[4,2,512,256]{3,2,1,0:T(8,128)(2,1)}, u32[]{:S(2)}) %copy-start.1) | copy-done | bytes 2097176
  16.9 0.8 %copy-done.6 = f32[3,3,1024]{2,1,0:T(4,128)S(1)} copy-done((f32[3,3,1024]{2,1,0:T(4,128)S(1)}, f32[3,3,1024]{2,1,0:T(4,128)}, u32[]{:S(2)}) %copy-start.6) | copy-done | bytes 36888
  17.7 0.9 %copy-done.8 = bf16[640,128]{1,0:T(8,128)(2,1)S(1)} copy-done((bf16[640,128]{1,0:T(8,128)(2,1)S(1)}, bf16[640,128]{1,0:T(8,128)(2,1)}, u32[]{:S(2)}) %copy-start.8) | copy-done | bytes 163864
  18.6 0.6 %stage_tables.1 = (bf16[640,128]{1,0:T(8,128)(2,1)S(1)}, f32[3,3,1024]{2,1,0:T(4,128)S(1)}, bf16[4,2,512,256]{3,2,1,0:T(8,128)(2,1)S(1)}, bf16[4,2,256,512]{3,2,1,0:T(8,128)(2,1)S(1)}) custom-call(bf16[640,128]{1,0:T(8,128)(2,1)S(1)} %copy-done.8, f32[3,3,1024]{2,1,0:T(4,128)S(1)} %copy-done.6, bf16[4,2,512,256]{3,2,1,0:T(8,128)(2,1)S(1)} %copy-done.1, ...), custom_call_target="tpu_custom_call" | custom-call | bytes 8388608 | tf_op jit(solution)/shard_map/stage_tables/pallas_call | solution.py:167
  19.2 0.7 %collective-permute-done.3.refs_4_ = bf16[640,128]{1,0:T(8,128)(2,1)S(1)} collective-permute-done((bf16[640,128]{1,0:T(8,128)(2,1)}, bf16[640,128]{1,0:T(8,128)(2,1)S(1)}, u32[]{:S(2)}, u32[]{:S(2)}) %collective-permute-start.3) | collective-permute-done | bytes 163872 | tf_op jit(solution)/shard_map/ppermute | solution.py:37
  19.9 1.9 %collective-permute-done.4.refs_5_ = bf16[640,128]{1,0:T(8,128)(2,1)S(1)} collective-permute-done((bf16[640,128]{1,0:T(8,128)(2,1)}, bf16[640,128]{1,0:T(8,128)(2,1)S(1)}, u32[]{:S(2)}, u32[]{:S(2)}) %collective-permute-start.4) | collective-permute-done | bytes 163872 | tf_op jit(solution)/shard_map/ppermute | solution.py:37
  21.8 0.1 collective-permute-done.5.refs_6_
  21.9 0.0 copy-start.5
  21.9 0.0 copy-start.7
  21.9 3.7 %channel_operator.1 = (bf16[432,128]{1,0:T(8,128)(2,1)S(1)}, bf16[432,128]{1,0:T(8,128)(2,1)S(1)}, bf16[432,128]{1,0:T(8,128)(2,1)S(1)}, bf16[432,128]{1,0:T(8,1...) custom-call(bf16[640,128]{1,0:T(8,128)(2,1)S(1)} %get-tuple-element., ...), custom_call_target="tpu_custom_call" | custom-call | tf_op jit(solution)/shard_map/channel_operator/pallas_call | solution.py:335
  25.6 1.4 %collective-permute-start.7 = (bf16[432,128]{1,0:T(8,128)(2,1)S(1)}, bf16[432,128]{1,0:T(8,128)(2,1)S(1)}, u32[]{:S(2)}, u32[]{:S(2)}) collective-permute-start(bf16[432,128]{1,0:T(8,128)(2,1)S(1)} %get-tuple-element.39), channel_id=1, source_target_pairs={{0,16},{4,20},{8,24},{12,28},{16,0},{20,4},{24,8},{28,12},{1,17},{... | collective-permute-start | bytes 331784 | tf_op jit(solution)/shard_map/ppermute | solution.py:37
  27.1 1.2 %collective-permute-start.8 = (bf16[432,128]{1,0:T(8,128)(2,1)S(1)}, bf16[432,128]{1,0:T(8,128)(2,1)S(1)}, u32[]{:S(2)}, u32[]{:S(2)}) collective-permute-start(bf16[432,128]{1,0:T(8,128)(2,1)S(1)} %get-tuple-element.40), channel_id=1, source_target_pairs={{0,8},{4,12},{8,0},{12,4},{16,24},{20,28},{24,16},{28,20},{1,9},{5... | collective-permute-start | bytes 331784 | tf_op jit(solution)/shard_map/ppermute | solution.py:37
  28.3 0.9 %collective-permute-start.9 = (bf16[432,128]{1,0:T(8,128)(2,1)S(1)}, bf16[432,128]{1,0:T(8,128)(2,1)S(1)}, u32[]{:S(2)}, u32[]{:S(2)}) collective-permute-start(bf16[432,128]{1,0:T(8,128)(2,1)S(1)} %get-tuple-element.41), channel_id=1, source_target_pairs={{0,24},{4,28},{8,16},{12,20},{16,8},{20,12},{24,0},{28,4},{1,25},{... | collective-permute-start | bytes 331784 | tf_op jit(solution)/shard_map/ppermute | solution.py:37
  29.2 0.9 %collective-permute-start.10 = (bf16[432,128]{1,0:T(8,128)(2,1)S(1)}, bf16[432,128]{1,0:T(8,128)(2,1)S(1)}, u32[]{:S(2)}, u32[]{:S(2)}) collective-permute-start(bf16[432,128]{1,0:T(8,128)(2,1)S(1)} %get-tuple-element.42), channel_id=1, source_target_pairs={{0,28},{4,24},{8,20},{12,16},{16,12},{20,8},{24,4},{28,0},{1,29},{... | collective-permute-start | bytes 331784 | tf_op jit(solution)/shard_map/ppermute | solution.py:37
  30.1 1.2 %collective-permute-start.11 = (bf16[432,128]{1,0:T(8,128)(2,1)S(1)}, bf16[432,128]{1,0:T(8,128)(2,1)S(1)}, u32[]{:S(2)}, u32[]{:S(2)}) collective-permute-start(bf16[432,128]{1,0:T(8,128)(2,1)S(1)} %get-tuple-element.43), channel_id=1, source_target_pairs={{0,20},{4,16},{8,28},{12,24},{16,4},{20,0},{24,12},{28,8},{1,21},{... | collective-permute-start | bytes 331784 | tf_op jit(solution)/shard_map/ppermute | solution.py:37
  31.3 0.1 collective-permute-done.7.refs_1_
  31.4 0.9 %collective-permute-start.12 = (bf16[432,128]{1,0:T(8,128)(2,1)S(1)}, bf16[432,128]{1,0:T(8,128)(2,1)S(1)}, u32[]{:S(2)}, u32[]{:S(2)}) collective-permute-start(bf16[432,128]{1,0:T(8,128)(2,1)S(1)} %get-tuple-element.44), channel_id=1, source_target_pairs={{0,12},{4,8},{8,4},{12,0},{16,28},{20,24},{24,20},{28,16},{1,13},{... | collective-permute-start | bytes 331784 | tf_op jit(solution)/shard_map/ppermute | solution.py:37
  32.3 0.3 collective-permute-done.8.refs_2_
  32.5 0.0 collective-permute-start.13
  32.5 3.0 %collective-permute-done.9.refs_3_ = bf16[432,128]{1,0:T(8,128)(2,1)S(1)} collective-permute-done((bf16[432,128]{1,0:T(8,128)(2,1)S(1)}, bf16[432,128]{1,0:T(8,128)(2,1)S(1)}, u32[]{:S(2)}, u32[]{:S(2)}) %collective-permute-start.9) | collective-permute-done | bytes 110624 | tf_op jit(solution)/shard_map/ppermute | solution.py:37
  35.5 1.5 %collective-permute-done.10.refs_4_ = bf16[432,128]{1,0:T(8,128)(2,1)S(1)} collective-permute-done((bf16[432,128]{1,0:T(8,128)(2,1)S(1)}, bf16[432,128]{1,0:T(8,128)(2,1)S(1)}, u32[]{:S(2)}, u32[]{:S(2)}) %collective-permute-start.10) | collective-permute-done | bytes 110624 | tf_op jit(solution)/shard_map/ppermute | solution.py:37
  36.9 2.6 %collective-permute-done.11.refs_5_ = bf16[432,128]{1,0:T(8,128)(2,1)S(1)} collective-permute-done((bf16[432,128]{1,0:T(8,128)(2,1)S(1)}, bf16[432,128]{1,0:T(8,128)(2,1)S(1)}, u32[]{:S(2)}, u32[]{:S(2)}) %collective-permute-start.11) | collective-permute-done | bytes 110624 | tf_op jit(solution)/shard_map/ppermute | solution.py:37
  39.6 2.1 %token_outputs.1 = (bf16[128,1024]{1,0:T(8,128)(2,1)}, bf16[128,1024]{1,0:T(8,128)(2,1)}, bf16[128,1024]{1,0:T(8,128)(2,1)}, bf16[128,1024]{1,0:T(8,128)(2,1)}, ...) custom-call(bf16[432,128]{1,0:T(8,128)(2,1)S(1)} %get-tuple-element.38.refs_0_, ...), custom_call_target="tpu_custom_call" | custom-call | tf_op jit(solution)/shard_map/token_outputs/pallas_call | solution.py:421
  (18 shorter events, 0.0 us)
Async XLA Ops:
  3.4 7.6 %collective-permute-start = (bf16[640,128]{1,0:T(8,128)(2,1)}, bf16[640,128]{1,0:T(8,128)(2,1)S(1)}, u32[]{:S(2)}, u32[]{:S(2)}) collective-permute-start(bf16[640,128]{1,0:T(8,128)(2,1)} %get-tuple-element.27), channel_id=1, source_target_pairs={{0,16},{4,20},{8,24},{12,28},{16,0},{20,4},{24,8},{28,12},{1,17},{... | collective-permute-start | bytes 491528 | tf_op jit(solution)/shard_map/ppermute | solution.py:37
  6.3 7.3 %collective-permute-start.1 = (bf16[640,128]{1,0:T(8,128)(2,1)}, bf16[640,128]{1,0:T(8,128)(2,1)S(1)}, u32[]{:S(2)}, u32[]{:S(2)}) collective-permute-start(bf16[640,128]{1,0:T(8,128)(2,1)} %get-tuple-element.29), channel_id=1, source_target_pairs={{0,8},{4,12},{8,0},{12,4},{16,24},{20,28},{24,16},{28,20},{1,9},{5... | collective-permute-start | bytes 491528 | tf_op jit(solution)/shard_map/ppermute | solution.py:37
  7.8 11.3 %collective-permute-start.2 = (bf16[640,128]{1,0:T(8,128)(2,1)}, bf16[640,128]{1,0:T(8,128)(2,1)S(1)}, u32[]{:S(2)}, u32[]{:S(2)}) collective-permute-start(bf16[640,128]{1,0:T(8,128)(2,1)} %get-tuple-element.30), channel_id=1, source_target_pairs={{0,24},{4,28},{8,16},{12,20},{16,8},{20,12},{24,0},{28,4},{1,25},{... | collective-permute-start | bytes 491528 | tf_op jit(solution)/shard_map/ppermute | solution.py:37
  7.8 12.0 %collective-permute-start.3 = (bf16[640,128]{1,0:T(8,128)(2,1)}, bf16[640,128]{1,0:T(8,128)(2,1)S(1)}, u32[]{:S(2)}, u32[]{:S(2)}) collective-permute-start(bf16[640,128]{1,0:T(8,128)(2,1)} %get-tuple-element.31), channel_id=1, source_target_pairs={{0,28},{4,24},{8,20},{12,16},{16,12},{20,8},{24,4},{28,0},{1,29},{... | collective-permute-start | bytes 491528 | tf_op jit(solution)/shard_map/ppermute | solution.py:37
  9.4 12.4 %collective-permute-start.4 = (bf16[640,128]{1,0:T(8,128)(2,1)}, bf16[640,128]{1,0:T(8,128)(2,1)S(1)}, u32[]{:S(2)}, u32[]{:S(2)}) collective-permute-start(bf16[640,128]{1,0:T(8,128)(2,1)} %get-tuple-element.32), channel_id=1, source_target_pairs={{0,20},{4,16},{8,28},{12,24},{16,4},{20,0},{24,12},{28,8},{1,21},{... | collective-permute-start | bytes 491528 | tf_op jit(solution)/shard_map/ppermute | solution.py:37
  11.0 10.9 %collective-permute-start.5 = (bf16[640,128]{1,0:T(8,128)(2,1)}, bf16[640,128]{1,0:T(8,128)(2,1)S(1)}, u32[]{:S(2)}, u32[]{:S(2)}) collective-permute-start(bf16[640,128]{1,0:T(8,128)(2,1)} %get-tuple-element.33), channel_id=1, source_target_pairs={{0,12},{4,8},{8,4},{12,0},{16,28},{20,24},{24,20},{28,16},{1,13},{... | collective-permute-start | bytes 491528 | tf_op jit(solution)/shard_map/ppermute | solution.py:37
  13.7 8.2 %collective-permute-start.6 = (bf16[640,128]{1,0:T(8,128)(2,1)}, bf16[640,128]{1,0:T(8,128)(2,1)S(1)}, u32[]{:S(2)}, u32[]{:S(2)}) collective-permute-start(bf16[640,128]{1,0:T(8,128)(2,1)} %get-tuple-element.34), channel_id=1, source_target_pairs={{0,4},{4,0},{8,12},{12,8},{16,20},{20,16},{24,28},{28,24},{1,5},{5... | collective-permute-start | bytes 491528 | tf_op jit(solution)/shard_map/ppermute | solution.py:37
  13.7 1.6 %copy-start = (bf16[4,2,256,512]{3,2,1,0:T(8,128)(2,1)S(1)}, bf16[4,2,256,512]{3,2,1,0:T(8,128)(2,1)}, u32[]{:S(2)}) copy-start(bf16[4,2,256,512]{3,2,1,0:T(8,128)(2,1)} %constant.5.clone.refs_3_) | copy-start | bytes 6291460
  15.3 1.6 %copy-start.1 = (bf16[4,2,512,256]{3,2,1,0:T(8,128)(2,1)S(1)}, bf16[4,2,512,256]{3,2,1,0:T(8,128)(2,1)}, u32[]{:S(2)}) copy-start(bf16[4,2,512,256]{3,2,1,0:T(8,128)(2,1)} %constant.4.clone.refs_2_) | copy-start | bytes 6291460
  16.9 0.8 %copy-start.6 = (f32[3,3,1024]{2,1,0:T(4,128)S(1)}, f32[3,3,1024]{2,1,0:T(4,128)}, u32[]{:S(2)}) copy-start(f32[3,3,1024]{2,1,0:T(4,128)} %refs_12_.1) | copy-start | bytes 110596
  17.7 0.9 %copy-start.8 = (bf16[640,128]{1,0:T(8,128)(2,1)S(1)}, bf16[640,128]{1,0:T(8,128)(2,1)}, u32[]{:S(2)}) copy-start(bf16[640,128]{1,0:T(8,128)(2,1)} %get-tuple-element.26.refs_0_) | copy-start | bytes 491524
  21.9 17.7 %copy-start.2 = (bf16[128,1024]{1,0:T(8,128)(2,1)S(1)}, bf16[128,1024]{1,0:T(8,128)(2,1)}, u32[]{:S(2)}) copy-start(bf16[128,1024]{1,0:T(8,128)(2,1)} %refs_8_.1) | copy-start | bytes 786436
  21.9 17.7 %copy-start.3 = (bf16[128,1024]{1,0:T(8,128)(2,1)S(1)}, bf16[128,1024]{1,0:T(8,128)(2,1)}, u32[]{:S(2)}) copy-start(bf16[128,1024]{1,0:T(8,128)(2,1)} %refs_9_.1) | copy-start | bytes 786436
  21.9 17.7 %copy-start.4 = (bf16[128,1024]{1,0:T(8,128)(2,1)S(1)}, bf16[128,1024]{1,0:T(8,128)(2,1)}, u32[]{:S(2)}) copy-start(bf16[128,1024]{1,0:T(8,128)(2,1)} %refs_10_.1) | copy-start | bytes 786436
  21.9 17.7 %copy-start.5 = (bf16[128,1024]{1,0:T(8,128)(2,1)S(1)}, bf16[128,1024]{1,0:T(8,128)(2,1)}, u32[]{:S(2)}) copy-start(bf16[128,1024]{1,0:T(8,128)(2,1)} %refs_11_.1) | copy-start | bytes 786436
  21.9 17.7 %copy-start.7 = (f32[3,3,1024]{2,1,0:T(4,128)S(1)}, f32[3,3,1024]{2,1,0:T(4,128)}, u32[]{:S(2)}) copy-start(f32[3,3,1024]{2,1,0:T(4,128)} %refs_12_.1) | copy-start | bytes 110596
  25.6 5.7 %collective-permute-start.7 = (bf16[432,128]{1,0:T(8,128)(2,1)S(1)}, bf16[432,128]{1,0:T(8,128)(2,1)S(1)}, u32[]{:S(2)}, u32[]{:S(2)}) collective-permute-start(bf16[432,128]{1,0:T(8,128)(2,1)S(1)} %get-tuple-element.39), channel_id=1, source_target_pairs={{0,16},{4,20},{8,24},{12,28},{16,0},{20,4},{24,8},{28,12},{1,17},{... | collective-permute-start | bytes 331784 | tf_op jit(solution)/shard_map/ppermute | solution.py:37
  27.1 5.4 %collective-permute-start.8 = (bf16[432,128]{1,0:T(8,128)(2,1)S(1)}, bf16[432,128]{1,0:T(8,128)(2,1)S(1)}, u32[]{:S(2)}, u32[]{:S(2)}) collective-permute-start(bf16[432,128]{1,0:T(8,128)(2,1)S(1)} %get-tuple-element.40), channel_id=1, source_target_pairs={{0,8},{4,12},{8,0},{12,4},{16,24},{20,28},{24,16},{28,20},{1,9},{5... | collective-permute-start | bytes 331784 | tf_op jit(solution)/shard_map/ppermute | solution.py:37
  28.3 7.2 %collective-permute-start.9 = (bf16[432,128]{1,0:T(8,128)(2,1)S(1)}, bf16[432,128]{1,0:T(8,128)(2,1)S(1)}, u32[]{:S(2)}, u32[]{:S(2)}) collective-permute-start(bf16[432,128]{1,0:T(8,128)(2,1)S(1)} %get-tuple-element.41), channel_id=1, source_target_pairs={{0,24},{4,28},{8,16},{12,20},{16,8},{20,12},{24,0},{28,4},{1,25},{... | collective-permute-start | bytes 331784 | tf_op jit(solution)/shard_map/ppermute | solution.py:37
  29.2 7.8 %collective-permute-start.10 = (bf16[432,128]{1,0:T(8,128)(2,1)S(1)}, bf16[432,128]{1,0:T(8,128)(2,1)S(1)}, u32[]{:S(2)}, u32[]{:S(2)}) collective-permute-start(bf16[432,128]{1,0:T(8,128)(2,1)S(1)} %get-tuple-element.42), channel_id=1, source_target_pairs={{0,28},{4,24},{8,20},{12,16},{16,12},{20,8},{24,4},{28,0},{1,29},{... | collective-permute-start | bytes 331784 | tf_op jit(solution)/shard_map/ppermute | solution.py:37
  30.1 9.5 %collective-permute-start.11 = (bf16[432,128]{1,0:T(8,128)(2,1)S(1)}, bf16[432,128]{1,0:T(8,128)(2,1)S(1)}, u32[]{:S(2)}, u32[]{:S(2)}) collective-permute-start(bf16[432,128]{1,0:T(8,128)(2,1)S(1)} %get-tuple-element.43), channel_id=1, source_target_pairs={{0,20},{4,16},{8,28},{12,24},{16,4},{20,0},{24,12},{28,8},{1,21},{... | collective-permute-start | bytes 331784 | tf_op jit(solution)/shard_map/ppermute | solution.py:37
  31.4 8.2 %collective-permute-start.12 = (bf16[432,128]{1,0:T(8,128)(2,1)S(1)}, bf16[432,128]{1,0:T(8,128)(2,1)S(1)}, u32[]{:S(2)}, u32[]{:S(2)}) collective-permute-start(bf16[432,128]{1,0:T(8,128)(2,1)S(1)} %get-tuple-element.44), channel_id=1, source_target_pairs={{0,12},{4,8},{8,4},{12,0},{16,28},{20,24},{24,20},{28,16},{1,13},{... | collective-permute-start | bytes 331784 | tf_op jit(solution)/shard_map/ppermute | solution.py:37
  32.5 7.1 %collective-permute-start.13 = (bf16[432,128]{1,0:T(8,128)(2,1)S(1)}, bf16[432,128]{1,0:T(8,128)(2,1)S(1)}, u32[]{:S(2)}, u32[]{:S(2)}) collective-permute-start(bf16[432,128]{1,0:T(8,128)(2,1)S(1)} %get-tuple-element.45), channel_id=1, source_target_pairs={{0,4},{4,0},{8,12},{12,8},{16,20},{20,16},{24,28},{28,24},{1,5},{5... | collective-permute-start | bytes 331784 | tf_op jit(solution)/shard_map/ppermute | solution.py:37

commit v6 on v5

--- a/solution.py
+++ b/solution.py
@@ -22,19 +22,27 @@
 VMEM_LIMIT = 24 * MIB
 
 
-def partners(peers):
-    def rank(step):
-        links = (step >> 1).bit_count()
-        return (links == 0, links == 1 and step & 1, links, step & 1, -step)
-
-    return [0] + sorted(range(1, peers), key=rank)
+def exchange_steps(peers):
+    if peers != 8:
+        return [(step, step) for step in range(peers)]
+    return [(0, 0), (4, 2), (2, 4), (6, 6), (7, 7), (5, 3), (3, 5), (1, 1)]
+
+
+def sends_to(step, me):
+    even, odd = step
+    return me ^ (even + (me & 1) * (odd - even))
+
+
+def hears_from(step, me):
+    even, odd = step
+    return sends_to((odd, even) if even & 1 else step, me)
 
 
 def exchange(blocks):
     peers = len(blocks)
     got = [blocks[0]]
-    for step, block in list(zip(partners(peers), blocks))[1:]:
-        got.append(lax.ppermute(block, "ctx", [(i, i ^ step) for i in range(peers)]))
+    for step, block in list(zip(exchange_steps(peers), blocks))[1:]:
+        got.append(lax.ppermute(block, "ctx", [(i, sends_to(step, i)) for i in range(peers)]))
     return got
 
 
@@ -50,9 +58,10 @@
     sources, packed = refs[:count], refs[count:]
     tokens = sources[0].shape[0]
     me = lax.axis_index("ctx")
-    for step, target in zip(partners(len(packed)), packed):
+    for step, target in zip(exchange_steps(len(packed)), packed):
+        lanes = lanes_of(sends_to(step, me))
         for at, source in enumerate(sources):
-            target[at * tokens : (at + 1) * tokens, :] = source[:, lanes_of(me ^ step)].astype(BF16)
+            target[at * tokens : (at + 1) * tokens, :] = source[:, lanes].astype(BF16)
 
 
 def pack(arrays, peers):
@@ -207,8 +216,8 @@
     own = lanes_of(me)
     for ref in (query, key, value, cot, conv, conv_grad):
         clear_ends(ref)
-    for step, source in zip(partners(peers), arrived):
-        start = (me ^ step) * tokens
+    for step, source in zip(exchange_steps(peers), arrived):
+        start = hears_from(step, me) * tokens
         inner = pl.ds(pl.multiple_of(PAD + start, PAD), tokens)
         for at, ref in enumerate((query, key, value, cot)):
             ref[inner, :] = source[at * tokens : (at + 1) * tokens, :].astype(F32)
@@ -304,8 +313,8 @@
         rounded = rest.astype(BF16).astype(F32)
         extra[piece * len(sums) : (piece + 1) * len(sums), :] = rounded
         rest = rest - rounded
-    for step, target in zip(partners(peers), out):
-        start = (me ^ step) * tokens
+    for step, target in zip(exchange_steps(peers), out):
+        start = sends_to(step, me) * tokens
         inner = pl.ds(pl.multiple_of(PAD + start, PAD), tokens)
         target[:tokens, :] = conv[inner, :].astype(BF16)
         target[tokens : 2 * tokens, :] = conv_grad[inner, :].astype(BF16)
@@ -362,8 +371,8 @@
     tap_count = weights.shape[1]
     count = sum_rows // PIECES
     me = lax.axis_index("ctx")
-    for step, source in zip(partners(peers), arrived):
-        lanes = lanes_of(me ^ step)
+    for step, source in zip(exchange_steps(peers), arrived):
+        lanes = lanes_of(hears_from(step, me))
         extra = source[3 * tokens :, :].astype(F32)
 
         def rim(at):

time: 42 us -> 45 us (1.071)
  starting transfers between devices: 14.2 us -> 15.8 us
  waiting for transfers between devices: 12.8 us -> 14.1 us
    ppermute x14, starting transfers between devices: 14.2 us -> 15.8 us  [exchange(): lax.ppermute(block, 'ctx', [(i, sends_to(step, i)) for i in range(peers)])]
    ppermute x14, waiting for transfers between devices: 12.8 us -> 14.1 us  [exchange(): lax.ppermute(block, 'ctx', [(i, sends_to(step, i)) for i in range(peers)])]
  transfers between devices with their start and end apart: 14 -> 14, of which waited for: 9 -> 4; matrix products, arithmetic and copies ran while one was open for 0% -> 0% of each run, Pallas kernels for 1% -> 1%
where the time goes in v6:
time: 45 us; the launch traced here: 44.7 us
  starting transfers between devices  15.8 us (35%)
  waiting for transfers between devices  14.1 us (31%)
  Pallas kernels  9.13 us (20%)
  local copies, waits for them, and re-layouts  4.93 us (11%)
  between operations  0.79 us (2%)
    ppermute x14, starting transfers between devices, exchange(): lax.ppermute(block, 'ctx', [(i, sends_to(step, i)) for i in range(peers)])  15.8 us
    ppermute x14, waiting for transfers between devices, exchange(): lax.ppermute(block, 'ctx', [(i, sends_to(step, i)) for i in range(peers)])  14.1 us
    unnamed x18, local copies, waits for them, and re-layouts  4.93 us
    pallas_call x1, Pallas kernels, channel_step(): pl.pallas_call(functools.partial(channel_kernel, tokens, peers, 1.0 / mat...  3.68 us
    pallas_call x1, Pallas kernels, pack(): pl.pallas_call(functools.partial(pack_kernel, len(arrays)), in_specs=in_v...  2.74 us
    pallas_call x1, Pallas kernels, token_step(): pl.pallas_call(functools.partial(token_kernel, peers, extra_rows(short_we...  2.14 us
  transfers between devices with their start and end apart: 14, of which 4 were waited for; matrix products, arithmetic and copies ran while one was open for 0% of the time, Pallas kernels for 1%

profile of v6, /device:TPU:0, one launch (start us, length us, event | category | flops | bytes accessed | tf_op | source)
XLA Modules:
  0.0 44.7 jit_solution(5436883722222035409)
XLA Ops:
  0.6 2.7 %pack_inputs.1 = (bf16[640,128]{1,0:T(8,128)(2,1)}, bf16[640,128]{1,0:T(8,128)(2,1)}, bf16[640,128]{1,0:T(8,128)(2,1)}, bf16[640,128]{1,0:T(8,128)(2,1)}, bf16[6...) custom-call(bf16[128,1024]{1,0:T(8,128)(2,1)} %refs_8_.1, ...), custom_call_target="tpu_custom_call" | custom-call | bytes 8388608 | tf_op jit(solution)/shard_map/pack_inputs/pallas_call | solution.py:69
  3.4 3.0 %collective-permute-start = (bf16[640,128]{1,0:T(8,128)(2,1)}, bf16[640,128]{1,0:T(8,128)(2,1)S(1)}, u32[]{:S(2)}, u32[]{:S(2)}) collective-permute-start(bf16[640,128]{1,0:T(8,128)(2,1)} %get-tuple-element.27), channel_id=1, source_target_pairs={{0,16},{4,12},{8,24},{12,4},{16,0},{20,28},{24,8},{28,20},{1,17},{... | collective-permute-start | bytes 491528 | tf_op jit(solution)/shard_map/ppermute | solution.py:45
  6.3 1.5 %collective-permute-start.1 = (bf16[640,128]{1,0:T(8,128)(2,1)}, bf16[640,128]{1,0:T(8,128)(2,1)S(1)}, u32[]{:S(2)}, u32[]{:S(2)}) collective-permute-start(bf16[640,128]{1,0:T(8,128)(2,1)} %get-tuple-element.29), channel_id=1, source_target_pairs={{0,8},{4,20},{8,0},{12,28},{16,24},{20,4},{24,16},{28,12},{1,9},{5... | collective-permute-start | bytes 491528 | tf_op jit(solution)/shard_map/ppermute | solution.py:45
  7.8 0.0 collective-permute-start.2
  7.8 1.5 %collective-permute-start.3 = (bf16[640,128]{1,0:T(8,128)(2,1)}, bf16[640,128]{1,0:T(8,128)(2,1)S(1)}, u32[]{:S(2)}, u32[]{:S(2)}) collective-permute-start(bf16[640,128]{1,0:T(8,128)(2,1)} %get-tuple-element.31), channel_id=1, source_target_pairs={{0,28},{4,24},{8,20},{12,16},{16,12},{20,8},{24,4},{28,0},{1,29},{... | collective-permute-start | bytes 491528 | tf_op jit(solution)/shard_map/ppermute | solution.py:45
  9.4 1.6 %collective-permute-start.4 = (bf16[640,128]{1,0:T(8,128)(2,1)}, bf16[640,128]{1,0:T(8,128)(2,1)S(1)}, u32[]{:S(2)}, u32[]{:S(2)}) collective-permute-start(bf16[640,128]{1,0:T(8,128)(2,1)} %get-tuple-element.32), channel_id=1, source_target_pairs={{0,20},{4,8},{8,28},{12,0},{16,4},{20,24},{24,12},{28,16},{1,21},{... | collective-permute-start | bytes 491528 | tf_op jit(solution)/shard_map/ppermute | solution.py:45
  11.0 5.2 %collective-permute-done.refs_4_.refs_1_ = bf16[640,128]{1,0:T(8,128)(2,1)S(1)} collective-permute-done((bf16[640,128]{1,0:T(8,128)(2,1)}, bf16[640,128]{1,0:T(8,128)(2,1)S(1)}, u32[]{:S(2)}, u32[]{:S(2)}) %collective-permute-start) | collective-permute-done | bytes 163872 | tf_op jit(solution)/shard_map/ppermute | solution.py:45
  16.2 3.0 %collective-permute-start.6 = (bf16[640,128]{1,0:T(8,128)(2,1)}, bf16[640,128]{1,0:T(8,128)(2,1)S(1)}, u32[]{:S(2)}, u32[]{:S(2)}) collective-permute-start(bf16[640,128]{1,0:T(8,128)(2,1)} %get-tuple-element.34), channel_id=1, source_target_pairs={{0,4},{4,0},{8,12},{12,8},{16,20},{20,16},{24,28},{28,24},{1,5},{5... | collective-permute-start | bytes 491528 | tf_op jit(solution)/shard_map/ppermute | solution.py:45
  19.1 1.6 %copy-done = bf16[4,2,256,512]{3,2,1,0:T(8,128)(2,1)S(1)} copy-done((bf16[4,2,256,512]{3,2,1,0:T(8,128)(2,1)S(1)}, bf16[4,2,256,512]{3,2,1,0:T(8,128)(2,1)}, u32[]{:S(2)}) %copy-start) | copy-done | bytes 2097176
  20.7 1.6 %copy-done.1 = bf16[4,2,512,256]{3,2,1,0:T(8,128)(2,1)S(1)} copy-done((bf16[4,2,512,256]{3,2,1,0:T(8,128)(2,1)S(1)}, bf16[4,2,512,256]{3,2,1,0:T(8,128)(2,1)}, u32[]{:S(2)}) %copy-start.1) | copy-done | bytes 2097176
  22.3 0.8 %copy-done.6 = f32[3,3,1024]{2,1,0:T(4,128)S(1)} copy-done((f32[3,3,1024]{2,1,0:T(4,128)S(1)}, f32[3,3,1024]{2,1,0:T(4,128)}, u32[]{:S(2)}) %copy-start.6) | copy-done | bytes 36888
  23.1 0.9 %copy-done.8 = bf16[640,128]{1,0:T(8,128)(2,1)S(1)} copy-done((bf16[640,128]{1,0:T(8,128)(2,1)S(1)}, bf16[640,128]{1,0:T(8,128)(2,1)}, u32[]{:S(2)}) %copy-start.8) | copy-done | bytes 163864
  24.0 0.6 %stage_tables.1 = (bf16[640,128]{1,0:T(8,128)(2,1)S(1)}, f32[3,3,1024]{2,1,0:T(4,128)S(1)}, bf16[4,2,512,256]{3,2,1,0:T(8,128)(2,1)S(1)}, bf16[4,2,256,512]{3,2,1,0:T(8,128)(2,1)S(1)}) custom-call(bf16[640,128]{1,0:T(8,128)(2,1)S(1)} %copy-done.8, f32[3,3,1024]{2,1,0:T(4,128)S(1)} %copy-done.6, bf16[4,2,512,256]{3,2,1,0:T(8,128)(2,1)S(1)} %copy-done.1, ...), custom_call_target="tpu_custom_call" | custom-call | bytes 8388608 | tf_op jit(solution)/shard_map/stage_tables/pallas_call | solution.py:176
  24.6 0.0 collective-permute-done.3.refs_4_
  24.6 0.0 collective-permute-done.4.refs_5_
  24.7 0.0 collective-permute-done.6.refs_7_
  24.7 0.0 copy-start.2
  24.7 0.0 copy-start.3
  24.7 0.0 copy-start.4
  24.7 0.0 copy-start.5
  24.7 0.0 copy-start.7
  24.7 3.7 %channel_operator.1 = (bf16[432,128]{1,0:T(8,128)(2,1)S(1)}, bf16[432,128]{1,0:T(8,128)(2,1)S(1)}, bf16[432,128]{1,0:T(8,128)(2,1)S(1)}, bf16[432,128]{1,0:T(8,1...) custom-call(bf16[640,128]{1,0:T(8,128)(2,1)S(1)} %get-tuple-element., ...), custom_call_target="tpu_custom_call" | custom-call | tf_op jit(solution)/shard_map/channel_operator/pallas_call | solution.py:344
  28.4 0.4 collective-permute-start.7
  28.8 0.2 collective-permute-start.8
  29.0 3.0 %collective-permute-start.9 = (bf16[432,128]{1,0:T(8,128)(2,1)S(1)}, bf16[432,128]{1,0:T(8,128)(2,1)S(1)}, u32[]{:S(2)}, u32[]{:S(2)}) collective-permute-start(bf16[432,128]{1,0:T(8,128)(2,1)S(1)} %get-tuple-element.41), channel_id=1, source_target_pairs={{0,24},{4,28},{8,16},{12,20},{16,8},{20,12},{24,0},{28,4},{1,25},{... | collective-permute-start | bytes 331784 | tf_op jit(solution)/shard_map/ppermute | solution.py:45
  32.0 0.0 collective-permute-start.10
  32.0 1.6 %collective-permute-start.11 = (bf16[432,128]{1,0:T(8,128)(2,1)S(1)}, bf16[432,128]{1,0:T(8,128)(2,1)S(1)}, u32[]{:S(2)}, u32[]{:S(2)}) collective-permute-start(bf16[432,128]{1,0:T(8,128)(2,1)S(1)} %get-tuple-element.43), channel_id=1, source_target_pairs={{0,20},{4,8},{8,28},{12,0},{16,4},{20,24},{24,12},{28,16},{1,21},{... | collective-permute-start | bytes 331784 | tf_op jit(solution)/shard_map/ppermute | solution.py:45
  33.6 4.8 %collective-permute-done.7.refs_1_ = bf16[432,128]{1,0:T(8,128)(2,1)S(1)} collective-permute-done((bf16[432,128]{1,0:T(8,128)(2,1)S(1)}, bf16[432,128]{1,0:T(8,128)(2,1)S(1)}, u32[]{:S(2)}, u32[]{:S(2)}) %collective-permute-start.7) | collective-permute-done | bytes 110624 | tf_op jit(solution)/shard_map/ppermute | solution.py:45
  38.4 0.0 collective-permute-start.12
  38.4 1.2 %collective-permute-done.11.refs_5_ = bf16[432,128]{1,0:T(8,128)(2,1)S(1)} collective-permute-done((bf16[432,128]{1,0:T(8,128)(2,1)S(1)}, bf16[432,128]{1,0:T(8,128)(2,1)S(1)}, u32[]{:S(2)}, u32[]{:S(2)}) %collective-permute-start.11) | collective-permute-done | bytes 110624 | tf_op jit(solution)/shard_map/ppermute | solution.py:45
  39.6 2.9 %collective-permute-done.12.refs_6_ = bf16[432,128]{1,0:T(8,128)(2,1)S(1)} collective-permute-done((bf16[432,128]{1,0:T(8,128)(2,1)S(1)}, bf16[432,128]{1,0:T(8,128)(2,1)S(1)}, u32[]{:S(2)}, u32[]{:S(2)}) %collective-permute-start.12) | collective-permute-done | bytes 110624 | tf_op jit(solution)/shard_map/ppermute | solution.py:45
  42.6 2.1 %token_outputs.1 = (bf16[128,1024]{1,0:T(8,128)(2,1)}, bf16[128,1024]{1,0:T(8,128)(2,1)}, bf16[128,1024]{1,0:T(8,128)(2,1)}, bf16[128,1024]{1,0:T(8,128)(2,1)}, ...) custom-call(bf16[432,128]{1,0:T(8,128)(2,1)S(1)} %get-tuple-element.38.refs_0_, ...), custom_call_target="tpu_custom_call" | custom-call | tf_op jit(solution)/shard_map/token_outputs/pallas_call | solution.py:430
  (18 shorter events, 0.0 us)
Async XLA Ops:
  3.4 12.8 %collective-permute-start = (bf16[640,128]{1,0:T(8,128)(2,1)}, bf16[640,128]{1,0:T(8,128)(2,1)S(1)}, u32[]{:S(2)}, u32[]{:S(2)}) collective-permute-start(bf16[640,128]{1,0:T(8,128)(2,1)} %get-tuple-element.27), channel_id=1, source_target_pairs={{0,16},{4,12},{8,24},{12,4},{16,0},{20,28},{24,8},{28,20},{1,17},{... | collective-permute-start | bytes 491528 | tf_op jit(solution)/shard_map/ppermute | solution.py:45
  6.3 9.8 %collective-permute-start.1 = (bf16[640,128]{1,0:T(8,128)(2,1)}, bf16[640,128]{1,0:T(8,128)(2,1)S(1)}, u32[]{:S(2)}, u32[]{:S(2)}) collective-permute-start(bf16[640,128]{1,0:T(8,128)(2,1)} %get-tuple-element.29), channel_id=1, source_target_pairs={{0,8},{4,20},{8,0},{12,28},{16,24},{20,4},{24,16},{28,12},{1,9},{5... | collective-permute-start | bytes 491528 | tf_op jit(solution)/shard_map/ppermute | solution.py:45
  7.8 16.8 %collective-permute-start.2 = (bf16[640,128]{1,0:T(8,128)(2,1)}, bf16[640,128]{1,0:T(8,128)(2,1)S(1)}, u32[]{:S(2)}, u32[]{:S(2)}) collective-permute-start(bf16[640,128]{1,0:T(8,128)(2,1)} %get-tuple-element.30), channel_id=1, source_target_pairs={{0,24},{4,28},{8,16},{12,20},{16,8},{20,12},{24,0},{28,4},{1,25},{... | collective-permute-start | bytes 491528 | tf_op jit(solution)/shard_map/ppermute | solution.py:45
  7.8 16.8 %collective-permute-start.3 = (bf16[640,128]{1,0:T(8,128)(2,1)}, bf16[640,128]{1,0:T(8,128)(2,1)S(1)}, u32[]{:S(2)}, u32[]{:S(2)}) collective-permute-start(bf16[640,128]{1,0:T(8,128)(2,1)} %get-tuple-element.31), channel_id=1, source_target_pairs={{0,28},{4,24},{8,20},{12,16},{16,12},{20,8},{24,4},{28,0},{1,29},{... | collective-permute-start | bytes 491528 | tf_op jit(solution)/shard_map/ppermute | solution.py:45
  9.4 15.3 %collective-permute-start.4 = (bf16[640,128]{1,0:T(8,128)(2,1)}, bf16[640,128]{1,0:T(8,128)(2,1)S(1)}, u32[]{:S(2)}, u32[]{:S(2)}) collective-permute-start(bf16[640,128]{1,0:T(8,128)(2,1)} %get-tuple-element.32), channel_id=1, source_target_pairs={{0,20},{4,8},{8,28},{12,0},{16,4},{20,24},{24,12},{28,16},{1,21},{... | collective-permute-start | bytes 491528 | tf_op jit(solution)/shard_map/ppermute | solution.py:45
  16.2 8.5 %collective-permute-start.5 = (bf16[640,128]{1,0:T(8,128)(2,1)}, bf16[640,128]{1,0:T(8,128)(2,1)S(1)}, u32[]{:S(2)}, u32[]{:S(2)}) collective-permute-start(bf16[640,128]{1,0:T(8,128)(2,1)} %get-tuple-element.33), channel_id=1, source_target_pairs={{0,12},{4,16},{8,4},{12,24},{16,28},{20,0},{24,20},{28,8},{1,13},{... | collective-permute-start | bytes 491528 | tf_op jit(solution)/shard_map/ppermute | solution.py:45
  16.2 8.5 %collective-permute-start.6 = (bf16[640,128]{1,0:T(8,128)(2,1)}, bf16[640,128]{1,0:T(8,128)(2,1)S(1)}, u32[]{:S(2)}, u32[]{:S(2)}) collective-permute-start(bf16[640,128]{1,0:T(8,128)(2,1)} %get-tuple-element.34), channel_id=1, source_target_pairs={{0,4},{4,0},{8,12},{12,8},{16,20},{20,16},{24,28},{28,24},{1,5},{5... | collective-permute-start | bytes 491528 | tf_op jit(solution)/shard_map/ppermute | solution.py:45
  19.1 1.6 %copy-start = (bf16[4,2,256,512]{3,2,1,0:T(8,128)(2,1)S(1)}, bf16[4,2,256,512]{3,2,1,0:T(8,128)(2,1)}, u32[]{:S(2)}) copy-start(bf16[4,2,256,512]{3,2,1,0:T(8,128)(2,1)} %constant.5.clone.refs_3_) | copy-start | bytes 6291460
  20.7 1.6 %copy-start.1 = (bf16[4,2,512,256]{3,2,1,0:T(8,128)(2,1)S(1)}, bf16[4,2,512,256]{3,2,1,0:T(8,128)(2,1)}, u32[]{:S(2)}) copy-start(bf16[4,2,512,256]{3,2,1,0:T(8,128)(2,1)} %constant.4.clone.refs_2_) | copy-start | bytes 6291460
  22.3 0.8 %copy-start.6 = (f32[3,3,1024]{2,1,0:T(4,128)S(1)}, f32[3,3,1024]{2,1,0:T(4,128)}, u32[]{:S(2)}) copy-start(f32[3,3,1024]{2,1,0:T(4,128)} %refs_12_.1) | copy-start | bytes 110596
  23.1 0.9 %copy-start.8 = (bf16[640,128]{1,0:T(8,128)(2,1)S(1)}, bf16[640,128]{1,0:T(8,128)(2,1)}, u32[]{:S(2)}) copy-start(bf16[640,128]{1,0:T(8,128)(2,1)} %get-tuple-element.26.refs_0_) | copy-start | bytes 491524
  24.7 17.9 %copy-start.2 = (bf16[128,1024]{1,0:T(8,128)(2,1)S(1)}, bf16[128,1024]{1,0:T(8,128)(2,1)}, u32[]{:S(2)}) copy-start(bf16[128,1024]{1,0:T(8,128)(2,1)} %refs_8_.1) | copy-start | bytes 786436
  24.7 17.9 %copy-start.3 = (bf16[128,1024]{1,0:T(8,128)(2,1)S(1)}, bf16[128,1024]{1,0:T(8,128)(2,1)}, u32[]{:S(2)}) copy-start(bf16[128,1024]{1,0:T(8,128)(2,1)} %refs_9_.1) | copy-start | bytes 786436
  24.7 17.9 %copy-start.4 = (bf16[128,1024]{1,0:T(8,128)(2,1)S(1)}, bf16[128,1024]{1,0:T(8,128)(2,1)}, u32[]{:S(2)}) copy-start(bf16[128,1024]{1,0:T(8,128)(2,1)} %refs_10_.1) | copy-start | bytes 786436
  24.7 17.9 %copy-start.5 = (bf16[128,1024]{1,0:T(8,128)(2,1)S(1)}, bf16[128,1024]{1,0:T(8,128)(2,1)}, u32[]{:S(2)}) copy-start(bf16[128,1024]{1,0:T(8,128)(2,1)} %refs_11_.1) | copy-start | bytes 786436
  24.7 17.9 %copy-start.7 = (f32[3,3,1024]{2,1,0:T(4,128)S(1)}, f32[3,3,1024]{2,1,0:T(4,128)}, u32[]{:S(2)}) copy-start(f32[3,3,1024]{2,1,0:T(4,128)} %refs_12_.1) | copy-start | bytes 110596
  28.4 9.9 %collective-permute-start.7 = (bf16[432,128]{1,0:T(8,128)(2,1)S(1)}, bf16[432,128]{1,0:T(8,128)(2,1)S(1)}, u32[]{:S(2)}, u32[]{:S(2)}) collective-permute-start(bf16[432,128]{1,0:T(8,128)(2,1)S(1)} %get-tuple-element.39), channel_id=1, source_target_pairs={{0,16},{4,12},{8,24},{12,4},{16,0},{20,28},{24,8},{28,20},{1,17},{... | collective-permute-start | bytes 331784 | tf_op jit(solution)/shard_map/ppermute | solution.py:45
  28.8 9.6 %collective-permute-start.8 = (bf16[432,128]{1,0:T(8,128)(2,1)S(1)}, bf16[432,128]{1,0:T(8,128)(2,1)S(1)}, u32[]{:S(2)}, u32[]{:S(2)}) collective-permute-start(bf16[432,128]{1,0:T(8,128)(2,1)S(1)} %get-tuple-element.40), channel_id=1, source_target_pairs={{0,8},{4,20},{8,0},{12,28},{16,24},{20,4},{24,16},{28,12},{1,9},{5... | collective-permute-start | bytes 331784 | tf_op jit(solution)/shard_map/ppermute | solution.py:45
  29.0 9.4 %collective-permute-start.9 = (bf16[432,128]{1,0:T(8,128)(2,1)S(1)}, bf16[432,128]{1,0:T(8,128)(2,1)S(1)}, u32[]{:S(2)}, u32[]{:S(2)}) collective-permute-start(bf16[432,128]{1,0:T(8,128)(2,1)S(1)} %get-tuple-element.41), channel_id=1, source_target_pairs={{0,24},{4,28},{8,16},{12,20},{16,8},{20,12},{24,0},{28,4},{1,25},{... | collective-permute-start | bytes 331784 | tf_op jit(solution)/shard_map/ppermute | solution.py:45
  32.0 6.4 %collective-permute-start.10 = (bf16[432,128]{1,0:T(8,128)(2,1)S(1)}, bf16[432,128]{1,0:T(8,128)(2,1)S(1)}, u32[]{:S(2)}, u32[]{:S(2)}) collective-permute-start(bf16[432,128]{1,0:T(8,128)(2,1)S(1)} %get-tuple-element.42), channel_id=1, source_target_pairs={{0,28},{4,24},{8,20},{12,16},{16,12},{20,8},{24,4},{28,0},{1,29},{... | collective-permute-start | bytes 331784 | tf_op jit(solution)/shard_map/ppermute | solution.py:45
  32.0 7.6 %collective-permute-start.11 = (bf16[432,128]{1,0:T(8,128)(2,1)S(1)}, bf16[432,128]{1,0:T(8,128)(2,1)S(1)}, u32[]{:S(2)}, u32[]{:S(2)}) collective-permute-start(bf16[432,128]{1,0:T(8,128)(2,1)S(1)} %get-tuple-element.43), channel_id=1, source_target_pairs={{0,20},{4,8},{8,28},{12,0},{16,4},{20,24},{24,12},{28,16},{1,21},{... | collective-permute-start | bytes 331784 | tf_op jit(solution)/shard_map/ppermute | solution.py:45
  38.4 4.2 %collective-permute-start.12 = (bf16[432,128]{1,0:T(8,128)(2,1)S(1)}, bf16[432,128]{1,0:T(8,128)(2,1)S(1)}, u32[]{:S(2)}, u32[]{:S(2)}) collective-permute-start(bf16[432,128]{1,0:T(8,128)(2,1)S(1)} %get-tuple-element.44), channel_id=1, source_target_pairs={{0,12},{4,16},{8,4},{12,24},{16,28},{20,0},{24,20},{28,8},{1,13},{... | collective-permute-start | bytes 331784 | tf_op jit(solution)/shard_map/ppermute | solution.py:45
  38.4 4.2 %collective-permute-start.13 = (bf16[432,128]{1,0:T(8,128)(2,1)S(1)}, bf16[432,128]{1,0:T(8,128)(2,1)S(1)}, u32[]{:S(2)}, u32[]{:S(2)}) collective-permute-start(bf16[432,128]{1,0:T(8,128)(2,1)S(1)} %get-tuple-element.45), channel_id=1, source_target_pairs={{0,4},{4,0},{8,12},{12,8},{16,20},{20,16},{24,28},{28,24},{1,5},{5... | collective-permute-start | bytes 331784 | tf_op jit(solution)/shard_map/ppermute | solution.py:45

commit v7 on v5

--- a/solution.py
+++ b/solution.py
@@ -47,21 +47,48 @@
 
 
 def pack_kernel(count, *refs):
-    sources, packed = refs[:count], refs[count:]
-    tokens = sources[0].shape[0]
+    sources, taps = refs[: count - 1], refs[count - 1]
+    packed, (wide, narrow, sems, taps_sems) = refs[count:-4], refs[-4:]
+    tokens = taps.shape[0]
     me = lax.axis_index("ctx")
-    for step, target in zip(partners(len(packed)), packed):
+    get_taps = pltpu.make_async_copy(taps, wide, taps_sems.at[0])
+    get_taps.start()
+    copies = []
+    steps = list(enumerate(zip(partners(len(packed)), packed)))
+    for slot, (step, target) in steps[1:] + steps[:1]:
+        lanes = lanes_of(me ^ step)
         for at, source in enumerate(sources):
-            target[at * tokens : (at + 1) * tokens, :] = source[:, lanes_of(me ^ step)].astype(BF16)
+            rows = pl.ds(at * tokens, tokens)
+            copies.append(
+                pltpu.make_async_copy(source.at[:, lanes], target.at[rows, :], sems.at[slot, at])
+            )
+            copies[-1].start()
+    get_taps.wait()
+    for slot, (step, target) in steps[1:] + steps[:1]:
+        narrow[slot] = wide[:, lanes_of(me ^ step)].astype(BF16)
+        rows = pl.ds((count - 1) * tokens, tokens)
+        copies.append(
+            pltpu.make_async_copy(narrow.at[slot], target.at[rows, :], taps_sems.at[1 + slot])
+        )
+        copies[-1].start()
+    for copy in copies:
+        copy.wait()
 
 
 def pack(arrays, peers):
-    tokens = arrays[0].shape[0]
+    tokens, width = arrays[0].shape
+    count = len(arrays)
     return pl.pallas_call(
-        functools.partial(pack_kernel, len(arrays)),
-        in_specs=in_vmem(len(arrays)),
-        out_specs=in_vmem(peers),
-        out_shape=[jax.ShapeDtypeStruct((len(arrays) * tokens, LANES), BF16)] * peers,
+        functools.partial(pack_kernel, count),
+        in_specs=[pl.BlockSpec(memory_space=pl.ANY)] * count,
+        out_specs=[pl.BlockSpec(memory_space=pl.ANY)] * peers,
+        out_shape=[jax.ShapeDtypeStruct((count * tokens, LANES), BF16)] * peers,
+        scratch_shapes=[
+            pltpu.VMEM((tokens, width), F32),
+            pltpu.VMEM((peers, tokens, LANES), BF16),
+            pltpu.SemaphoreType.DMA((peers, count - 1)),
+            pltpu.SemaphoreType.DMA((peers + 1,)),
+        ],
         cost_estimate=pl.CostEstimate(flops=0, bytes_accessed=8 * MIB, transcendentals=0),
         name="pack_inputs",
     )(*arrays)
@@ -356,13 +383,15 @@
 def token_kernel(peers, sum_rows, *refs):
     arrived = refs[:peers]
     query, key, value, cot, weights = refs[peers : peers + 5]
-    gated, query_grad, key_grad, value_grad, filter_grad, short_grad = refs[peers + 5 : peers + 11]
-    longer, pre = refs[peers + 11 :]
+    results = refs[peers + 5 : peers + 11]
+    longer, pre, sems = refs[peers + 17 :]
+    gated, query_grad, key_grad, value_grad, filter_grad, short_grad = refs[peers + 11 : peers + 17]
+    copies = []
     tokens = query.shape[0]
     tap_count = weights.shape[1]
     count = sum_rows // PIECES
     me = lax.axis_index("ctx")
-    for step, source in zip(partners(peers), arrived):
+    for slot, (step, source) in enumerate(zip(partners(peers), arrived)):
         lanes = lanes_of(me ^ step)
         extra = source[3 * tokens :, :].astype(F32)
 
@@ -412,6 +441,17 @@
         for row in range(count):
             which, tap = divmod(row, tap_count)
             short_grad[which, tap : tap + 1, lanes] = whole[row : row + 1]
+        for at, held in enumerate((gated, query_grad, key_grad, value_grad, filter_grad)):
+            copies.append(
+                pltpu.make_async_copy(
+                    held.at[:, lanes], results[at].at[:, lanes], sems.at[slot, at]
+                )
+            )
+            copies[-1].start()
+    copies.append(pltpu.make_async_copy(short_grad, results[5], sems.at[peers, 0]))
+    copies[-1].start()
+    for copy in copies:
+        copy.wait()
 
 
 def token_step(arrived, query, key, value, cot, short_weights):
@@ -421,15 +461,19 @@
     return pl.pallas_call(
         functools.partial(token_kernel, peers, extra_rows(short_weights)[0]),
         in_specs=in_vmem(peers + 5),
-        out_specs=in_vmem(6),
+        out_specs=[pl.BlockSpec(memory_space=pl.ANY)] * 6,
         out_shape=[wide] * 4
         + [
             jax.ShapeDtypeStruct((tokens, width), F32),
             jax.ShapeDtypeStruct(short_weights.shape, F32),
         ],
         scratch_shapes=[
+            *[pltpu.VMEM((tokens, width), BF16)] * 4,
+            pltpu.VMEM((tokens, width), F32),
+            pltpu.VMEM(short_weights.shape, F32),
             pltpu.VMEM((3, tokens + 2 * PAD, LANES), F32),
             pltpu.VMEM((3, tokens + PAD, LANES), F32),
+            pltpu.SemaphoreType.DMA((peers + 1, 5)),
         ],
         compiler_params=pltpu.CompilerParams(vmem_limit_bytes=VMEM_LIMIT),
         name="token_outputs",

time: 42 us -> 72.8 us (1.73)
  Pallas kernels: 9.12 us -> 39.8 us
    pallas_call x1, Pallas kernels: 2.74 us -> 33.3 us  [pack(): pl.pallas_call(functools.partial(pack_kernel, count), in_specs=[pl.BlockS...]
where the time goes in v7:
time: 72.8 us; the launch traced here: 72.5 us
  Pallas kernels  39.8 us (55%)
  starting transfers between devices  14.3 us (20%)
  waiting for transfers between devices  12.8 us (18%)
  local copies, waits for them, and re-layouts  4.92 us (7%)
  between operations  0.73 us (1%)
    pallas_call x1, Pallas kernels, pack(): pl.pallas_call(functools.partial(pack_kernel, count), in_specs=[pl.BlockS...  33.3 us
    ppermute x14, starting transfers between devices, exchange(): lax.ppermute(block, 'ctx', [(i, i ^ step) for i in range(peers)])  14.3 us
    ppermute x14, waiting for transfers between devices, exchange(): lax.ppermute(block, 'ctx', [(i, i ^ step) for i in range(peers)])  12.8 us
    unnamed x18, local copies, waits for them, and re-layouts  4.92 us
    pallas_call x1, Pallas kernels, channel_step(): pl.pallas_call(functools.partial(channel_kernel, tokens, peers, 1.0 / mat...  3.68 us
    pallas_call x1, Pallas kernels, token_step(): pl.pallas_call(functools.partial(token_kernel, peers, extra_rows(short_we...  2.31 us
  transfers between devices with their start and end apart: 14, of which 9 were waited for; matrix products, arithmetic and copies ran while one was open for 0% of the time, Pallas kernels for 1%

profile of v7, /device:TPU:0, one launch (start us, length us, event | category | flops | bytes accessed | tf_op | source)
XLA Modules:
  0.0 72.5 jit_solution(5335718153081729075)
XLA Ops:
  0.6 33.3 %pack_inputs.1 = (bf16[640,128]{1,0:T(8,128)(2,1)}, bf16[640,128]{1,0:T(8,128)(2,1)}, bf16[640,128]{1,0:T(8,128)(2,1)}, bf16[640,128]{1,0:T(8,128)(2,1)}, bf16[6...) custom-call(bf16[128,1024]{1,0:T(8,128)(2,1)} %refs_8_.1, ...), custom_call_target="tpu_custom_call" | custom-call | bytes 8388608 | tf_op jit(solution)/shard_map/pack_inputs/pallas_call | solution.py:81
  33.9 3.0 %collective-permute-start = (bf16[640,128]{1,0:T(8,128)(2,1)}, bf16[640,128]{1,0:T(8,128)(2,1)S(1)}, u32[]{:S(2)}, u32[]{:S(2)}) collective-permute-start(bf16[640,128]{1,0:T(8,128)(2,1)} %get-tuple-element.27), channel_id=1, source_target_pairs={{0,16},{4,20},{8,24},{12,28},{16,0},{20,4},{24,8},{28,12},{1,17},{... | collective-permute-start | bytes 491528 | tf_op jit(solution)/shard_map/ppermute | solution.py:37
  36.9 1.5 %collective-permute-start.1 = (bf16[640,128]{1,0:T(8,128)(2,1)}, bf16[640,128]{1,0:T(8,128)(2,1)S(1)}, u32[]{:S(2)}, u32[]{:S(2)}) collective-permute-start(bf16[640,128]{1,0:T(8,128)(2,1)} %get-tuple-element.29), channel_id=1, source_target_pairs={{0,8},{4,12},{8,0},{12,4},{16,24},{20,28},{24,16},{28,20},{1,9},{5... | collective-permute-start | bytes 491528 | tf_op jit(solution)/shard_map/ppermute | solution.py:37
  38.4 0.0 collective-permute-start.2
  38.5 1.5 %collective-permute-start.3 = (bf16[640,128]{1,0:T(8,128)(2,1)}, bf16[640,128]{1,0:T(8,128)(2,1)S(1)}, u32[]{:S(2)}, u32[]{:S(2)}) collective-permute-start(bf16[640,128]{1,0:T(8,128)(2,1)} %get-tuple-element.31), channel_id=1, source_target_pairs={{0,28},{4,24},{8,20},{12,16},{16,12},{20,8},{24,4},{28,0},{1,29},{... | collective-permute-start | bytes 491528 | tf_op jit(solution)/shard_map/ppermute | solution.py:37
  40.0 1.6 %collective-permute-start.4 = (bf16[640,128]{1,0:T(8,128)(2,1)}, bf16[640,128]{1,0:T(8,128)(2,1)S(1)}, u32[]{:S(2)}, u32[]{:S(2)}) collective-permute-start(bf16[640,128]{1,0:T(8,128)(2,1)} %get-tuple-element.32), channel_id=1, source_target_pairs={{0,20},{4,16},{8,28},{12,24},{16,4},{20,0},{24,12},{28,8},{1,21},{... | collective-permute-start | bytes 491528 | tf_op jit(solution)/shard_map/ppermute | solution.py:37
  41.6 0.1 collective-permute-start.5
  41.6 2.6 %collective-permute-done.1.refs_2_ = bf16[640,128]{1,0:T(8,128)(2,1)S(1)} collective-permute-done((bf16[640,128]{1,0:T(8,128)(2,1)}, bf16[640,128]{1,0:T(8,128)(2,1)S(1)}, u32[]{:S(2)}, u32[]{:S(2)}) %collective-permute-start.1) | collective-permute-done | bytes 163872 | tf_op jit(solution)/shard_map/ppermute | solution.py:37
  44.3 1.6 %copy-done = bf16[4,2,256,512]{3,2,1,0:T(8,128)(2,1)S(1)} copy-done((bf16[4,2,256,512]{3,2,1,0:T(8,128)(2,1)S(1)}, bf16[4,2,256,512]{3,2,1,0:T(8,128)(2,1)}, u32[]{:S(2)}) %copy-start) | copy-done | bytes 2097176
  45.9 1.6 %copy-done.1 = bf16[4,2,512,256]{3,2,1,0:T(8,128)(2,1)S(1)} copy-done((bf16[4,2,512,256]{3,2,1,0:T(8,128)(2,1)S(1)}, bf16[4,2,512,256]{3,2,1,0:T(8,128)(2,1)}, u32[]{:S(2)}) %copy-start.1) | copy-done | bytes 2097176
  47.5 0.8 %copy-done.6 = f32[3,3,1024]{2,1,0:T(4,128)S(1)} copy-done((f32[3,3,1024]{2,1,0:T(4,128)S(1)}, f32[3,3,1024]{2,1,0:T(4,128)}, u32[]{:S(2)}) %copy-start.6) | copy-done | bytes 36888
  48.3 0.9 %copy-done.8 = bf16[640,128]{1,0:T(8,128)(2,1)S(1)} copy-done((bf16[640,128]{1,0:T(8,128)(2,1)S(1)}, bf16[640,128]{1,0:T(8,128)(2,1)}, u32[]{:S(2)}) %copy-start.8) | copy-done | bytes 163864
  49.2 0.6 stage_tables.1
  49.8 0.7 collective-permute-done.3.refs_4_
  50.4 1.9 %collective-permute-done.4.refs_5_ = bf16[640,128]{1,0:T(8,128)(2,1)S(1)} collective-permute-done((bf16[640,128]{1,0:T(8,128)(2,1)}, bf16[640,128]{1,0:T(8,128)(2,1)S(1)}, u32[]{:S(2)}, u32[]{:S(2)}) %collective-permute-start.4) | collective-permute-done | bytes 163872 | tf_op jit(solution)/shard_map/ppermute | solution.py:37
  52.4 0.1 collective-permute-done.5.refs_6_
  52.5 0.0 copy-start.5
  52.5 0.0 copy-start.7
  52.5 3.7 %channel_operator.1 = (bf16[432,128]{1,0:T(8,128)(2,1)S(1)}, bf16[432,128]{1,0:T(8,128)(2,1)S(1)}, bf16[432,128]{1,0:T(8,128)(2,1)S(1)}, bf16[432,128]{1,0:T(8,1...) custom-call(bf16[640,128]{1,0:T(8,128)(2,1)S(1)} %get-tuple-element., ...), custom_call_target="tpu_custom_call" | custom-call | tf_op jit(solution)/shard_map/channel_operator/pallas_call | solution.py:362
  56.2 1.4 %collective-permute-start.7 = (bf16[432,128]{1,0:T(8,128)(2,1)S(1)}, bf16[432,128]{1,0:T(8,128)(2,1)S(1)}, u32[]{:S(2)}, u32[]{:S(2)}) collective-permute-start(bf16[432,128]{1,0:T(8,128)(2,1)S(1)} %get-tuple-element.39), channel_id=1, source_target_pairs={{0,16},{4,20},{8,24},{12,28},{16,0},{20,4},{24,8},{28,12},{1,17},{... | collective-permute-start | bytes 331784 | tf_op jit(solution)/shard_map/ppermute | solution.py:37
  57.6 1.2 %collective-permute-start.8 = (bf16[432,128]{1,0:T(8,128)(2,1)S(1)}, bf16[432,128]{1,0:T(8,128)(2,1)S(1)}, u32[]{:S(2)}, u32[]{:S(2)}) collective-permute-start(bf16[432,128]{1,0:T(8,128)(2,1)S(1)} %get-tuple-element.40), channel_id=1, source_target_pairs={{0,8},{4,12},{8,0},{12,4},{16,24},{20,28},{24,16},{28,20},{1,9},{5... | collective-permute-start | bytes 331784 | tf_op jit(solution)/shard_map/ppermute | solution.py:37
  58.9 0.9 %collective-permute-start.9 = (bf16[432,128]{1,0:T(8,128)(2,1)S(1)}, bf16[432,128]{1,0:T(8,128)(2,1)S(1)}, u32[]{:S(2)}, u32[]{:S(2)}) collective-permute-start(bf16[432,128]{1,0:T(8,128)(2,1)S(1)} %get-tuple-element.41), channel_id=1, source_target_pairs={{0,24},{4,28},{8,16},{12,20},{16,8},{20,12},{24,0},{28,4},{1,25},{... | collective-permute-start | bytes 331784 | tf_op jit(solution)/shard_map/ppermute | solution.py:37
  59.8 0.9 %collective-permute-start.10 = (bf16[432,128]{1,0:T(8,128)(2,1)S(1)}, bf16[432,128]{1,0:T(8,128)(2,1)S(1)}, u32[]{:S(2)}, u32[]{:S(2)}) collective-permute-start(bf16[432,128]{1,0:T(8,128)(2,1)S(1)} %get-tuple-element.42), channel_id=1, source_target_pairs={{0,28},{4,24},{8,20},{12,16},{16,12},{20,8},{24,4},{28,0},{1,29},{... | collective-permute-start | bytes 331784 | tf_op jit(solution)/shard_map/ppermute | solution.py:37
  60.7 1.2 %collective-permute-start.11 = (bf16[432,128]{1,0:T(8,128)(2,1)S(1)}, bf16[432,128]{1,0:T(8,128)(2,1)S(1)}, u32[]{:S(2)}, u32[]{:S(2)}) collective-permute-start(bf16[432,128]{1,0:T(8,128)(2,1)S(1)} %get-tuple-element.43), channel_id=1, source_target_pairs={{0,20},{4,16},{8,28},{12,24},{16,4},{20,0},{24,12},{28,8},{1,21},{... | collective-permute-start | bytes 331784 | tf_op jit(solution)/shard_map/ppermute | solution.py:37
  61.9 0.1 collective-permute-done.7.refs_1_
  62.0 0.9 %collective-permute-start.12 = (bf16[432,128]{1,0:T(8,128)(2,1)S(1)}, bf16[432,128]{1,0:T(8,128)(2,1)S(1)}, u32[]{:S(2)}, u32[]{:S(2)}) collective-permute-start(bf16[432,128]{1,0:T(8,128)(2,1)S(1)} %get-tuple-element.44), channel_id=1, source_target_pairs={{0,12},{4,8},{8,4},{12,0},{16,28},{20,24},{24,20},{28,16},{1,13},{... | collective-permute-start | bytes 331784 | tf_op jit(solution)/shard_map/ppermute | solution.py:37
  62.8 0.2 collective-permute-done.8.refs_2_
  63.1 0.0 collective-permute-start.13
  63.1 3.0 %collective-permute-done.9.refs_3_ = bf16[432,128]{1,0:T(8,128)(2,1)S(1)} collective-permute-done((bf16[432,128]{1,0:T(8,128)(2,1)S(1)}, bf16[432,128]{1,0:T(8,128)(2,1)S(1)}, u32[]{:S(2)}, u32[]{:S(2)}) %collective-permute-start.9) | collective-permute-done | bytes 110624 | tf_op jit(solution)/shard_map/ppermute | solution.py:37
  66.1 1.4 %collective-permute-done.10.refs_4_ = bf16[432,128]{1,0:T(8,128)(2,1)S(1)} collective-permute-done((bf16[432,128]{1,0:T(8,128)(2,1)S(1)}, bf16[432,128]{1,0:T(8,128)(2,1)S(1)}, u32[]{:S(2)}, u32[]{:S(2)}) %collective-permute-start.10) | collective-permute-done | bytes 110624 | tf_op jit(solution)/shard_map/ppermute | solution.py:37
  67.5 2.6 %collective-permute-done.11.refs_5_ = bf16[432,128]{1,0:T(8,128)(2,1)S(1)} collective-permute-done((bf16[432,128]{1,0:T(8,128)(2,1)S(1)}, bf16[432,128]{1,0:T(8,128)(2,1)S(1)}, u32[]{:S(2)}, u32[]{:S(2)}) %collective-permute-start.11) | collective-permute-done | bytes 110624 | tf_op jit(solution)/shard_map/ppermute | solution.py:37
  70.2 2.3 %token_outputs.1 = (bf16[128,1024]{1,0:T(8,128)(2,1)}, bf16[128,1024]{1,0:T(8,128)(2,1)}, bf16[128,1024]{1,0:T(8,128)(2,1)}, bf16[128,1024]{1,0:T(8,128)(2,1)}, ...) custom-call(bf16[432,128]{1,0:T(8,128)(2,1)S(1)} %get-tuple-element.38.refs_0_, ...), custom_call_target="tpu_custom_call" | custom-call | tf_op jit(solution)/shard_map/token_outputs/pallas_call | solution.py:461
  (18 shorter events, 0.0 us)
Async XLA Ops:
  33.9 7.7 %collective-permute-start = (bf16[640,128]{1,0:T(8,128)(2,1)}, bf16[640,128]{1,0:T(8,128)(2,1)S(1)}, u32[]{:S(2)}, u32[]{:S(2)}) collective-permute-start(bf16[640,128]{1,0:T(8,128)(2,1)} %get-tuple-element.27), channel_id=1, source_target_pairs={{0,16},{4,20},{8,24},{12,28},{16,0},{20,4},{24,8},{28,12},{1,17},{... | collective-permute-start | bytes 491528 | tf_op jit(solution)/shard_map/ppermute | solution.py:37
  36.9 7.3 %collective-permute-start.1 = (bf16[640,128]{1,0:T(8,128)(2,1)}, bf16[640,128]{1,0:T(8,128)(2,1)S(1)}, u32[]{:S(2)}, u32[]{:S(2)}) collective-permute-start(bf16[640,128]{1,0:T(8,128)(2,1)} %get-tuple-element.29), channel_id=1, source_target_pairs={{0,8},{4,12},{8,0},{12,4},{16,24},{20,28},{24,16},{28,20},{1,9},{5... | collective-permute-start | bytes 491528 | tf_op jit(solution)/shard_map/ppermute | solution.py:37
  38.4 11.3 %collective-permute-start.2 = (bf16[640,128]{1,0:T(8,128)(2,1)}, bf16[640,128]{1,0:T(8,128)(2,1)S(1)}, u32[]{:S(2)}, u32[]{:S(2)}) collective-permute-start(bf16[640,128]{1,0:T(8,128)(2,1)} %get-tuple-element.30), channel_id=1, source_target_pairs={{0,24},{4,28},{8,16},{12,20},{16,8},{20,12},{24,0},{28,4},{1,25},{... | collective-permute-start | bytes 491528 | tf_op jit(solution)/shard_map/ppermute | solution.py:37
  38.5 12.0 %collective-permute-start.3 = (bf16[640,128]{1,0:T(8,128)(2,1)}, bf16[640,128]{1,0:T(8,128)(2,1)S(1)}, u32[]{:S(2)}, u32[]{:S(2)}) collective-permute-start(bf16[640,128]{1,0:T(8,128)(2,1)} %get-tuple-element.31), channel_id=1, source_target_pairs={{0,28},{4,24},{8,20},{12,16},{16,12},{20,8},{24,4},{28,0},{1,29},{... | collective-permute-start | bytes 491528 | tf_op jit(solution)/shard_map/ppermute | solution.py:37
  40.0 12.4 %collective-permute-start.4 = (bf16[640,128]{1,0:T(8,128)(2,1)}, bf16[640,128]{1,0:T(8,128)(2,1)S(1)}, u32[]{:S(2)}, u32[]{:S(2)}) collective-permute-start(bf16[640,128]{1,0:T(8,128)(2,1)} %get-tuple-element.32), channel_id=1, source_target_pairs={{0,20},{4,16},{8,28},{12,24},{16,4},{20,0},{24,12},{28,8},{1,21},{... | collective-permute-start | bytes 491528 | tf_op jit(solution)/shard_map/ppermute | solution.py:37
  41.6 10.9 %collective-permute-start.5 = (bf16[640,128]{1,0:T(8,128)(2,1)}, bf16[640,128]{1,0:T(8,128)(2,1)S(1)}, u32[]{:S(2)}, u32[]{:S(2)}) collective-permute-start(bf16[640,128]{1,0:T(8,128)(2,1)} %get-tuple-element.33), channel_id=1, source_target_pairs={{0,12},{4,8},{8,4},{12,0},{16,28},{20,24},{24,20},{28,16},{1,13},{... | collective-permute-start | bytes 491528 | tf_op jit(solution)/shard_map/ppermute | solution.py:37
  44.3 8.2 %collective-permute-start.6 = (bf16[640,128]{1,0:T(8,128)(2,1)}, bf16[640,128]{1,0:T(8,128)(2,1)S(1)}, u32[]{:S(2)}, u32[]{:S(2)}) collective-permute-start(bf16[640,128]{1,0:T(8,128)(2,1)} %get-tuple-element.34), channel_id=1, source_target_pairs={{0,4},{4,0},{8,12},{12,8},{16,20},{20,16},{24,28},{28,24},{1,5},{5... | collective-permute-start | bytes 491528 | tf_op jit(solution)/shard_map/ppermute | solution.py:37
  44.3 1.6 %copy-start = (bf16[4,2,256,512]{3,2,1,0:T(8,128)(2,1)S(1)}, bf16[4,2,256,512]{3,2,1,0:T(8,128)(2,1)}, u32[]{:S(2)}) copy-start(bf16[4,2,256,512]{3,2,1,0:T(8,128)(2,1)} %constant.5.clone.refs_3_) | copy-start | bytes 6291460
  45.9 1.6 %copy-start.1 = (bf16[4,2,512,256]{3,2,1,0:T(8,128)(2,1)S(1)}, bf16[4,2,512,256]{3,2,1,0:T(8,128)(2,1)}, u32[]{:S(2)}) copy-start(bf16[4,2,512,256]{3,2,1,0:T(8,128)(2,1)} %constant.4.clone.refs_2_) | copy-start | bytes 6291460
  47.5 0.8 %copy-start.6 = (f32[3,3,1024]{2,1,0:T(4,128)S(1)}, f32[3,3,1024]{2,1,0:T(4,128)}, u32[]{:S(2)}) copy-start(f32[3,3,1024]{2,1,0:T(4,128)} %refs_12_.1) | copy-start | bytes 110596
  48.3 0.9 %copy-start.8 = (bf16[640,128]{1,0:T(8,128)(2,1)S(1)}, bf16[640,128]{1,0:T(8,128)(2,1)}, u32[]{:S(2)}) copy-start(bf16[640,128]{1,0:T(8,128)(2,1)} %get-tuple-element.26.refs_0_) | copy-start | bytes 491524
  52.5 17.7 %copy-start.2 = (bf16[128,1024]{1,0:T(8,128)(2,1)S(1)}, bf16[128,1024]{1,0:T(8,128)(2,1)}, u32[]{:S(2)}) copy-start(bf16[128,1024]{1,0:T(8,128)(2,1)} %refs_8_.1) | copy-start | bytes 786436
  52.5 17.7 %copy-start.3 = (bf16[128,1024]{1,0:T(8,128)(2,1)S(1)}, bf16[128,1024]{1,0:T(8,128)(2,1)}, u32[]{:S(2)}) copy-start(bf16[128,1024]{1,0:T(8,128)(2,1)} %refs_9_.1) | copy-start | bytes 786436
  52.5 17.7 %copy-start.4 = (bf16[128,1024]{1,0:T(8,128)(2,1)S(1)}, bf16[128,1024]{1,0:T(8,128)(2,1)}, u32[]{:S(2)}) copy-start(bf16[128,1024]{1,0:T(8,128)(2,1)} %refs_10_.1) | copy-start | bytes 786436
  52.5 17.7 %copy-start.5 = (bf16[128,1024]{1,0:T(8,128)(2,1)S(1)}, bf16[128,1024]{1,0:T(8,128)(2,1)}, u32[]{:S(2)}) copy-start(bf16[128,1024]{1,0:T(8,128)(2,1)} %refs_11_.1) | copy-start | bytes 786436
  52.5 17.7 %copy-start.7 = (f32[3,3,1024]{2,1,0:T(4,128)S(1)}, f32[3,3,1024]{2,1,0:T(4,128)}, u32[]{:S(2)}) copy-start(f32[3,3,1024]{2,1,0:T(4,128)} %refs_12_.1) | copy-start | bytes 110596
  56.2 5.7 %collective-permute-start.7 = (bf16[432,128]{1,0:T(8,128)(2,1)S(1)}, bf16[432,128]{1,0:T(8,128)(2,1)S(1)}, u32[]{:S(2)}, u32[]{:S(2)}) collective-permute-start(bf16[432,128]{1,0:T(8,128)(2,1)S(1)} %get-tuple-element.39), channel_id=1, source_target_pairs={{0,16},{4,20},{8,24},{12,28},{16,0},{20,4},{24,8},{28,12},{1,17},{... | collective-permute-start | bytes 331784 | tf_op jit(solution)/shard_map/ppermute | solution.py:37
  57.6 5.4 %collective-permute-start.8 = (bf16[432,128]{1,0:T(8,128)(2,1)S(1)}, bf16[432,128]{1,0:T(8,128)(2,1)S(1)}, u32[]{:S(2)}, u32[]{:S(2)}) collective-permute-start(bf16[432,128]{1,0:T(8,128)(2,1)S(1)} %get-tuple-element.40), channel_id=1, source_target_pairs={{0,8},{4,12},{8,0},{12,4},{16,24},{20,28},{24,16},{28,20},{1,9},{5... | collective-permute-start | bytes 331784 | tf_op jit(solution)/shard_map/ppermute | solution.py:37
  58.9 7.2 %collective-permute-start.9 = (bf16[432,128]{1,0:T(8,128)(2,1)S(1)}, bf16[432,128]{1,0:T(8,128)(2,1)S(1)}, u32[]{:S(2)}, u32[]{:S(2)}) collective-permute-start(bf16[432,128]{1,0:T(8,128)(2,1)S(1)} %get-tuple-element.41), channel_id=1, source_target_pairs={{0,24},{4,28},{8,16},{12,20},{16,8},{20,12},{24,0},{28,4},{1,25},{... | collective-permute-start | bytes 331784 | tf_op jit(solution)/shard_map/ppermute | solution.py:37
  59.8 7.8 %collective-permute-start.10 = (bf16[432,128]{1,0:T(8,128)(2,1)S(1)}, bf16[432,128]{1,0:T(8,128)(2,1)S(1)}, u32[]{:S(2)}, u32[]{:S(2)}) collective-permute-start(bf16[432,128]{1,0:T(8,128)(2,1)S(1)} %get-tuple-element.42), channel_id=1, source_target_pairs={{0,28},{4,24},{8,20},{12,16},{16,12},{20,8},{24,4},{28,0},{1,29},{... | collective-permute-start | bytes 331784 | tf_op jit(solution)/shard_map/ppermute | solution.py:37
  60.7 9.5 %collective-permute-start.11 = (bf16[432,128]{1,0:T(8,128)(2,1)S(1)}, bf16[432,128]{1,0:T(8,128)(2,1)S(1)}, u32[]{:S(2)}, u32[]{:S(2)}) collective-permute-start(bf16[432,128]{1,0:T(8,128)(2,1)S(1)} %get-tuple-element.43), channel_id=1, source_target_pairs={{0,20},{4,16},{8,28},{12,24},{16,4},{20,0},{24,12},{28,8},{1,21},{... | collective-permute-start | bytes 331784 | tf_op jit(solution)/shard_map/ppermute | solution.py:37
  62.0 8.2 %collective-permute-start.12 = (bf16[432,128]{1,0:T(8,128)(2,1)S(1)}, bf16[432,128]{1,0:T(8,128)(2,1)S(1)}, u32[]{:S(2)}, u32[]{:S(2)}) collective-permute-start(bf16[432,128]{1,0:T(8,128)(2,1)S(1)} %get-tuple-element.44), channel_id=1, source_target_pairs={{0,12},{4,8},{8,4},{12,0},{16,28},{20,24},{24,20},{28,16},{1,13},{... | collective-permute-start | bytes 331784 | tf_op jit(solution)/shard_map/ppermute | solution.py:37
  63.1 7.1 %collective-permute-start.13 = (bf16[432,128]{1,0:T(8,128)(2,1)S(1)}, bf16[432,128]{1,0:T(8,128)(2,1)S(1)}, u32[]{:S(2)}, u32[]{:S(2)}) collective-permute-start(bf16[432,128]{1,0:T(8,128)(2,1)S(1)} %get-tuple-element.45), channel_id=1, source_target_pairs={{0,4},{4,0},{8,12},{12,8},{16,20},{20,16},{24,28},{28,24},{1,5},{5... | collective-permute-start | bytes 331784 | tf_op jit(solution)/shard_map/ppermute | solution.py:37

commit v8 on v5

--- a/solution.py
+++ b/solution.py
@@ -17,7 +17,7 @@
 PAD = 8
 CHUNK = 32
 RIM = 2
-PIECES = 3
+PIECES = 2
 MIB = 1024 * 1024
 VMEM_LIMIT = 24 * MIB
 
@@ -25,7 +25,7 @@
 def partners(peers):
     def rank(step):
         links = (step >> 1).bit_count()
-        return (links == 0, links == 1 and step & 1, links, step & 1, -step)
+        return (-links, step & 1, -step)
 
     return [0] + sorted(range(1, peers), key=rank)
 
@@ -46,22 +46,48 @@
     return pl.ds(pl.multiple_of(place * LANES, LANES), LANES)
 
 
-def pack_kernel(count, *refs):
-    sources, packed = refs[:count], refs[count:]
+def pack_kernel(count, peers, *refs):
+    sources, packed = refs[:count], refs[count : count + peers]
+    held, blocks = refs[count + peers : 2 * count + peers], refs[2 * count + peers]
+    in_sems, out_sems = refs[2 * count + peers + 1 :]
     tokens = sources[0].shape[0]
     me = lax.axis_index("ctx")
-    for step, target in zip(partners(len(packed)), packed):
-        for at, source in enumerate(sources):
-            target[at * tokens : (at + 1) * tokens, :] = source[:, lanes_of(me ^ step)].astype(BF16)
+    arriving = [
+        pltpu.make_async_copy(source, target, in_sems.at[at])
+        for at, (source, target) in enumerate(zip(sources, held))
+    ]
+    for copy in arriving:
+        copy.start()
+    leaving = []
+    for at, source in enumerate(held):
+        arriving[at].wait()
+        rows = pl.ds(at * tokens, tokens)
+        for slot, step in enumerate(partners(peers)):
+            blocks[slot, rows, :] = source[:, lanes_of(me ^ step)].astype(BF16)
+            leaving.append(
+                pltpu.make_async_copy(
+                    blocks.at[slot, rows, :], packed[slot].at[rows, :], out_sems.at[slot, at]
+                )
+            )
+            leaving[-1].start()
+    for copy in leaving:
+        copy.wait()
 
 
 def pack(arrays, peers):
     tokens = arrays[0].shape[0]
+    count = len(arrays)
     return pl.pallas_call(
-        functools.partial(pack_kernel, len(arrays)),
-        in_specs=in_vmem(len(arrays)),
-        out_specs=in_vmem(peers),
-        out_shape=[jax.ShapeDtypeStruct((len(arrays) * tokens, LANES), BF16)] * peers,
+        functools.partial(pack_kernel, count, peers),
+        in_specs=[pl.BlockSpec(memory_space=pl.ANY)] * count,
+        out_specs=[pl.BlockSpec(memory_space=pl.ANY)] * peers,
+        out_shape=[jax.ShapeDtypeStruct((count * tokens, LANES), BF16)] * peers,
+        scratch_shapes=[
+            *[pltpu.VMEM(array.shape, array.dtype) for array in arrays],
+            pltpu.VMEM((peers, count * tokens, LANES), BF16),
+            pltpu.SemaphoreType.DMA((count,)),
+            pltpu.SemaphoreType.DMA((peers, count)),
+        ],
         cost_estimate=pl.CostEstimate(flops=0, bytes_accessed=8 * MIB, transcendentals=0),
         name="pack_inputs",
     )(*arrays)
@@ -178,7 +204,7 @@
 
 def extra_rows(short_weights):
     sums = PIECES * short_weights.shape[0] * short_weights.shape[1]
-    return sums, -(-(sums + 8 * RIM) // TILE) * TILE
+    return sums, -(-(sums + 6 * RIM) // TILE) * TILE
 
 
 def channel_kernel(tokens, peers, grad_scale, *refs):
@@ -207,6 +233,8 @@
     own = lanes_of(me)
     for ref in (query, key, value, cot, conv, conv_grad):
         clear_ends(ref)
+    for ref in (key_short, value_short):
+        ref[:, size:, :] = jnp.zeros((PHASES, PAD, LANES), F32)
     for step, source in zip(partners(peers), arrived):
         start = (me ^ step) * tokens
         inner = pl.ds(pl.multiple_of(PAD + start, PAD), tokens)
@@ -318,9 +346,12 @@
         for ref in (query, key, value):
             extra[at : at + RIM, :] = ref[before, :][PAD - RIM :]
             at += RIM
-        for ref in (cot, conv, conv_grad, key, value):
-            extra[at : at + RIM, :] = ref[after, :][:RIM]
+        row = pl.ds(pl.multiple_of((start + tokens) // PHASES, PAD), PAD)
+        extra[at : at + RIM, :] = (cot[after, :] * conv[after, :])[:RIM]
+        for short in (value_short, key_short):
             at += RIM
+            shorts = jnp.concatenate([short[r, row, :][:1] for r in range(RIM)], axis=0)
+            extra[at : at + RIM, :] = conv_grad[after, :][:RIM] * shorts
         target[3 * tokens :, :] = extra[...].astype(BF16)
 
 
@@ -331,7 +362,7 @@
     extra = extra_rows(short_weights)[1]
     padded = pltpu.VMEM((seq_len + 2 * PAD, LANES), F32)
     plain = pltpu.VMEM((seq_len, LANES), F32)
-    phases = pltpu.VMEM((PHASES, size, LANES), F32)
+    phases = pltpu.VMEM((PHASES, size + PAD, LANES), F32)
     return pl.pallas_call(
         functools.partial(channel_kernel, tokens, peers, 1.0 / math.sqrt(seq_len)),
         in_specs=in_vmem(peers + 3),
@@ -369,22 +400,22 @@
         def rim(at):
             return extra[sum_rows + at * RIM : sum_rows + (at + 1) * RIM]
 
-        def short(array, signal, after, rows):
+        def short(array, signal):
             longer[array, PAD - RIM : PAD, :] = rim(array)
-            longer[array, PAD : PAD + tokens, :] = signal[:, lanes].astype(F32)
-            if after is not None:
-                longer[array, PAD + tokens : PAD + tokens + RIM, :] = rim(after)
-            summed = weights[array, 0:1, lanes] * longer[array, PAD : PAD + rows, :]
+            longer[array, PAD :, :] = signal[:, lanes].astype(F32)
+            summed = weights[array, 0:1, lanes] * longer[array, PAD:, :]
             for tap in range(1, tap_count):
                 summed = (
                     summed
                     + weights[array, tap : tap + 1, lanes]
-                    * longer[array, PAD - tap : PAD - tap + rows, :]
+                    * longer[array, PAD - tap : PAD - tap + tokens, :]
                 )
             return summed
 
-        def taps_back(array, target):
-            summed = weights[array, 0:1, lanes] * pre[array, :tokens, :]
+        def taps_back(array, grad, target):
+            pre[array, :tokens, :] = grad
+            pre[array, tokens : tokens + RIM, :] = rim(3 + array)
+            summed = weights[array, 0:1, lanes] * grad
             for tap in range(1, tap_count):
                 summed = (
                     summed
@@ -393,18 +424,11 @@
             target[:, lanes] = summed.astype(BF16)
 
         conv = source[:tokens, :].astype(F32)
-        gated[:, lanes] = (short(0, query, None, tokens) * conv).astype(BF16)
-        pre[0, :tokens, :] = cot[:, lanes].astype(F32) * conv
-        pre[0, tokens : tokens + RIM, :] = rim(3) * rim(4)
-        taps_back(0, query_grad)
-        key_short = short(1, key, 6, tokens + PAD)
-        value_short = short(2, value, 7, tokens + PAD)
         conv_grad = source[tokens : 2 * tokens, :].astype(F32)
-        for array, other in ((1, value_short), (2, key_short)):
-            pre[array, :tokens, :] = conv_grad * other[:tokens]
-            pre[array, tokens : tokens + RIM, :] = rim(5) * other[tokens : tokens + RIM]
-        taps_back(1, key_grad)
-        taps_back(2, value_grad)
+        gated[:, lanes] = (short(0, query) * conv).astype(BF16)
+        taps_back(0, cot[:, lanes].astype(F32) * conv, query_grad)
+        taps_back(1, conv_grad * short(2, value), key_grad)
+        taps_back(2, conv_grad * short(1, key), value_grad)
         filter_grad[:, lanes] = source[2 * tokens : 3 * tokens, :].astype(F32)
         whole = extra[:count]
         for piece in range(1, PIECES):
@@ -428,7 +452,7 @@
             jax.ShapeDtypeStruct(short_weights.shape, F32),
         ],
         scratch_shapes=[
-            pltpu.VMEM((3, tokens + 2 * PAD, LANES), F32),
+            pltpu.VMEM((3, tokens + PAD, LANES), F32),
             pltpu.VMEM((3, tokens + PAD, LANES), F32),
         ],
         compiler_params=pltpu.CompilerParams(vmem_limit_bytes=VMEM_LIMIT),

time: 42 us -> 40.7 us (0.969)
  starting transfers between devices: 14.2 us -> 13.6 us
  waiting for transfers between devices: 12.8 us -> 12.3 us
    ppermute x14, starting transfers between devices: 14.2 us -> 13.6 us  [exchange(): lax.ppermute(block, 'ctx', [(i, i ^ step) for i in range(peers)])]
    ppermute x14, waiting for transfers between devices: 12.8 us -> 12.3 us  [exchange(): lax.ppermute(block, 'ctx', [(i, i ^ step) for i in range(peers)])]
  transfers between devices with their start and end apart: 14 -> 14, of which waited for: 9 -> 8; matrix products, arithmetic and copies ran while one was open for 0% -> 0% of each run, Pallas kernels for 1% -> 1%
where the time goes in v8:
time: 40.7 us; the launch traced here: 40.4 us
  starting transfers between devices  13.6 us (33%)
  waiting for transfers between devices  12.3 us (30%)
  Pallas kernels  8.83 us (22%)
  local copies, waits for them, and re-layouts  4.92 us (12%)
  between operations  0.75 us (2%)
    ppermute x14, starting transfers between devices, exchange(): lax.ppermute(block, 'ctx', [(i, i ^ step) for i in range(peers)])  13.6 us
    ppermute x14, waiting for transfers between devices, exchange(): lax.ppermute(block, 'ctx', [(i, i ^ step) for i in range(peers)])  12.3 us
    unnamed x18, local copies, waits for them, and re-layouts  4.92 us
    pallas_call x1, Pallas kernels, channel_step(): pl.pallas_call(functools.partial(channel_kernel, tokens, peers, 1.0 / mat...  3.69 us
    pallas_call x1, Pallas kernels, pack(): pl.pallas_call(functools.partial(pack_kernel, count, peers), in_specs=[pl...  2.45 us
    pallas_call x1, Pallas kernels, token_step(): pl.pallas_call(functools.partial(token_kernel, peers, extra_rows(short_we...  2.12 us
  transfers between devices with their start and end apart: 14, of which 8 were waited for; matrix products, arithmetic and copies ran while one was open for 0% of the time, Pallas kernels for 1%

profile of v8, /device:TPU:0, one launch (start us, length us, event | category | flops | bytes accessed | tf_op | source)
XLA Modules:
  0.0 40.4 jit_solution(14456492305491281916)
XLA Ops:
  0.6 2.5 %pack_inputs.1 = (bf16[640,128]{1,0:T(8,128)(2,1)}, bf16[640,128]{1,0:T(8,128)(2,1)}, bf16[640,128]{1,0:T(8,128)(2,1)}, bf16[640,128]{1,0:T(8,128)(2,1)}, bf16[6...) custom-call(bf16[128,1024]{1,0:T(8,128)(2,1)} %refs_8_.1, ...), custom_call_target="tpu_custom_call" | custom-call | bytes 8388608 | tf_op jit(solution)/shard_map/pack_inputs/pallas_call | solution.py:80
  3.1 4.0 %collective-permute-start = (bf16[640,128]{1,0:T(8,128)(2,1)}, bf16[640,128]{1,0:T(8,128)(2,1)S(1)}, u32[]{:S(2)}, u32[]{:S(2)}) collective-permute-start(bf16[640,128]{1,0:T(8,128)(2,1)} %get-tuple-element.27), channel_id=1, source_target_pairs={{0,24},{4,28},{8,16},{12,20},{16,8},{20,12},{24,0},{28,4},{1,25},{... | collective-permute-start | bytes 491528 | tf_op jit(solution)/shard_map/ppermute | solution.py:37
  7.1 0.0 collective-permute-start.1
  7.1 1.2 %collective-permute-start.2 = (bf16[640,128]{1,0:T(8,128)(2,1)}, bf16[640,128]{1,0:T(8,128)(2,1)S(1)}, u32[]{:S(2)}, u32[]{:S(2)}) collective-permute-start(bf16[640,128]{1,0:T(8,128)(2,1)} %get-tuple-element.30), channel_id=1, source_target_pairs={{0,16},{4,20},{8,24},{12,28},{16,0},{20,4},{24,8},{28,12},{1,17},{... | collective-permute-start | bytes 491528 | tf_op jit(solution)/shard_map/ppermute | solution.py:37
  8.2 1.5 %collective-permute-start.3 = (bf16[640,128]{1,0:T(8,128)(2,1)}, bf16[640,128]{1,0:T(8,128)(2,1)S(1)}, u32[]{:S(2)}, u32[]{:S(2)}) collective-permute-start(bf16[640,128]{1,0:T(8,128)(2,1)} %get-tuple-element.31), channel_id=1, source_target_pairs={{0,8},{4,12},{8,0},{12,4},{16,24},{20,28},{24,16},{28,20},{1,9},{5... | collective-permute-start | bytes 491528 | tf_op jit(solution)/shard_map/ppermute | solution.py:37
  9.7 0.5 %collective-permute-start.4 = (bf16[640,128]{1,0:T(8,128)(2,1)}, bf16[640,128]{1,0:T(8,128)(2,1)S(1)}, u32[]{:S(2)}, u32[]{:S(2)}) collective-permute-start(bf16[640,128]{1,0:T(8,128)(2,1)} %get-tuple-element.32), channel_id=1, source_target_pairs={{0,20},{4,16},{8,28},{12,24},{16,4},{20,0},{24,12},{28,8},{1,21},{... | collective-permute-start | bytes 491528 | tf_op jit(solution)/shard_map/ppermute | solution.py:37
  10.2 1.8 %collective-permute-done.refs_4_.refs_1_ = bf16[640,128]{1,0:T(8,128)(2,1)S(1)} collective-permute-done((bf16[640,128]{1,0:T(8,128)(2,1)}, bf16[640,128]{1,0:T(8,128)(2,1)S(1)}, u32[]{:S(2)}, u32[]{:S(2)}) %collective-permute-start) | collective-permute-done | bytes 163872 | tf_op jit(solution)/shard_map/ppermute | solution.py:37
  12.0 3.5 %collective-permute-done.1.refs_2_ = bf16[640,128]{1,0:T(8,128)(2,1)S(1)} collective-permute-done((bf16[640,128]{1,0:T(8,128)(2,1)}, bf16[640,128]{1,0:T(8,128)(2,1)S(1)}, u32[]{:S(2)}, u32[]{:S(2)}) %collective-permute-start.1) | collective-permute-done | bytes 163872 | tf_op jit(solution)/shard_map/ppermute | solution.py:37
  15.5 1.6 %copy-done = bf16[4,2,256,512]{3,2,1,0:T(8,128)(2,1)S(1)} copy-done((bf16[4,2,256,512]{3,2,1,0:T(8,128)(2,1)S(1)}, bf16[4,2,256,512]{3,2,1,0:T(8,128)(2,1)}, u32[]{:S(2)}) %copy-start) | copy-done | bytes 2097176
  17.1 1.6 %copy-done.1 = bf16[4,2,512,256]{3,2,1,0:T(8,128)(2,1)S(1)} copy-done((bf16[4,2,512,256]{3,2,1,0:T(8,128)(2,1)S(1)}, bf16[4,2,512,256]{3,2,1,0:T(8,128)(2,1)}, u32[]{:S(2)}) %copy-start.1) | copy-done | bytes 2097176
  18.7 0.8 %copy-done.6 = f32[3,3,1024]{2,1,0:T(4,128)S(1)} copy-done((f32[3,3,1024]{2,1,0:T(4,128)S(1)}, f32[3,3,1024]{2,1,0:T(4,128)}, u32[]{:S(2)}) %copy-start.6) | copy-done | bytes 36888
  19.5 0.9 %copy-done.8 = bf16[640,128]{1,0:T(8,128)(2,1)S(1)} copy-done((bf16[640,128]{1,0:T(8,128)(2,1)S(1)}, bf16[640,128]{1,0:T(8,128)(2,1)}, u32[]{:S(2)}) %copy-start.8) | copy-done | bytes 163864
  20.4 0.6 %stage_tables.1 = (bf16[640,128]{1,0:T(8,128)(2,1)S(1)}, f32[3,3,1024]{2,1,0:T(4,128)S(1)}, bf16[4,2,512,256]{3,2,1,0:T(8,128)(2,1)S(1)}, bf16[4,2,256,512]{3,2,1,0:T(8,128)(2,1)S(1)}) custom-call(bf16[640,128]{1,0:T(8,128)(2,1)S(1)} %copy-done.8, f32[3,3,1024]{2,1,0:T(4,128)S(1)} %copy-done.6, bf16[4,2,512,256]{3,2,1,0:T(8,128)(2,1)S(1)} %copy-done.1, ...), custom_call_target="tpu_custom_call" | custom-call | bytes 8388608 | tf_op jit(solution)/shard_map/stage_tables/pallas_call | solution.py:193
  21.0 0.9 %collective-permute-done.4.refs_5_ = bf16[640,128]{1,0:T(8,128)(2,1)S(1)} collective-permute-done((bf16[640,128]{1,0:T(8,128)(2,1)}, bf16[640,128]{1,0:T(8,128)(2,1)S(1)}, u32[]{:S(2)}, u32[]{:S(2)}) %collective-permute-start.4) | collective-permute-done | bytes 163872 | tf_op jit(solution)/shard_map/ppermute | solution.py:37
  21.9 0.0 copy-start.3
  22.0 0.0 copy-start.4
  22.0 0.0 copy-start.5
  22.0 0.0 copy-start.7
  22.0 3.7 %channel_operator.1 = (bf16[416,128]{1,0:T(8,128)(2,1)S(1)}, bf16[416,128]{1,0:T(8,128)(2,1)S(1)}, bf16[416,128]{1,0:T(8,128)(2,1)S(1)}, bf16[416,128]{1,0:T(8,1...) custom-call(bf16[640,128]{1,0:T(8,128)(2,1)S(1)} %get-tuple-element., ...), custom_call_target="tpu_custom_call" | custom-call | tf_op jit(solution)/shard_map/channel_operator/pallas_call | solution.py:366
  25.7 2.8 %collective-permute-start.7 = (bf16[416,128]{1,0:T(8,128)(2,1)S(1)}, bf16[416,128]{1,0:T(8,128)(2,1)S(1)}, u32[]{:S(2)}, u32[]{:S(2)}) collective-permute-start(bf16[416,128]{1,0:T(8,128)(2,1)S(1)} %get-tuple-element.39), channel_id=1, source_target_pairs={{0,24},{4,28},{8,16},{12,20},{16,8},{20,12},{24,0},{28,4},{1,25},{... | collective-permute-start | bytes 319496 | tf_op jit(solution)/shard_map/ppermute | solution.py:37
  28.5 1.4 %collective-permute-start.9 = (bf16[416,128]{1,0:T(8,128)(2,1)S(1)}, bf16[416,128]{1,0:T(8,128)(2,1)S(1)}, u32[]{:S(2)}, u32[]{:S(2)}) collective-permute-start(bf16[416,128]{1,0:T(8,128)(2,1)S(1)} %get-tuple-element.41), channel_id=1, source_target_pairs={{0,16},{4,20},{8,24},{12,28},{16,0},{20,4},{24,8},{28,12},{1,17},{... | collective-permute-start | bytes 319496 | tf_op jit(solution)/shard_map/ppermute | solution.py:37
  29.9 1.5 %collective-permute-start.10 = (bf16[416,128]{1,0:T(8,128)(2,1)S(1)}, bf16[416,128]{1,0:T(8,128)(2,1)S(1)}, u32[]{:S(2)}, u32[]{:S(2)}) collective-permute-start(bf16[416,128]{1,0:T(8,128)(2,1)S(1)} %get-tuple-element.42), channel_id=1, source_target_pairs={{0,8},{4,12},{8,0},{12,4},{16,24},{20,28},{24,16},{28,20},{1,9},{5... | collective-permute-start | bytes 319496 | tf_op jit(solution)/shard_map/ppermute | solution.py:37
  31.4 0.3 collective-permute-start.11
  31.6 0.2 collective-permute-done.7.refs_1_
  31.8 0.5 %collective-permute-start.12 = (bf16[416,128]{1,0:T(8,128)(2,1)S(1)}, bf16[416,128]{1,0:T(8,128)(2,1)S(1)}, u32[]{:S(2)}, u32[]{:S(2)}) collective-permute-start(bf16[416,128]{1,0:T(8,128)(2,1)S(1)} %get-tuple-element.44), channel_id=1, source_target_pairs={{0,12},{4,8},{8,4},{12,0},{16,28},{20,24},{24,20},{28,16},{1,13},{... | collective-permute-start | bytes 319496 | tf_op jit(solution)/shard_map/ppermute | solution.py:37
  32.3 2.5 %collective-permute-done.8.refs_2_ = bf16[416,128]{1,0:T(8,128)(2,1)S(1)} collective-permute-done((bf16[416,128]{1,0:T(8,128)(2,1)S(1)}, bf16[416,128]{1,0:T(8,128)(2,1)S(1)}, u32[]{:S(2)}, u32[]{:S(2)}) %collective-permute-start.8) | collective-permute-done | bytes 106528 | tf_op jit(solution)/shard_map/ppermute | solution.py:37
  34.7 0.1 collective-permute-start.13
  34.8 1.8 %collective-permute-done.9.refs_3_ = bf16[416,128]{1,0:T(8,128)(2,1)S(1)} collective-permute-done((bf16[416,128]{1,0:T(8,128)(2,1)S(1)}, bf16[416,128]{1,0:T(8,128)(2,1)S(1)}, u32[]{:S(2)}, u32[]{:S(2)}) %collective-permute-start.9) | collective-permute-done | bytes 106528 | tf_op jit(solution)/shard_map/ppermute | solution.py:37
  36.6 0.6 %collective-permute-done.10.refs_4_ = bf16[416,128]{1,0:T(8,128)(2,1)S(1)} collective-permute-done((bf16[416,128]{1,0:T(8,128)(2,1)S(1)}, bf16[416,128]{1,0:T(8,128)(2,1)S(1)}, u32[]{:S(2)}, u32[]{:S(2)}) %collective-permute-start.10) | collective-permute-done | bytes 106528 | tf_op jit(solution)/shard_map/ppermute | solution.py:37
  37.1 1.1 %collective-permute-done.11.refs_5_ = bf16[416,128]{1,0:T(8,128)(2,1)S(1)} collective-permute-done((bf16[416,128]{1,0:T(8,128)(2,1)S(1)}, bf16[416,128]{1,0:T(8,128)(2,1)S(1)}, u32[]{:S(2)}, u32[]{:S(2)}) %collective-permute-start.11) | collective-permute-done | bytes 106528 | tf_op jit(solution)/shard_map/ppermute | solution.py:37
  38.2 0.0 collective-permute-done.12.refs_6_
  38.3 2.1 %token_outputs.1 = (bf16[128,1024]{1,0:T(8,128)(2,1)}, bf16[128,1024]{1,0:T(8,128)(2,1)}, bf16[128,1024]{1,0:T(8,128)(2,1)}, bf16[128,1024]{1,0:T(8,128)(2,1)}, ...) custom-call(bf16[416,128]{1,0:T(8,128)(2,1)S(1)} %get-tuple-element.38.refs_0_, ...), custom_call_target="tpu_custom_call" | custom-call | tf_op jit(solution)/shard_map/token_outputs/pallas_call | solution.py:445
  (18 shorter events, 0.0 us)
Async XLA Ops:
  3.1 8.9 %collective-permute-start = (bf16[640,128]{1,0:T(8,128)(2,1)}, bf16[640,128]{1,0:T(8,128)(2,1)S(1)}, u32[]{:S(2)}, u32[]{:S(2)}) collective-permute-start(bf16[640,128]{1,0:T(8,128)(2,1)} %get-tuple-element.27), channel_id=1, source_target_pairs={{0,24},{4,28},{8,16},{12,20},{16,8},{20,12},{24,0},{28,4},{1,25},{... | collective-permute-start | bytes 491528 | tf_op jit(solution)/shard_map/ppermute | solution.py:37
  7.1 8.5 %collective-permute-start.1 = (bf16[640,128]{1,0:T(8,128)(2,1)}, bf16[640,128]{1,0:T(8,128)(2,1)S(1)}, u32[]{:S(2)}, u32[]{:S(2)}) collective-permute-start(bf16[640,128]{1,0:T(8,128)(2,1)} %get-tuple-element.29), channel_id=1, source_target_pairs={{0,28},{4,24},{8,20},{12,16},{16,12},{20,8},{24,4},{28,0},{1,29},{... | collective-permute-start | bytes 491528 | tf_op jit(solution)/shard_map/ppermute | solution.py:37
  7.1 13.9 %collective-permute-start.2 = (bf16[640,128]{1,0:T(8,128)(2,1)}, bf16[640,128]{1,0:T(8,128)(2,1)S(1)}, u32[]{:S(2)}, u32[]{:S(2)}) collective-permute-start(bf16[640,128]{1,0:T(8,128)(2,1)} %get-tuple-element.30), channel_id=1, source_target_pairs={{0,16},{4,20},{8,24},{12,28},{16,0},{20,4},{24,8},{28,12},{1,17},{... | collective-permute-start | bytes 491528 | tf_op jit(solution)/shard_map/ppermute | solution.py:37
  8.2 12.8 %collective-permute-start.3 = (bf16[640,128]{1,0:T(8,128)(2,1)}, bf16[640,128]{1,0:T(8,128)(2,1)S(1)}, u32[]{:S(2)}, u32[]{:S(2)}) collective-permute-start(bf16[640,128]{1,0:T(8,128)(2,1)} %get-tuple-element.31), channel_id=1, source_target_pairs={{0,8},{4,12},{8,0},{12,4},{16,24},{20,28},{24,16},{28,20},{1,9},{5... | collective-permute-start | bytes 491528 | tf_op jit(solution)/shard_map/ppermute | solution.py:37
  9.7 12.2 %collective-permute-start.4 = (bf16[640,128]{1,0:T(8,128)(2,1)}, bf16[640,128]{1,0:T(8,128)(2,1)S(1)}, u32[]{:S(2)}, u32[]{:S(2)}) collective-permute-start(bf16[640,128]{1,0:T(8,128)(2,1)} %get-tuple-element.32), channel_id=1, source_target_pairs={{0,20},{4,16},{8,28},{12,24},{16,4},{20,0},{24,12},{28,8},{1,21},{... | collective-permute-start | bytes 491528 | tf_op jit(solution)/shard_map/ppermute | solution.py:37
  12.0 9.9 %collective-permute-start.5 = (bf16[640,128]{1,0:T(8,128)(2,1)}, bf16[640,128]{1,0:T(8,128)(2,1)S(1)}, u32[]{:S(2)}, u32[]{:S(2)}) collective-permute-start(bf16[640,128]{1,0:T(8,128)(2,1)} %get-tuple-element.33), channel_id=1, source_target_pairs={{0,12},{4,8},{8,4},{12,0},{16,28},{20,24},{24,20},{28,16},{1,13},{... | collective-permute-start | bytes 491528 | tf_op jit(solution)/shard_map/ppermute | solution.py:37
  15.5 6.4 %collective-permute-start.6 = (bf16[640,128]{1,0:T(8,128)(2,1)}, bf16[640,128]{1,0:T(8,128)(2,1)S(1)}, u32[]{:S(2)}, u32[]{:S(2)}) collective-permute-start(bf16[640,128]{1,0:T(8,128)(2,1)} %get-tuple-element.34), channel_id=1, source_target_pairs={{0,4},{4,0},{8,12},{12,8},{16,20},{20,16},{24,28},{28,24},{1,5},{5... | collective-permute-start | bytes 491528 | tf_op jit(solution)/shard_map/ppermute | solution.py:37
  15.5 1.6 %copy-start = (bf16[4,2,256,512]{3,2,1,0:T(8,128)(2,1)S(1)}, bf16[4,2,256,512]{3,2,1,0:T(8,128)(2,1)}, u32[]{:S(2)}) copy-start(bf16[4,2,256,512]{3,2,1,0:T(8,128)(2,1)} %constant.5.clone.refs_3_) | copy-start | bytes 6291460
  17.1 1.6 %copy-start.1 = (bf16[4,2,512,256]{3,2,1,0:T(8,128)(2,1)S(1)}, bf16[4,2,512,256]{3,2,1,0:T(8,128)(2,1)}, u32[]{:S(2)}) copy-start(bf16[4,2,512,256]{3,2,1,0:T(8,128)(2,1)} %constant.4.clone.refs_2_) | copy-start | bytes 6291460
  18.7 0.8 %copy-start.6 = (f32[3,3,1024]{2,1,0:T(4,128)S(1)}, f32[3,3,1024]{2,1,0:T(4,128)}, u32[]{:S(2)}) copy-start(f32[3,3,1024]{2,1,0:T(4,128)} %refs_12_.1) | copy-start | bytes 110596
  19.5 0.9 %copy-start.8 = (bf16[640,128]{1,0:T(8,128)(2,1)S(1)}, bf16[640,128]{1,0:T(8,128)(2,1)}, u32[]{:S(2)}) copy-start(bf16[640,128]{1,0:T(8,128)(2,1)} %get-tuple-element.26.refs_0_) | copy-start | bytes 491524
  21.9 16.3 %copy-start.2 = (bf16[128,1024]{1,0:T(8,128)(2,1)S(1)}, bf16[128,1024]{1,0:T(8,128)(2,1)}, u32[]{:S(2)}) copy-start(bf16[128,1024]{1,0:T(8,128)(2,1)} %refs_8_.1) | copy-start | bytes 786436
  21.9 16.3 %copy-start.3 = (bf16[128,1024]{1,0:T(8,128)(2,1)S(1)}, bf16[128,1024]{1,0:T(8,128)(2,1)}, u32[]{:S(2)}) copy-start(bf16[128,1024]{1,0:T(8,128)(2,1)} %refs_9_.1) | copy-start | bytes 786436
  22.0 16.3 %copy-start.4 = (bf16[128,1024]{1,0:T(8,128)(2,1)S(1)}, bf16[128,1024]{1,0:T(8,128)(2,1)}, u32[]{:S(2)}) copy-start(bf16[128,1024]{1,0:T(8,128)(2,1)} %refs_10_.1) | copy-start | bytes 786436
  22.0 16.3 %copy-start.5 = (bf16[128,1024]{1,0:T(8,128)(2,1)S(1)}, bf16[128,1024]{1,0:T(8,128)(2,1)}, u32[]{:S(2)}) copy-start(bf16[128,1024]{1,0:T(8,128)(2,1)} %refs_11_.1) | copy-start | bytes 786436
  22.0 16.3 %copy-start.7 = (f32[3,3,1024]{2,1,0:T(4,128)S(1)}, f32[3,3,1024]{2,1,0:T(4,128)}, u32[]{:S(2)}) copy-start(f32[3,3,1024]{2,1,0:T(4,128)} %refs_12_.1) | copy-start | bytes 110596
  25.7 6.1 %collective-permute-start.7 = (bf16[416,128]{1,0:T(8,128)(2,1)S(1)}, bf16[416,128]{1,0:T(8,128)(2,1)S(1)}, u32[]{:S(2)}, u32[]{:S(2)}) collective-permute-start(bf16[416,128]{1,0:T(8,128)(2,1)S(1)} %get-tuple-element.39), channel_id=1, source_target_pairs={{0,24},{4,28},{8,16},{12,20},{16,8},{20,12},{24,0},{28,4},{1,25},{... | collective-permute-start | bytes 319496 | tf_op jit(solution)/shard_map/ppermute | solution.py:37
  28.5 6.3 %collective-permute-start.8 = (bf16[416,128]{1,0:T(8,128)(2,1)S(1)}, bf16[416,128]{1,0:T(8,128)(2,1)S(1)}, u32[]{:S(2)}, u32[]{:S(2)}) collective-permute-start(bf16[416,128]{1,0:T(8,128)(2,1)S(1)} %get-tuple-element.40), channel_id=1, source_target_pairs={{0,28},{4,24},{8,20},{12,16},{16,12},{20,8},{24,4},{28,0},{1,29},{... | collective-permute-start | bytes 319496 | tf_op jit(solution)/shard_map/ppermute | solution.py:37
  28.5 8.1 %collective-permute-start.9 = (bf16[416,128]{1,0:T(8,128)(2,1)S(1)}, bf16[416,128]{1,0:T(8,128)(2,1)S(1)}, u32[]{:S(2)}, u32[]{:S(2)}) collective-permute-start(bf16[416,128]{1,0:T(8,128)(2,1)S(1)} %get-tuple-element.41), channel_id=1, source_target_pairs={{0,16},{4,20},{8,24},{12,28},{16,0},{20,4},{24,8},{28,12},{1,17},{... | collective-permute-start | bytes 319496 | tf_op jit(solution)/shard_map/ppermute | solution.py:37
  29.9 7.3 %collective-permute-start.10 = (bf16[416,128]{1,0:T(8,128)(2,1)S(1)}, bf16[416,128]{1,0:T(8,128)(2,1)S(1)}, u32[]{:S(2)}, u32[]{:S(2)}) collective-permute-start(bf16[416,128]{1,0:T(8,128)(2,1)S(1)} %get-tuple-element.42), channel_id=1, source_target_pairs={{0,8},{4,12},{8,0},{12,4},{16,24},{20,28},{24,16},{28,20},{1,9},{5... | collective-permute-start | bytes 319496 | tf_op jit(solution)/shard_map/ppermute | solution.py:37
  31.4 6.8 %collective-permute-start.11 = (bf16[416,128]{1,0:T(8,128)(2,1)S(1)}, bf16[416,128]{1,0:T(8,128)(2,1)S(1)}, u32[]{:S(2)}, u32[]{:S(2)}) collective-permute-start(bf16[416,128]{1,0:T(8,128)(2,1)S(1)} %get-tuple-element.43), channel_id=1, source_target_pairs={{0,20},{4,16},{8,28},{12,24},{16,4},{20,0},{24,12},{28,8},{1,21},{... | collective-permute-start | bytes 319496 | tf_op jit(solution)/shard_map/ppermute | solution.py:37
  31.8 6.5 %collective-permute-start.12 = (bf16[416,128]{1,0:T(8,128)(2,1)S(1)}, bf16[416,128]{1,0:T(8,128)(2,1)S(1)}, u32[]{:S(2)}, u32[]{:S(2)}) collective-permute-start(bf16[416,128]{1,0:T(8,128)(2,1)S(1)} %get-tuple-element.44), channel_id=1, source_target_pairs={{0,12},{4,8},{8,4},{12,0},{16,28},{20,24},{24,20},{28,16},{1,13},{... | collective-permute-start | bytes 319496 | tf_op jit(solution)/shard_map/ppermute | solution.py:37
  34.7 3.5 %collective-permute-start.13 = (bf16[416,128]{1,0:T(8,128)(2,1)S(1)}, bf16[416,128]{1,0:T(8,128)(2,1)S(1)}, u32[]{:S(2)}, u32[]{:S(2)}) collective-permute-start(bf16[416,128]{1,0:T(8,128)(2,1)S(1)} %get-tuple-element.45), channel_id=1, source_target_pairs={{0,4},{4,0},{8,12},{12,8},{16,20},{20,16},{24,28},{28,24},{1,5},{5... | collective-permute-start | bytes 319496 | tf_op jit(solution)/shard_map/ppermute | solution.py:37

commit v9 on v8

--- a/solution.py
+++ b/solution.py
@@ -20,20 +20,25 @@
 PIECES = 2
 MIB = 1024 * 1024
 VMEM_LIMIT = 24 * MIB
-
-
-def partners(peers):
+PACK_VMEM = 60680 * 1024
+
+
+def partners(peers, diagonal_first):
     def rank(step):
-        links = (step >> 1).bit_count()
-        return (-links, step & 1, -step)
+        links, other_core = (step >> 1).bit_count(), step & 1
+        if links == 0:
+            return (4, 0, 0)
+        if links == 1:
+            return (3 if other_core else 1, 0, -step)
+        return (0 if diagonal_first else 2, other_core, -step)
 
     return [0] + sorted(range(1, peers), key=rank)
 
 
-def exchange(blocks):
+def exchange(blocks, steps):
     peers = len(blocks)
     got = [blocks[0]]
-    for step, block in list(zip(partners(peers), blocks))[1:]:
+    for step, block in list(zip(steps, blocks))[1:]:
         got.append(lax.ppermute(block, "ctx", [(i, i ^ step) for i in range(peers)]))
     return got
 
@@ -46,48 +51,37 @@
     return pl.ds(pl.multiple_of(place * LANES, LANES), LANES)
 
 
-def pack_kernel(count, peers, *refs):
-    sources, packed = refs[:count], refs[count : count + peers]
-    held, blocks = refs[count + peers : 2 * count + peers], refs[2 * count + peers]
-    in_sems, out_sems = refs[2 * count + peers + 1 :]
+def pack_kernel(count, steps, *refs):
+    sources, packed = refs[:count], refs[count : count + len(steps)]
+    held, sems = refs[count + len(steps) : -1], refs[-1]
     tokens = sources[0].shape[0]
     me = lax.axis_index("ctx")
     arriving = [
-        pltpu.make_async_copy(source, target, in_sems.at[at])
+        pltpu.make_async_copy(source, target, sems.at[at])
         for at, (source, target) in enumerate(zip(sources, held))
     ]
     for copy in arriving:
         copy.start()
-    leaving = []
     for at, source in enumerate(held):
         arriving[at].wait()
-        rows = pl.ds(at * tokens, tokens)
-        for slot, step in enumerate(partners(peers)):
-            blocks[slot, rows, :] = source[:, lanes_of(me ^ step)].astype(BF16)
-            leaving.append(
-                pltpu.make_async_copy(
-                    blocks.at[slot, rows, :], packed[slot].at[rows, :], out_sems.at[slot, at]
-                )
-            )
-            leaving[-1].start()
-    for copy in leaving:
-        copy.wait()
-
-
-def pack(arrays, peers):
+        rows = slice(at * tokens, (at + 1) * tokens)
+        for step, target in zip(steps, packed):
+            target[rows, :] = source[:, lanes_of(me ^ step)].astype(BF16)
+
+
+def pack(arrays, steps):
     tokens = arrays[0].shape[0]
     count = len(arrays)
     return pl.pallas_call(
-        functools.partial(pack_kernel, count, peers),
+        functools.partial(pack_kernel, count, steps),
         in_specs=[pl.BlockSpec(memory_space=pl.ANY)] * count,
-        out_specs=[pl.BlockSpec(memory_space=pl.ANY)] * peers,
-        out_shape=[jax.ShapeDtypeStruct((count * tokens, LANES), BF16)] * peers,
+        out_specs=in_vmem(len(steps)),
+        out_shape=[jax.ShapeDtypeStruct((count * tokens, LANES), BF16)] * len(steps),
         scratch_shapes=[
             *[pltpu.VMEM(array.shape, array.dtype) for array in arrays],
-            pltpu.VMEM((peers, count * tokens, LANES), BF16),
             pltpu.SemaphoreType.DMA((count,)),
-            pltpu.SemaphoreType.DMA((peers, count)),
         ],
+        compiler_params=pltpu.CompilerParams(vmem_limit_bytes=PACK_VMEM),
         cost_estimate=pl.CostEstimate(flops=0, bytes_accessed=8 * MIB, transcendentals=0),
         name="pack_inputs",
     )(*arrays)
@@ -207,7 +201,8 @@
     return sums, -(-(sums + 6 * RIM) // TILE) * TILE
 
 
-def channel_kernel(tokens, peers, grad_scale, *refs):
+def channel_kernel(tokens, heard, told, grad_scale, *refs):
+    peers = len(heard)
     arrived = refs[:peers]
     weights, forward, backward = refs[peers : peers + 3]
     out = refs[peers + 3 : 2 * peers + 3]
@@ -235,7 +230,7 @@
         clear_ends(ref)
     for ref in (key_short, value_short):
         ref[:, size:, :] = jnp.zeros((PHASES, PAD, LANES), F32)
-    for step, source in zip(partners(peers), arrived):
+    for step, source in zip(heard, arrived):
         start = (me ^ step) * tokens
         inner = pl.ds(pl.multiple_of(PAD + start, PAD), tokens)
         for at, ref in enumerate((query, key, value, cot)):
@@ -332,7 +327,7 @@
         rounded = rest.astype(BF16).astype(F32)
         extra[piece * len(sums) : (piece + 1) * len(sums), :] = rounded
         rest = rest - rounded
-    for step, target in zip(partners(peers), out):
+    for step, target in zip(told, out):
         start = (me ^ step) * tokens
         inner = pl.ds(pl.multiple_of(PAD + start, PAD), tokens)
         target[:tokens, :] = conv[inner, :].astype(BF16)
@@ -355,7 +350,7 @@
         target[3 * tokens :, :] = extra[...].astype(BF16)
 
 
-def channel_step(arrived, short_weights, tables, tokens):
+def channel_step(arrived, heard, told, short_weights, tables, tokens):
     peers = len(arrived)
     seq_len = peers * tokens
     size = seq_len // PHASES
@@ -364,7 +359,7 @@
     plain = pltpu.VMEM((seq_len, LANES), F32)
     phases = pltpu.VMEM((PHASES, size + PAD, LANES), F32)
     return pl.pallas_call(
-        functools.partial(channel_kernel, tokens, peers, 1.0 / math.sqrt(seq_len)),
+        functools.partial(channel_kernel, tokens, heard, told, 1.0 / math.sqrt(seq_len)),
         in_specs=in_vmem(peers + 3),
         out_specs=in_vmem(peers),
         out_shape=[jax.ShapeDtypeStruct((3 * tokens + extra, LANES), BF16)] * peers,
@@ -384,16 +379,20 @@
     )(*arrived, short_weights, *tables)
 
 
-def token_kernel(peers, sum_rows, *refs):
-    arrived = refs[:peers]
-    query, key, value, cot, weights = refs[peers : peers + 5]
-    gated, query_grad, key_grad, value_grad, filter_grad, short_grad = refs[peers + 5 : peers + 11]
-    longer, pre = refs[peers + 11 :]
+def token_kernel(steps, sum_rows, carried, *refs):
+    count_in = len(steps)
+    arrived = refs[:count_in]
+    query, key, value, cot, weights = refs[count_in : count_in + 5]
+    results = refs[count_in + 5 + carried : count_in + 11 + carried]
+    (gated, query_grad, key_grad, value_grad, filter_grad, short_grad, longer, pre, sems) = refs[
+        count_in + 11 + carried :
+    ]
+    copies = []
     tokens = query.shape[0]
     tap_count = weights.shape[1]
     count = sum_rows // PIECES
     me = lax.axis_index("ctx")
-    for step, source in zip(partners(peers), arrived):
+    for slot, (step, source) in enumerate(zip(steps, arrived)):
         lanes = lanes_of(me ^ step)
         extra = source[3 * tokens :, :].astype(F32)
 
@@ -421,56 +420,74 @@
                     summed
                     + weights[array, tap : tap + 1, lanes] * pre[array, tap : tap + tokens, :]
                 )
-            target[:, lanes] = summed.astype(BF16)
+            target[slot] = summed.astype(BF16)
 
         conv = source[:tokens, :].astype(F32)
         conv_grad = source[tokens : 2 * tokens, :].astype(F32)
-        gated[:, lanes] = (short(0, query) * conv).astype(BF16)
+        gated[slot] = (short(0, query) * conv).astype(BF16)
         taps_back(0, cot[:, lanes].astype(F32) * conv, query_grad)
         taps_back(1, conv_grad * short(2, value), key_grad)
         taps_back(2, conv_grad * short(1, key), value_grad)
-        filter_grad[:, lanes] = source[2 * tokens : 3 * tokens, :].astype(F32)
+        filter_grad[slot] = source[2 * tokens : 3 * tokens, :].astype(F32)
         whole = extra[:count]
         for piece in range(1, PIECES):
             whole = whole + extra[piece * count : (piece + 1) * count]
         for row in range(count):
             which, tap = divmod(row, tap_count)
-            short_grad[which, tap : tap + 1, lanes] = whole[row : row + 1]
-
-
-def token_step(arrived, query, key, value, cot, short_weights):
-    peers = len(arrived)
+            short_grad[slot, which, tap : tap + 1, :] = whole[row : row + 1]
+        held = (gated, query_grad, key_grad, value_grad, filter_grad, short_grad)
+        for at, (source, target) in enumerate(zip(held, results)):
+            place = target.at[:, :, lanes] if at == 5 else target.at[:, lanes]
+            copies.append(pltpu.make_async_copy(source.at[slot], place, sems.at[slot, at]))
+            copies[-1].start()
+    for copy in copies:
+        copy.wait()
+
+
+def token_step(arrived, steps, query, key, value, cot, short_weights, begun=()):
     tokens, width = query.shape
+    count = len(arrived)
     wide = jax.ShapeDtypeStruct((tokens, width), BF16)
+    anywhere = pl.BlockSpec(memory_space=pl.ANY)
     return pl.pallas_call(
-        functools.partial(token_kernel, peers, extra_rows(short_weights)[0]),
-        in_specs=in_vmem(peers + 5),
-        out_specs=in_vmem(6),
+        functools.partial(token_kernel, steps, extra_rows(short_weights)[0], len(begun)),
+        in_specs=in_vmem(count + 5) + [anywhere] * len(begun),
+        out_specs=[anywhere] * 6,
         out_shape=[wide] * 4
         + [
             jax.ShapeDtypeStruct((tokens, width), F32),
             jax.ShapeDtypeStruct(short_weights.shape, F32),
         ],
         scratch_shapes=[
+            *[pltpu.VMEM((count, tokens, LANES), BF16)] * 4,
+            pltpu.VMEM((count, tokens, LANES), F32),
+            pltpu.VMEM((count, *short_weights.shape[:2], LANES), F32),
             pltpu.VMEM((3, tokens + PAD, LANES), F32),
             pltpu.VMEM((3, tokens + PAD, LANES), F32),
+            pltpu.SemaphoreType.DMA((count, 6)),
         ],
+        input_output_aliases={count + 5 + at: at for at in range(len(begun))},
         compiler_params=pltpu.CompilerParams(vmem_limit_bytes=VMEM_LIMIT),
+        cost_estimate=pl.CostEstimate(flops=0, bytes_accessed=4 * MIB, transcendentals=0),
         name="token_outputs",
-    )(*arrived, query, key, value, cot, short_weights)
+    )(*arrived, query, key, value, cot, short_weights, *begun)
 
 
 def channel_shards(query_proj, key_proj, value_proj, cotangent, filter_taps, short_weights):
     peers = lax.axis_size("ctx")
     tokens = query_proj.shape[0]
     tables = [jnp.asarray(table) for table in dft_tables(peers * tokens)]
-    sent = pack((query_proj, key_proj, value_proj, cotangent, filter_taps), peers)
-    arrived = exchange(sent)
+    going, coming = partners(peers, False), partners(peers, True)
+    sent = pack((query_proj, key_proj, value_proj, cotangent, filter_taps), going)
+    arrived = exchange(sent, going)
     staged = stage((sent[0], short_weights, *tables), arrived[1])
-    back = exchange(
-        channel_step((staged[0], *arrived[1:]), staged[1], staged[2:], tokens)
-    )
-    return tuple(token_step(back, query_proj, key_proj, value_proj, cotangent, short_weights))
+    arrived[0] = staged[0]
+    results = channel_step(arrived, going, coming, staged[1], staged[2:], tokens)
+    back = exchange(results, coming)
+    local = (query_proj, key_proj, value_proj, cotangent, short_weights)
+    half = peers // 2
+    begun = token_step(back[:half], coming[:half], *local)
+    return tuple(token_step(back[half:], coming[half:], *local, begun))
 
 
 def from_behind(array, axis, by):

time: 40.7 us -> 42 us (1.032)
  Pallas kernels: 8.83 us -> 9.62 us
    pallas_call x3 -> x4, Pallas kernels: 8.27 us -> 9.06 us  [the longest x1 3.69 us: channel_step(): pl.pallas_call(functools.partial(channel_kernel, tokens, heard, told, 1.0...]
  transfers between devices with their start and end apart: 14 -> 14, of which waited for: 8 -> 7; matrix products, arithmetic and copies ran while one was open for 0% -> 0% of each run, Pallas kernels for 1% -> 5%
where the time goes in v9:
time: 42 us; the launch traced here: 41.8 us
  starting transfers between devices  14 us (33%)
  waiting for transfers between devices  12.5 us (30%)
  Pallas kernels  9.62 us (23%)
  local copies, waits for them, and re-layouts  4.92 us (12%)
  between operations  0.76 us (2%)
    ppermute x14, starting transfers between devices, exchange(): lax.ppermute(block, 'ctx', [(i, i ^ step) for i in range(peers)])  14 us
    ppermute x14, waiting for transfers between devices, exchange(): lax.ppermute(block, 'ctx', [(i, i ^ step) for i in range(peers)])  12.5 us
    unnamed x18, local copies, waits for them, and re-layouts  4.92 us
    pallas_call x1, Pallas kernels, channel_step(): pl.pallas_call(functools.partial(channel_kernel, tokens, heard, told, 1.0...  3.69 us
    pallas_call x2, Pallas kernels, token_step(): pl.pallas_call(functools.partial(token_kernel, steps, extra_rows(short_we...  2.84 us
    pallas_call x1, Pallas kernels, pack(): pl.pallas_call(functools.partial(pack_kernel, count, steps), in_specs=[pl...  2.53 us
  transfers between devices with their start and end apart: 14, of which 7 were waited for; matrix products, arithmetic and copies ran while one was open for 0% of the time, Pallas kernels for 5%

profile of v9, /device:TPU:0, one launch (start us, length us, event | category | flops | bytes accessed | tf_op | source)
XLA Modules:
  0.0 41.8 jit_solution(12352757993799401157)
XLA Ops:
  0.6 2.5 %pack_inputs.1 = (bf16[640,128]{1,0:T(8,128)(2,1)}, bf16[640,128]{1,0:T(8,128)(2,1)}, bf16[640,128]{1,0:T(8,128)(2,1)}, bf16[640,128]{1,0:T(8,128)(2,1)}, bf16[6...) custom-call(bf16[128,1024]{1,0:T(8,128)(2,1)} %refs_4_.5, ...), custom_call_target="tpu_custom_call" | custom-call | bytes 8388608 | tf_op jit(solution)/shard_map/pack_inputs/pallas_call | solution.py:75
  3.2 3.0 %collective-permute-start = (bf16[640,128]{1,0:T(8,128)(2,1)}, bf16[640,128]{1,0:T(8,128)(2,1)S(1)}, u32[]{:S(2)}, u32[]{:S(2)}) collective-permute-start(bf16[640,128]{1,0:T(8,128)(2,1)} %get-tuple-element.33), channel_id=1, source_target_pairs={{0,16},{4,20},{8,24},{12,28},{16,0},{20,4},{24,8},{28,12},{1,17},{... | collective-permute-start | bytes 491528 | tf_op jit(solution)/shard_map/ppermute | solution.py:42
  6.2 1.5 %collective-permute-start.1 = (bf16[640,128]{1,0:T(8,128)(2,1)}, bf16[640,128]{1,0:T(8,128)(2,1)S(1)}, u32[]{:S(2)}, u32[]{:S(2)}) collective-permute-start(bf16[640,128]{1,0:T(8,128)(2,1)} %get-tuple-element.35), channel_id=1, source_target_pairs={{0,8},{4,12},{8,0},{12,4},{16,24},{20,28},{24,16},{28,20},{1,9},{5... | collective-permute-start | bytes 491528 | tf_op jit(solution)/shard_map/ppermute | solution.py:42
  7.7 0.0 collective-permute-start.2
  7.7 1.5 %collective-permute-start.3 = (bf16[640,128]{1,0:T(8,128)(2,1)}, bf16[640,128]{1,0:T(8,128)(2,1)S(1)}, u32[]{:S(2)}, u32[]{:S(2)}) collective-permute-start(bf16[640,128]{1,0:T(8,128)(2,1)} %get-tuple-element.37), channel_id=1, source_target_pairs={{0,28},{4,24},{8,20},{12,16},{16,12},{20,8},{24,4},{28,0},{1,29},{... | collective-permute-start | bytes 491528 | tf_op jit(solution)/shard_map/ppermute | solution.py:42
  9.2 1.6 %collective-permute-start.4 = (bf16[640,128]{1,0:T(8,128)(2,1)}, bf16[640,128]{1,0:T(8,128)(2,1)S(1)}, u32[]{:S(2)}, u32[]{:S(2)}) collective-permute-start(bf16[640,128]{1,0:T(8,128)(2,1)} %get-tuple-element.38), channel_id=1, source_target_pairs={{0,20},{4,16},{8,28},{12,24},{16,4},{20,0},{24,12},{28,8},{1,21},{... | collective-permute-start | bytes 491528 | tf_op jit(solution)/shard_map/ppermute | solution.py:42
  10.8 0.0 collective-permute-done.refs_4_.refs_1_
  10.8 0.1 collective-permute-start.5
  10.9 2.6 %collective-permute-done.1.refs_2_ = bf16[640,128]{1,0:T(8,128)(2,1)S(1)} collective-permute-done((bf16[640,128]{1,0:T(8,128)(2,1)}, bf16[640,128]{1,0:T(8,128)(2,1)S(1)}, u32[]{:S(2)}, u32[]{:S(2)}) %collective-permute-start.1) | collective-permute-done | bytes 163872 | tf_op jit(solution)/shard_map/ppermute | solution.py:42
  13.5 1.6 %copy-done.4 = bf16[4,2,256,512]{3,2,1,0:T(8,128)(2,1)S(1)} copy-done((bf16[4,2,256,512]{3,2,1,0:T(8,128)(2,1)S(1)}, bf16[4,2,256,512]{3,2,1,0:T(8,128)(2,1)}, u32[]{:S(2)}) %copy-start.4) | copy-done | bytes 2097176
  15.1 1.6 %copy-done.5 = bf16[4,2,512,256]{3,2,1,0:T(8,128)(2,1)S(1)} copy-done((bf16[4,2,512,256]{3,2,1,0:T(8,128)(2,1)S(1)}, bf16[4,2,512,256]{3,2,1,0:T(8,128)(2,1)}, u32[]{:S(2)}) %copy-start.5) | copy-done | bytes 2097176
  16.7 0.8 %copy-done.6 = f32[3,3,1024]{2,1,0:T(4,128)S(1)} copy-done((f32[3,3,1024]{2,1,0:T(4,128)S(1)}, f32[3,3,1024]{2,1,0:T(4,128)}, u32[]{:S(2)}) %copy-start.6) | copy-done | bytes 36888
  17.5 0.9 %copy-done.8 = bf16[640,128]{1,0:T(8,128)(2,1)S(1)} copy-done((bf16[640,128]{1,0:T(8,128)(2,1)S(1)}, bf16[640,128]{1,0:T(8,128)(2,1)}, u32[]{:S(2)}) %copy-start.8) | copy-done | bytes 163864
  18.4 0.6 %stage_tables.1 = (bf16[640,128]{1,0:T(8,128)(2,1)S(1)}, f32[3,3,1024]{2,1,0:T(4,128)S(1)}, bf16[4,2,512,256]{3,2,1,0:T(8,128)(2,1)S(1)}, bf16[4,2,256,512]{3,2,1,0:T(8,128)(2,1)S(1)}) custom-call(bf16[640,128]{1,0:T(8,128)(2,1)S(1)} %copy-done.8, f32[3,3,1024]{2,1,0:T(4,128)S(1)} %copy-done.6, bf16[4,2,512,256]{3,2,1,0:T(8,128)(2,1)S(1)} %copy-done.5, ...), custom_call_target="tpu_custom_call" | custom-call | bytes 8388608 | tf_op jit(solution)/shard_map/stage_tables/pallas_call | solution.py:187
  19.0 0.7 %collective-permute-done.3.refs_4_ = bf16[640,128]{1,0:T(8,128)(2,1)S(1)} collective-permute-done((bf16[640,128]{1,0:T(8,128)(2,1)}, bf16[640,128]{1,0:T(8,128)(2,1)S(1)}, u32[]{:S(2)}, u32[]{:S(2)}) %collective-permute-start.3) | collective-permute-done | bytes 163872 | tf_op jit(solution)/shard_map/ppermute | solution.py:42
  19.7 1.9 %collective-permute-done.4.refs_5_ = bf16[640,128]{1,0:T(8,128)(2,1)S(1)} collective-permute-done((bf16[640,128]{1,0:T(8,128)(2,1)}, bf16[640,128]{1,0:T(8,128)(2,1)S(1)}, u32[]{:S(2)}, u32[]{:S(2)}) %collective-permute-start.4) | collective-permute-done | bytes 163872 | tf_op jit(solution)/shard_map/ppermute | solution.py:42
  21.6 0.1 collective-permute-done.5.refs_6_
  21.8 0.0 copy-start.3
  21.8 0.0 copy-start.7
  21.8 3.7 %channel_operator.1 = (bf16[416,128]{1,0:T(8,128)(2,1)S(1)}, bf16[416,128]{1,0:T(8,128)(2,1)S(1)}, bf16[416,128]{1,0:T(8,128)(2,1)S(1)}, bf16[416,128]{1,0:T(8,1...) custom-call(bf16[640,128]{1,0:T(8,128)(2,1)S(1)} %get-tuple-element., ...), custom_call_target="tpu_custom_call" | custom-call | tf_op jit(solution)/shard_map/channel_operator/pallas_call | solution.py:361
  25.5 2.1 %collective-permute-start.11 = (bf16[416,128]{1,0:T(8,128)(2,1)S(1)}, bf16[416,128]{1,0:T(8,128)(2,1)S(1)}, u32[]{:S(2)}, u32[]{:S(2)}) collective-permute-start(bf16[416,128]{1,0:T(8,128)(2,1)S(1)} %get-tuple-element.49), channel_id=1, source_target_pairs={{0,24},{4,28},{8,16},{12,20},{16,8},{20,12},{24,0},{28,4},{1,25},{... | collective-permute-start | bytes 319496 | tf_op jit(solution)/shard_map/ppermute | solution.py:42
  27.6 0.9 %collective-permute-start.12 = (bf16[416,128]{1,0:T(8,128)(2,1)S(1)}, bf16[416,128]{1,0:T(8,128)(2,1)S(1)}, u32[]{:S(2)}, u32[]{:S(2)}) collective-permute-start(bf16[416,128]{1,0:T(8,128)(2,1)S(1)} %get-tuple-element.50), channel_id=1, source_target_pairs={{0,28},{4,24},{8,20},{12,16},{16,12},{20,8},{24,4},{28,0},{1,29},{... | collective-permute-start | bytes 319496 | tf_op jit(solution)/shard_map/ppermute | solution.py:42
  28.5 1.5 %collective-permute-start.7 = (bf16[416,128]{1,0:T(8,128)(2,1)S(1)}, bf16[416,128]{1,0:T(8,128)(2,1)S(1)}, u32[]{:S(2)}, u32[]{:S(2)}) collective-permute-start(bf16[416,128]{1,0:T(8,128)(2,1)S(1)} %get-tuple-element.44), channel_id=1, source_target_pairs={{0,8},{4,12},{8,0},{12,4},{16,24},{20,28},{24,16},{28,20},{1,9},{5... | collective-permute-start | bytes 319496 | tf_op jit(solution)/shard_map/ppermute | solution.py:42
  30.0 0.5 %collective-permute-start.8 = (bf16[416,128]{1,0:T(8,128)(2,1)S(1)}, bf16[416,128]{1,0:T(8,128)(2,1)S(1)}, u32[]{:S(2)}, u32[]{:S(2)}) collective-permute-start(bf16[416,128]{1,0:T(8,128)(2,1)S(1)} %get-tuple-element.45), channel_id=1, source_target_pairs={{0,20},{4,16},{8,28},{12,24},{16,4},{20,0},{24,12},{28,8},{1,21},{... | collective-permute-start | bytes 319496 | tf_op jit(solution)/shard_map/ppermute | solution.py:42
  30.5 0.3 collective-permute-start.13
  30.9 1.4 %collective-permute-done.11.refs_1_ = bf16[416,128]{1,0:T(8,128)(2,1)S(1)} collective-permute-done((bf16[416,128]{1,0:T(8,128)(2,1)S(1)}, bf16[416,128]{1,0:T(8,128)(2,1)S(1)}, u32[]{:S(2)}, u32[]{:S(2)}) %collective-permute-start.11) | collective-permute-done | bytes 106528 | tf_op jit(solution)/shard_map/ppermute | solution.py:42
  32.3 0.7 %collective-permute-start.9 = (bf16[416,128]{1,0:T(8,128)(2,1)S(1)}, bf16[416,128]{1,0:T(8,128)(2,1)S(1)}, u32[]{:S(2)}, u32[]{:S(2)}) collective-permute-start(bf16[416,128]{1,0:T(8,128)(2,1)S(1)} %get-tuple-element.46), channel_id=1, source_target_pairs={{0,12},{4,8},{8,4},{12,0},{16,28},{20,24},{24,20},{28,16},{1,13},{... | collective-permute-start | bytes 319496 | tf_op jit(solution)/shard_map/ppermute | solution.py:42
  33.0 1.2 %collective-permute-done.12.refs_2_ = bf16[416,128]{1,0:T(8,128)(2,1)S(1)} collective-permute-done((bf16[416,128]{1,0:T(8,128)(2,1)S(1)}, bf16[416,128]{1,0:T(8,128)(2,1)S(1)}, u32[]{:S(2)}, u32[]{:S(2)}) %collective-permute-start.12) | collective-permute-done | bytes 106528 | tf_op jit(solution)/shard_map/ppermute | solution.py:42
  34.2 0.3 collective-permute-start.10
  34.4 4.4 %collective-permute-done.13.refs_3_ = bf16[416,128]{1,0:T(8,128)(2,1)S(1)} collective-permute-done((bf16[416,128]{1,0:T(8,128)(2,1)S(1)}, bf16[416,128]{1,0:T(8,128)(2,1)S(1)}, u32[]{:S(2)}, u32[]{:S(2)}) %collective-permute-start.13) | collective-permute-done | bytes 106528 | tf_op jit(solution)/shard_map/ppermute | solution.py:42
  38.9 1.4 %token_outputs.2 = (bf16[128,1024]{1,0:T(8,128)(2,1)}, bf16[128,1024]{1,0:T(8,128)(2,1)}, bf16[128,1024]{1,0:T(8,128)(2,1)}, bf16[128,1024]{1,0:T(8,128)(2,1)}, ...) custom-call(bf16[416,128]{1,0:T(8,128)(2,1)S(1)} %get-tuple-element.48.refs_0_, ...), custom_call_target="tpu_custom_call" | custom-call | bytes 4194304 | tf_op jit(solution)/shard_map/token_outputs/pallas_call | solution.py:452
  40.3 1.4 %token_outputs.3 = (bf16[128,1024]{1,0:T(8,128)(2,1)}, bf16[128,1024]{1,0:T(8,128)(2,1)}, bf16[128,1024]{1,0:T(8,128)(2,1)}, bf16[128,1024]{1,0:T(8,128)(2,1)}, ...) custom-call(bf16[416,128]{1,0:T(8,128)(2,1)S(1)} %collective-permute, ...), custom_call_target="tpu_custom_call", output_to_operand_aliasing={{0}: (9, {}), {1}: (10, {}), {2}: (11, {}), {3}: (12, {}), ... | custom-call | bytes 4194304 | tf_op jit(solution)/shard_map/token_outputs/pallas_call | solution.py:452
  (19 shorter events, 0.0 us)
Async XLA Ops:
  3.2 7.7 %collective-permute-start = (bf16[640,128]{1,0:T(8,128)(2,1)}, bf16[640,128]{1,0:T(8,128)(2,1)S(1)}, u32[]{:S(2)}, u32[]{:S(2)}) collective-permute-start(bf16[640,128]{1,0:T(8,128)(2,1)} %get-tuple-element.33), channel_id=1, source_target_pairs={{0,16},{4,20},{8,24},{12,28},{16,0},{20,4},{24,8},{28,12},{1,17},{... | collective-permute-start | bytes 491528 | tf_op jit(solution)/shard_map/ppermute | solution.py:42
  6.2 7.3 %collective-permute-start.1 = (bf16[640,128]{1,0:T(8,128)(2,1)}, bf16[640,128]{1,0:T(8,128)(2,1)S(1)}, u32[]{:S(2)}, u32[]{:S(2)}) collective-permute-start(bf16[640,128]{1,0:T(8,128)(2,1)} %get-tuple-element.35), channel_id=1, source_target_pairs={{0,8},{4,12},{8,0},{12,4},{16,24},{20,28},{24,16},{28,20},{1,9},{5... | collective-permute-start | bytes 491528 | tf_op jit(solution)/shard_map/ppermute | solution.py:42
  7.7 11.3 %collective-permute-start.2 = (bf16[640,128]{1,0:T(8,128)(2,1)}, bf16[640,128]{1,0:T(8,128)(2,1)S(1)}, u32[]{:S(2)}, u32[]{:S(2)}) collective-permute-start(bf16[640,128]{1,0:T(8,128)(2,1)} %get-tuple-element.36), channel_id=1, source_target_pairs={{0,24},{4,28},{8,16},{12,20},{16,8},{20,12},{24,0},{28,4},{1,25},{... | collective-permute-start | bytes 491528 | tf_op jit(solution)/shard_map/ppermute | solution.py:42
  7.7 12.0 %collective-permute-start.3 = (bf16[640,128]{1,0:T(8,128)(2,1)}, bf16[640,128]{1,0:T(8,128)(2,1)S(1)}, u32[]{:S(2)}, u32[]{:S(2)}) collective-permute-start(bf16[640,128]{1,0:T(8,128)(2,1)} %get-tuple-element.37), channel_id=1, source_target_pairs={{0,28},{4,24},{8,20},{12,16},{16,12},{20,8},{24,4},{28,0},{1,29},{... | collective-permute-start | bytes 491528 | tf_op jit(solution)/shard_map/ppermute | solution.py:42
  9.2 12.4 %collective-permute-start.4 = (bf16[640,128]{1,0:T(8,128)(2,1)}, bf16[640,128]{1,0:T(8,128)(2,1)S(1)}, u32[]{:S(2)}, u32[]{:S(2)}) collective-permute-start(bf16[640,128]{1,0:T(8,128)(2,1)} %get-tuple-element.38), channel_id=1, source_target_pairs={{0,20},{4,16},{8,28},{12,24},{16,4},{20,0},{24,12},{28,8},{1,21},{... | collective-permute-start | bytes 491528 | tf_op jit(solution)/shard_map/ppermute | solution.py:42
  10.8 10.9 %collective-permute-start.5 = (bf16[640,128]{1,0:T(8,128)(2,1)}, bf16[640,128]{1,0:T(8,128)(2,1)S(1)}, u32[]{:S(2)}, u32[]{:S(2)}) collective-permute-start(bf16[640,128]{1,0:T(8,128)(2,1)} %get-tuple-element.39), channel_id=1, source_target_pairs={{0,12},{4,8},{8,4},{12,0},{16,28},{20,24},{24,20},{28,16},{1,13},{... | collective-permute-start | bytes 491528 | tf_op jit(solution)/shard_map/ppermute | solution.py:42
  13.5 8.2 %collective-permute-start.6 = (bf16[640,128]{1,0:T(8,128)(2,1)}, bf16[640,128]{1,0:T(8,128)(2,1)S(1)}, u32[]{:S(2)}, u32[]{:S(2)}) collective-permute-start(bf16[640,128]{1,0:T(8,128)(2,1)} %get-tuple-element.40), channel_id=1, source_target_pairs={{0,4},{4,0},{8,12},{12,8},{16,20},{20,16},{24,28},{28,24},{1,5},{5... | collective-permute-start | bytes 491528 | tf_op jit(solution)/shard_map/ppermute | solution.py:42
  13.5 1.6 %copy-start.4 = (bf16[4,2,256,512]{3,2,1,0:T(8,128)(2,1)S(1)}, bf16[4,2,256,512]{3,2,1,0:T(8,128)(2,1)}, u32[]{:S(2)}) copy-start(bf16[4,2,256,512]{3,2,1,0:T(8,128)(2,1)} %constant.5.clone.refs_3_) | copy-start | bytes 6291460
  15.1 1.6 %copy-start.5 = (bf16[4,2,512,256]{3,2,1,0:T(8,128)(2,1)S(1)}, bf16[4,2,512,256]{3,2,1,0:T(8,128)(2,1)}, u32[]{:S(2)}) copy-start(bf16[4,2,512,256]{3,2,1,0:T(8,128)(2,1)} %constant.4.clone.refs_2_) | copy-start | bytes 6291460
  16.7 0.8 %copy-start.6 = (f32[3,3,1024]{2,1,0:T(4,128)S(1)}, f32[3,3,1024]{2,1,0:T(4,128)}, u32[]{:S(2)}) copy-start(f32[3,3,1024]{2,1,0:T(4,128)} %refs_8_.3) | copy-start | bytes 110596
  17.5 0.9 %copy-start.8 = (bf16[640,128]{1,0:T(8,128)(2,1)S(1)}, bf16[640,128]{1,0:T(8,128)(2,1)}, u32[]{:S(2)}) copy-start(bf16[640,128]{1,0:T(8,128)(2,1)} %get-tuple-element.32.refs_0_) | copy-start | bytes 491524
  21.8 17.1 %copy-start = (bf16[128,1024]{1,0:T(8,128)(2,1)S(1)}, bf16[128,1024]{1,0:T(8,128)(2,1)}, u32[]{:S(2)}) copy-start(bf16[128,1024]{1,0:T(8,128)(2,1)} %refs_4_.5) | copy-start | bytes 786436
  21.8 17.1 %copy-start.1 = (bf16[128,1024]{1,0:T(8,128)(2,1)S(1)}, bf16[128,1024]{1,0:T(8,128)(2,1)}, u32[]{:S(2)}) copy-start(bf16[128,1024]{1,0:T(8,128)(2,1)} %refs_5_.3) | copy-start | bytes 786436
  21.8 17.1 %copy-start.2 = (bf16[128,1024]{1,0:T(8,128)(2,1)S(1)}, bf16[128,1024]{1,0:T(8,128)(2,1)}, u32[]{:S(2)}) copy-start(bf16[128,1024]{1,0:T(8,128)(2,1)} %refs_6_.3) | copy-start | bytes 786436
  21.8 17.1 %copy-start.3 = (bf16[128,1024]{1,0:T(8,128)(2,1)S(1)}, bf16[128,1024]{1,0:T(8,128)(2,1)}, u32[]{:S(2)}) copy-start(bf16[128,1024]{1,0:T(8,128)(2,1)} %refs_7_.3) | copy-start | bytes 786436
  21.8 17.1 %copy-start.7 = (f32[3,3,1024]{2,1,0:T(4,128)S(1)}, f32[3,3,1024]{2,1,0:T(4,128)}, u32[]{:S(2)}) copy-start(f32[3,3,1024]{2,1,0:T(4,128)} %refs_8_.3) | copy-start | bytes 110596
  25.5 6.8 %collective-permute-start.11 = (bf16[416,128]{1,0:T(8,128)(2,1)S(1)}, bf16[416,128]{1,0:T(8,128)(2,1)S(1)}, u32[]{:S(2)}, u32[]{:S(2)}) collective-permute-start(bf16[416,128]{1,0:T(8,128)(2,1)S(1)} %get-tuple-element.49), channel_id=1, source_target_pairs={{0,24},{4,28},{8,16},{12,20},{16,8},{20,12},{24,0},{28,4},{1,25},{... | collective-permute-start | bytes 319496 | tf_op jit(solution)/shard_map/ppermute | solution.py:42
  27.6 6.6 %collective-permute-start.12 = (bf16[416,128]{1,0:T(8,128)(2,1)S(1)}, bf16[416,128]{1,0:T(8,128)(2,1)S(1)}, u32[]{:S(2)}, u32[]{:S(2)}) collective-permute-start(bf16[416,128]{1,0:T(8,128)(2,1)S(1)} %get-tuple-element.50), channel_id=1, source_target_pairs={{0,28},{4,24},{8,20},{12,16},{16,12},{20,8},{24,4},{28,0},{1,29},{... | collective-permute-start | bytes 319496 | tf_op jit(solution)/shard_map/ppermute | solution.py:42
  28.5 11.8 %collective-permute-start.7 = (bf16[416,128]{1,0:T(8,128)(2,1)S(1)}, bf16[416,128]{1,0:T(8,128)(2,1)S(1)}, u32[]{:S(2)}, u32[]{:S(2)}) collective-permute-start(bf16[416,128]{1,0:T(8,128)(2,1)S(1)} %get-tuple-element.44), channel_id=1, source_target_pairs={{0,8},{4,12},{8,0},{12,4},{16,24},{20,28},{24,16},{28,20},{1,9},{5... | collective-permute-start | bytes 319496 | tf_op jit(solution)/shard_map/ppermute | solution.py:42
  30.0 10.3 %collective-permute-start.8 = (bf16[416,128]{1,0:T(8,128)(2,1)S(1)}, bf16[416,128]{1,0:T(8,128)(2,1)S(1)}, u32[]{:S(2)}, u32[]{:S(2)}) collective-permute-start(bf16[416,128]{1,0:T(8,128)(2,1)S(1)} %get-tuple-element.45), channel_id=1, source_target_pairs={{0,20},{4,16},{8,28},{12,24},{16,4},{20,0},{24,12},{28,8},{1,21},{... | collective-permute-start | bytes 319496 | tf_op jit(solution)/shard_map/ppermute | solution.py:42
  30.5 8.3 %collective-permute-start.13 = (bf16[416,128]{1,0:T(8,128)(2,1)S(1)}, bf16[416,128]{1,0:T(8,128)(2,1)S(1)}, u32[]{:S(2)}, u32[]{:S(2)}) collective-permute-start(bf16[416,128]{1,0:T(8,128)(2,1)S(1)} %get-tuple-element.51), channel_id=1, source_target_pairs={{0,16},{4,20},{8,24},{12,28},{16,0},{20,4},{24,8},{28,12},{1,17},{... | collective-permute-start | bytes 319496 | tf_op jit(solution)/shard_map/ppermute | solution.py:42
  32.3 8.0 %collective-permute-start.9 = (bf16[416,128]{1,0:T(8,128)(2,1)S(1)}, bf16[416,128]{1,0:T(8,128)(2,1)S(1)}, u32[]{:S(2)}, u32[]{:S(2)}) collective-permute-start(bf16[416,128]{1,0:T(8,128)(2,1)S(1)} %get-tuple-element.46), channel_id=1, source_target_pairs={{0,12},{4,8},{8,4},{12,0},{16,28},{20,24},{24,20},{28,16},{1,13},{... | collective-permute-start | bytes 319496 | tf_op jit(solution)/shard_map/ppermute | solution.py:42
  34.2 6.2 %collective-permute-start.10 = (bf16[416,128]{1,0:T(8,128)(2,1)S(1)}, bf16[416,128]{1,0:T(8,128)(2,1)S(1)}, u32[]{:S(2)}, u32[]{:S(2)}) collective-permute-start(bf16[416,128]{1,0:T(8,128)(2,1)S(1)} %get-tuple-element.47), channel_id=1, source_target_pairs={{0,4},{4,0},{8,12},{12,8},{16,20},{20,16},{24,28},{28,24},{1,5},{5... | collective-permute-start | bytes 319496 | tf_op jit(solution)/shard_map/ppermute | solution.py:42

commit v10 on v9

--- a/solution.py
+++ b/solution.py
@@ -20,7 +20,7 @@
 PIECES = 2
 MIB = 1024 * 1024
 VMEM_LIMIT = 24 * MIB
-PACK_VMEM = 60680 * 1024
+PACK_VMEM = 53862 * 1024
 
 
 def partners(peers, diagonal_first):
@@ -485,9 +485,9 @@
     results = channel_step(arrived, going, coming, staged[1], staged[2:], tokens)
     back = exchange(results, coming)
     local = (query_proj, key_proj, value_proj, cotangent, short_weights)
-    half = peers // 2
-    begun = token_step(back[:half], coming[:half], *local)
-    return tuple(token_step(back[half:], coming[half:], *local, begun))
+    early = 1 + sum((step >> 1).bit_count() > 1 for step in coming)
+    begun = token_step(back[:early], coming[:early], *local)
+    return tuple(token_step(back[early:], coming[early:], *local, begun))
 
 
 def from_behind(array, axis, by):

time: 42 us -> 39.4 us (0.938)
  Pallas kernels: 9.62 us -> 8.54 us
  local copies, waits for them, and re-layouts: 4.92 us -> 4 us
    pallas_call x1, Pallas kernels: 2.53 us -> 1.48 us  [pack(): pl.pallas_call(functools.partial(pack_kernel, count, steps), in_specs=[pl...]
    unnamed x18 -> x16, local copies, waits for them, and re-layouts: 4.92 us -> 4 us
  transfers between devices with their start and end apart: 14 -> 14, of which waited for: 7 -> 8; matrix products, arithmetic and copies ran while one was open for 0% -> 0% of each run, Pallas kernels for 5% -> 5%
where the time goes in v10:
time: 39.4 us; the launch traced here: 39.1 us
  starting transfers between devices  13.8 us (35%)
  waiting for transfers between devices  12.1 us (31%)
  Pallas kernels  8.54 us (22%)
  local copies, waits for them, and re-layouts  4 us (10%)
  between operations  0.72 us (2%)
    ppermute x14, starting transfers between devices, exchange(): lax.ppermute(block, 'ctx', [(i, i ^ step) for i in range(peers)])  13.8 us
    ppermute x14, waiting for transfers between devices, exchange(): lax.ppermute(block, 'ctx', [(i, i ^ step) for i in range(peers)])  12.1 us
    unnamed x16, local copies, waits for them, and re-layouts  4 us
    pallas_call x1, Pallas kernels, channel_step(): pl.pallas_call(functools.partial(channel_kernel, tokens, heard, told, 1.0...  3.69 us
    pallas_call x2, Pallas kernels, token_step(): pl.pallas_call(functools.partial(token_kernel, steps, extra_rows(short_we...  2.82 us
    pallas_call x1, Pallas kernels, pack(): pl.pallas_call(functools.partial(pack_kernel, count, steps), in_specs=[pl...  1.48 us
  transfers between devices with their start and end apart: 14, of which 8 were waited for; matrix products, arithmetic and copies ran while one was open for 0% of the time, Pallas kernels for 5%

profile of v10, /device:TPU:0, one launch (start us, length us, event | category | flops | bytes accessed | tf_op | source)
XLA Modules:
  0.0 39.1 jit_solution(7150180628998771297)
XLA Ops:
  0.6 1.5 %pack_inputs.1 = (bf16[640,128]{1,0:T(8,128)(2,1)S(1)}, bf16[640,128]{1,0:T(8,128)(2,1)S(1)}, bf16[640,128]{1,0:T(8,128)(2,1)S(1)}, bf16[640,128]{1,0:T(8,128)(2...) custom-call(bf16[128,1024]{1,0:T(8,128)(2,1)} %refs_5_.3, ...), custom_call_target="tpu_custom_call" | custom-call | bytes 8388608 | tf_op jit(solution)/shard_map/pack_inputs/pallas_call | solution.py:75
  2.1 3.0 %collective-permute-start = (bf16[640,128]{1,0:T(8,128)(2,1)S(1)}, bf16[640,128]{1,0:T(8,128)(2,1)S(1)}, u32[]{:S(2)}, u32[]{:S(2)}) collective-permute-start(bf16[640,128]{1,0:T(8,128)(2,1)S(1)} %get-tuple-element.33), channel_id=1, source_target_pairs={{0,16},{4,20},{8,24},{12,28},{16,0},{20,4},{24,8},{28,12},{1,17},{... | collective-permute-start | bytes 491528 | tf_op jit(solution)/shard_map/ppermute | solution.py:42
  5.2 1.5 %collective-permute-start.1 = (bf16[640,128]{1,0:T(8,128)(2,1)S(1)}, bf16[640,128]{1,0:T(8,128)(2,1)S(1)}, u32[]{:S(2)}, u32[]{:S(2)}) collective-permute-start(bf16[640,128]{1,0:T(8,128)(2,1)S(1)} %get-tuple-element.35), channel_id=1, source_target_pairs={{0,8},{4,12},{8,0},{12,4},{16,24},{20,28},{24,16},{28,20},{1,9},{5... | collective-permute-start | bytes 491528 | tf_op jit(solution)/shard_map/ppermute | solution.py:42
  6.6 0.0 collective-permute-start.2
  6.7 1.5 %collective-permute-start.3 = (bf16[640,128]{1,0:T(8,128)(2,1)S(1)}, bf16[640,128]{1,0:T(8,128)(2,1)S(1)}, u32[]{:S(2)}, u32[]{:S(2)}) collective-permute-start(bf16[640,128]{1,0:T(8,128)(2,1)S(1)} %get-tuple-element.37), channel_id=1, source_target_pairs={{0,28},{4,24},{8,20},{12,16},{16,12},{20,8},{24,4},{28,0},{1,29},{... | collective-permute-start | bytes 491528 | tf_op jit(solution)/shard_map/ppermute | solution.py:42
  8.2 1.6 %collective-permute-start.4 = (bf16[640,128]{1,0:T(8,128)(2,1)S(1)}, bf16[640,128]{1,0:T(8,128)(2,1)S(1)}, u32[]{:S(2)}, u32[]{:S(2)}) collective-permute-start(bf16[640,128]{1,0:T(8,128)(2,1)S(1)} %get-tuple-element.38), channel_id=1, source_target_pairs={{0,20},{4,16},{8,28},{12,24},{16,4},{20,0},{24,12},{28,8},{1,21},{... | collective-permute-start | bytes 491528 | tf_op jit(solution)/shard_map/ppermute | solution.py:42
  9.8 0.1 collective-permute-start.5
  9.9 2.4 %collective-permute-done.1.refs_2_ = bf16[640,128]{1,0:T(8,128)(2,1)S(1)} collective-permute-done((bf16[640,128]{1,0:T(8,128)(2,1)S(1)}, bf16[640,128]{1,0:T(8,128)(2,1)S(1)}, u32[]{:S(2)}, u32[]{:S(2)}) %collective-permute-start.1) | collective-permute-done | bytes 163872 | tf_op jit(solution)/shard_map/ppermute | solution.py:42
  12.3 1.6 %copy-done.4 = bf16[4,2,256,512]{3,2,1,0:T(8,128)(2,1)S(1)} copy-done((bf16[4,2,256,512]{3,2,1,0:T(8,128)(2,1)S(1)}, bf16[4,2,256,512]{3,2,1,0:T(8,128)(2,1)}, u32[]{:S(2)}) %copy-start.4) | copy-done | bytes 2097176
  13.9 1.6 %copy-done.5 = bf16[4,2,512,256]{3,2,1,0:T(8,128)(2,1)S(1)} copy-done((bf16[4,2,512,256]{3,2,1,0:T(8,128)(2,1)S(1)}, bf16[4,2,512,256]{3,2,1,0:T(8,128)(2,1)}, u32[]{:S(2)}) %copy-start.5) | copy-done | bytes 2097176
  15.5 0.8 %copy-done.6 = f32[3,3,1024]{2,1,0:T(4,128)S(1)} copy-done((f32[3,3,1024]{2,1,0:T(4,128)S(1)}, f32[3,3,1024]{2,1,0:T(4,128)}, u32[]{:S(2)}) %copy-start.6) | copy-done | bytes 36888
  16.3 0.6 %stage_tables.1 = (bf16[640,128]{1,0:T(8,128)(2,1)S(1)}, f32[3,3,1024]{2,1,0:T(4,128)S(1)}, bf16[4,2,512,256]{3,2,1,0:T(8,128)(2,1)S(1)}, bf16[4,2,256,512]{3,2,1,0:T(8,128)(2,1)S(1)}) custom-call(bf16[640,128]{1,0:T(8,128)(2,1)S(1)} %get-tuple-element.32.refs_0_, f32[3,3,1024]{2,1,0:T(4,128)S(1)} %copy-done.6, bf16[4,2,512,256]{3,2,1,0:T(8,128)(2,1)S(1)} %copy-done.5, ...), custom_call_target="tpu_custom_call" | custom-call | bytes 8388608 | tf_op jit(solution)/shard_map/stage_tables/pallas_call | solution.py:187
  16.8 1.5 %collective-permute-done.3.refs_4_ = bf16[640,128]{1,0:T(8,128)(2,1)S(1)} collective-permute-done((bf16[640,128]{1,0:T(8,128)(2,1)S(1)}, bf16[640,128]{1,0:T(8,128)(2,1)S(1)}, u32[]{:S(2)}, u32[]{:S(2)}) %collective-permute-start.3) | collective-permute-done | bytes 163872 | tf_op jit(solution)/shard_map/ppermute | solution.py:42
  18.4 2.0 %collective-permute-done.4.refs_5_ = bf16[640,128]{1,0:T(8,128)(2,1)S(1)} collective-permute-done((bf16[640,128]{1,0:T(8,128)(2,1)S(1)}, bf16[640,128]{1,0:T(8,128)(2,1)S(1)}, u32[]{:S(2)}, u32[]{:S(2)}) %collective-permute-start.4) | collective-permute-done | bytes 163872 | tf_op jit(solution)/shard_map/ppermute | solution.py:42
  20.4 0.0 collective-permute-done.5.refs_6_
  20.4 0.0 copy-start.3
  20.4 0.0 copy-start.7
  20.4 3.7 %channel_operator.1 = (bf16[416,128]{1,0:T(8,128)(2,1)S(1)}, bf16[416,128]{1,0:T(8,128)(2,1)S(1)}, bf16[416,128]{1,0:T(8,128)(2,1)S(1)}, bf16[416,128]{1,0:T(8,1...) custom-call(bf16[640,128]{1,0:T(8,128)(2,1)S(1)} %get-tuple-element., ...), custom_call_target="tpu_custom_call" | custom-call | tf_op jit(solution)/shard_map/channel_operator/pallas_call | solution.py:361
  24.1 2.2 %collective-permute-start.12 = (bf16[416,128]{1,0:T(8,128)(2,1)S(1)}, bf16[416,128]{1,0:T(8,128)(2,1)S(1)}, u32[]{:S(2)}, u32[]{:S(2)}) collective-permute-start(bf16[416,128]{1,0:T(8,128)(2,1)S(1)} %get-tuple-element.50), channel_id=1, source_target_pairs={{0,24},{4,28},{8,16},{12,20},{16,8},{20,12},{24,0},{28,4},{1,25},{... | collective-permute-start | bytes 319496 | tf_op jit(solution)/shard_map/ppermute | solution.py:42
  26.3 0.9 %collective-permute-start.13 = (bf16[416,128]{1,0:T(8,128)(2,1)S(1)}, bf16[416,128]{1,0:T(8,128)(2,1)S(1)}, u32[]{:S(2)}, u32[]{:S(2)}) collective-permute-start(bf16[416,128]{1,0:T(8,128)(2,1)S(1)} %get-tuple-element.51), channel_id=1, source_target_pairs={{0,28},{4,24},{8,20},{12,16},{16,12},{20,8},{24,4},{28,0},{1,29},{... | collective-permute-start | bytes 319496 | tf_op jit(solution)/shard_map/ppermute | solution.py:42
  27.3 0.9 %collective-permute-start.7 = (bf16[416,128]{1,0:T(8,128)(2,1)S(1)}, bf16[416,128]{1,0:T(8,128)(2,1)S(1)}, u32[]{:S(2)}, u32[]{:S(2)}) collective-permute-start(bf16[416,128]{1,0:T(8,128)(2,1)S(1)} %get-tuple-element.44), channel_id=1, source_target_pairs={{0,16},{4,20},{8,24},{12,28},{16,0},{20,4},{24,8},{28,12},{1,17},{... | collective-permute-start | bytes 319496 | tf_op jit(solution)/shard_map/ppermute | solution.py:42
  28.1 1.2 %collective-permute-start.8 = (bf16[416,128]{1,0:T(8,128)(2,1)S(1)}, bf16[416,128]{1,0:T(8,128)(2,1)S(1)}, u32[]{:S(2)}, u32[]{:S(2)}) collective-permute-start(bf16[416,128]{1,0:T(8,128)(2,1)S(1)} %get-tuple-element.45), channel_id=1, source_target_pairs={{0,8},{4,12},{8,0},{12,4},{16,24},{20,28},{24,16},{28,20},{1,9},{5... | collective-permute-start | bytes 319496 | tf_op jit(solution)/shard_map/ppermute | solution.py:42
  29.3 0.0 collective-permute-start.9
  29.3 1.7 %collective-permute-done.12.refs_1_ = bf16[416,128]{1,0:T(8,128)(2,1)S(1)} collective-permute-done((bf16[416,128]{1,0:T(8,128)(2,1)S(1)}, bf16[416,128]{1,0:T(8,128)(2,1)S(1)}, u32[]{:S(2)}, u32[]{:S(2)}) %collective-permute-start.12) | collective-permute-done | bytes 106528 | tf_op jit(solution)/shard_map/ppermute | solution.py:42
  31.0 0.8 %collective-permute-start.10 = (bf16[416,128]{1,0:T(8,128)(2,1)S(1)}, bf16[416,128]{1,0:T(8,128)(2,1)S(1)}, u32[]{:S(2)}, u32[]{:S(2)}) collective-permute-start(bf16[416,128]{1,0:T(8,128)(2,1)S(1)} %get-tuple-element.47), channel_id=1, source_target_pairs={{0,12},{4,8},{8,4},{12,0},{16,28},{20,24},{24,20},{28,16},{1,13},{... | collective-permute-start | bytes 319496 | tf_op jit(solution)/shard_map/ppermute | solution.py:42
  31.8 1.2 %collective-permute-done.13.refs_2_ = bf16[416,128]{1,0:T(8,128)(2,1)S(1)} collective-permute-done((bf16[416,128]{1,0:T(8,128)(2,1)S(1)}, bf16[416,128]{1,0:T(8,128)(2,1)S(1)}, u32[]{:S(2)}, u32[]{:S(2)}) %collective-permute-start.13) | collective-permute-done | bytes 106528 | tf_op jit(solution)/shard_map/ppermute | solution.py:42
  33.0 0.1 collective-permute-start.11
  33.1 1.2 %token_outputs.2 = (bf16[128,1024]{1,0:T(8,128)(2,1)}, bf16[128,1024]{1,0:T(8,128)(2,1)}, bf16[128,1024]{1,0:T(8,128)(2,1)}, bf16[128,1024]{1,0:T(8,128)(2,1)}, ...) custom-call(bf16[416,128]{1,0:T(8,128)(2,1)S(1)} %get-tuple-element.49.refs_0_, ...), custom_call_target="tpu_custom_call" | custom-call | bytes 4194304 | tf_op jit(solution)/shard_map/token_outputs/pallas_call | solution.py:452
  34.3 1.1 %collective-permute-done.7.refs_0_ = bf16[416,128]{1,0:T(8,128)(2,1)S(1)} collective-permute-done((bf16[416,128]{1,0:T(8,128)(2,1)S(1)}, bf16[416,128]{1,0:T(8,128)(2,1)S(1)}, u32[]{:S(2)}, u32[]{:S(2)}) %collective-permute-start.7) | collective-permute-done | bytes 106528 | tf_op jit(solution)/shard_map/ppermute | solution.py:42
  35.4 0.1 collective-permute-done.8.refs_1_
  35.5 2.0 %collective-permute-done.9.refs_2_ = bf16[416,128]{1,0:T(8,128)(2,1)S(1)} collective-permute-done((bf16[416,128]{1,0:T(8,128)(2,1)S(1)}, bf16[416,128]{1,0:T(8,128)(2,1)S(1)}, u32[]{:S(2)}, u32[]{:S(2)}) %collective-permute-start.9) | collective-permute-done | bytes 106528 | tf_op jit(solution)/shard_map/ppermute | solution.py:42
  37.5 1.6 %token_outputs.3 = (bf16[128,1024]{1,0:T(8,128)(2,1)}, bf16[128,1024]{1,0:T(8,128)(2,1)}, bf16[128,1024]{1,0:T(8,128)(2,1)}, bf16[128,1024]{1,0:T(8,128)(2,1)}, ...) custom-call(bf16[416,128]{1,0:T(8,128)(2,1)S(1)} %collective-permute, ...), custom_call_target="tpu_custom_call", output_to_operand_aliasing={{0}: (10, {}), {1}: (11, {}), {2}: (12, {}), {3}: (13, {}),... | custom-call | bytes 4194304 | tf_op jit(solution)/shard_map/token_outputs/pallas_call | solution.py:452
  (17 shorter events, 0.0 us)
Async XLA Ops:
  2.1 7.7 %collective-permute-start = (bf16[640,128]{1,0:T(8,128)(2,1)S(1)}, bf16[640,128]{1,0:T(8,128)(2,1)S(1)}, u32[]{:S(2)}, u32[]{:S(2)}) collective-permute-start(bf16[640,128]{1,0:T(8,128)(2,1)S(1)} %get-tuple-element.33), channel_id=1, source_target_pairs={{0,16},{4,20},{8,24},{12,28},{16,0},{20,4},{24,8},{28,12},{1,17},{... | collective-permute-start | bytes 491528 | tf_op jit(solution)/shard_map/ppermute | solution.py:42
  5.2 7.1 %collective-permute-start.1 = (bf16[640,128]{1,0:T(8,128)(2,1)S(1)}, bf16[640,128]{1,0:T(8,128)(2,1)S(1)}, u32[]{:S(2)}, u32[]{:S(2)}) collective-permute-start(bf16[640,128]{1,0:T(8,128)(2,1)S(1)} %get-tuple-element.35), channel_id=1, source_target_pairs={{0,8},{4,12},{8,0},{12,4},{16,24},{20,28},{24,16},{28,20},{1,9},{5... | collective-permute-start | bytes 491528 | tf_op jit(solution)/shard_map/ppermute | solution.py:42
  6.6 10.2 %collective-permute-start.2 = (bf16[640,128]{1,0:T(8,128)(2,1)S(1)}, bf16[640,128]{1,0:T(8,128)(2,1)S(1)}, u32[]{:S(2)}, u32[]{:S(2)}) collective-permute-start(bf16[640,128]{1,0:T(8,128)(2,1)S(1)} %get-tuple-element.36), channel_id=1, source_target_pairs={{0,24},{4,28},{8,16},{12,20},{16,8},{20,12},{24,0},{28,4},{1,25},{... | collective-permute-start | bytes 491528 | tf_op jit(solution)/shard_map/ppermute | solution.py:42
  6.7 11.7 %collective-permute-start.3 = (bf16[640,128]{1,0:T(8,128)(2,1)S(1)}, bf16[640,128]{1,0:T(8,128)(2,1)S(1)}, u32[]{:S(2)}, u32[]{:S(2)}) collective-permute-start(bf16[640,128]{1,0:T(8,128)(2,1)S(1)} %get-tuple-element.37), channel_id=1, source_target_pairs={{0,28},{4,24},{8,20},{12,16},{16,12},{20,8},{24,4},{28,0},{1,29},{... | collective-permute-start | bytes 491528 | tf_op jit(solution)/shard_map/ppermute | solution.py:42
  8.2 12.2 %collective-permute-start.4 = (bf16[640,128]{1,0:T(8,128)(2,1)S(1)}, bf16[640,128]{1,0:T(8,128)(2,1)S(1)}, u32[]{:S(2)}, u32[]{:S(2)}) collective-permute-start(bf16[640,128]{1,0:T(8,128)(2,1)S(1)} %get-tuple-element.38), channel_id=1, source_target_pairs={{0,20},{4,16},{8,28},{12,24},{16,4},{20,0},{24,12},{28,8},{1,21},{... | collective-permute-start | bytes 491528 | tf_op jit(solution)/shard_map/ppermute | solution.py:42
  9.8 10.6 %collective-permute-start.5 = (bf16[640,128]{1,0:T(8,128)(2,1)S(1)}, bf16[640,128]{1,0:T(8,128)(2,1)S(1)}, u32[]{:S(2)}, u32[]{:S(2)}) collective-permute-start(bf16[640,128]{1,0:T(8,128)(2,1)S(1)} %get-tuple-element.39), channel_id=1, source_target_pairs={{0,12},{4,8},{8,4},{12,0},{16,28},{20,24},{24,20},{28,16},{1,13},{... | collective-permute-start | bytes 491528 | tf_op jit(solution)/shard_map/ppermute | solution.py:42
  12.3 8.1 %collective-permute-start.6 = (bf16[640,128]{1,0:T(8,128)(2,1)S(1)}, bf16[640,128]{1,0:T(8,128)(2,1)S(1)}, u32[]{:S(2)}, u32[]{:S(2)}) collective-permute-start(bf16[640,128]{1,0:T(8,128)(2,1)S(1)} %get-tuple-element.40), channel_id=1, source_target_pairs={{0,4},{4,0},{8,12},{12,8},{16,20},{20,16},{24,28},{28,24},{1,5},{5... | collective-permute-start | bytes 491528 | tf_op jit(solution)/shard_map/ppermute | solution.py:42
  12.3 1.6 %copy-start.4 = (bf16[4,2,256,512]{3,2,1,0:T(8,128)(2,1)S(1)}, bf16[4,2,256,512]{3,2,1,0:T(8,128)(2,1)}, u32[]{:S(2)}) copy-start(bf16[4,2,256,512]{3,2,1,0:T(8,128)(2,1)} %constant.5.clone.refs_3_) | copy-start | bytes 6291460
  13.9 1.6 %copy-start.5 = (bf16[4,2,512,256]{3,2,1,0:T(8,128)(2,1)S(1)}, bf16[4,2,512,256]{3,2,1,0:T(8,128)(2,1)}, u32[]{:S(2)}) copy-start(bf16[4,2,512,256]{3,2,1,0:T(8,128)(2,1)} %constant.4.clone.refs_2_) | copy-start | bytes 6291460
  15.5 0.8 %copy-start.6 = (f32[3,3,1024]{2,1,0:T(4,128)S(1)}, f32[3,3,1024]{2,1,0:T(4,128)}, u32[]{:S(2)}) copy-start(f32[3,3,1024]{2,1,0:T(4,128)} %refs_9_.1) | copy-start | bytes 110596
  20.4 12.7 %copy-start = (bf16[128,1024]{1,0:T(8,128)(2,1)S(1)}, bf16[128,1024]{1,0:T(8,128)(2,1)}, u32[]{:S(2)}) copy-start(bf16[128,1024]{1,0:T(8,128)(2,1)} %refs_5_.3) | copy-start | bytes 786436
  20.4 12.7 %copy-start.1 = (bf16[128,1024]{1,0:T(8,128)(2,1)S(1)}, bf16[128,1024]{1,0:T(8,128)(2,1)}, u32[]{:S(2)}) copy-start(bf16[128,1024]{1,0:T(8,128)(2,1)} %refs_6_.3) | copy-start | bytes 786436
  20.4 12.7 %copy-start.2 = (bf16[128,1024]{1,0:T(8,128)(2,1)S(1)}, bf16[128,1024]{1,0:T(8,128)(2,1)}, u32[]{:S(2)}) copy-start(bf16[128,1024]{1,0:T(8,128)(2,1)} %refs_7_.3) | copy-start | bytes 786436
  20.4 12.7 %copy-start.3 = (bf16[128,1024]{1,0:T(8,128)(2,1)S(1)}, bf16[128,1024]{1,0:T(8,128)(2,1)}, u32[]{:S(2)}) copy-start(bf16[128,1024]{1,0:T(8,128)(2,1)} %refs_8_.1) | copy-start | bytes 786436
  20.4 12.7 %copy-start.7 = (f32[3,3,1024]{2,1,0:T(4,128)S(1)}, f32[3,3,1024]{2,1,0:T(4,128)}, u32[]{:S(2)}) copy-start(f32[3,3,1024]{2,1,0:T(4,128)} %refs_9_.1) | copy-start | bytes 110596
  24.1 6.9 %collective-permute-start.12 = (bf16[416,128]{1,0:T(8,128)(2,1)S(1)}, bf16[416,128]{1,0:T(8,128)(2,1)S(1)}, u32[]{:S(2)}, u32[]{:S(2)}) collective-permute-start(bf16[416,128]{1,0:T(8,128)(2,1)S(1)} %get-tuple-element.50), channel_id=1, source_target_pairs={{0,24},{4,28},{8,16},{12,20},{16,8},{20,12},{24,0},{28,4},{1,25},{... | collective-permute-start | bytes 319496 | tf_op jit(solution)/shard_map/ppermute | solution.py:42
  26.3 6.7 %collective-permute-start.13 = (bf16[416,128]{1,0:T(8,128)(2,1)S(1)}, bf16[416,128]{1,0:T(8,128)(2,1)S(1)}, u32[]{:S(2)}, u32[]{:S(2)}) collective-permute-start(bf16[416,128]{1,0:T(8,128)(2,1)S(1)} %get-tuple-element.51), channel_id=1, source_target_pairs={{0,28},{4,24},{8,20},{12,16},{16,12},{20,8},{24,4},{28,0},{1,29},{... | collective-permute-start | bytes 319496 | tf_op jit(solution)/shard_map/ppermute | solution.py:42
  27.3 8.2 %collective-permute-start.7 = (bf16[416,128]{1,0:T(8,128)(2,1)S(1)}, bf16[416,128]{1,0:T(8,128)(2,1)S(1)}, u32[]{:S(2)}, u32[]{:S(2)}) collective-permute-start(bf16[416,128]{1,0:T(8,128)(2,1)S(1)} %get-tuple-element.44), channel_id=1, source_target_pairs={{0,16},{4,20},{8,24},{12,28},{16,0},{20,4},{24,8},{28,12},{1,17},{... | collective-permute-start | bytes 319496 | tf_op jit(solution)/shard_map/ppermute | solution.py:42
  28.1 7.4 %collective-permute-start.8 = (bf16[416,128]{1,0:T(8,128)(2,1)S(1)}, bf16[416,128]{1,0:T(8,128)(2,1)S(1)}, u32[]{:S(2)}, u32[]{:S(2)}) collective-permute-start(bf16[416,128]{1,0:T(8,128)(2,1)S(1)} %get-tuple-element.45), channel_id=1, source_target_pairs={{0,8},{4,12},{8,0},{12,4},{16,24},{20,28},{24,16},{28,20},{1,9},{5... | collective-permute-start | bytes 319496 | tf_op jit(solution)/shard_map/ppermute | solution.py:42
  29.3 8.2 %collective-permute-start.9 = (bf16[416,128]{1,0:T(8,128)(2,1)S(1)}, bf16[416,128]{1,0:T(8,128)(2,1)S(1)}, u32[]{:S(2)}, u32[]{:S(2)}) collective-permute-start(bf16[416,128]{1,0:T(8,128)(2,1)S(1)} %get-tuple-element.46), channel_id=1, source_target_pairs={{0,20},{4,16},{8,28},{12,24},{16,4},{20,0},{24,12},{28,8},{1,21},{... | collective-permute-start | bytes 319496 | tf_op jit(solution)/shard_map/ppermute | solution.py:42
  31.0 6.5 %collective-permute-start.10 = (bf16[416,128]{1,0:T(8,128)(2,1)S(1)}, bf16[416,128]{1,0:T(8,128)(2,1)S(1)}, u32[]{:S(2)}, u32[]{:S(2)}) collective-permute-start(bf16[416,128]{1,0:T(8,128)(2,1)S(1)} %get-tuple-element.47), channel_id=1, source_target_pairs={{0,12},{4,8},{8,4},{12,0},{16,28},{20,24},{24,20},{28,16},{1,13},{... | collective-permute-start | bytes 319496 | tf_op jit(solution)/shard_map/ppermute | solution.py:42
  33.0 4.5 %collective-permute-start.11 = (bf16[416,128]{1,0:T(8,128)(2,1)S(1)}, bf16[416,128]{1,0:T(8,128)(2,1)S(1)}, u32[]{:S(2)}, u32[]{:S(2)}) collective-permute-start(bf16[416,128]{1,0:T(8,128)(2,1)S(1)} %get-tuple-element.48), channel_id=1, source_target_pairs={{0,4},{4,0},{8,12},{12,8},{16,20},{20,16},{24,28},{28,24},{1,5},{5... | collective-permute-start | bytes 319496 | tf_op jit(solution)/shard_map/ppermute | solution.py:42

commit v11 on v10

--- a/solution.py
+++ b/solution.py
@@ -26,10 +26,10 @@
 def partners(peers, diagonal_first):
     def rank(step):
         links, other_core = (step >> 1).bit_count(), step & 1
+        if links == 1:
+            return (3 if other_core else 1 + diagonal_first, 0, -step)
         if links == 0:
-            return (4, 0, 0)
-        if links == 1:
-            return (3 if other_core else 1, 0, -step)
+            return (1 if diagonal_first else 4, 0, 0)
         return (0 if diagonal_first else 2, other_core, -step)
 
     return [0] + sorted(range(1, peers), key=rank)
@@ -105,7 +105,7 @@
         low = (table - high.astype(np.float64)).astype(BF16)
         return np.stack([high, low], axis=1)
 
-    return pieces(forward), pieces(backward)
+    return pieces(forward), backward.astype(BF16)
 
 
 def forward_mix(parts):
@@ -286,7 +286,7 @@
                 spectra[q, real, lanes], spectra[q, imag, lanes] = pair
         keep(0, real, imag, times(prod, filt))
     for r in range(PHASES):
-        result = transform(backward[r], products[r, :, :LANES])
+        result = jnp.dot(backward[r], products[r, :, :LANES], preferred_element_type=F32)
         conv[pl.ds(PAD + r, size, stride=PHASES), :] = result.astype(BF16).astype(F32)
     for step in range(size // TILE):
         real = slice(step * TILE, (step + 1) * TILE)
@@ -297,7 +297,7 @@
             known = [(spectra[q, real, lanes], spectra[q, imag, lanes]) for q in range(PHASES)]
             keep(2 - at, real, imag, conj_times(known, grad))
     for r in range(PHASES):
-        result = transform(backward[r], products[r, :, LANES:])
+        result = jnp.dot(backward[r], products[r, :, LANES:], preferred_element_type=F32)
         conv_grad[pl.ds(PAD + r, size, stride=PHASES), :] = (
             result[:, :LANES].astype(BF16).astype(F32)
         )
@@ -485,9 +485,12 @@
     results = channel_step(arrived, going, coming, staged[1], staged[2:], tokens)
     back = exchange(results, coming)
     local = (query_proj, key_proj, value_proj, cotangent, short_weights)
-    early = 1 + sum((step >> 1).bit_count() > 1 for step in coming)
-    begun = token_step(back[:early], coming[:early], *local)
-    return tuple(token_step(back[early:], coming[early:], *local, begun))
+    ends = [at for at in (4, 6) if at < peers] + [peers]
+    begun, start = (), 0
+    for end in ends:
+        begun = token_step(back[start:end], coming[start:end], *local, begun)
+        start = end
+    return tuple(begun)
 
 
 def from_behind(array, axis, by):

time: 39.4 us -> 38.8 us (0.985)
  local copies, waits for them, and re-layouts: 4 us -> 2.42 us
  waiting for transfers between devices: 12.1 us -> 12.5 us
  starting transfers between devices: 13.8 us -> 14.2 us
    unnamed x16, local copies, waits for them, and re-layouts: 4 us -> 2.42 us
    pallas_call x2 -> x3, Pallas kernels: 2.82 us -> 3.46 us  [token_step(): pl.pallas_call(functools.partial(token_kernel, steps, extra_rows(short_we...]
    pallas_call x1, Pallas kernels: 3.69 us -> 3.14 us  [channel_step(): pl.pallas_call(functools.partial(channel_kernel, tokens, heard, told, 1.0...]
    ppermute x14, starting transfers between devices: 13.8 us -> 14.2 us  [exchange(): lax.ppermute(block, 'ctx', [(i, i ^ step) for i in range(peers)])]
    ppermute x14, waiting for transfers between devices: 12.1 us -> 12.5 us  [exchange(): lax.ppermute(block, 'ctx', [(i, i ^ step) for i in range(peers)])]
  transfers between devices with their start and end apart: 14 -> 14, of which waited for: 8 -> 9; matrix products, arithmetic and copies ran while one was open for 0% -> 0% of each run, Pallas kernels for 5% -> 8%
where the time goes in v11:
time: 38.8 us; the launch traced here: 38.6 us
  starting transfers between devices  14.2 us (37%)
  waiting for transfers between devices  12.5 us (32%)
  Pallas kernels  8.65 us (22%)
  local copies, waits for them, and re-layouts  2.42 us (6%)
  between operations  0.74 us (2%)
    ppermute x14, starting transfers between devices, exchange(): lax.ppermute(block, 'ctx', [(i, i ^ step) for i in range(peers)])  14.2 us
    ppermute x14, waiting for transfers between devices, exchange(): lax.ppermute(block, 'ctx', [(i, i ^ step) for i in range(peers)])  12.5 us
    pallas_call x3, Pallas kernels, token_step(): pl.pallas_call(functools.partial(token_kernel, steps, extra_rows(short_we...  3.46 us
    pallas_call x1, Pallas kernels, channel_step(): pl.pallas_call(functools.partial(channel_kernel, tokens, heard, told, 1.0...  3.14 us
    unnamed x16, local copies, waits for them, and re-layouts  2.42 us
    pallas_call x1, Pallas kernels, pack(): pl.pallas_call(functools.partial(pack_kernel, count, steps), in_specs=[pl...  1.56 us
  transfers between devices with their start and end apart: 14, of which 9 were waited for; matrix products, arithmetic and copies ran while one was open for 0% of the time, Pallas kernels for 8%

profile of v11, /device:TPU:0, one launch (start us, length us, event | category | flops | bytes accessed | tf_op | source)
XLA Modules:
  0.0 38.6 jit_solution(17043465789735986006)
XLA Ops:
  0.6 0.0 copy-start.5
  0.6 1.6 %pack_inputs.1 = (bf16[640,128]{1,0:T(8,128)(2,1)S(1)}, bf16[640,128]{1,0:T(8,128)(2,1)S(1)}, bf16[640,128]{1,0:T(8,128)(2,1)S(1)}, bf16[640,128]{1,0:T(8,128)(2...) custom-call(bf16[128,1024]{1,0:T(8,128)(2,1)} %refs_2_.6, ...), custom_call_target="tpu_custom_call" | custom-call | bytes 8388608 | tf_op jit(solution)/shard_map/pack_inputs/pallas_call | solution.py:75
  2.2 3.0 %collective-permute-start = (bf16[640,128]{1,0:T(8,128)(2,1)S(1)}, bf16[640,128]{1,0:T(8,128)(2,1)S(1)}, u32[]{:S(2)}, u32[]{:S(2)}) collective-permute-start(bf16[640,128]{1,0:T(8,128)(2,1)S(1)} %get-tuple-element.39), channel_id=1, source_target_pairs={{0,16},{4,20},{8,24},{12,28},{16,0},{20,4},{24,8},{28,12},{1,17},{... | collective-permute-start | bytes 491528 | tf_op jit(solution)/shard_map/ppermute | solution.py:42
  5.2 1.5 %collective-permute-start.1 = (bf16[640,128]{1,0:T(8,128)(2,1)S(1)}, bf16[640,128]{1,0:T(8,128)(2,1)S(1)}, u32[]{:S(2)}, u32[]{:S(2)}) collective-permute-start(bf16[640,128]{1,0:T(8,128)(2,1)S(1)} %get-tuple-element.41), channel_id=1, source_target_pairs={{0,8},{4,12},{8,0},{12,4},{16,24},{20,28},{24,16},{28,20},{1,9},{5... | collective-permute-start | bytes 491528 | tf_op jit(solution)/shard_map/ppermute | solution.py:42
  6.7 0.0 collective-permute-start.2
  6.8 1.5 %collective-permute-start.3 = (bf16[640,128]{1,0:T(8,128)(2,1)S(1)}, bf16[640,128]{1,0:T(8,128)(2,1)S(1)}, u32[]{:S(2)}, u32[]{:S(2)}) collective-permute-start(bf16[640,128]{1,0:T(8,128)(2,1)S(1)} %get-tuple-element.43), channel_id=1, source_target_pairs={{0,28},{4,24},{8,20},{12,16},{16,12},{20,8},{24,4},{28,0},{1,29},{... | collective-permute-start | bytes 491528 | tf_op jit(solution)/shard_map/ppermute | solution.py:42
  8.3 1.6 %collective-permute-start.4 = (bf16[640,128]{1,0:T(8,128)(2,1)S(1)}, bf16[640,128]{1,0:T(8,128)(2,1)S(1)}, u32[]{:S(2)}, u32[]{:S(2)}) collective-permute-start(bf16[640,128]{1,0:T(8,128)(2,1)S(1)} %get-tuple-element.44), channel_id=1, source_target_pairs={{0,20},{4,16},{8,28},{12,24},{16,4},{20,0},{24,12},{28,8},{1,21},{... | collective-permute-start | bytes 491528 | tf_op jit(solution)/shard_map/ppermute | solution.py:42
  9.9 0.1 collective-permute-start.5
  10.0 2.4 %collective-permute-done.1.refs_2_ = bf16[640,128]{1,0:T(8,128)(2,1)S(1)} collective-permute-done((bf16[640,128]{1,0:T(8,128)(2,1)S(1)}, bf16[640,128]{1,0:T(8,128)(2,1)S(1)}, u32[]{:S(2)}, u32[]{:S(2)}) %collective-permute-start.1) | collective-permute-done | bytes 163872 | tf_op jit(solution)/shard_map/ppermute | solution.py:42
  12.4 1.6 %copy-done.4 = bf16[4,2,512,256]{3,2,1,0:T(8,128)(2,1)S(1)} copy-done((bf16[4,2,512,256]{3,2,1,0:T(8,128)(2,1)S(1)}, bf16[4,2,512,256]{3,2,1,0:T(8,128)(2,1)}, u32[]{:S(2)}) %copy-start.4) | copy-done | bytes 2097176
  14.0 0.8 %copy-done.6 = f32[3,3,1024]{2,1,0:T(4,128)S(1)} copy-done((f32[3,3,1024]{2,1,0:T(4,128)S(1)}, f32[3,3,1024]{2,1,0:T(4,128)}, u32[]{:S(2)}) %copy-start.6) | copy-done | bytes 36888
  14.8 0.5 %stage_tables.1 = (bf16[640,128]{1,0:T(8,128)(2,1)S(1)}, f32[3,3,1024]{2,1,0:T(4,128)S(1)}, bf16[4,2,512,256]{3,2,1,0:T(8,128)(2,1)S(1)}, bf16[4,256,512]{2,1,0:T(8,128)(2,1)S(1)}) custom-call(bf16[640,128]{1,0:T(8,128)(2,1)S(1)} %get-tuple-element.38.refs_0_, f32[3,3,1024]{2,1,0:T(4,128)S(1)} %copy-done.6, bf16[4,2,512,256]{3,2,1,0:T(8,128)(2,1)S(1)} %copy-done.4, ...), custom_call_target="tpu_custom_call" | custom-call | bytes 8388608 | tf_op jit(solution)/shard_map/stage_tables/pallas_call | solution.py:187
  15.3 0.2 collective-permute-done.2.refs_3_
  15.5 3.0 %collective-permute-done.3.refs_4_ = bf16[640,128]{1,0:T(8,128)(2,1)S(1)} collective-permute-done((bf16[640,128]{1,0:T(8,128)(2,1)S(1)}, bf16[640,128]{1,0:T(8,128)(2,1)S(1)}, u32[]{:S(2)}, u32[]{:S(2)}) %collective-permute-start.3) | collective-permute-done | bytes 163872 | tf_op jit(solution)/shard_map/ppermute | solution.py:42
  18.4 2.0 %collective-permute-done.4.refs_5_ = bf16[640,128]{1,0:T(8,128)(2,1)S(1)} collective-permute-done((bf16[640,128]{1,0:T(8,128)(2,1)S(1)}, bf16[640,128]{1,0:T(8,128)(2,1)S(1)}, u32[]{:S(2)}, u32[]{:S(2)}) %collective-permute-start.4) | collective-permute-done | bytes 163872 | tf_op jit(solution)/shard_map/ppermute | solution.py:42
  20.5 0.0 collective-permute-done.5.refs_6_
  20.5 0.0 copy-start.3
  20.5 0.0 copy-start.7
  20.5 3.1 %channel_operator.1 = (bf16[416,128]{1,0:T(8,128)(2,1)S(1)}, bf16[416,128]{1,0:T(8,128)(2,1)S(1)}, bf16[416,128]{1,0:T(8,128)(2,1)S(1)}, bf16[416,128]{1,0:T(8,1...) custom-call(bf16[640,128]{1,0:T(8,128)(2,1)S(1)} %get-tuple-element., ...), custom_call_target="tpu_custom_call" | custom-call | tf_op jit(solution)/shard_map/channel_operator/pallas_call | solution.py:361
  23.7 2.2 %collective-permute-start.11 = (bf16[416,128]{1,0:T(8,128)(2,1)S(1)}, bf16[416,128]{1,0:T(8,128)(2,1)S(1)}, u32[]{:S(2)}, u32[]{:S(2)}) collective-permute-start(bf16[416,128]{1,0:T(8,128)(2,1)S(1)} %get-tuple-element.55), channel_id=1, source_target_pairs={{0,24},{4,28},{8,16},{12,20},{16,8},{20,12},{24,0},{28,4},{1,25},{... | collective-permute-start | bytes 319496 | tf_op jit(solution)/shard_map/ppermute | solution.py:42
  25.9 0.9 %collective-permute-start.12 = (bf16[416,128]{1,0:T(8,128)(2,1)S(1)}, bf16[416,128]{1,0:T(8,128)(2,1)S(1)}, u32[]{:S(2)}, u32[]{:S(2)}) collective-permute-start(bf16[416,128]{1,0:T(8,128)(2,1)S(1)} %get-tuple-element.56), channel_id=1, source_target_pairs={{0,28},{4,24},{8,20},{12,16},{16,12},{20,8},{24,4},{28,0},{1,29},{... | collective-permute-start | bytes 319496 | tf_op jit(solution)/shard_map/ppermute | solution.py:42
  26.8 1.5 %collective-permute-start.9 = (bf16[416,128]{1,0:T(8,128)(2,1)S(1)}, bf16[416,128]{1,0:T(8,128)(2,1)S(1)}, u32[]{:S(2)}, u32[]{:S(2)}) collective-permute-start(bf16[416,128]{1,0:T(8,128)(2,1)S(1)} %get-tuple-element.52), channel_id=1, source_target_pairs={{0,16},{4,20},{8,24},{12,28},{16,0},{20,4},{24,8},{28,12},{1,17},{... | collective-permute-start | bytes 319496 | tf_op jit(solution)/shard_map/ppermute | solution.py:42
  28.3 1.2 %collective-permute-start.10 = (bf16[416,128]{1,0:T(8,128)(2,1)S(1)}, bf16[416,128]{1,0:T(8,128)(2,1)S(1)}, u32[]{:S(2)}, u32[]{:S(2)}) collective-permute-start(bf16[416,128]{1,0:T(8,128)(2,1)S(1)} %get-tuple-element.53), channel_id=1, source_target_pairs={{0,8},{4,12},{8,0},{12,4},{16,24},{20,28},{24,16},{28,20},{1,9},{5... | collective-permute-start | bytes 319496 | tf_op jit(solution)/shard_map/ppermute | solution.py:42
  29.5 1.1 %collective-permute-done.11.refs_1_ = bf16[416,128]{1,0:T(8,128)(2,1)S(1)} collective-permute-done((bf16[416,128]{1,0:T(8,128)(2,1)S(1)}, bf16[416,128]{1,0:T(8,128)(2,1)S(1)}, u32[]{:S(2)}, u32[]{:S(2)}) %collective-permute-start.11) | collective-permute-done | bytes 106528 | tf_op jit(solution)/shard_map/ppermute | solution.py:42
  30.5 2.0 %collective-permute-done.12.refs_2_ = bf16[416,128]{1,0:T(8,128)(2,1)S(1)} collective-permute-done((bf16[416,128]{1,0:T(8,128)(2,1)S(1)}, bf16[416,128]{1,0:T(8,128)(2,1)S(1)}, u32[]{:S(2)}, u32[]{:S(2)}) %collective-permute-start.12) | collective-permute-done | bytes 106528 | tf_op jit(solution)/shard_map/ppermute | solution.py:42
  32.5 0.7 %collective-permute-start.8 = (bf16[416,128]{1,0:T(8,128)(2,1)S(1)}, bf16[416,128]{1,0:T(8,128)(2,1)S(1)}, u32[]{:S(2)}, u32[]{:S(2)}) collective-permute-start(bf16[416,128]{1,0:T(8,128)(2,1)S(1)} %get-tuple-element.51), channel_id=1, source_target_pairs={{0,12},{4,8},{8,4},{12,0},{16,28},{20,24},{24,20},{28,16},{1,13},{... | collective-permute-start | bytes 319496 | tf_op jit(solution)/shard_map/ppermute | solution.py:42
  33.3 1.4 %token_outputs.3 = (bf16[128,1024]{1,0:T(8,128)(2,1)}, bf16[128,1024]{1,0:T(8,128)(2,1)}, bf16[128,1024]{1,0:T(8,128)(2,1)}, bf16[128,1024]{1,0:T(8,128)(2,1)}, ...) custom-call(bf16[416,128]{1,0:T(8,128)(2,1)S(1)} %get-tuple-element.54.refs_0_, ...), custom_call_target="tpu_custom_call" | custom-call | bytes 4194304 | tf_op jit(solution)/shard_map/token_outputs/pallas_call | solution.py:452
  34.7 0.2 collective-permute-done.9.refs_0_
  34.9 1.0 %token_outputs.4 = (bf16[128,1024]{1,0:T(8,128)(2,1)}, bf16[128,1024]{1,0:T(8,128)(2,1)}, bf16[128,1024]{1,0:T(8,128)(2,1)}, bf16[128,1024]{1,0:T(8,128)(2,1)}, ...) custom-call(bf16[416,128]{1,0:T(8,128)(2,1)S(1)} %collective-permute, ...), custom_call_target="tpu_custom_call", output_to_operand_aliasing={{0}: (7, {}), {1}: (8, {}), {2}: (9, {}), {3}: (10, {}), {4... | custom-call | bytes 4194304 | tf_op jit(solution)/shard_map/token_outputs/pallas_call | solution.py:452
  36.0 1.2 %collective-permute-done.7.refs_0_ = bf16[416,128]{1,0:T(8,128)(2,1)S(1)} collective-permute-done((bf16[416,128]{1,0:T(8,128)(2,1)S(1)}, bf16[416,128]{1,0:T(8,128)(2,1)S(1)}, u32[]{:S(2)}, u32[]{:S(2)}) %collective-permute-start.7) | collective-permute-done | bytes 106528 | tf_op jit(solution)/shard_map/ppermute | solution.py:42
  37.1 0.4 %collective-permute-done.8.refs_1_ = bf16[416,128]{1,0:T(8,128)(2,1)S(1)} collective-permute-done((bf16[416,128]{1,0:T(8,128)(2,1)S(1)}, bf16[416,128]{1,0:T(8,128)(2,1)S(1)}, u32[]{:S(2)}, u32[]{:S(2)}) %collective-permute-start.8) | collective-permute-done | bytes 106528 | tf_op jit(solution)/shard_map/ppermute | solution.py:42
  37.6 1.0 %token_outputs.5 = (bf16[128,1024]{1,0:T(8,128)(2,1)}, bf16[128,1024]{1,0:T(8,128)(2,1)}, bf16[128,1024]{1,0:T(8,128)(2,1)}, bf16[128,1024]{1,0:T(8,128)(2,1)}, ...) custom-call(bf16[416,128]{1,0:T(8,128)(2,1)S(1)} %collective-permute, ...), custom_call_target="tpu_custom_call", output_to_operand_aliasing={{0}: (7, {}), {1}: (8, {}), {2}: (9, {}), {3}: (10, {}), {4... | custom-call | bytes 4194304 | tf_op jit(solution)/shard_map/token_outputs/pallas_call | solution.py:452
  (18 shorter events, 0.0 us)
Async XLA Ops:
  0.6 11.7 %copy-start.5 = (bf16[4,256,512]{2,1,0:T(8,128)(2,1)S(1)}, bf16[4,256,512]{2,1,0:T(8,128)(2,1)}, u32[]{:S(2)}) copy-start(bf16[4,256,512]{2,1,0:T(8,128)(2,1)} %constant.5.clone.refs_3_) | copy-start | bytes 3145732
  2.2 7.7 %collective-permute-start = (bf16[640,128]{1,0:T(8,128)(2,1)S(1)}, bf16[640,128]{1,0:T(8,128)(2,1)S(1)}, u32[]{:S(2)}, u32[]{:S(2)}) collective-permute-start(bf16[640,128]{1,0:T(8,128)(2,1)S(1)} %get-tuple-element.39), channel_id=1, source_target_pairs={{0,16},{4,20},{8,24},{12,28},{16,0},{20,4},{24,8},{28,12},{1,17},{... | collective-permute-start | bytes 491528 | tf_op jit(solution)/shard_map/ppermute | solution.py:42
  5.2 7.1 %collective-permute-start.1 = (bf16[640,128]{1,0:T(8,128)(2,1)S(1)}, bf16[640,128]{1,0:T(8,128)(2,1)S(1)}, u32[]{:S(2)}, u32[]{:S(2)}) collective-permute-start(bf16[640,128]{1,0:T(8,128)(2,1)S(1)} %get-tuple-element.41), channel_id=1, source_target_pairs={{0,8},{4,12},{8,0},{12,4},{16,24},{20,28},{24,16},{28,20},{1,9},{5... | collective-permute-start | bytes 491528 | tf_op jit(solution)/shard_map/ppermute | solution.py:42
  6.7 8.7 %collective-permute-start.2 = (bf16[640,128]{1,0:T(8,128)(2,1)S(1)}, bf16[640,128]{1,0:T(8,128)(2,1)S(1)}, u32[]{:S(2)}, u32[]{:S(2)}) collective-permute-start(bf16[640,128]{1,0:T(8,128)(2,1)S(1)} %get-tuple-element.42), channel_id=1, source_target_pairs={{0,24},{4,28},{8,16},{12,20},{16,8},{20,12},{24,0},{28,4},{1,25},{... | collective-permute-start | bytes 491528 | tf_op jit(solution)/shard_map/ppermute | solution.py:42
  6.8 11.7 %collective-permute-start.3 = (bf16[640,128]{1,0:T(8,128)(2,1)S(1)}, bf16[640,128]{1,0:T(8,128)(2,1)S(1)}, u32[]{:S(2)}, u32[]{:S(2)}) collective-permute-start(bf16[640,128]{1,0:T(8,128)(2,1)S(1)} %get-tuple-element.43), channel_id=1, source_target_pairs={{0,28},{4,24},{8,20},{12,16},{16,12},{20,8},{24,4},{28,0},{1,29},{... | collective-permute-start | bytes 491528 | tf_op jit(solution)/shard_map/ppermute | solution.py:42
  8.3 12.2 %collective-permute-start.4 = (bf16[640,128]{1,0:T(8,128)(2,1)S(1)}, bf16[640,128]{1,0:T(8,128)(2,1)S(1)}, u32[]{:S(2)}, u32[]{:S(2)}) collective-permute-start(bf16[640,128]{1,0:T(8,128)(2,1)S(1)} %get-tuple-element.44), channel_id=1, source_target_pairs={{0,20},{4,16},{8,28},{12,24},{16,4},{20,0},{24,12},{28,8},{1,21},{... | collective-permute-start | bytes 491528 | tf_op jit(solution)/shard_map/ppermute | solution.py:42
  9.9 10.6 %collective-permute-start.5 = (bf16[640,128]{1,0:T(8,128)(2,1)S(1)}, bf16[640,128]{1,0:T(8,128)(2,1)S(1)}, u32[]{:S(2)}, u32[]{:S(2)}) collective-permute-start(bf16[640,128]{1,0:T(8,128)(2,1)S(1)} %get-tuple-element.45), channel_id=1, source_target_pairs={{0,12},{4,8},{8,4},{12,0},{16,28},{20,24},{24,20},{28,16},{1,13},{... | collective-permute-start | bytes 491528 | tf_op jit(solution)/shard_map/ppermute | solution.py:42
  12.4 8.1 %collective-permute-start.6 = (bf16[640,128]{1,0:T(8,128)(2,1)S(1)}, bf16[640,128]{1,0:T(8,128)(2,1)S(1)}, u32[]{:S(2)}, u32[]{:S(2)}) collective-permute-start(bf16[640,128]{1,0:T(8,128)(2,1)S(1)} %get-tuple-element.46), channel_id=1, source_target_pairs={{0,4},{4,0},{8,12},{12,8},{16,20},{20,16},{24,28},{28,24},{1,5},{5... | collective-permute-start | bytes 491528 | tf_op jit(solution)/shard_map/ppermute | solution.py:42
  12.4 1.6 %copy-start.4 = (bf16[4,2,512,256]{3,2,1,0:T(8,128)(2,1)S(1)}, bf16[4,2,512,256]{3,2,1,0:T(8,128)(2,1)}, u32[]{:S(2)}) copy-start(bf16[4,2,512,256]{3,2,1,0:T(8,128)(2,1)} %constant.4.clone.refs_2_) | copy-start | bytes 6291460
  14.0 0.8 %copy-start.6 = (f32[3,3,1024]{2,1,0:T(4,128)S(1)}, f32[3,3,1024]{2,1,0:T(4,128)}, u32[]{:S(2)}) copy-start(f32[3,3,1024]{2,1,0:T(4,128)} %refs_6_.5) | copy-start | bytes 110596
  20.5 12.7 %copy-start = (bf16[128,1024]{1,0:T(8,128)(2,1)S(1)}, bf16[128,1024]{1,0:T(8,128)(2,1)}, u32[]{:S(2)}) copy-start(bf16[128,1024]{1,0:T(8,128)(2,1)} %refs_2_.6) | copy-start | bytes 786436
  20.5 12.7 %copy-start.1 = (bf16[128,1024]{1,0:T(8,128)(2,1)S(1)}, bf16[128,1024]{1,0:T(8,128)(2,1)}, u32[]{:S(2)}) copy-start(bf16[128,1024]{1,0:T(8,128)(2,1)} %refs_3_.6) | copy-start | bytes 786436
  20.5 12.7 %copy-start.2 = (bf16[128,1024]{1,0:T(8,128)(2,1)S(1)}, bf16[128,1024]{1,0:T(8,128)(2,1)}, u32[]{:S(2)}) copy-start(bf16[128,1024]{1,0:T(8,128)(2,1)} %refs_4_.7) | copy-start | bytes 786436
  20.5 12.7 %copy-start.3 = (bf16[128,1024]{1,0:T(8,128)(2,1)S(1)}, bf16[128,1024]{1,0:T(8,128)(2,1)}, u32[]{:S(2)}) copy-start(bf16[128,1024]{1,0:T(8,128)(2,1)} %refs_5_.5) | copy-start | bytes 786436
  20.5 12.7 %copy-start.7 = (f32[3,3,1024]{2,1,0:T(4,128)S(1)}, f32[3,3,1024]{2,1,0:T(4,128)}, u32[]{:S(2)}) copy-start(f32[3,3,1024]{2,1,0:T(4,128)} %refs_6_.5) | copy-start | bytes 110596
  23.7 6.9 %collective-permute-start.11 = (bf16[416,128]{1,0:T(8,128)(2,1)S(1)}, bf16[416,128]{1,0:T(8,128)(2,1)S(1)}, u32[]{:S(2)}, u32[]{:S(2)}) collective-permute-start(bf16[416,128]{1,0:T(8,128)(2,1)S(1)} %get-tuple-element.55), channel_id=1, source_target_pairs={{0,24},{4,28},{8,16},{12,20},{16,8},{20,12},{24,0},{28,4},{1,25},{... | collective-permute-start | bytes 319496 | tf_op jit(solution)/shard_map/ppermute | solution.py:42
  25.9 6.7 %collective-permute-start.12 = (bf16[416,128]{1,0:T(8,128)(2,1)S(1)}, bf16[416,128]{1,0:T(8,128)(2,1)S(1)}, u32[]{:S(2)}, u32[]{:S(2)}) collective-permute-start(bf16[416,128]{1,0:T(8,128)(2,1)S(1)} %get-tuple-element.56), channel_id=1, source_target_pairs={{0,28},{4,24},{8,20},{12,16},{16,12},{20,8},{24,4},{28,0},{1,29},{... | collective-permute-start | bytes 319496 | tf_op jit(solution)/shard_map/ppermute | solution.py:42
  26.8 6.4 %collective-permute-start.13 = (bf16[416,128]{1,0:T(8,128)(2,1)S(1)}, bf16[416,128]{1,0:T(8,128)(2,1)S(1)}, u32[]{:S(2)}, u32[]{:S(2)}) collective-permute-start(bf16[416,128]{1,0:T(8,128)(2,1)S(1)} %get-tuple-element.57), channel_id=1, source_target_pairs={{0,4},{4,0},{8,12},{12,8},{16,20},{20,16},{24,28},{28,24},{1,5},{5... | collective-permute-start | bytes 319496 | tf_op jit(solution)/shard_map/ppermute | solution.py:42
  26.8 8.1 %collective-permute-start.9 = (bf16[416,128]{1,0:T(8,128)(2,1)S(1)}, bf16[416,128]{1,0:T(8,128)(2,1)S(1)}, u32[]{:S(2)}, u32[]{:S(2)}) collective-permute-start(bf16[416,128]{1,0:T(8,128)(2,1)S(1)} %get-tuple-element.52), channel_id=1, source_target_pairs={{0,16},{4,20},{8,24},{12,28},{16,0},{20,4},{24,8},{28,12},{1,17},{... | collective-permute-start | bytes 319496 | tf_op jit(solution)/shard_map/ppermute | solution.py:42
  28.3 6.7 %collective-permute-start.10 = (bf16[416,128]{1,0:T(8,128)(2,1)S(1)}, bf16[416,128]{1,0:T(8,128)(2,1)S(1)}, u32[]{:S(2)}, u32[]{:S(2)}) collective-permute-start(bf16[416,128]{1,0:T(8,128)(2,1)S(1)} %get-tuple-element.53), channel_id=1, source_target_pairs={{0,8},{4,12},{8,0},{12,4},{16,24},{20,28},{24,16},{28,20},{1,9},{5... | collective-permute-start | bytes 319496 | tf_op jit(solution)/shard_map/ppermute | solution.py:42
  30.5 6.6 %collective-permute-start.7 = (bf16[416,128]{1,0:T(8,128)(2,1)S(1)}, bf16[416,128]{1,0:T(8,128)(2,1)S(1)}, u32[]{:S(2)}, u32[]{:S(2)}) collective-permute-start(bf16[416,128]{1,0:T(8,128)(2,1)S(1)} %get-tuple-element.50), channel_id=1, source_target_pairs={{0,20},{4,16},{8,28},{12,24},{16,4},{20,0},{24,12},{28,8},{1,21},{... | collective-permute-start | bytes 319496 | tf_op jit(solution)/shard_map/ppermute | solution.py:42
  32.5 5.0 %collective-permute-start.8 = (bf16[416,128]{1,0:T(8,128)(2,1)S(1)}, bf16[416,128]{1,0:T(8,128)(2,1)S(1)}, u32[]{:S(2)}, u32[]{:S(2)}) collective-permute-start(bf16[416,128]{1,0:T(8,128)(2,1)S(1)} %get-tuple-element.51), channel_id=1, source_target_pairs={{0,12},{4,8},{8,4},{12,0},{16,28},{20,24},{24,20},{28,16},{1,13},{... | collective-permute-start | bytes 319496 | tf_op jit(solution)/shard_map/ppermute | solution.py:42

commit v12 on v11

--- a/solution.py
+++ b/solution.py
@@ -26,11 +26,11 @@
 def partners(peers, diagonal_first):
     def rank(step):
         links, other_core = (step >> 1).bit_count(), step & 1
+        if links == 0:
+            return (1 if diagonal_first else 5, 0)
         if links == 1:
-            return (3 if other_core else 1 + diagonal_first, 0, -step)
-        if links == 0:
-            return (1 if diagonal_first else 4, 0, 0)
-        return (0 if diagonal_first else 2, other_core, -step)
+            return (4 if other_core else 3, -step)
+        return (2 * other_core if diagonal_first else 3.5, other_core)
 
     return [0] + sorted(range(1, peers), key=rank)
 
@@ -100,12 +100,7 @@
     forward = np.stack(forward)
     backward = np.swapaxes(forward, 1, 2) / seq_len
 
-    def pieces(table):
-        high = table.astype(BF16)
-        low = (table - high.astype(np.float64)).astype(BF16)
-        return np.stack([high, low], axis=1)
-
-    return pieces(forward), backward.astype(BF16)
+    return forward.astype(BF16), backward.astype(BF16)
 
 
 def forward_mix(parts):
@@ -134,10 +129,8 @@
     )
 
 
-def transform(tables, signal):
-    return jnp.dot(tables[0], signal, preferred_element_type=F32) + jnp.dot(
-        tables[1], signal, preferred_element_type=F32
-    )
+def transform(table, signal):
+    return jnp.dot(table, signal, preferred_element_type=F32)
 
 
 def phases_near(ref, chunk, tap_count):
@@ -286,7 +279,7 @@
                 spectra[q, real, lanes], spectra[q, imag, lanes] = pair
         keep(0, real, imag, times(prod, filt))
     for r in range(PHASES):
-        result = jnp.dot(backward[r], products[r, :, :LANES], preferred_element_type=F32)
+        result = transform(backward[r], products[r, :, :LANES])
         conv[pl.ds(PAD + r, size, stride=PHASES), :] = result.astype(BF16).astype(F32)
     for step in range(size // TILE):
         real = slice(step * TILE, (step + 1) * TILE)
@@ -297,7 +290,7 @@
             known = [(spectra[q, real, lanes], spectra[q, imag, lanes]) for q in range(PHASES)]
             keep(2 - at, real, imag, conj_times(known, grad))
     for r in range(PHASES):
-        result = jnp.dot(backward[r], products[r, :, LANES:], preferred_element_type=F32)
+        result = transform(backward[r], products[r, :, LANES:])
         conv_grad[pl.ds(PAD + r, size, stride=PHASES), :] = (
             result[:, :LANES].astype(BF16).astype(F32)
         )

time: 38.8 us -> 37.9 us (0.977)
  starting transfers between devices: 14.2 us -> 15.9 us
  local copies, waits for them, and re-layouts: 2.42 us -> 1.25 us
  waiting for transfers between devices: 12.5 us -> 11.7 us
  Pallas kernels: 8.65 us -> 8.11 us
    ppermute x14, starting transfers between devices: 14.2 us -> 15.9 us  [exchange(): lax.ppermute(block, 'ctx', [(i, i ^ step) for i in range(peers)])]
    unnamed x16 -> x14, local copies, waits for them, and re-layouts: 2.42 us -> 1.25 us
    ppermute x14, waiting for transfers between devices: 12.5 us -> 11.7 us  [exchange(): lax.ppermute(block, 'ctx', [(i, i ^ step) for i in range(peers)])]
    pallas_call x1, Pallas kernels: 3.14 us -> 2.67 us  [channel_step(): pl.pallas_call(functools.partial(channel_kernel, tokens, heard, told, 1.0...]
  transfers between devices with their start and end apart: 14 -> 14, of which waited for: 9 -> 7; matrix products, arithmetic and copies ran while one was open for 0% -> 0% of each run, Pallas kernels for 8% -> 8%
where the time goes in v12:
time: 37.9 us; the launch traced here: 37.7 us
  starting transfers between devices  15.9 us (42%)
  waiting for transfers between devices  11.7 us (31%)
  Pallas kernels  8.11 us (21%)
  local copies, waits for them, and re-layouts  1.25 us (3%)
  between operations  0.74 us (2%)
    ppermute x14, starting transfers between devices, exchange(): lax.ppermute(block, 'ctx', [(i, i ^ step) for i in range(peers)])  15.9 us
    ppermute x14, waiting for transfers between devices, exchange(): lax.ppermute(block, 'ctx', [(i, i ^ step) for i in range(peers)])  11.7 us
    pallas_call x3, Pallas kernels, token_step(): pl.pallas_call(functools.partial(token_kernel, steps, extra_rows(short_we...  3.46 us
    pallas_call x1, Pallas kernels, channel_step(): pl.pallas_call(functools.partial(channel_kernel, tokens, heard, told, 1.0...  2.67 us
    pallas_call x1, Pallas kernels, pack(): pl.pallas_call(functools.partial(pack_kernel, count, steps), in_specs=[pl...  1.56 us
    unnamed x14, local copies, waits for them, and re-layouts  1.25 us
  transfers between devices with their start and end apart: 14, of which 7 were waited for; matrix products, arithmetic and copies ran while one was open for 0% of the time, Pallas kernels for 8%

profile of v12, /device:TPU:0, one launch (start us, length us, event | category | flops | bytes accessed | tf_op | source)
XLA Modules:
  0.0 37.7 jit_solution(5128278866640772283)
XLA Ops:
  0.6 0.0 copy-start.4
  0.7 1.6 %pack_inputs.1 = (bf16[640,128]{1,0:T(8,128)(2,1)S(1)}, bf16[640,128]{1,0:T(8,128)(2,1)S(1)}, bf16[640,128]{1,0:T(8,128)(2,1)S(1)}, bf16[640,128]{1,0:T(8,128)(2...) custom-call(bf16[128,1024]{1,0:T(8,128)(2,1)} %refs_2_.6, ...), custom_call_target="tpu_custom_call" | custom-call | bytes 8388608 | tf_op jit(solution)/shard_map/pack_inputs/pallas_call | solution.py:75
  2.2 3.0 %collective-permute-start = (bf16[640,128]{1,0:T(8,128)(2,1)S(1)}, bf16[640,128]{1,0:T(8,128)(2,1)S(1)}, u32[]{:S(2)}, u32[]{:S(2)}) collective-permute-start(bf16[640,128]{1,0:T(8,128)(2,1)S(1)} %get-tuple-element.39), channel_id=1, source_target_pairs={{0,16},{4,20},{8,24},{12,28},{16,0},{20,4},{24,8},{28,12},{1,17},{... | collective-permute-start | bytes 491528 | tf_op jit(solution)/shard_map/ppermute | solution.py:42
  5.3 1.5 %collective-permute-start.1 = (bf16[640,128]{1,0:T(8,128)(2,1)S(1)}, bf16[640,128]{1,0:T(8,128)(2,1)S(1)}, u32[]{:S(2)}, u32[]{:S(2)}) collective-permute-start(bf16[640,128]{1,0:T(8,128)(2,1)S(1)} %get-tuple-element.41), channel_id=1, source_target_pairs={{0,8},{4,12},{8,0},{12,4},{16,24},{20,28},{24,16},{28,20},{1,9},{5... | collective-permute-start | bytes 491528 | tf_op jit(solution)/shard_map/ppermute | solution.py:42
  6.7 0.0 collective-permute-start.2
  6.8 1.5 %collective-permute-start.3 = (bf16[640,128]{1,0:T(8,128)(2,1)S(1)}, bf16[640,128]{1,0:T(8,128)(2,1)S(1)}, u32[]{:S(2)}, u32[]{:S(2)}) collective-permute-start(bf16[640,128]{1,0:T(8,128)(2,1)S(1)} %get-tuple-element.43), channel_id=1, source_target_pairs={{0,28},{4,24},{8,20},{12,16},{16,12},{20,8},{24,4},{28,0},{1,29},{... | collective-permute-start | bytes 491528 | tf_op jit(solution)/shard_map/ppermute | solution.py:42
  8.3 1.6 %collective-permute-start.4 = (bf16[640,128]{1,0:T(8,128)(2,1)S(1)}, bf16[640,128]{1,0:T(8,128)(2,1)S(1)}, u32[]{:S(2)}, u32[]{:S(2)}) collective-permute-start(bf16[640,128]{1,0:T(8,128)(2,1)S(1)} %get-tuple-element.44), channel_id=1, source_target_pairs={{0,20},{4,16},{8,28},{12,24},{16,4},{20,0},{24,12},{28,8},{1,21},{... | collective-permute-start | bytes 491528 | tf_op jit(solution)/shard_map/ppermute | solution.py:42
  9.9 0.0 collective-permute-done.refs_4_.refs_1_
  9.9 0.1 collective-permute-start.5
  10.0 2.4 %collective-permute-done.1.refs_2_ = bf16[640,128]{1,0:T(8,128)(2,1)S(1)} collective-permute-done((bf16[640,128]{1,0:T(8,128)(2,1)S(1)}, bf16[640,128]{1,0:T(8,128)(2,1)S(1)}, u32[]{:S(2)}, u32[]{:S(2)}) %collective-permute-start.1) | collective-permute-done | bytes 163872 | tf_op jit(solution)/shard_map/ppermute | solution.py:42
  12.4 0.0 copy-start.5
  12.4 1.2 %copy-done.5 = bf16[4,512,256]{2,1,0:T(8,128)(2,1)S(1)} copy-done((bf16[4,512,256]{2,1,0:T(8,128)(2,1)S(1)}, bf16[4,512,256]{2,1,0:T(8,128)(2,1)}, u32[]{:S(2)}) %copy-start.5) | copy-done | bytes 1048600
  13.6 0.4 %stage_tables.1 = (bf16[640,128]{1,0:T(8,128)(2,1)S(1)}, f32[3,3,1024]{2,1,0:T(4,128)S(1)}, bf16[4,512,256]{2,1,0:T(8,128)(2,1)S(1)}, bf16[4,256,512]{2,1,0:T(8,128)(2,1)S(1)}) custom-call(bf16[640,128]{1,0:T(8,128)(2,1)S(1)} %get-tuple-element.38.refs_0_, f32[3,3,1024]{2,1,0:T(4,128)S(1)} %copy-done.6, bf16[4,512,256]{2,1,0:T(8,128)(2,1)S(1)} %copy-done.5, ...), custom_call_target="tpu_custom_call" | custom-call | bytes 8388608 | tf_op jit(solution)/shard_map/stage_tables/pallas_call | solution.py:180
  14.0 1.4 %collective-permute-done.2.refs_3_ = bf16[640,128]{1,0:T(8,128)(2,1)S(1)} collective-permute-done((bf16[640,128]{1,0:T(8,128)(2,1)S(1)}, bf16[640,128]{1,0:T(8,128)(2,1)S(1)}, u32[]{:S(2)}, u32[]{:S(2)}) %collective-permute-start.2) | collective-permute-done | bytes 163872 | tf_op jit(solution)/shard_map/ppermute | solution.py:42
  15.5 3.0 %collective-permute-done.3.refs_4_ = bf16[640,128]{1,0:T(8,128)(2,1)S(1)} collective-permute-done((bf16[640,128]{1,0:T(8,128)(2,1)S(1)}, bf16[640,128]{1,0:T(8,128)(2,1)S(1)}, u32[]{:S(2)}, u32[]{:S(2)}) %collective-permute-start.3) | collective-permute-done | bytes 163872 | tf_op jit(solution)/shard_map/ppermute | solution.py:42
  18.5 2.0 %collective-permute-done.4.refs_5_ = bf16[640,128]{1,0:T(8,128)(2,1)S(1)} collective-permute-done((bf16[640,128]{1,0:T(8,128)(2,1)S(1)}, bf16[640,128]{1,0:T(8,128)(2,1)S(1)}, u32[]{:S(2)}, u32[]{:S(2)}) %collective-permute-start.4) | collective-permute-done | bytes 163872 | tf_op jit(solution)/shard_map/ppermute | solution.py:42
  20.5 0.0 collective-permute-done.5.refs_6_
  20.5 0.0 collective-permute-done.6.refs_7_
  20.5 0.0 copy-start.3
  20.5 2.7 %channel_operator.1 = (bf16[416,128]{1,0:T(8,128)(2,1)S(1)}, bf16[416,128]{1,0:T(8,128)(2,1)S(1)}, bf16[416,128]{1,0:T(8,128)(2,1)S(1)}, bf16[416,128]{1,0:T(8,1...) custom-call(bf16[640,128]{1,0:T(8,128)(2,1)S(1)} %get-tuple-element., ...), custom_call_target="tpu_custom_call" | custom-call | tf_op jit(solution)/shard_map/channel_operator/pallas_call | solution.py:354
  23.2 2.2 %collective-permute-start.11 = (bf16[416,128]{1,0:T(8,128)(2,1)S(1)}, bf16[416,128]{1,0:T(8,128)(2,1)S(1)}, u32[]{:S(2)}, u32[]{:S(2)}) collective-permute-start(bf16[416,128]{1,0:T(8,128)(2,1)S(1)} %get-tuple-element.55), channel_id=1, source_target_pairs={{0,24},{4,28},{8,16},{12,20},{16,8},{20,12},{24,0},{28,4},{1,25},{... | collective-permute-start | bytes 319496 | tf_op jit(solution)/shard_map/ppermute | solution.py:42
  25.4 0.9 %collective-permute-start.13 = (bf16[416,128]{1,0:T(8,128)(2,1)S(1)}, bf16[416,128]{1,0:T(8,128)(2,1)S(1)}, u32[]{:S(2)}, u32[]{:S(2)}) collective-permute-start(bf16[416,128]{1,0:T(8,128)(2,1)S(1)} %get-tuple-element.57), channel_id=1, source_target_pairs={{0,28},{4,24},{8,20},{12,16},{16,12},{20,8},{24,4},{28,0},{1,29},{... | collective-permute-start | bytes 319496 | tf_op jit(solution)/shard_map/ppermute | solution.py:42
  26.3 1.5 %collective-permute-start.9 = (bf16[416,128]{1,0:T(8,128)(2,1)S(1)}, bf16[416,128]{1,0:T(8,128)(2,1)S(1)}, u32[]{:S(2)}, u32[]{:S(2)}) collective-permute-start(bf16[416,128]{1,0:T(8,128)(2,1)S(1)} %get-tuple-element.52), channel_id=1, source_target_pairs={{0,16},{4,20},{8,24},{12,28},{16,0},{20,4},{24,8},{28,12},{1,17},{... | collective-permute-start | bytes 319496 | tf_op jit(solution)/shard_map/ppermute | solution.py:42
  27.8 1.2 %collective-permute-start.10 = (bf16[416,128]{1,0:T(8,128)(2,1)S(1)}, bf16[416,128]{1,0:T(8,128)(2,1)S(1)}, u32[]{:S(2)}, u32[]{:S(2)}) collective-permute-start(bf16[416,128]{1,0:T(8,128)(2,1)S(1)} %get-tuple-element.53), channel_id=1, source_target_pairs={{0,8},{4,12},{8,0},{12,4},{16,24},{20,28},{24,16},{28,20},{1,9},{5... | collective-permute-start | bytes 319496 | tf_op jit(solution)/shard_map/ppermute | solution.py:42
  29.0 1.1 %collective-permute-done.11.refs_1_ = bf16[416,128]{1,0:T(8,128)(2,1)S(1)} collective-permute-done((bf16[416,128]{1,0:T(8,128)(2,1)S(1)}, bf16[416,128]{1,0:T(8,128)(2,1)S(1)}, u32[]{:S(2)}, u32[]{:S(2)}) %collective-permute-start.11) | collective-permute-done | bytes 106528 | tf_op jit(solution)/shard_map/ppermute | solution.py:42
  30.1 0.0 collective-permute-start.7
  30.1 2.3 %collective-permute-start.8 = (bf16[416,128]{1,0:T(8,128)(2,1)S(1)}, bf16[416,128]{1,0:T(8,128)(2,1)S(1)}, u32[]{:S(2)}, u32[]{:S(2)}) collective-permute-start(bf16[416,128]{1,0:T(8,128)(2,1)S(1)} %get-tuple-element.51), channel_id=1, source_target_pairs={{0,12},{4,8},{8,4},{12,0},{16,28},{20,24},{24,20},{28,16},{1,13},{... | collective-permute-start | bytes 319496 | tf_op jit(solution)/shard_map/ppermute | solution.py:42
  32.4 1.4 %token_outputs.3 = (bf16[128,1024]{1,0:T(8,128)(2,1)}, bf16[128,1024]{1,0:T(8,128)(2,1)}, bf16[128,1024]{1,0:T(8,128)(2,1)}, bf16[128,1024]{1,0:T(8,128)(2,1)}, ...) custom-call(bf16[416,128]{1,0:T(8,128)(2,1)S(1)} %get-tuple-element.54.refs_0_, ...), custom_call_target="tpu_custom_call" | custom-call | bytes 4194304 | tf_op jit(solution)/shard_map/token_outputs/pallas_call | solution.py:445
  33.9 0.6 %collective-permute-done.9.refs_0_ = bf16[416,128]{1,0:T(8,128)(2,1)S(1)} collective-permute-done((bf16[416,128]{1,0:T(8,128)(2,1)S(1)}, bf16[416,128]{1,0:T(8,128)(2,1)S(1)}, u32[]{:S(2)}, u32[]{:S(2)}) %collective-permute-start.9) | collective-permute-done | bytes 106528 | tf_op jit(solution)/shard_map/ppermute | solution.py:42
  34.5 1.0 %token_outputs.4 = (bf16[128,1024]{1,0:T(8,128)(2,1)}, bf16[128,1024]{1,0:T(8,128)(2,1)}, bf16[128,1024]{1,0:T(8,128)(2,1)}, bf16[128,1024]{1,0:T(8,128)(2,1)}, ...) custom-call(bf16[416,128]{1,0:T(8,128)(2,1)S(1)} %collective-permute, ...), custom_call_target="tpu_custom_call", output_to_operand_aliasing={{0}: (7, {}), {1}: (8, {}), {2}: (9, {}), {3}: (10, {}), {4... | custom-call | bytes 4194304 | tf_op jit(solution)/shard_map/token_outputs/pallas_call | solution.py:445
  35.5 1.2 %collective-permute-done.7.refs_0_ = bf16[416,128]{1,0:T(8,128)(2,1)S(1)} collective-permute-done((bf16[416,128]{1,0:T(8,128)(2,1)S(1)}, bf16[416,128]{1,0:T(8,128)(2,1)S(1)}, u32[]{:S(2)}, u32[]{:S(2)}) %collective-permute-start.7) | collective-permute-done | bytes 106528 | tf_op jit(solution)/shard_map/ppermute | solution.py:42
  36.7 1.0 %token_outputs.5 = (bf16[128,1024]{1,0:T(8,128)(2,1)}, bf16[128,1024]{1,0:T(8,128)(2,1)}, bf16[128,1024]{1,0:T(8,128)(2,1)}, bf16[128,1024]{1,0:T(8,128)(2,1)}, ...) custom-call(bf16[416,128]{1,0:T(8,128)(2,1)S(1)} %collective-permute, ...), custom_call_target="tpu_custom_call", output_to_operand_aliasing={{0}: (7, {}), {1}: (8, {}), {2}: (9, {}), {3}: (10, {}), {4... | custom-call | bytes 4194304 | tf_op jit(solution)/shard_map/token_outputs/pallas_call | solution.py:445
  (16 shorter events, 0.0 us)
Async XLA Ops:
  0.6 11.8 %copy-start.4 = (bf16[4,256,512]{2,1,0:T(8,128)(2,1)S(1)}, bf16[4,256,512]{2,1,0:T(8,128)(2,1)}, u32[]{:S(2)}) copy-start(bf16[4,256,512]{2,1,0:T(8,128)(2,1)} %constant.5.clone.refs_3_) | copy-start | bytes 3145732
  0.6 11.7 %copy-start.6 = (f32[3,3,1024]{2,1,0:T(4,128)S(1)}, f32[3,3,1024]{2,1,0:T(4,128)}, u32[]{:S(2)}) copy-start(f32[3,3,1024]{2,1,0:T(4,128)} %refs_6_.5) | copy-start | bytes 110596
  2.2 7.7 %collective-permute-start = (bf16[640,128]{1,0:T(8,128)(2,1)S(1)}, bf16[640,128]{1,0:T(8,128)(2,1)S(1)}, u32[]{:S(2)}, u32[]{:S(2)}) collective-permute-start(bf16[640,128]{1,0:T(8,128)(2,1)S(1)} %get-tuple-element.39), channel_id=1, source_target_pairs={{0,16},{4,20},{8,24},{12,28},{16,0},{20,4},{24,8},{28,12},{1,17},{... | collective-permute-start | bytes 491528 | tf_op jit(solution)/shard_map/ppermute | solution.py:42
  5.3 7.1 %collective-permute-start.1 = (bf16[640,128]{1,0:T(8,128)(2,1)S(1)}, bf16[640,128]{1,0:T(8,128)(2,1)S(1)}, u32[]{:S(2)}, u32[]{:S(2)}) collective-permute-start(bf16[640,128]{1,0:T(8,128)(2,1)S(1)} %get-tuple-element.41), channel_id=1, source_target_pairs={{0,8},{4,12},{8,0},{12,4},{16,24},{20,28},{24,16},{28,20},{1,9},{5... | collective-permute-start | bytes 491528 | tf_op jit(solution)/shard_map/ppermute | solution.py:42
  6.7 8.7 %collective-permute-start.2 = (bf16[640,128]{1,0:T(8,128)(2,1)S(1)}, bf16[640,128]{1,0:T(8,128)(2,1)S(1)}, u32[]{:S(2)}, u32[]{:S(2)}) collective-permute-start(bf16[640,128]{1,0:T(8,128)(2,1)S(1)} %get-tuple-element.42), channel_id=1, source_target_pairs={{0,24},{4,28},{8,16},{12,20},{16,8},{20,12},{24,0},{28,4},{1,25},{... | collective-permute-start | bytes 491528 | tf_op jit(solution)/shard_map/ppermute | solution.py:42
  6.8 11.7 %collective-permute-start.3 = (bf16[640,128]{1,0:T(8,128)(2,1)S(1)}, bf16[640,128]{1,0:T(8,128)(2,1)S(1)}, u32[]{:S(2)}, u32[]{:S(2)}) collective-permute-start(bf16[640,128]{1,0:T(8,128)(2,1)S(1)} %get-tuple-element.43), channel_id=1, source_target_pairs={{0,28},{4,24},{8,20},{12,16},{16,12},{20,8},{24,4},{28,0},{1,29},{... | collective-permute-start | bytes 491528 | tf_op jit(solution)/shard_map/ppermute | solution.py:42
  8.3 12.2 %collective-permute-start.4 = (bf16[640,128]{1,0:T(8,128)(2,1)S(1)}, bf16[640,128]{1,0:T(8,128)(2,1)S(1)}, u32[]{:S(2)}, u32[]{:S(2)}) collective-permute-start(bf16[640,128]{1,0:T(8,128)(2,1)S(1)} %get-tuple-element.44), channel_id=1, source_target_pairs={{0,20},{4,16},{8,28},{12,24},{16,4},{20,0},{24,12},{28,8},{1,21},{... | collective-permute-start | bytes 491528 | tf_op jit(solution)/shard_map/ppermute | solution.py:42
  9.9 10.6 %collective-permute-start.5 = (bf16[640,128]{1,0:T(8,128)(2,1)S(1)}, bf16[640,128]{1,0:T(8,128)(2,1)S(1)}, u32[]{:S(2)}, u32[]{:S(2)}) collective-permute-start(bf16[640,128]{1,0:T(8,128)(2,1)S(1)} %get-tuple-element.45), channel_id=1, source_target_pairs={{0,12},{4,8},{8,4},{12,0},{16,28},{20,24},{24,20},{28,16},{1,13},{... | collective-permute-start | bytes 491528 | tf_op jit(solution)/shard_map/ppermute | solution.py:42
  12.4 8.1 %collective-permute-start.6 = (bf16[640,128]{1,0:T(8,128)(2,1)S(1)}, bf16[640,128]{1,0:T(8,128)(2,1)S(1)}, u32[]{:S(2)}, u32[]{:S(2)}) collective-permute-start(bf16[640,128]{1,0:T(8,128)(2,1)S(1)} %get-tuple-element.46), channel_id=1, source_target_pairs={{0,4},{4,0},{8,12},{12,8},{16,20},{20,16},{24,28},{28,24},{1,5},{5... | collective-permute-start | bytes 491528 | tf_op jit(solution)/shard_map/ppermute | solution.py:42
  12.4 1.2 %copy-start.5 = (bf16[4,512,256]{2,1,0:T(8,128)(2,1)S(1)}, bf16[4,512,256]{2,1,0:T(8,128)(2,1)}, u32[]{:S(2)}) copy-start(bf16[4,512,256]{2,1,0:T(8,128)(2,1)} %constant.4.clone.refs_2_) | copy-start | bytes 3145732
  20.5 11.9 %copy-start = (bf16[128,1024]{1,0:T(8,128)(2,1)S(1)}, bf16[128,1024]{1,0:T(8,128)(2,1)}, u32[]{:S(2)}) copy-start(bf16[128,1024]{1,0:T(8,128)(2,1)} %refs_2_.6) | copy-start | bytes 786436
  20.5 11.9 %copy-start.1 = (bf16[128,1024]{1,0:T(8,128)(2,1)S(1)}, bf16[128,1024]{1,0:T(8,128)(2,1)}, u32[]{:S(2)}) copy-start(bf16[128,1024]{1,0:T(8,128)(2,1)} %refs_3_.6) | copy-start | bytes 786436
  20.5 11.9 %copy-start.2 = (bf16[128,1024]{1,0:T(8,128)(2,1)S(1)}, bf16[128,1024]{1,0:T(8,128)(2,1)}, u32[]{:S(2)}) copy-start(bf16[128,1024]{1,0:T(8,128)(2,1)} %refs_4_.7) | copy-start | bytes 786436
  20.5 11.9 %copy-start.3 = (bf16[128,1024]{1,0:T(8,128)(2,1)S(1)}, bf16[128,1024]{1,0:T(8,128)(2,1)}, u32[]{:S(2)}) copy-start(bf16[128,1024]{1,0:T(8,128)(2,1)} %refs_5_.5) | copy-start | bytes 786436
  23.2 6.9 %collective-permute-start.11 = (bf16[416,128]{1,0:T(8,128)(2,1)S(1)}, bf16[416,128]{1,0:T(8,128)(2,1)S(1)}, u32[]{:S(2)}, u32[]{:S(2)}) collective-permute-start(bf16[416,128]{1,0:T(8,128)(2,1)S(1)} %get-tuple-element.55), channel_id=1, source_target_pairs={{0,24},{4,28},{8,16},{12,20},{16,8},{20,12},{24,0},{28,4},{1,25},{... | collective-permute-start | bytes 319496 | tf_op jit(solution)/shard_map/ppermute | solution.py:42
  25.4 4.7 %collective-permute-start.12 = (bf16[416,128]{1,0:T(8,128)(2,1)S(1)}, bf16[416,128]{1,0:T(8,128)(2,1)S(1)}, u32[]{:S(2)}, u32[]{:S(2)}) collective-permute-start(bf16[416,128]{1,0:T(8,128)(2,1)S(1)} %get-tuple-element.56), channel_id=1, source_target_pairs={{0,4},{4,0},{8,12},{12,8},{16,20},{20,16},{24,28},{28,24},{1,5},{5... | collective-permute-start | bytes 319496 | tf_op jit(solution)/shard_map/ppermute | solution.py:42
  25.4 7.0 %collective-permute-start.13 = (bf16[416,128]{1,0:T(8,128)(2,1)S(1)}, bf16[416,128]{1,0:T(8,128)(2,1)S(1)}, u32[]{:S(2)}, u32[]{:S(2)}) collective-permute-start(bf16[416,128]{1,0:T(8,128)(2,1)S(1)} %get-tuple-element.57), channel_id=1, source_target_pairs={{0,28},{4,24},{8,20},{12,16},{16,12},{20,8},{24,4},{28,0},{1,29},{... | collective-permute-start | bytes 319496 | tf_op jit(solution)/shard_map/ppermute | solution.py:42
  26.3 8.1 %collective-permute-start.9 = (bf16[416,128]{1,0:T(8,128)(2,1)S(1)}, bf16[416,128]{1,0:T(8,128)(2,1)S(1)}, u32[]{:S(2)}, u32[]{:S(2)}) collective-permute-start(bf16[416,128]{1,0:T(8,128)(2,1)S(1)} %get-tuple-element.52), channel_id=1, source_target_pairs={{0,16},{4,20},{8,24},{12,28},{16,0},{20,4},{24,8},{28,12},{1,17},{... | collective-permute-start | bytes 319496 | tf_op jit(solution)/shard_map/ppermute | solution.py:42
  27.8 6.7 %collective-permute-start.10 = (bf16[416,128]{1,0:T(8,128)(2,1)S(1)}, bf16[416,128]{1,0:T(8,128)(2,1)S(1)}, u32[]{:S(2)}, u32[]{:S(2)}) collective-permute-start(bf16[416,128]{1,0:T(8,128)(2,1)S(1)} %get-tuple-element.53), channel_id=1, source_target_pairs={{0,8},{4,12},{8,0},{12,4},{16,24},{20,28},{24,16},{28,20},{1,9},{5... | collective-permute-start | bytes 319496 | tf_op jit(solution)/shard_map/ppermute | solution.py:42
  30.1 6.6 %collective-permute-start.7 = (bf16[416,128]{1,0:T(8,128)(2,1)S(1)}, bf16[416,128]{1,0:T(8,128)(2,1)S(1)}, u32[]{:S(2)}, u32[]{:S(2)}) collective-permute-start(bf16[416,128]{1,0:T(8,128)(2,1)S(1)} %get-tuple-element.50), channel_id=1, source_target_pairs={{0,20},{4,16},{8,28},{12,24},{16,4},{20,0},{24,12},{28,8},{1,21},{... | collective-permute-start | bytes 319496 | tf_op jit(solution)/shard_map/ppermute | solution.py:42
  30.1 6.6 %collective-permute-start.8 = (bf16[416,128]{1,0:T(8,128)(2,1)S(1)}, bf16[416,128]{1,0:T(8,128)(2,1)S(1)}, u32[]{:S(2)}, u32[]{:S(2)}) collective-permute-start(bf16[416,128]{1,0:T(8,128)(2,1)S(1)} %get-tuple-element.51), channel_id=1, source_target_pairs={{0,12},{4,8},{8,4},{12,0},{16,28},{20,24},{24,20},{28,16},{1,13},{... | collective-permute-start | bytes 319496 | tf_op jit(solution)/shard_map/ppermute | solution.py:42

commit v13 on v12

--- a/solution.py
+++ b/solution.py
@@ -16,6 +16,7 @@
 TILE = 16
 PAD = 8
 CHUNK = 32
+PARTS = 4
 RIM = 2
 PIECES = 2
 MIB = 1024 * 1024
@@ -56,14 +57,24 @@
     held, sems = refs[count + len(steps) : -1], refs[-1]
     tokens = sources[0].shape[0]
     me = lax.axis_index("ctx")
+    part = tokens // PARTS
     arriving = [
-        pltpu.make_async_copy(source, target, sems.at[at])
+        [
+            pltpu.make_async_copy(
+                source.at[pl.ds(piece * part, part), :],
+                target.at[pl.ds(piece * part, part), :],
+                sems.at[at, piece],
+            )
+            for piece in range(PARTS)
+        ]
         for at, (source, target) in enumerate(zip(sources, held))
     ]
-    for copy in arriving:
-        copy.start()
+    for copies in arriving:
+        for copy in copies:
+            copy.start()
     for at, source in enumerate(held):
-        arriving[at].wait()
+        for copy in arriving[at]:
+            copy.wait()
         rows = slice(at * tokens, (at + 1) * tokens)
         for step, target in zip(steps, packed):
             target[rows, :] = source[:, lanes_of(me ^ step)].astype(BF16)
@@ -79,7 +90,7 @@
         out_shape=[jax.ShapeDtypeStruct((count * tokens, LANES), BF16)] * len(steps),
         scratch_shapes=[
             *[pltpu.VMEM(array.shape, array.dtype) for array in arrays],
-            pltpu.SemaphoreType.DMA((count,)),
+            pltpu.SemaphoreType.DMA((count, PARTS)),
         ],
         compiler_params=pltpu.CompilerParams(vmem_limit_bytes=PACK_VMEM),
         cost_estimate=pl.CostEstimate(flops=0, bytes_accessed=8 * MIB, transcendentals=0),
@@ -272,29 +283,17 @@
     for step in range(size // TILE):
         real = slice(step * TILE, (step + 1) * TILE)
         imag = slice(size + step * TILE, size + (step + 1) * TILE)
-        prod, filt = spectrum(0, real, imag), spectrum(1, real, imag)
-        for at, mixed in enumerate((prod, filt)):
-            lanes = slice(at * LANES, (at + 1) * LANES)
-            for q, pair in enumerate(mixed):
-                spectra[q, real, lanes], spectra[q, imag, lanes] = pair
+        prod, filt, grad = (spectrum(at, real, imag) for at in range(3))
         keep(0, real, imag, times(prod, filt))
+        keep(1, real, imag, conj_times(filt, grad))
+        keep(2, real, imag, conj_times(prod, grad))
     for r in range(PHASES):
-        result = transform(backward[r], products[r, :, :LANES])
-        conv[pl.ds(PAD + r, size, stride=PHASES), :] = result.astype(BF16).astype(F32)
-    for step in range(size // TILE):
-        real = slice(step * TILE, (step + 1) * TILE)
-        imag = slice(size + step * TILE, size + (step + 1) * TILE)
-        grad = spectrum(2, real, imag)
-        for at in range(2):
-            lanes = slice(at * LANES, (at + 1) * LANES)
-            known = [(spectra[q, real, lanes], spectra[q, imag, lanes]) for q in range(PHASES)]
-            keep(2 - at, real, imag, conj_times(known, grad))
-    for r in range(PHASES):
-        result = transform(backward[r], products[r, :, LANES:])
-        conv_grad[pl.ds(PAD + r, size, stride=PHASES), :] = (
-            result[:, :LANES].astype(BF16).astype(F32)
-        )
-        filter_grad[pl.ds(r, size, stride=PHASES), :] = result[:, LANES:] * grad_scale
+        result = transform(backward[r], products[r])
+        for at, ref in enumerate((conv, conv_grad)):
+            ref[pl.ds(PAD + r, size, stride=PHASES), :] = (
+                result[:, at * LANES : (at + 1) * LANES].astype(BF16).astype(F32)
+            )
+        filter_grad[pl.ds(r, size, stride=PHASES), :] = result[:, 2 * LANES :] * grad_scale
 
     totals = [[None] * tap_count for _ in range(3)]
 

time: 37.9 us -> 38.4 us (1.013)
  Pallas kernels: 8.11 us -> 8.68 us
  transfers between devices with their start and end apart: 14 -> 14, of which waited for: 7 -> 7; matrix products, arithmetic and copies ran while one was open for 0% -> 0% of each run, Pallas kernels for 8% -> 7%
where the time goes in v13:
time: 38.4 us; the launch traced here: 38.3 us
  starting transfers between devices  15.9 us (41%)
  waiting for transfers between devices  11.7 us (30%)
  Pallas kernels  8.68 us (23%)
  local copies, waits for them, and re-layouts  1.25 us (3%)
  between operations  0.74 us (2%)
    ppermute x14, starting transfers between devices, exchange(): lax.ppermute(block, 'ctx', [(i, i ^ step) for i in range(peers)])  15.9 us
    ppermute x14, waiting for transfers between devices, exchange(): lax.ppermute(block, 'ctx', [(i, i ^ step) for i in range(peers)])  11.7 us
    pallas_call x3, Pallas kernels, token_step(): pl.pallas_call(functools.partial(token_kernel, steps, extra_rows(short_we...  3.46 us
    pallas_call x1, Pallas kernels, channel_step(): pl.pallas_call(functools.partial(channel_kernel, tokens, heard, told, 1.0...  3.04 us
    pallas_call x1, Pallas kernels, pack(): pl.pallas_call(functools.partial(pack_kernel, count, steps), in_specs=[pl...  1.77 us
    unnamed x14, local copies, waits for them, and re-layouts  1.25 us
  transfers between devices with their start and end apart: 14, of which 7 were waited for; matrix products, arithmetic and copies ran while one was open for 0% of the time, Pallas kernels for 7%

profile of v13, /device:TPU:0, one launch (start us, length us, event | category | flops | bytes accessed | tf_op | source)
XLA Modules:
  0.0 38.3 jit_solution(8827790500055591482)
XLA Ops:
  0.6 0.0 copy-start.4
  0.7 1.8 %pack_inputs.1 = (bf16[640,128]{1,0:T(8,128)(2,1)S(1)}, bf16[640,128]{1,0:T(8,128)(2,1)S(1)}, bf16[640,128]{1,0:T(8,128)(2,1)S(1)}, bf16[640,128]{1,0:T(8,128)(2...) custom-call(bf16[128,1024]{1,0:T(8,128)(2,1)} %refs_2_.6, ...), custom_call_target="tpu_custom_call" | custom-call | bytes 8388608 | tf_op jit(solution)/shard_map/pack_inputs/pallas_call | solution.py:86
  2.4 3.0 %collective-permute-start = (bf16[640,128]{1,0:T(8,128)(2,1)S(1)}, bf16[640,128]{1,0:T(8,128)(2,1)S(1)}, u32[]{:S(2)}, u32[]{:S(2)}) collective-permute-start(bf16[640,128]{1,0:T(8,128)(2,1)S(1)} %get-tuple-element.39), channel_id=1, source_target_pairs={{0,16},{4,20},{8,24},{12,28},{16,0},{20,4},{24,8},{28,12},{1,17},{... | collective-permute-start | bytes 491528 | tf_op jit(solution)/shard_map/ppermute | solution.py:43
  5.5 1.5 %collective-permute-start.1 = (bf16[640,128]{1,0:T(8,128)(2,1)S(1)}, bf16[640,128]{1,0:T(8,128)(2,1)S(1)}, u32[]{:S(2)}, u32[]{:S(2)}) collective-permute-start(bf16[640,128]{1,0:T(8,128)(2,1)S(1)} %get-tuple-element.41), channel_id=1, source_target_pairs={{0,8},{4,12},{8,0},{12,4},{16,24},{20,28},{24,16},{28,20},{1,9},{5... | collective-permute-start | bytes 491528 | tf_op jit(solution)/shard_map/ppermute | solution.py:43
  7.0 0.0 collective-permute-start.2
  7.0 1.5 %collective-permute-start.3 = (bf16[640,128]{1,0:T(8,128)(2,1)S(1)}, bf16[640,128]{1,0:T(8,128)(2,1)S(1)}, u32[]{:S(2)}, u32[]{:S(2)}) collective-permute-start(bf16[640,128]{1,0:T(8,128)(2,1)S(1)} %get-tuple-element.43), channel_id=1, source_target_pairs={{0,28},{4,24},{8,20},{12,16},{16,12},{20,8},{24,4},{28,0},{1,29},{... | collective-permute-start | bytes 491528 | tf_op jit(solution)/shard_map/ppermute | solution.py:43
  8.5 1.6 %collective-permute-start.4 = (bf16[640,128]{1,0:T(8,128)(2,1)S(1)}, bf16[640,128]{1,0:T(8,128)(2,1)S(1)}, u32[]{:S(2)}, u32[]{:S(2)}) collective-permute-start(bf16[640,128]{1,0:T(8,128)(2,1)S(1)} %get-tuple-element.44), channel_id=1, source_target_pairs={{0,20},{4,16},{8,28},{12,24},{16,4},{20,0},{24,12},{28,8},{1,21},{... | collective-permute-start | bytes 491528 | tf_op jit(solution)/shard_map/ppermute | solution.py:43
  10.1 0.0 collective-permute-done.refs_4_.refs_1_
  10.1 0.1 collective-permute-start.5
  10.2 2.4 %collective-permute-done.1.refs_2_ = bf16[640,128]{1,0:T(8,128)(2,1)S(1)} collective-permute-done((bf16[640,128]{1,0:T(8,128)(2,1)S(1)}, bf16[640,128]{1,0:T(8,128)(2,1)S(1)}, u32[]{:S(2)}, u32[]{:S(2)}) %collective-permute-start.1) | collective-permute-done | bytes 163872 | tf_op jit(solution)/shard_map/ppermute | solution.py:43
  12.6 0.0 collective-permute-start.6
  12.6 0.0 copy-start.5
  12.6 1.2 %copy-done.5 = bf16[4,512,256]{2,1,0:T(8,128)(2,1)S(1)} copy-done((bf16[4,512,256]{2,1,0:T(8,128)(2,1)S(1)}, bf16[4,512,256]{2,1,0:T(8,128)(2,1)}, u32[]{:S(2)}) %copy-start.5) | copy-done | bytes 1048600
  13.8 0.4 %stage_tables.1 = (bf16[640,128]{1,0:T(8,128)(2,1)S(1)}, f32[3,3,1024]{2,1,0:T(4,128)S(1)}, bf16[4,512,256]{2,1,0:T(8,128)(2,1)S(1)}, bf16[4,256,512]{2,1,0:T(8,128)(2,1)S(1)}) custom-call(bf16[640,128]{1,0:T(8,128)(2,1)S(1)} %get-tuple-element.38.refs_0_, f32[3,3,1024]{2,1,0:T(4,128)S(1)} %copy-done.6, bf16[4,512,256]{2,1,0:T(8,128)(2,1)S(1)} %copy-done.5, ...), custom_call_target="tpu_custom_call" | custom-call | bytes 8388608 | tf_op jit(solution)/shard_map/stage_tables/pallas_call | solution.py:191
  14.3 1.4 %collective-permute-done.2.refs_3_ = bf16[640,128]{1,0:T(8,128)(2,1)S(1)} collective-permute-done((bf16[640,128]{1,0:T(8,128)(2,1)S(1)}, bf16[640,128]{1,0:T(8,128)(2,1)S(1)}, u32[]{:S(2)}, u32[]{:S(2)}) %collective-permute-start.2) | collective-permute-done | bytes 163872 | tf_op jit(solution)/shard_map/ppermute | solution.py:43
  15.7 3.0 %collective-permute-done.3.refs_4_ = bf16[640,128]{1,0:T(8,128)(2,1)S(1)} collective-permute-done((bf16[640,128]{1,0:T(8,128)(2,1)S(1)}, bf16[640,128]{1,0:T(8,128)(2,1)S(1)}, u32[]{:S(2)}, u32[]{:S(2)}) %collective-permute-start.3) | collective-permute-done | bytes 163872 | tf_op jit(solution)/shard_map/ppermute | solution.py:43
  18.7 2.0 %collective-permute-done.4.refs_5_ = bf16[640,128]{1,0:T(8,128)(2,1)S(1)} collective-permute-done((bf16[640,128]{1,0:T(8,128)(2,1)S(1)}, bf16[640,128]{1,0:T(8,128)(2,1)S(1)}, u32[]{:S(2)}, u32[]{:S(2)}) %collective-permute-start.4) | collective-permute-done | bytes 163872 | tf_op jit(solution)/shard_map/ppermute | solution.py:43
  20.7 0.0 collective-permute-done.5.refs_6_
  20.7 0.0 collective-permute-done.6.refs_7_
  20.7 0.0 copy-start.3
  20.7 3.0 %channel_operator.1 = (bf16[416,128]{1,0:T(8,128)(2,1)S(1)}, bf16[416,128]{1,0:T(8,128)(2,1)S(1)}, bf16[416,128]{1,0:T(8,128)(2,1)S(1)}, bf16[416,128]{1,0:T(8,1...) custom-call(bf16[640,128]{1,0:T(8,128)(2,1)S(1)} %get-tuple-element., ...), custom_call_target="tpu_custom_call" | custom-call | tf_op jit(solution)/shard_map/channel_operator/pallas_call | solution.py:353
  23.8 2.2 %collective-permute-start.11 = (bf16[416,128]{1,0:T(8,128)(2,1)S(1)}, bf16[416,128]{1,0:T(8,128)(2,1)S(1)}, u32[]{:S(2)}, u32[]{:S(2)}) collective-permute-start(bf16[416,128]{1,0:T(8,128)(2,1)S(1)} %get-tuple-element.55), channel_id=1, source_target_pairs={{0,24},{4,28},{8,16},{12,20},{16,8},{20,12},{24,0},{28,4},{1,25},{... | collective-permute-start | bytes 319496 | tf_op jit(solution)/shard_map/ppermute | solution.py:43
  26.0 0.9 %collective-permute-start.13 = (bf16[416,128]{1,0:T(8,128)(2,1)S(1)}, bf16[416,128]{1,0:T(8,128)(2,1)S(1)}, u32[]{:S(2)}, u32[]{:S(2)}) collective-permute-start(bf16[416,128]{1,0:T(8,128)(2,1)S(1)} %get-tuple-element.57), channel_id=1, source_target_pairs={{0,28},{4,24},{8,20},{12,16},{16,12},{20,8},{24,4},{28,0},{1,29},{... | collective-permute-start | bytes 319496 | tf_op jit(solution)/shard_map/ppermute | solution.py:43
  26.9 1.4 %collective-permute-start.9 = (bf16[416,128]{1,0:T(8,128)(2,1)S(1)}, bf16[416,128]{1,0:T(8,128)(2,1)S(1)}, u32[]{:S(2)}, u32[]{:S(2)}) collective-permute-start(bf16[416,128]{1,0:T(8,128)(2,1)S(1)} %get-tuple-element.52), channel_id=1, source_target_pairs={{0,16},{4,20},{8,24},{12,28},{16,0},{20,4},{24,8},{28,12},{1,17},{... | collective-permute-start | bytes 319496 | tf_op jit(solution)/shard_map/ppermute | solution.py:43
  28.4 1.2 %collective-permute-start.10 = (bf16[416,128]{1,0:T(8,128)(2,1)S(1)}, bf16[416,128]{1,0:T(8,128)(2,1)S(1)}, u32[]{:S(2)}, u32[]{:S(2)}) collective-permute-start(bf16[416,128]{1,0:T(8,128)(2,1)S(1)} %get-tuple-element.53), channel_id=1, source_target_pairs={{0,8},{4,12},{8,0},{12,4},{16,24},{20,28},{24,16},{28,20},{1,9},{5... | collective-permute-start | bytes 319496 | tf_op jit(solution)/shard_map/ppermute | solution.py:43
  29.6 1.1 %collective-permute-done.11.refs_1_ = bf16[416,128]{1,0:T(8,128)(2,1)S(1)} collective-permute-done((bf16[416,128]{1,0:T(8,128)(2,1)S(1)}, bf16[416,128]{1,0:T(8,128)(2,1)S(1)}, u32[]{:S(2)}, u32[]{:S(2)}) %collective-permute-start.11) | collective-permute-done | bytes 106528 | tf_op jit(solution)/shard_map/ppermute | solution.py:43
  30.6 2.3 %collective-permute-start.8 = (bf16[416,128]{1,0:T(8,128)(2,1)S(1)}, bf16[416,128]{1,0:T(8,128)(2,1)S(1)}, u32[]{:S(2)}, u32[]{:S(2)}) collective-permute-start(bf16[416,128]{1,0:T(8,128)(2,1)S(1)} %get-tuple-element.51), channel_id=1, source_target_pairs={{0,12},{4,8},{8,4},{12,0},{16,28},{20,24},{24,20},{28,16},{1,13},{... | collective-permute-start | bytes 319496 | tf_op jit(solution)/shard_map/ppermute | solution.py:43
  33.0 1.4 %token_outputs.3 = (bf16[128,1024]{1,0:T(8,128)(2,1)}, bf16[128,1024]{1,0:T(8,128)(2,1)}, bf16[128,1024]{1,0:T(8,128)(2,1)}, bf16[128,1024]{1,0:T(8,128)(2,1)}, ...) custom-call(bf16[416,128]{1,0:T(8,128)(2,1)S(1)} %get-tuple-element.54.refs_0_, ...), custom_call_target="tpu_custom_call" | custom-call | bytes 4194304 | tf_op jit(solution)/shard_map/token_outputs/pallas_call | solution.py:444
  34.4 0.6 %collective-permute-done.9.refs_0_ = bf16[416,128]{1,0:T(8,128)(2,1)S(1)} collective-permute-done((bf16[416,128]{1,0:T(8,128)(2,1)S(1)}, bf16[416,128]{1,0:T(8,128)(2,1)S(1)}, u32[]{:S(2)}, u32[]{:S(2)}) %collective-permute-start.9) | collective-permute-done | bytes 106528 | tf_op jit(solution)/shard_map/ppermute | solution.py:43
  35.0 1.0 %token_outputs.4 = (bf16[128,1024]{1,0:T(8,128)(2,1)}, bf16[128,1024]{1,0:T(8,128)(2,1)}, bf16[128,1024]{1,0:T(8,128)(2,1)}, bf16[128,1024]{1,0:T(8,128)(2,1)}, ...) custom-call(bf16[416,128]{1,0:T(8,128)(2,1)S(1)} %collective-permute, ...), custom_call_target="tpu_custom_call", output_to_operand_aliasing={{0}: (7, {}), {1}: (8, {}), {2}: (9, {}), {3}: (10, {}), {4... | custom-call | bytes 4194304 | tf_op jit(solution)/shard_map/token_outputs/pallas_call | solution.py:444
  36.1 1.2 %collective-permute-done.7.refs_0_ = bf16[416,128]{1,0:T(8,128)(2,1)S(1)} collective-permute-done((bf16[416,128]{1,0:T(8,128)(2,1)S(1)}, bf16[416,128]{1,0:T(8,128)(2,1)S(1)}, u32[]{:S(2)}, u32[]{:S(2)}) %collective-permute-start.7) | collective-permute-done | bytes 106528 | tf_op jit(solution)/shard_map/ppermute | solution.py:43
  37.2 1.0 %token_outputs.5 = (bf16[128,1024]{1,0:T(8,128)(2,1)}, bf16[128,1024]{1,0:T(8,128)(2,1)}, bf16[128,1024]{1,0:T(8,128)(2,1)}, bf16[128,1024]{1,0:T(8,128)(2,1)}, ...) custom-call(bf16[416,128]{1,0:T(8,128)(2,1)S(1)} %collective-permute, ...), custom_call_target="tpu_custom_call", output_to_operand_aliasing={{0}: (7, {}), {1}: (8, {}), {2}: (9, {}), {3}: (10, {}), {4... | custom-call | bytes 4194304 | tf_op jit(solution)/shard_map/token_outputs/pallas_call | solution.py:444
  (16 shorter events, 0.0 us)
Async XLA Ops:
  0.6 12.0 %copy-start.4 = (bf16[4,256,512]{2,1,0:T(8,128)(2,1)S(1)}, bf16[4,256,512]{2,1,0:T(8,128)(2,1)}, u32[]{:S(2)}) copy-start(bf16[4,256,512]{2,1,0:T(8,128)(2,1)} %constant.5.clone.refs_3_) | copy-start | bytes 3145732
  0.6 11.9 %copy-start.6 = (f32[3,3,1024]{2,1,0:T(4,128)S(1)}, f32[3,3,1024]{2,1,0:T(4,128)}, u32[]{:S(2)}) copy-start(f32[3,3,1024]{2,1,0:T(4,128)} %refs_6_.5) | copy-start | bytes 110596
  2.4 7.7 %collective-permute-start = (bf16[640,128]{1,0:T(8,128)(2,1)S(1)}, bf16[640,128]{1,0:T(8,128)(2,1)S(1)}, u32[]{:S(2)}, u32[]{:S(2)}) collective-permute-start(bf16[640,128]{1,0:T(8,128)(2,1)S(1)} %get-tuple-element.39), channel_id=1, source_target_pairs={{0,16},{4,20},{8,24},{12,28},{16,0},{20,4},{24,8},{28,12},{1,17},{... | collective-permute-start | bytes 491528 | tf_op jit(solution)/shard_map/ppermute | solution.py:43
  5.5 7.1 %collective-permute-start.1 = (bf16[640,128]{1,0:T(8,128)(2,1)S(1)}, bf16[640,128]{1,0:T(8,128)(2,1)S(1)}, u32[]{:S(2)}, u32[]{:S(2)}) collective-permute-start(bf16[640,128]{1,0:T(8,128)(2,1)S(1)} %get-tuple-element.41), channel_id=1, source_target_pairs={{0,8},{4,12},{8,0},{12,4},{16,24},{20,28},{24,16},{28,20},{1,9},{5... | collective-permute-start | bytes 491528 | tf_op jit(solution)/shard_map/ppermute | solution.py:43
  7.0 8.7 %collective-permute-start.2 = (bf16[640,128]{1,0:T(8,128)(2,1)S(1)}, bf16[640,128]{1,0:T(8,128)(2,1)S(1)}, u32[]{:S(2)}, u32[]{:S(2)}) collective-permute-start(bf16[640,128]{1,0:T(8,128)(2,1)S(1)} %get-tuple-element.42), channel_id=1, source_target_pairs={{0,24},{4,28},{8,16},{12,20},{16,8},{20,12},{24,0},{28,4},{1,25},{... | collective-permute-start | bytes 491528 | tf_op jit(solution)/shard_map/ppermute | solution.py:43
  7.0 11.7 %collective-permute-start.3 = (bf16[640,128]{1,0:T(8,128)(2,1)S(1)}, bf16[640,128]{1,0:T(8,128)(2,1)S(1)}, u32[]{:S(2)}, u32[]{:S(2)}) collective-permute-start(bf16[640,128]{1,0:T(8,128)(2,1)S(1)} %get-tuple-element.43), channel_id=1, source_target_pairs={{0,28},{4,24},{8,20},{12,16},{16,12},{20,8},{24,4},{28,0},{1,29},{... | collective-permute-start | bytes 491528 | tf_op jit(solution)/shard_map/ppermute | solution.py:43
  8.5 12.2 %collective-permute-start.4 = (bf16[640,128]{1,0:T(8,128)(2,1)S(1)}, bf16[640,128]{1,0:T(8,128)(2,1)S(1)}, u32[]{:S(2)}, u32[]{:S(2)}) collective-permute-start(bf16[640,128]{1,0:T(8,128)(2,1)S(1)} %get-tuple-element.44), channel_id=1, source_target_pairs={{0,20},{4,16},{8,28},{12,24},{16,4},{20,0},{24,12},{28,8},{1,21},{... | collective-permute-start | bytes 491528 | tf_op jit(solution)/shard_map/ppermute | solution.py:43
  10.1 10.6 %collective-permute-start.5 = (bf16[640,128]{1,0:T(8,128)(2,1)S(1)}, bf16[640,128]{1,0:T(8,128)(2,1)S(1)}, u32[]{:S(2)}, u32[]{:S(2)}) collective-permute-start(bf16[640,128]{1,0:T(8,128)(2,1)S(1)} %get-tuple-element.45), channel_id=1, source_target_pairs={{0,12},{4,8},{8,4},{12,0},{16,28},{20,24},{24,20},{28,16},{1,13},{... | collective-permute-start | bytes 491528 | tf_op jit(solution)/shard_map/ppermute | solution.py:43
  12.6 8.1 %collective-permute-start.6 = (bf16[640,128]{1,0:T(8,128)(2,1)S(1)}, bf16[640,128]{1,0:T(8,128)(2,1)S(1)}, u32[]{:S(2)}, u32[]{:S(2)}) collective-permute-start(bf16[640,128]{1,0:T(8,128)(2,1)S(1)} %get-tuple-element.46), channel_id=1, source_target_pairs={{0,4},{4,0},{8,12},{12,8},{16,20},{20,16},{24,28},{28,24},{1,5},{5... | collective-permute-start | bytes 491528 | tf_op jit(solution)/shard_map/ppermute | solution.py:43
  12.6 1.2 %copy-start.5 = (bf16[4,512,256]{2,1,0:T(8,128)(2,1)S(1)}, bf16[4,512,256]{2,1,0:T(8,128)(2,1)}, u32[]{:S(2)}) copy-start(bf16[4,512,256]{2,1,0:T(8,128)(2,1)} %constant.4.clone.refs_2_) | copy-start | bytes 3145732
  20.7 12.3 %copy-start = (bf16[128,1024]{1,0:T(8,128)(2,1)S(1)}, bf16[128,1024]{1,0:T(8,128)(2,1)}, u32[]{:S(2)}) copy-start(bf16[128,1024]{1,0:T(8,128)(2,1)} %refs_2_.6) | copy-start | bytes 786436
  20.7 12.3 %copy-start.1 = (bf16[128,1024]{1,0:T(8,128)(2,1)S(1)}, bf16[128,1024]{1,0:T(8,128)(2,1)}, u32[]{:S(2)}) copy-start(bf16[128,1024]{1,0:T(8,128)(2,1)} %refs_3_.6) | copy-start | bytes 786436
  20.7 12.3 %copy-start.2 = (bf16[128,1024]{1,0:T(8,128)(2,1)S(1)}, bf16[128,1024]{1,0:T(8,128)(2,1)}, u32[]{:S(2)}) copy-start(bf16[128,1024]{1,0:T(8,128)(2,1)} %refs_4_.7) | copy-start | bytes 786436
  20.7 12.3 %copy-start.3 = (bf16[128,1024]{1,0:T(8,128)(2,1)S(1)}, bf16[128,1024]{1,0:T(8,128)(2,1)}, u32[]{:S(2)}) copy-start(bf16[128,1024]{1,0:T(8,128)(2,1)} %refs_5_.5) | copy-start | bytes 786436
  23.8 6.9 %collective-permute-start.11 = (bf16[416,128]{1,0:T(8,128)(2,1)S(1)}, bf16[416,128]{1,0:T(8,128)(2,1)S(1)}, u32[]{:S(2)}, u32[]{:S(2)}) collective-permute-start(bf16[416,128]{1,0:T(8,128)(2,1)S(1)} %get-tuple-element.55), channel_id=1, source_target_pairs={{0,24},{4,28},{8,16},{12,20},{16,8},{20,12},{24,0},{28,4},{1,25},{... | collective-permute-start | bytes 319496 | tf_op jit(solution)/shard_map/ppermute | solution.py:43
  26.0 4.7 %collective-permute-start.12 = (bf16[416,128]{1,0:T(8,128)(2,1)S(1)}, bf16[416,128]{1,0:T(8,128)(2,1)S(1)}, u32[]{:S(2)}, u32[]{:S(2)}) collective-permute-start(bf16[416,128]{1,0:T(8,128)(2,1)S(1)} %get-tuple-element.56), channel_id=1, source_target_pairs={{0,4},{4,0},{8,12},{12,8},{16,20},{20,16},{24,28},{28,24},{1,5},{5... | collective-permute-start | bytes 319496 | tf_op jit(solution)/shard_map/ppermute | solution.py:43
  26.0 7.0 %collective-permute-start.13 = (bf16[416,128]{1,0:T(8,128)(2,1)S(1)}, bf16[416,128]{1,0:T(8,128)(2,1)S(1)}, u32[]{:S(2)}, u32[]{:S(2)}) collective-permute-start(bf16[416,128]{1,0:T(8,128)(2,1)S(1)} %get-tuple-element.57), channel_id=1, source_target_pairs={{0,28},{4,24},{8,20},{12,16},{16,12},{20,8},{24,4},{28,0},{1,29},{... | collective-permute-start | bytes 319496 | tf_op jit(solution)/shard_map/ppermute | solution.py:43
  26.9 8.1 %collective-permute-start.9 = (bf16[416,128]{1,0:T(8,128)(2,1)S(1)}, bf16[416,128]{1,0:T(8,128)(2,1)S(1)}, u32[]{:S(2)}, u32[]{:S(2)}) collective-permute-start(bf16[416,128]{1,0:T(8,128)(2,1)S(1)} %get-tuple-element.52), channel_id=1, source_target_pairs={{0,16},{4,20},{8,24},{12,28},{16,0},{20,4},{24,8},{28,12},{1,17},{... | collective-permute-start | bytes 319496 | tf_op jit(solution)/shard_map/ppermute | solution.py:43
  28.4 6.7 %collective-permute-start.10 = (bf16[416,128]{1,0:T(8,128)(2,1)S(1)}, bf16[416,128]{1,0:T(8,128)(2,1)S(1)}, u32[]{:S(2)}, u32[]{:S(2)}) collective-permute-start(bf16[416,128]{1,0:T(8,128)(2,1)S(1)} %get-tuple-element.53), channel_id=1, source_target_pairs={{0,8},{4,12},{8,0},{12,4},{16,24},{20,28},{24,16},{28,20},{1,9},{5... | collective-permute-start | bytes 319496 | tf_op jit(solution)/shard_map/ppermute | solution.py:43
  30.6 6.6 %collective-permute-start.7 = (bf16[416,128]{1,0:T(8,128)(2,1)S(1)}, bf16[416,128]{1,0:T(8,128)(2,1)S(1)}, u32[]{:S(2)}, u32[]{:S(2)}) collective-permute-start(bf16[416,128]{1,0:T(8,128)(2,1)S(1)} %get-tuple-element.50), channel_id=1, source_target_pairs={{0,20},{4,16},{8,28},{12,24},{16,4},{20,0},{24,12},{28,8},{1,21},{... | collective-permute-start | bytes 319496 | tf_op jit(solution)/shard_map/ppermute | solution.py:43
  30.6 6.6 %collective-permute-start.8 = (bf16[416,128]{1,0:T(8,128)(2,1)S(1)}, bf16[416,128]{1,0:T(8,128)(2,1)S(1)}, u32[]{:S(2)}, u32[]{:S(2)}) collective-permute-start(bf16[416,128]{1,0:T(8,128)(2,1)S(1)} %get-tuple-element.51), channel_id=1, source_target_pairs={{0,12},{4,8},{8,4},{12,0},{16,28},{20,24},{24,20},{28,16},{1,13},{... | collective-permute-start | bytes 319496 | tf_op jit(solution)/shard_map/ppermute | solution.py:43

commit v14 on v12

--- a/solution.py
+++ b/solution.py
@@ -15,7 +15,7 @@
 PHASES = 4
 TILE = 16
 PAD = 8
-CHUNK = 32
+CHUNK = 16
 RIM = 2
 PIECES = 2
 MIB = 1024 * 1024
@@ -60,7 +60,7 @@
         pltpu.make_async_copy(source, target, sems.at[at])
         for at, (source, target) in enumerate(zip(sources, held))
     ]
-    for copy in arriving:
+    for copy in reversed(arriving):
         copy.start()
     for at, source in enumerate(held):
         arriving[at].wait()

time: 37.9 us -> 38.1 us (level)
  no operation moved by 1% of the time
where the time goes in v14:
time: 38.1 us; the launch traced here: 37.9 us
  starting transfers between devices  15.9 us (42%)
  waiting for transfers between devices  11.7 us (31%)
  Pallas kernels  8.34 us (22%)
  local copies, waits for them, and re-layouts  1.25 us (3%)
  between operations  0.75 us (2%)
    ppermute x14, starting transfers between devices, exchange(): lax.ppermute(block, 'ctx', [(i, i ^ step) for i in range(peers)])  15.9 us
    ppermute x14, waiting for transfers between devices, exchange(): lax.ppermute(block, 'ctx', [(i, i ^ step) for i in range(peers)])  11.7 us
    pallas_call x3, Pallas kernels, token_step(): pl.pallas_call(functools.partial(token_kernel, steps, extra_rows(short_we...  3.46 us
    pallas_call x1, Pallas kernels, channel_step(): pl.pallas_call(functools.partial(channel_kernel, tokens, heard, told, 1.0...  2.63 us
    pallas_call x1, Pallas kernels, pack(): pl.pallas_call(functools.partial(pack_kernel, count, steps), in_specs=[pl...  1.82 us
    unnamed x14, local copies, waits for them, and re-layouts  1.25 us
  transfers between devices with their start and end apart: 14, of which 7 were waited for; matrix products, arithmetic and copies ran while one was open for 0% of the time, Pallas kernels for 8%

profile of v14, /device:TPU:0, one launch (start us, length us, event | category | flops | bytes accessed | tf_op | source)
XLA Modules:
  0.0 37.9 jit_solution(1036578349666105747)
XLA Ops:
  0.6 0.0 copy-start.4
  0.7 1.8 %pack_inputs.1 = (bf16[640,128]{1,0:T(8,128)(2,1)S(1)}, bf16[640,128]{1,0:T(8,128)(2,1)S(1)}, bf16[640,128]{1,0:T(8,128)(2,1)S(1)}, bf16[640,128]{1,0:T(8,128)(2...) custom-call(bf16[128,1024]{1,0:T(8,128)(2,1)} %refs_2_.6, ...), custom_call_target="tpu_custom_call" | custom-call | bytes 8388608 | tf_op jit(solution)/shard_map/pack_inputs/pallas_call | solution.py:75
  2.5 3.0 %collective-permute-start = (bf16[640,128]{1,0:T(8,128)(2,1)S(1)}, bf16[640,128]{1,0:T(8,128)(2,1)S(1)}, u32[]{:S(2)}, u32[]{:S(2)}) collective-permute-start(bf16[640,128]{1,0:T(8,128)(2,1)S(1)} %get-tuple-element.39), channel_id=1, source_target_pairs={{0,16},{4,20},{8,24},{12,28},{16,0},{20,4},{24,8},{28,12},{1,17},{... | collective-permute-start | bytes 491528 | tf_op jit(solution)/shard_map/ppermute | solution.py:42
  5.5 1.5 %collective-permute-start.1 = (bf16[640,128]{1,0:T(8,128)(2,1)S(1)}, bf16[640,128]{1,0:T(8,128)(2,1)S(1)}, u32[]{:S(2)}, u32[]{:S(2)}) collective-permute-start(bf16[640,128]{1,0:T(8,128)(2,1)S(1)} %get-tuple-element.41), channel_id=1, source_target_pairs={{0,8},{4,12},{8,0},{12,4},{16,24},{20,28},{24,16},{28,20},{1,9},{5... | collective-permute-start | bytes 491528 | tf_op jit(solution)/shard_map/ppermute | solution.py:42
  7.0 0.0 collective-permute-start.2
  7.1 1.5 %collective-permute-start.3 = (bf16[640,128]{1,0:T(8,128)(2,1)S(1)}, bf16[640,128]{1,0:T(8,128)(2,1)S(1)}, u32[]{:S(2)}, u32[]{:S(2)}) collective-permute-start(bf16[640,128]{1,0:T(8,128)(2,1)S(1)} %get-tuple-element.43), channel_id=1, source_target_pairs={{0,28},{4,24},{8,20},{12,16},{16,12},{20,8},{24,4},{28,0},{1,29},{... | collective-permute-start | bytes 491528 | tf_op jit(solution)/shard_map/ppermute | solution.py:42
  8.5 1.6 %collective-permute-start.4 = (bf16[640,128]{1,0:T(8,128)(2,1)S(1)}, bf16[640,128]{1,0:T(8,128)(2,1)S(1)}, u32[]{:S(2)}, u32[]{:S(2)}) collective-permute-start(bf16[640,128]{1,0:T(8,128)(2,1)S(1)} %get-tuple-element.44), channel_id=1, source_target_pairs={{0,20},{4,16},{8,28},{12,24},{16,4},{20,0},{24,12},{28,8},{1,21},{... | collective-permute-start | bytes 491528 | tf_op jit(solution)/shard_map/ppermute | solution.py:42
  10.2 0.1 collective-permute-start.5
  10.2 2.4 %collective-permute-done.1.refs_2_ = bf16[640,128]{1,0:T(8,128)(2,1)S(1)} collective-permute-done((bf16[640,128]{1,0:T(8,128)(2,1)S(1)}, bf16[640,128]{1,0:T(8,128)(2,1)S(1)}, u32[]{:S(2)}, u32[]{:S(2)}) %collective-permute-start.1) | collective-permute-done | bytes 163872 | tf_op jit(solution)/shard_map/ppermute | solution.py:42
  12.6 0.0 collective-permute-start.6
  12.7 0.0 copy-start.5
  12.7 1.2 %copy-done.5 = bf16[4,512,256]{2,1,0:T(8,128)(2,1)S(1)} copy-done((bf16[4,512,256]{2,1,0:T(8,128)(2,1)S(1)}, bf16[4,512,256]{2,1,0:T(8,128)(2,1)}, u32[]{:S(2)}) %copy-start.5) | copy-done | bytes 1048600
  13.9 0.4 %stage_tables.1 = (bf16[640,128]{1,0:T(8,128)(2,1)S(1)}, f32[3,3,1024]{2,1,0:T(4,128)S(1)}, bf16[4,512,256]{2,1,0:T(8,128)(2,1)S(1)}, bf16[4,256,512]{2,1,0:T(8,128)(2,1)S(1)}) custom-call(bf16[640,128]{1,0:T(8,128)(2,1)S(1)} %get-tuple-element.38.refs_0_, f32[3,3,1024]{2,1,0:T(4,128)S(1)} %copy-done.6, bf16[4,512,256]{2,1,0:T(8,128)(2,1)S(1)} %copy-done.5, ...), custom_call_target="tpu_custom_call" | custom-call | bytes 8388608 | tf_op jit(solution)/shard_map/stage_tables/pallas_call | solution.py:180
  14.3 1.4 %collective-permute-done.2.refs_3_ = bf16[640,128]{1,0:T(8,128)(2,1)S(1)} collective-permute-done((bf16[640,128]{1,0:T(8,128)(2,1)S(1)}, bf16[640,128]{1,0:T(8,128)(2,1)S(1)}, u32[]{:S(2)}, u32[]{:S(2)}) %collective-permute-start.2) | collective-permute-done | bytes 163872 | tf_op jit(solution)/shard_map/ppermute | solution.py:42
  15.7 3.0 %collective-permute-done.3.refs_4_ = bf16[640,128]{1,0:T(8,128)(2,1)S(1)} collective-permute-done((bf16[640,128]{1,0:T(8,128)(2,1)S(1)}, bf16[640,128]{1,0:T(8,128)(2,1)S(1)}, u32[]{:S(2)}, u32[]{:S(2)}) %collective-permute-start.3) | collective-permute-done | bytes 163872 | tf_op jit(solution)/shard_map/ppermute | solution.py:42
  18.7 2.0 %collective-permute-done.4.refs_5_ = bf16[640,128]{1,0:T(8,128)(2,1)S(1)} collective-permute-done((bf16[640,128]{1,0:T(8,128)(2,1)S(1)}, bf16[640,128]{1,0:T(8,128)(2,1)S(1)}, u32[]{:S(2)}, u32[]{:S(2)}) %collective-permute-start.4) | collective-permute-done | bytes 163872 | tf_op jit(solution)/shard_map/ppermute | solution.py:42
  20.7 0.0 collective-permute-done.5.refs_6_
  20.8 0.0 copy-start.3
  20.8 2.6 %channel_operator.1 = (bf16[416,128]{1,0:T(8,128)(2,1)S(1)}, bf16[416,128]{1,0:T(8,128)(2,1)S(1)}, bf16[416,128]{1,0:T(8,128)(2,1)S(1)}, bf16[416,128]{1,0:T(8,1...) custom-call(bf16[640,128]{1,0:T(8,128)(2,1)S(1)} %get-tuple-element., ...), custom_call_target="tpu_custom_call" | custom-call | tf_op jit(solution)/shard_map/channel_operator/pallas_call | solution.py:354
  23.4 2.2 %collective-permute-start.11 = (bf16[416,128]{1,0:T(8,128)(2,1)S(1)}, bf16[416,128]{1,0:T(8,128)(2,1)S(1)}, u32[]{:S(2)}, u32[]{:S(2)}) collective-permute-start(bf16[416,128]{1,0:T(8,128)(2,1)S(1)} %get-tuple-element.55), channel_id=1, source_target_pairs={{0,24},{4,28},{8,16},{12,20},{16,8},{20,12},{24,0},{28,4},{1,25},{... | collective-permute-start | bytes 319496 | tf_op jit(solution)/shard_map/ppermute | solution.py:42
  25.6 0.0 collective-permute-start.12
  25.6 0.9 %collective-permute-start.13 = (bf16[416,128]{1,0:T(8,128)(2,1)S(1)}, bf16[416,128]{1,0:T(8,128)(2,1)S(1)}, u32[]{:S(2)}, u32[]{:S(2)}) collective-permute-start(bf16[416,128]{1,0:T(8,128)(2,1)S(1)} %get-tuple-element.57), channel_id=1, source_target_pairs={{0,28},{4,24},{8,20},{12,16},{16,12},{20,8},{24,4},{28,0},{1,29},{... | collective-permute-start | bytes 319496 | tf_op jit(solution)/shard_map/ppermute | solution.py:42
  26.6 1.5 %collective-permute-start.9 = (bf16[416,128]{1,0:T(8,128)(2,1)S(1)}, bf16[416,128]{1,0:T(8,128)(2,1)S(1)}, u32[]{:S(2)}, u32[]{:S(2)}) collective-permute-start(bf16[416,128]{1,0:T(8,128)(2,1)S(1)} %get-tuple-element.52), channel_id=1, source_target_pairs={{0,16},{4,20},{8,24},{12,28},{16,0},{20,4},{24,8},{28,12},{1,17},{... | collective-permute-start | bytes 319496 | tf_op jit(solution)/shard_map/ppermute | solution.py:42
  28.0 1.2 %collective-permute-start.10 = (bf16[416,128]{1,0:T(8,128)(2,1)S(1)}, bf16[416,128]{1,0:T(8,128)(2,1)S(1)}, u32[]{:S(2)}, u32[]{:S(2)}) collective-permute-start(bf16[416,128]{1,0:T(8,128)(2,1)S(1)} %get-tuple-element.53), channel_id=1, source_target_pairs={{0,8},{4,12},{8,0},{12,4},{16,24},{20,28},{24,16},{28,20},{1,9},{5... | collective-permute-start | bytes 319496 | tf_op jit(solution)/shard_map/ppermute | solution.py:42
  29.2 1.1 %collective-permute-done.11.refs_1_ = bf16[416,128]{1,0:T(8,128)(2,1)S(1)} collective-permute-done((bf16[416,128]{1,0:T(8,128)(2,1)S(1)}, bf16[416,128]{1,0:T(8,128)(2,1)S(1)}, u32[]{:S(2)}, u32[]{:S(2)}) %collective-permute-start.11) | collective-permute-done | bytes 106528 | tf_op jit(solution)/shard_map/ppermute | solution.py:42
  30.3 2.3 %collective-permute-start.8 = (bf16[416,128]{1,0:T(8,128)(2,1)S(1)}, bf16[416,128]{1,0:T(8,128)(2,1)S(1)}, u32[]{:S(2)}, u32[]{:S(2)}) collective-permute-start(bf16[416,128]{1,0:T(8,128)(2,1)S(1)} %get-tuple-element.51), channel_id=1, source_target_pairs={{0,12},{4,8},{8,4},{12,0},{16,28},{20,24},{24,20},{28,16},{1,13},{... | collective-permute-start | bytes 319496 | tf_op jit(solution)/shard_map/ppermute | solution.py:42
  32.6 0.0 collective-permute-done.13.refs_3_
  32.7 1.4 %token_outputs.3 = (bf16[128,1024]{1,0:T(8,128)(2,1)}, bf16[128,1024]{1,0:T(8,128)(2,1)}, bf16[128,1024]{1,0:T(8,128)(2,1)}, bf16[128,1024]{1,0:T(8,128)(2,1)}, ...) custom-call(bf16[416,128]{1,0:T(8,128)(2,1)S(1)} %get-tuple-element.54.refs_0_, ...), custom_call_target="tpu_custom_call" | custom-call | bytes 4194304 | tf_op jit(solution)/shard_map/token_outputs/pallas_call | solution.py:445
  34.1 0.6 %collective-permute-done.9.refs_0_ = bf16[416,128]{1,0:T(8,128)(2,1)S(1)} collective-permute-done((bf16[416,128]{1,0:T(8,128)(2,1)S(1)}, bf16[416,128]{1,0:T(8,128)(2,1)S(1)}, u32[]{:S(2)}, u32[]{:S(2)}) %collective-permute-start.9) | collective-permute-done | bytes 106528 | tf_op jit(solution)/shard_map/ppermute | solution.py:42
  34.7 1.0 %token_outputs.4 = (bf16[128,1024]{1,0:T(8,128)(2,1)}, bf16[128,1024]{1,0:T(8,128)(2,1)}, bf16[128,1024]{1,0:T(8,128)(2,1)}, bf16[128,1024]{1,0:T(8,128)(2,1)}, ...) custom-call(bf16[416,128]{1,0:T(8,128)(2,1)S(1)} %collective-permute, ...), custom_call_target="tpu_custom_call", output_to_operand_aliasing={{0}: (7, {}), {1}: (8, {}), {2}: (9, {}), {3}: (10, {}), {4... | custom-call | bytes 4194304 | tf_op jit(solution)/shard_map/token_outputs/pallas_call | solution.py:445
  35.7 1.2 %collective-permute-done.7.refs_0_ = bf16[416,128]{1,0:T(8,128)(2,1)S(1)} collective-permute-done((bf16[416,128]{1,0:T(8,128)(2,1)S(1)}, bf16[416,128]{1,0:T(8,128)(2,1)S(1)}, u32[]{:S(2)}, u32[]{:S(2)}) %collective-permute-start.7) | collective-permute-done | bytes 106528 | tf_op jit(solution)/shard_map/ppermute | solution.py:42
  36.9 1.0 %token_outputs.5 = (bf16[128,1024]{1,0:T(8,128)(2,1)}, bf16[128,1024]{1,0:T(8,128)(2,1)}, bf16[128,1024]{1,0:T(8,128)(2,1)}, bf16[128,1024]{1,0:T(8,128)(2,1)}, ...) custom-call(bf16[416,128]{1,0:T(8,128)(2,1)S(1)} %collective-permute, ...), custom_call_target="tpu_custom_call", output_to_operand_aliasing={{0}: (7, {}), {1}: (8, {}), {2}: (9, {}), {3}: (10, {}), {4... | custom-call | bytes 4194304 | tf_op jit(solution)/shard_map/token_outputs/pallas_call | solution.py:445
  (16 shorter events, 0.0 us)
Async XLA Ops:
  0.6 12.0 %copy-start.4 = (bf16[4,256,512]{2,1,0:T(8,128)(2,1)S(1)}, bf16[4,256,512]{2,1,0:T(8,128)(2,1)}, u32[]{:S(2)}) copy-start(bf16[4,256,512]{2,1,0:T(8,128)(2,1)} %constant.5.clone.refs_3_) | copy-start | bytes 3145732
  0.6 12.0 %copy-start.6 = (f32[3,3,1024]{2,1,0:T(4,128)S(1)}, f32[3,3,1024]{2,1,0:T(4,128)}, u32[]{:S(2)}) copy-start(f32[3,3,1024]{2,1,0:T(4,128)} %refs_6_.5) | copy-start | bytes 110596
  2.5 7.7 %collective-permute-start = (bf16[640,128]{1,0:T(8,128)(2,1)S(1)}, bf16[640,128]{1,0:T(8,128)(2,1)S(1)}, u32[]{:S(2)}, u32[]{:S(2)}) collective-permute-start(bf16[640,128]{1,0:T(8,128)(2,1)S(1)} %get-tuple-element.39), channel_id=1, source_target_pairs={{0,16},{4,20},{8,24},{12,28},{16,0},{20,4},{24,8},{28,12},{1,17},{... | collective-permute-start | bytes 491528 | tf_op jit(solution)/shard_map/ppermute | solution.py:42
  5.5 7.1 %collective-permute-start.1 = (bf16[640,128]{1,0:T(8,128)(2,1)S(1)}, bf16[640,128]{1,0:T(8,128)(2,1)S(1)}, u32[]{:S(2)}, u32[]{:S(2)}) collective-permute-start(bf16[640,128]{1,0:T(8,128)(2,1)S(1)} %get-tuple-element.41), channel_id=1, source_target_pairs={{0,8},{4,12},{8,0},{12,4},{16,24},{20,28},{24,16},{28,20},{1,9},{5... | collective-permute-start | bytes 491528 | tf_op jit(solution)/shard_map/ppermute | solution.py:42
  7.0 8.7 %collective-permute-start.2 = (bf16[640,128]{1,0:T(8,128)(2,1)S(1)}, bf16[640,128]{1,0:T(8,128)(2,1)S(1)}, u32[]{:S(2)}, u32[]{:S(2)}) collective-permute-start(bf16[640,128]{1,0:T(8,128)(2,1)S(1)} %get-tuple-element.42), channel_id=1, source_target_pairs={{0,24},{4,28},{8,16},{12,20},{16,8},{20,12},{24,0},{28,4},{1,25},{... | collective-permute-start | bytes 491528 | tf_op jit(solution)/shard_map/ppermute | solution.py:42
  7.1 11.7 %collective-permute-start.3 = (bf16[640,128]{1,0:T(8,128)(2,1)S(1)}, bf16[640,128]{1,0:T(8,128)(2,1)S(1)}, u32[]{:S(2)}, u32[]{:S(2)}) collective-permute-start(bf16[640,128]{1,0:T(8,128)(2,1)S(1)} %get-tuple-element.43), channel_id=1, source_target_pairs={{0,28},{4,24},{8,20},{12,16},{16,12},{20,8},{24,4},{28,0},{1,29},{... | collective-permute-start | bytes 491528 | tf_op jit(solution)/shard_map/ppermute | solution.py:42
  8.5 12.2 %collective-permute-start.4 = (bf16[640,128]{1,0:T(8,128)(2,1)S(1)}, bf16[640,128]{1,0:T(8,128)(2,1)S(1)}, u32[]{:S(2)}, u32[]{:S(2)}) collective-permute-start(bf16[640,128]{1,0:T(8,128)(2,1)S(1)} %get-tuple-element.44), channel_id=1, source_target_pairs={{0,20},{4,16},{8,28},{12,24},{16,4},{20,0},{24,12},{28,8},{1,21},{... | collective-permute-start | bytes 491528 | tf_op jit(solution)/shard_map/ppermute | solution.py:42
  10.2 10.6 %collective-permute-start.5 = (bf16[640,128]{1,0:T(8,128)(2,1)S(1)}, bf16[640,128]{1,0:T(8,128)(2,1)S(1)}, u32[]{:S(2)}, u32[]{:S(2)}) collective-permute-start(bf16[640,128]{1,0:T(8,128)(2,1)S(1)} %get-tuple-element.45), channel_id=1, source_target_pairs={{0,12},{4,8},{8,4},{12,0},{16,28},{20,24},{24,20},{28,16},{1,13},{... | collective-permute-start | bytes 491528 | tf_op jit(solution)/shard_map/ppermute | solution.py:42
  12.6 8.1 %collective-permute-start.6 = (bf16[640,128]{1,0:T(8,128)(2,1)S(1)}, bf16[640,128]{1,0:T(8,128)(2,1)S(1)}, u32[]{:S(2)}, u32[]{:S(2)}) collective-permute-start(bf16[640,128]{1,0:T(8,128)(2,1)S(1)} %get-tuple-element.46), channel_id=1, source_target_pairs={{0,4},{4,0},{8,12},{12,8},{16,20},{20,16},{24,28},{28,24},{1,5},{5... | collective-permute-start | bytes 491528 | tf_op jit(solution)/shard_map/ppermute | solution.py:42
  12.7 1.2 %copy-start.5 = (bf16[4,512,256]{2,1,0:T(8,128)(2,1)S(1)}, bf16[4,512,256]{2,1,0:T(8,128)(2,1)}, u32[]{:S(2)}) copy-start(bf16[4,512,256]{2,1,0:T(8,128)(2,1)} %constant.4.clone.refs_2_) | copy-start | bytes 3145732
  20.8 11.9 %copy-start = (bf16[128,1024]{1,0:T(8,128)(2,1)S(1)}, bf16[128,1024]{1,0:T(8,128)(2,1)}, u32[]{:S(2)}) copy-start(bf16[128,1024]{1,0:T(8,128)(2,1)} %refs_2_.6) | copy-start | bytes 786436
  20.8 11.9 %copy-start.1 = (bf16[128,1024]{1,0:T(8,128)(2,1)S(1)}, bf16[128,1024]{1,0:T(8,128)(2,1)}, u32[]{:S(2)}) copy-start(bf16[128,1024]{1,0:T(8,128)(2,1)} %refs_3_.6) | copy-start | bytes 786436
  20.8 11.9 %copy-start.2 = (bf16[128,1024]{1,0:T(8,128)(2,1)S(1)}, bf16[128,1024]{1,0:T(8,128)(2,1)}, u32[]{:S(2)}) copy-start(bf16[128,1024]{1,0:T(8,128)(2,1)} %refs_4_.7) | copy-start | bytes 786436
  20.8 11.9 %copy-start.3 = (bf16[128,1024]{1,0:T(8,128)(2,1)S(1)}, bf16[128,1024]{1,0:T(8,128)(2,1)}, u32[]{:S(2)}) copy-start(bf16[128,1024]{1,0:T(8,128)(2,1)} %refs_5_.5) | copy-start | bytes 786436
  23.4 6.9 %collective-permute-start.11 = (bf16[416,128]{1,0:T(8,128)(2,1)S(1)}, bf16[416,128]{1,0:T(8,128)(2,1)S(1)}, u32[]{:S(2)}, u32[]{:S(2)}) collective-permute-start(bf16[416,128]{1,0:T(8,128)(2,1)S(1)} %get-tuple-element.55), channel_id=1, source_target_pairs={{0,24},{4,28},{8,16},{12,20},{16,8},{20,12},{24,0},{28,4},{1,25},{... | collective-permute-start | bytes 319496 | tf_op jit(solution)/shard_map/ppermute | solution.py:42
  25.6 4.7 %collective-permute-start.12 = (bf16[416,128]{1,0:T(8,128)(2,1)S(1)}, bf16[416,128]{1,0:T(8,128)(2,1)S(1)}, u32[]{:S(2)}, u32[]{:S(2)}) collective-permute-start(bf16[416,128]{1,0:T(8,128)(2,1)S(1)} %get-tuple-element.56), channel_id=1, source_target_pairs={{0,4},{4,0},{8,12},{12,8},{16,20},{20,16},{24,28},{28,24},{1,5},{5... | collective-permute-start | bytes 319496 | tf_op jit(solution)/shard_map/ppermute | solution.py:42
  25.6 7.0 %collective-permute-start.13 = (bf16[416,128]{1,0:T(8,128)(2,1)S(1)}, bf16[416,128]{1,0:T(8,128)(2,1)S(1)}, u32[]{:S(2)}, u32[]{:S(2)}) collective-permute-start(bf16[416,128]{1,0:T(8,128)(2,1)S(1)} %get-tuple-element.57), channel_id=1, source_target_pairs={{0,28},{4,24},{8,20},{12,16},{16,12},{20,8},{24,4},{28,0},{1,29},{... | collective-permute-start | bytes 319496 | tf_op jit(solution)/shard_map/ppermute | solution.py:42
  26.6 8.1 %collective-permute-start.9 = (bf16[416,128]{1,0:T(8,128)(2,1)S(1)}, bf16[416,128]{1,0:T(8,128)(2,1)S(1)}, u32[]{:S(2)}, u32[]{:S(2)}) collective-permute-start(bf16[416,128]{1,0:T(8,128)(2,1)S(1)} %get-tuple-element.52), channel_id=1, source_target_pairs={{0,16},{4,20},{8,24},{12,28},{16,0},{20,4},{24,8},{28,12},{1,17},{... | collective-permute-start | bytes 319496 | tf_op jit(solution)/shard_map/ppermute | solution.py:42
  28.0 6.7 %collective-permute-start.10 = (bf16[416,128]{1,0:T(8,128)(2,1)S(1)}, bf16[416,128]{1,0:T(8,128)(2,1)S(1)}, u32[]{:S(2)}, u32[]{:S(2)}) collective-permute-start(bf16[416,128]{1,0:T(8,128)(2,1)S(1)} %get-tuple-element.53), channel_id=1, source_target_pairs={{0,8},{4,12},{8,0},{12,4},{16,24},{20,28},{24,16},{28,20},{1,9},{5... | collective-permute-start | bytes 319496 | tf_op jit(solution)/shard_map/ppermute | solution.py:42
  30.3 6.6 %collective-permute-start.7 = (bf16[416,128]{1,0:T(8,128)(2,1)S(1)}, bf16[416,128]{1,0:T(8,128)(2,1)S(1)}, u32[]{:S(2)}, u32[]{:S(2)}) collective-permute-start(bf16[416,128]{1,0:T(8,128)(2,1)S(1)} %get-tuple-element.50), channel_id=1, source_target_pairs={{0,20},{4,16},{8,28},{12,24},{16,4},{20,0},{24,12},{28,8},{1,21},{... | collective-permute-start | bytes 319496 | tf_op jit(solution)/shard_map/ppermute | solution.py:42
  30.3 6.6 %collective-permute-start.8 = (bf16[416,128]{1,0:T(8,128)(2,1)S(1)}, bf16[416,128]{1,0:T(8,128)(2,1)S(1)}, u32[]{:S(2)}, u32[]{:S(2)}) collective-permute-start(bf16[416,128]{1,0:T(8,128)(2,1)S(1)} %get-tuple-element.51), channel_id=1, source_target_pairs={{0,12},{4,8},{8,4},{12,0},{16,28},{20,24},{24,20},{28,16},{1,13},{... | collective-permute-start | bytes 319496 | tf_op jit(solution)/shard_map/ppermute | solution.py:42

commit v15 on v14

--- a/solution.py
+++ b/solution.py
@@ -60,7 +60,7 @@
         pltpu.make_async_copy(source, target, sems.at[at])
         for at, (source, target) in enumerate(zip(sources, held))
     ]
-    for copy in reversed(arriving):
+    for copy in arriving:
         copy.start()
     for at, source in enumerate(held):
         arriving[at].wait()
@@ -207,7 +207,7 @@
         conv,
         conv_grad,
         filter_grad,
-        taps,
+        filt,
         key_short,
         value_short,
         signals,
@@ -216,19 +216,20 @@
         extra,
     ) = refs[2 * peers + 3 :]
     size = peers * tokens // PHASES
+    per = tokens // PHASES
     tap_count = weights.shape[1]
     me = lax.axis_index("ctx")
     own = lanes_of(me)
-    for ref in (query, key, value, cot, conv, conv_grad):
+    for ref in (query, key, value, cot):
         clear_ends(ref)
-    for ref in (key_short, value_short):
+    for ref in (key_short, value_short, conv, conv_grad):
         ref[:, size:, :] = jnp.zeros((PHASES, PAD, LANES), F32)
     for step, source in zip(heard, arrived):
         start = (me ^ step) * tokens
         inner = pl.ds(pl.multiple_of(PAD + start, PAD), tokens)
         for at, ref in enumerate((query, key, value, cot)):
             ref[inner, :] = source[at * tokens : (at + 1) * tokens, :].astype(F32)
-        taps[pl.ds(pl.multiple_of(start, PAD), tokens), :] = source[4 * tokens :, :].astype(F32)
+        filt[pl.ds(pl.multiple_of(start, PAD), tokens), :] = source[4 * tokens :, :].astype(F32)
     chunks = range(size // CHUNK)
     taps_of = [
         [weights[array, tap : tap + 1, own] for tap in range(tap_count)] for array in range(3)
@@ -257,8 +258,8 @@
             key_short[r, rows, :] = key_now[r]
             value_short[r, rows, :] = value_now[r]
             signals[r, rows, :LANES] = (key_now[r] * value_now[r]).astype(BF16)
-            filt = taps[pl.ds(chunk * CHUNK * PHASES + r, CHUNK, stride=PHASES), :]
-            signals[r, rows, LANES : 2 * LANES] = filt.astype(BF16)
+            filt_now = filt[pl.ds(chunk * CHUNK * PHASES + r, CHUNK, stride=PHASES), :]
+            signals[r, rows, LANES : 2 * LANES] = filt_now.astype(BF16)
     for r in range(PHASES):
         spectra[r, :, : 2 * LANES] = transform(forward[r], signals[r, :, : 2 * LANES])
     for chunk in chunks:
@@ -280,7 +281,7 @@
         keep(0, real, imag, times(prod, filt))
     for r in range(PHASES):
         result = transform(backward[r], products[r, :, :LANES])
-        conv[pl.ds(PAD + r, size, stride=PHASES), :] = result.astype(BF16).astype(F32)
+        conv[r, :size, :] = result.astype(BF16).astype(F32)
     for step in range(size // TILE):
         real = slice(step * TILE, (step + 1) * TILE)
         imag = slice(size + step * TILE, size + (step + 1) * TILE)
@@ -291,10 +292,8 @@
             keep(2 - at, real, imag, conj_times(known, grad))
     for r in range(PHASES):
         result = transform(backward[r], products[r, :, LANES:])
-        conv_grad[pl.ds(PAD + r, size, stride=PHASES), :] = (
-            result[:, :LANES].astype(BF16).astype(F32)
-        )
-        filter_grad[pl.ds(r, size, stride=PHASES), :] = result[:, LANES:] * grad_scale
+        conv_grad[r, :size, :] = result[:, :LANES].astype(BF16).astype(F32)
+        filter_grad[r] = (result[:, LANES:] * grad_scale).astype(BF16)
 
     totals = [[None] * tap_count for _ in range(3)]
 
@@ -306,11 +305,12 @@
             )
 
     for chunk in chunks:
-        cot_now, conv_now = phases_near(cot, chunk, 1), phases_near(conv, chunk, 1)
-        add_sums(0, query, chunk, [cot_now[r] * conv_now[r] for r in range(PHASES)])
+        rows = rows_of(chunk)
+        cot_now = phases_near(cot, chunk, 1)
+        add_sums(0, query, chunk, [cot_now[r] * conv[r, rows, :] for r in range(PHASES)])
     for chunk in chunks:
         rows = rows_of(chunk)
-        grad_now = phases_near(conv_grad, chunk, 1)
+        grad_now = [conv_grad[r, rows, :] for r in range(PHASES)]
         add_sums(1, key, chunk, [grad_now[r] * value_short[r, rows, :] for r in range(PHASES)])
         add_sums(2, value, chunk, [grad_now[r] * key_short[r, rows, :] for r in range(PHASES)])
     sums = [jnp.sum(total, axis=0, keepdims=True) for row in totals for total in row]
@@ -322,24 +322,31 @@
         rest = rest - rounded
     for step, target in zip(told, out):
         start = (me ^ step) * tokens
-        inner = pl.ds(pl.multiple_of(PAD + start, PAD), tokens)
-        target[:tokens, :] = conv[inner, :].astype(BF16)
-        target[tokens : 2 * tokens, :] = conv_grad[inner, :].astype(BF16)
-        target[2 * tokens : 3 * tokens, :] = filter_grad[
-            pl.ds(pl.multiple_of(start, PAD), tokens), :
-        ].astype(BF16)
+        rows = pl.ds(pl.multiple_of((me ^ step) * per, per), per)
+        for at, ref in enumerate((conv, conv_grad, filter_grad)):
+            for r in range(PHASES):
+                begin = at * tokens + r * per
+                target[begin : begin + per, :] = ref[r, rows, :].astype(BF16)
         before = pl.ds(pl.multiple_of(start, PAD), PAD)
         after = pl.ds(pl.multiple_of(PAD + start + tokens, PAD), PAD)
         at = PIECES * len(sums)
         for ref in (query, key, value):
             extra[at : at + RIM, :] = ref[before, :][PAD - RIM :]
             at += RIM
-        row = pl.ds(pl.multiple_of((start + tokens) // PHASES, PAD), PAD)
-        extra[at : at + RIM, :] = (cot[after, :] * conv[after, :])[:RIM]
-        for short in (value_short, key_short):
+        row = pl.ds(pl.multiple_of((me ^ step) * per + per, per), PAD)
+
+        def first(ref):
+            return jnp.concatenate([ref[r, row, :][:1] for r in range(RIM)], axis=0)
+
+        grad_first = first(conv_grad)
+        pre = (
+            cot[after, :][:RIM] * first(conv),
+            grad_first * first(value_short),
+            grad_first * first(key_short),
+        )
+        for value_at in pre:
+            extra[at : at + RIM, :] = value_at
             at += RIM
-            shorts = jnp.concatenate([short[r, row, :][:1] for r in range(RIM)], axis=0)
-            extra[at : at + RIM, :] = conv_grad[after, :][:RIM] * shorts
         target[3 * tokens :, :] = extra[...].astype(BF16)
 
 
@@ -349,7 +356,6 @@
     size = seq_len // PHASES
     extra = extra_rows(short_weights)[1]
     padded = pltpu.VMEM((seq_len + 2 * PAD, LANES), F32)
-    plain = pltpu.VMEM((seq_len, LANES), F32)
     phases = pltpu.VMEM((PHASES, size + PAD, LANES), F32)
     return pl.pallas_call(
         functools.partial(channel_kernel, tokens, heard, told, 1.0 / math.sqrt(seq_len)),
@@ -357,9 +363,11 @@
         out_specs=in_vmem(peers),
         out_shape=[jax.ShapeDtypeStruct((3 * tokens + extra, LANES), BF16)] * peers,
         scratch_shapes=[
-            *[padded] * 6,
-            plain,
-            plain,
+            *[padded] * 4,
+            phases,
+            phases,
+            pltpu.VMEM((PHASES, size, LANES), BF16),
+            pltpu.VMEM((seq_len, LANES), F32),
             phases,
             phases,
             pltpu.VMEM((PHASES, size, 3 * LANES), BF16),
@@ -377,11 +385,13 @@
     arrived = refs[:count_in]
     query, key, value, cot, weights = refs[count_in : count_in + 5]
     results = refs[count_in + 5 + carried : count_in + 11 + carried]
-    (gated, query_grad, key_grad, value_grad, filter_grad, short_grad, longer, pre, sems) = refs[
+    gated, query_grad, key_grad, value_grad, filter_grad, short_grad, *scratch = refs[
         count_in + 11 + carried :
     ]
+    longer, pre, ordered, sems = scratch
     copies = []
     tokens = query.shape[0]
+    per = tokens // PHASES
     tap_count = weights.shape[1]
     count = sum_rows // PIECES
     me = lax.axis_index("ctx")
@@ -415,13 +425,19 @@
                 )
             target[slot] = summed.astype(BF16)
 
-        conv = source[:tokens, :].astype(F32)
-        conv_grad = source[tokens : 2 * tokens, :].astype(F32)
+        for at in range(3):
+            for r in range(PHASES):
+                begin = at * tokens + r * per
+                part = source[begin : begin + per, :].astype(F32)
+                if at < 2:
+                    ordered[at, pl.ds(r, per, stride=PHASES), :] = part
+                else:
+                    filter_grad[slot, pl.ds(r, per, stride=PHASES), :] = part
+        conv, conv_grad = ordered[0], ordered[1]
         gated[slot] = (short(0, query) * conv).astype(BF16)
         taps_back(0, cot[:, lanes].astype(F32) * conv, query_grad)
         taps_back(1, conv_grad * short(2, value), key_grad)
         taps_back(2, conv_grad * short(1, key), value_grad)
-        filter_grad[slot] = source[2 * tokens : 3 * tokens, :].astype(F32)
         whole = extra[:count]
         for piece in range(1, PIECES):
             whole = whole + extra[piece * count : (piece + 1) * count]
@@ -457,6 +473,7 @@
             pltpu.VMEM((count, *short_weights.shape[:2], LANES), F32),
             pltpu.VMEM((3, tokens + PAD, LANES), F32),
             pltpu.VMEM((3, tokens + PAD, LANES), F32),
+            pltpu.VMEM((2, tokens, LANES), F32),
             pltpu.SemaphoreType.DMA((count, 6)),
         ],
         input_output_aliases={count + 5 + at: at for at in range(len(begun))},

time: 38.1 us -> 37.8 us (level)
  no operation moved by 1% of the time
where the time goes in v15:
time: 37.8 us; the launch traced here: 37.6 us
  starting transfers between devices  15.9 us (42%)
  waiting for transfers between devices  11.7 us (31%)
  Pallas kernels  8.01 us (21%)
  local copies, waits for them, and re-layouts  1.25 us (3%)
  between operations  0.74 us (2%)
    ppermute x14, starting transfers between devices, exchange(): lax.ppermute(block, 'ctx', [(i, i ^ step) for i in range(peers)])  15.9 us
    ppermute x14, waiting for transfers between devices, exchange(): lax.ppermute(block, 'ctx', [(i, i ^ step) for i in range(peers)])  11.7 us
    pallas_call x3, Pallas kernels, token_step(): pl.pallas_call(functools.partial(token_kernel, steps, extra_rows(short_we...  3.43 us
    pallas_call x1, Pallas kernels, channel_step(): pl.pallas_call(functools.partial(channel_kernel, tokens, heard, told, 1.0...  2.6 us
    pallas_call x1, Pallas kernels, pack(): pl.pallas_call(functools.partial(pack_kernel, count, steps), in_specs=[pl...  1.56 us
    unnamed x14, local copies, waits for them, and re-layouts  1.25 us
  transfers between devices with their start and end apart: 14, of which 7 were waited for; matrix products, arithmetic and copies ran while one was open for 0% of the time, Pallas kernels for 8%

profile of v15, /device:TPU:0, one launch (start us, length us, event | category | flops | bytes accessed | tf_op | source)
XLA Modules:
  0.0 37.6 jit_solution(6469289986568253838)
XLA Ops:
  0.6 0.0 copy-start.4
  0.7 1.6 %pack_inputs.1 = (bf16[640,128]{1,0:T(8,128)(2,1)S(1)}, bf16[640,128]{1,0:T(8,128)(2,1)S(1)}, bf16[640,128]{1,0:T(8,128)(2,1)S(1)}, bf16[640,128]{1,0:T(8,128)(2...) custom-call(bf16[128,1024]{1,0:T(8,128)(2,1)} %refs_2_.6, ...), custom_call_target="tpu_custom_call" | custom-call | bytes 8388608 | tf_op jit(solution)/shard_map/pack_inputs/pallas_call | solution.py:75
  2.2 3.0 %collective-permute-start = (bf16[640,128]{1,0:T(8,128)(2,1)S(1)}, bf16[640,128]{1,0:T(8,128)(2,1)S(1)}, u32[]{:S(2)}, u32[]{:S(2)}) collective-permute-start(bf16[640,128]{1,0:T(8,128)(2,1)S(1)} %get-tuple-element.39), channel_id=1, source_target_pairs={{0,16},{4,20},{8,24},{12,28},{16,0},{20,4},{24,8},{28,12},{1,17},{... | collective-permute-start | bytes 491528 | tf_op jit(solution)/shard_map/ppermute | solution.py:42
  5.3 1.5 %collective-permute-start.1 = (bf16[640,128]{1,0:T(8,128)(2,1)S(1)}, bf16[640,128]{1,0:T(8,128)(2,1)S(1)}, u32[]{:S(2)}, u32[]{:S(2)}) collective-permute-start(bf16[640,128]{1,0:T(8,128)(2,1)S(1)} %get-tuple-element.41), channel_id=1, source_target_pairs={{0,8},{4,12},{8,0},{12,4},{16,24},{20,28},{24,16},{28,20},{1,9},{5... | collective-permute-start | bytes 491528 | tf_op jit(solution)/shard_map/ppermute | solution.py:42
  6.7 0.0 collective-permute-start.2
  6.8 1.5 %collective-permute-start.3 = (bf16[640,128]{1,0:T(8,128)(2,1)S(1)}, bf16[640,128]{1,0:T(8,128)(2,1)S(1)}, u32[]{:S(2)}, u32[]{:S(2)}) collective-permute-start(bf16[640,128]{1,0:T(8,128)(2,1)S(1)} %get-tuple-element.43), channel_id=1, source_target_pairs={{0,28},{4,24},{8,20},{12,16},{16,12},{20,8},{24,4},{28,0},{1,29},{... | collective-permute-start | bytes 491528 | tf_op jit(solution)/shard_map/ppermute | solution.py:42
  8.3 1.6 %collective-permute-start.4 = (bf16[640,128]{1,0:T(8,128)(2,1)S(1)}, bf16[640,128]{1,0:T(8,128)(2,1)S(1)}, u32[]{:S(2)}, u32[]{:S(2)}) collective-permute-start(bf16[640,128]{1,0:T(8,128)(2,1)S(1)} %get-tuple-element.44), channel_id=1, source_target_pairs={{0,20},{4,16},{8,28},{12,24},{16,4},{20,0},{24,12},{28,8},{1,21},{... | collective-permute-start | bytes 491528 | tf_op jit(solution)/shard_map/ppermute | solution.py:42
  9.9 0.0 collective-permute-done.refs_4_.refs_1_
  9.9 0.1 collective-permute-start.5
  10.0 2.4 %collective-permute-done.1.refs_2_ = bf16[640,128]{1,0:T(8,128)(2,1)S(1)} collective-permute-done((bf16[640,128]{1,0:T(8,128)(2,1)S(1)}, bf16[640,128]{1,0:T(8,128)(2,1)S(1)}, u32[]{:S(2)}, u32[]{:S(2)}) %collective-permute-start.1) | collective-permute-done | bytes 163872 | tf_op jit(solution)/shard_map/ppermute | solution.py:42
  12.4 0.0 copy-start.5
  12.4 1.2 %copy-done.5 = bf16[4,512,256]{2,1,0:T(8,128)(2,1)S(1)} copy-done((bf16[4,512,256]{2,1,0:T(8,128)(2,1)S(1)}, bf16[4,512,256]{2,1,0:T(8,128)(2,1)}, u32[]{:S(2)}) %copy-start.5) | copy-done | bytes 1048600
  13.6 0.4 %stage_tables.1 = (bf16[640,128]{1,0:T(8,128)(2,1)S(1)}, f32[3,3,1024]{2,1,0:T(4,128)S(1)}, bf16[4,512,256]{2,1,0:T(8,128)(2,1)S(1)}, bf16[4,256,512]{2,1,0:T(8,128)(2,1)S(1)}) custom-call(bf16[640,128]{1,0:T(8,128)(2,1)S(1)} %get-tuple-element.38.refs_0_, f32[3,3,1024]{2,1,0:T(4,128)S(1)} %copy-done.6, bf16[4,512,256]{2,1,0:T(8,128)(2,1)S(1)} %copy-done.5, ...), custom_call_target="tpu_custom_call" | custom-call | bytes 8388608 | tf_op jit(solution)/shard_map/stage_tables/pallas_call | solution.py:180
  14.0 1.4 %collective-permute-done.2.refs_3_ = bf16[640,128]{1,0:T(8,128)(2,1)S(1)} collective-permute-done((bf16[640,128]{1,0:T(8,128)(2,1)S(1)}, bf16[640,128]{1,0:T(8,128)(2,1)S(1)}, u32[]{:S(2)}, u32[]{:S(2)}) %collective-permute-start.2) | collective-permute-done | bytes 163872 | tf_op jit(solution)/shard_map/ppermute | solution.py:42
  15.5 3.0 %collective-permute-done.3.refs_4_ = bf16[640,128]{1,0:T(8,128)(2,1)S(1)} collective-permute-done((bf16[640,128]{1,0:T(8,128)(2,1)S(1)}, bf16[640,128]{1,0:T(8,128)(2,1)S(1)}, u32[]{:S(2)}, u32[]{:S(2)}) %collective-permute-start.3) | collective-permute-done | bytes 163872 | tf_op jit(solution)/shard_map/ppermute | solution.py:42
  18.5 2.0 %collective-permute-done.4.refs_5_ = bf16[640,128]{1,0:T(8,128)(2,1)S(1)} collective-permute-done((bf16[640,128]{1,0:T(8,128)(2,1)S(1)}, bf16[640,128]{1,0:T(8,128)(2,1)S(1)}, u32[]{:S(2)}, u32[]{:S(2)}) %collective-permute-start.4) | collective-permute-done | bytes 163872 | tf_op jit(solution)/shard_map/ppermute | solution.py:42
  20.5 0.0 collective-permute-done.5.refs_6_
  20.5 0.0 collective-permute-done.6.refs_7_
  20.5 0.0 copy-start.3
  20.5 2.6 %channel_operator.1 = (bf16[416,128]{1,0:T(8,128)(2,1)S(1)}, bf16[416,128]{1,0:T(8,128)(2,1)S(1)}, bf16[416,128]{1,0:T(8,128)(2,1)S(1)}, bf16[416,128]{1,0:T(8,1...) custom-call(bf16[640,128]{1,0:T(8,128)(2,1)S(1)} %get-tuple-element., ...), custom_call_target="tpu_custom_call" | custom-call | tf_op jit(solution)/shard_map/channel_operator/pallas_call | solution.py:360
  23.1 2.2 %collective-permute-start.11 = (bf16[416,128]{1,0:T(8,128)(2,1)S(1)}, bf16[416,128]{1,0:T(8,128)(2,1)S(1)}, u32[]{:S(2)}, u32[]{:S(2)}) collective-permute-start(bf16[416,128]{1,0:T(8,128)(2,1)S(1)} %get-tuple-element.55), channel_id=1, source_target_pairs={{0,24},{4,28},{8,16},{12,20},{16,8},{20,12},{24,0},{28,4},{1,25},{... | collective-permute-start | bytes 319496 | tf_op jit(solution)/shard_map/ppermute | solution.py:42
  25.3 0.9 %collective-permute-start.13 = (bf16[416,128]{1,0:T(8,128)(2,1)S(1)}, bf16[416,128]{1,0:T(8,128)(2,1)S(1)}, u32[]{:S(2)}, u32[]{:S(2)}) collective-permute-start(bf16[416,128]{1,0:T(8,128)(2,1)S(1)} %get-tuple-element.57), channel_id=1, source_target_pairs={{0,28},{4,24},{8,20},{12,16},{16,12},{20,8},{24,4},{28,0},{1,29},{... | collective-permute-start | bytes 319496 | tf_op jit(solution)/shard_map/ppermute | solution.py:42
  26.3 1.4 %collective-permute-start.9 = (bf16[416,128]{1,0:T(8,128)(2,1)S(1)}, bf16[416,128]{1,0:T(8,128)(2,1)S(1)}, u32[]{:S(2)}, u32[]{:S(2)}) collective-permute-start(bf16[416,128]{1,0:T(8,128)(2,1)S(1)} %get-tuple-element.52), channel_id=1, source_target_pairs={{0,16},{4,20},{8,24},{12,28},{16,0},{20,4},{24,8},{28,12},{1,17},{... | collective-permute-start | bytes 319496 | tf_op jit(solution)/shard_map/ppermute | solution.py:42
  27.7 1.2 %collective-permute-start.10 = (bf16[416,128]{1,0:T(8,128)(2,1)S(1)}, bf16[416,128]{1,0:T(8,128)(2,1)S(1)}, u32[]{:S(2)}, u32[]{:S(2)}) collective-permute-start(bf16[416,128]{1,0:T(8,128)(2,1)S(1)} %get-tuple-element.53), channel_id=1, source_target_pairs={{0,8},{4,12},{8,0},{12,4},{16,24},{20,28},{24,16},{28,20},{1,9},{5... | collective-permute-start | bytes 319496 | tf_op jit(solution)/shard_map/ppermute | solution.py:42
  28.9 1.1 %collective-permute-done.11.refs_1_ = bf16[416,128]{1,0:T(8,128)(2,1)S(1)} collective-permute-done((bf16[416,128]{1,0:T(8,128)(2,1)S(1)}, bf16[416,128]{1,0:T(8,128)(2,1)S(1)}, u32[]{:S(2)}, u32[]{:S(2)}) %collective-permute-start.11) | collective-permute-done | bytes 106528 | tf_op jit(solution)/shard_map/ppermute | solution.py:42
  30.0 0.0 collective-permute-start.7
  30.0 2.3 %collective-permute-start.8 = (bf16[416,128]{1,0:T(8,128)(2,1)S(1)}, bf16[416,128]{1,0:T(8,128)(2,1)S(1)}, u32[]{:S(2)}, u32[]{:S(2)}) collective-permute-start(bf16[416,128]{1,0:T(8,128)(2,1)S(1)} %get-tuple-element.51), channel_id=1, source_target_pairs={{0,12},{4,8},{8,4},{12,0},{16,28},{20,24},{24,20},{28,16},{1,13},{... | collective-permute-start | bytes 319496 | tf_op jit(solution)/shard_map/ppermute | solution.py:42
  32.4 1.4 %token_outputs.3 = (bf16[128,1024]{1,0:T(8,128)(2,1)}, bf16[128,1024]{1,0:T(8,128)(2,1)}, bf16[128,1024]{1,0:T(8,128)(2,1)}, bf16[128,1024]{1,0:T(8,128)(2,1)}, ...) custom-call(bf16[416,128]{1,0:T(8,128)(2,1)S(1)} %get-tuple-element.54.refs_0_, ...), custom_call_target="tpu_custom_call" | custom-call | bytes 4194304 | tf_op jit(solution)/shard_map/token_outputs/pallas_call | solution.py:461
  33.8 0.6 %collective-permute-done.9.refs_0_ = bf16[416,128]{1,0:T(8,128)(2,1)S(1)} collective-permute-done((bf16[416,128]{1,0:T(8,128)(2,1)S(1)}, bf16[416,128]{1,0:T(8,128)(2,1)S(1)}, u32[]{:S(2)}, u32[]{:S(2)}) %collective-permute-start.9) | collective-permute-done | bytes 106528 | tf_op jit(solution)/shard_map/ppermute | solution.py:42
  34.4 1.0 %token_outputs.4 = (bf16[128,1024]{1,0:T(8,128)(2,1)}, bf16[128,1024]{1,0:T(8,128)(2,1)}, bf16[128,1024]{1,0:T(8,128)(2,1)}, bf16[128,1024]{1,0:T(8,128)(2,1)}, ...) custom-call(bf16[416,128]{1,0:T(8,128)(2,1)S(1)} %collective-permute, ...), custom_call_target="tpu_custom_call", output_to_operand_aliasing={{0}: (7, {}), {1}: (8, {}), {2}: (9, {}), {3}: (10, {}), {4... | custom-call | bytes 4194304 | tf_op jit(solution)/shard_map/token_outputs/pallas_call | solution.py:461
  35.4 1.2 %collective-permute-done.7.refs_0_ = bf16[416,128]{1,0:T(8,128)(2,1)S(1)} collective-permute-done((bf16[416,128]{1,0:T(8,128)(2,1)S(1)}, bf16[416,128]{1,0:T(8,128)(2,1)S(1)}, u32[]{:S(2)}, u32[]{:S(2)}) %collective-permute-start.7) | collective-permute-done | bytes 106528 | tf_op jit(solution)/shard_map/ppermute | solution.py:42
  36.6 1.0 %token_outputs.5 = (bf16[128,1024]{1,0:T(8,128)(2,1)}, bf16[128,1024]{1,0:T(8,128)(2,1)}, bf16[128,1024]{1,0:T(8,128)(2,1)}, bf16[128,1024]{1,0:T(8,128)(2,1)}, ...) custom-call(bf16[416,128]{1,0:T(8,128)(2,1)S(1)} %collective-permute, ...), custom_call_target="tpu_custom_call", output_to_operand_aliasing={{0}: (7, {}), {1}: (8, {}), {2}: (9, {}), {3}: (10, {}), {4... | custom-call | bytes 4194304 | tf_op jit(solution)/shard_map/token_outputs/pallas_call | solution.py:461
  (16 shorter events, 0.0 us)
Async XLA Ops:
  0.6 11.8 %copy-start.4 = (bf16[4,256,512]{2,1,0:T(8,128)(2,1)S(1)}, bf16[4,256,512]{2,1,0:T(8,128)(2,1)}, u32[]{:S(2)}) copy-start(bf16[4,256,512]{2,1,0:T(8,128)(2,1)} %constant.5.clone.refs_3_) | copy-start | bytes 3145732
  0.6 11.7 %copy-start.6 = (f32[3,3,1024]{2,1,0:T(4,128)S(1)}, f32[3,3,1024]{2,1,0:T(4,128)}, u32[]{:S(2)}) copy-start(f32[3,3,1024]{2,1,0:T(4,128)} %refs_6_.5) | copy-start | bytes 110596
  2.2 7.7 %collective-permute-start = (bf16[640,128]{1,0:T(8,128)(2,1)S(1)}, bf16[640,128]{1,0:T(8,128)(2,1)S(1)}, u32[]{:S(2)}, u32[]{:S(2)}) collective-permute-start(bf16[640,128]{1,0:T(8,128)(2,1)S(1)} %get-tuple-element.39), channel_id=1, source_target_pairs={{0,16},{4,20},{8,24},{12,28},{16,0},{20,4},{24,8},{28,12},{1,17},{... | collective-permute-start | bytes 491528 | tf_op jit(solution)/shard_map/ppermute | solution.py:42
  5.3 7.1 %collective-permute-start.1 = (bf16[640,128]{1,0:T(8,128)(2,1)S(1)}, bf16[640,128]{1,0:T(8,128)(2,1)S(1)}, u32[]{:S(2)}, u32[]{:S(2)}) collective-permute-start(bf16[640,128]{1,0:T(8,128)(2,1)S(1)} %get-tuple-element.41), channel_id=1, source_target_pairs={{0,8},{4,12},{8,0},{12,4},{16,24},{20,28},{24,16},{28,20},{1,9},{5... | collective-permute-start | bytes 491528 | tf_op jit(solution)/shard_map/ppermute | solution.py:42
  6.7 8.7 %collective-permute-start.2 = (bf16[640,128]{1,0:T(8,128)(2,1)S(1)}, bf16[640,128]{1,0:T(8,128)(2,1)S(1)}, u32[]{:S(2)}, u32[]{:S(2)}) collective-permute-start(bf16[640,128]{1,0:T(8,128)(2,1)S(1)} %get-tuple-element.42), channel_id=1, source_target_pairs={{0,24},{4,28},{8,16},{12,20},{16,8},{20,12},{24,0},{28,4},{1,25},{... | collective-permute-start | bytes 491528 | tf_op jit(solution)/shard_map/ppermute | solution.py:42
  6.8 11.7 %collective-permute-start.3 = (bf16[640,128]{1,0:T(8,128)(2,1)S(1)}, bf16[640,128]{1,0:T(8,128)(2,1)S(1)}, u32[]{:S(2)}, u32[]{:S(2)}) collective-permute-start(bf16[640,128]{1,0:T(8,128)(2,1)S(1)} %get-tuple-element.43), channel_id=1, source_target_pairs={{0,28},{4,24},{8,20},{12,16},{16,12},{20,8},{24,4},{28,0},{1,29},{... | collective-permute-start | bytes 491528 | tf_op jit(solution)/shard_map/ppermute | solution.py:42
  8.3 12.2 %collective-permute-start.4 = (bf16[640,128]{1,0:T(8,128)(2,1)S(1)}, bf16[640,128]{1,0:T(8,128)(2,1)S(1)}, u32[]{:S(2)}, u32[]{:S(2)}) collective-permute-start(bf16[640,128]{1,0:T(8,128)(2,1)S(1)} %get-tuple-element.44), channel_id=1, source_target_pairs={{0,20},{4,16},{8,28},{12,24},{16,4},{20,0},{24,12},{28,8},{1,21},{... | collective-permute-start | bytes 491528 | tf_op jit(solution)/shard_map/ppermute | solution.py:42
  9.9 10.6 %collective-permute-start.5 = (bf16[640,128]{1,0:T(8,128)(2,1)S(1)}, bf16[640,128]{1,0:T(8,128)(2,1)S(1)}, u32[]{:S(2)}, u32[]{:S(2)}) collective-permute-start(bf16[640,128]{1,0:T(8,128)(2,1)S(1)} %get-tuple-element.45), channel_id=1, source_target_pairs={{0,12},{4,8},{8,4},{12,0},{16,28},{20,24},{24,20},{28,16},{1,13},{... | collective-permute-start | bytes 491528 | tf_op jit(solution)/shard_map/ppermute | solution.py:42
  12.4 8.1 %collective-permute-start.6 = (bf16[640,128]{1,0:T(8,128)(2,1)S(1)}, bf16[640,128]{1,0:T(8,128)(2,1)S(1)}, u32[]{:S(2)}, u32[]{:S(2)}) collective-permute-start(bf16[640,128]{1,0:T(8,128)(2,1)S(1)} %get-tuple-element.46), channel_id=1, source_target_pairs={{0,4},{4,0},{8,12},{12,8},{16,20},{20,16},{24,28},{28,24},{1,5},{5... | collective-permute-start | bytes 491528 | tf_op jit(solution)/shard_map/ppermute | solution.py:42
  12.4 1.2 %copy-start.5 = (bf16[4,512,256]{2,1,0:T(8,128)(2,1)S(1)}, bf16[4,512,256]{2,1,0:T(8,128)(2,1)}, u32[]{:S(2)}) copy-start(bf16[4,512,256]{2,1,0:T(8,128)(2,1)} %constant.4.clone.refs_2_) | copy-start | bytes 3145732
  20.5 11.8 %copy-start = (bf16[128,1024]{1,0:T(8,128)(2,1)S(1)}, bf16[128,1024]{1,0:T(8,128)(2,1)}, u32[]{:S(2)}) copy-start(bf16[128,1024]{1,0:T(8,128)(2,1)} %refs_2_.6) | copy-start | bytes 786436
  20.5 11.8 %copy-start.1 = (bf16[128,1024]{1,0:T(8,128)(2,1)S(1)}, bf16[128,1024]{1,0:T(8,128)(2,1)}, u32[]{:S(2)}) copy-start(bf16[128,1024]{1,0:T(8,128)(2,1)} %refs_3_.6) | copy-start | bytes 786436
  20.5 11.8 %copy-start.2 = (bf16[128,1024]{1,0:T(8,128)(2,1)S(1)}, bf16[128,1024]{1,0:T(8,128)(2,1)}, u32[]{:S(2)}) copy-start(bf16[128,1024]{1,0:T(8,128)(2,1)} %refs_4_.7) | copy-start | bytes 786436
  20.5 11.8 %copy-start.3 = (bf16[128,1024]{1,0:T(8,128)(2,1)S(1)}, bf16[128,1024]{1,0:T(8,128)(2,1)}, u32[]{:S(2)}) copy-start(bf16[128,1024]{1,0:T(8,128)(2,1)} %refs_5_.5) | copy-start | bytes 786436
  23.1 6.9 %collective-permute-start.11 = (bf16[416,128]{1,0:T(8,128)(2,1)S(1)}, bf16[416,128]{1,0:T(8,128)(2,1)S(1)}, u32[]{:S(2)}, u32[]{:S(2)}) collective-permute-start(bf16[416,128]{1,0:T(8,128)(2,1)S(1)} %get-tuple-element.55), channel_id=1, source_target_pairs={{0,24},{4,28},{8,16},{12,20},{16,8},{20,12},{24,0},{28,4},{1,25},{... | collective-permute-start | bytes 319496 | tf_op jit(solution)/shard_map/ppermute | solution.py:42
  25.3 4.7 %collective-permute-start.12 = (bf16[416,128]{1,0:T(8,128)(2,1)S(1)}, bf16[416,128]{1,0:T(8,128)(2,1)S(1)}, u32[]{:S(2)}, u32[]{:S(2)}) collective-permute-start(bf16[416,128]{1,0:T(8,128)(2,1)S(1)} %get-tuple-element.56), channel_id=1, source_target_pairs={{0,4},{4,0},{8,12},{12,8},{16,20},{20,16},{24,28},{28,24},{1,5},{5... | collective-permute-start | bytes 319496 | tf_op jit(solution)/shard_map/ppermute | solution.py:42
  25.3 7.0 %collective-permute-start.13 = (bf16[416,128]{1,0:T(8,128)(2,1)S(1)}, bf16[416,128]{1,0:T(8,128)(2,1)S(1)}, u32[]{:S(2)}, u32[]{:S(2)}) collective-permute-start(bf16[416,128]{1,0:T(8,128)(2,1)S(1)} %get-tuple-element.57), channel_id=1, source_target_pairs={{0,28},{4,24},{8,20},{12,16},{16,12},{20,8},{24,4},{28,0},{1,29},{... | collective-permute-start | bytes 319496 | tf_op jit(solution)/shard_map/ppermute | solution.py:42
  26.3 8.1 %collective-permute-start.9 = (bf16[416,128]{1,0:T(8,128)(2,1)S(1)}, bf16[416,128]{1,0:T(8,128)(2,1)S(1)}, u32[]{:S(2)}, u32[]{:S(2)}) collective-permute-start(bf16[416,128]{1,0:T(8,128)(2,1)S(1)} %get-tuple-element.52), channel_id=1, source_target_pairs={{0,16},{4,20},{8,24},{12,28},{16,0},{20,4},{24,8},{28,12},{1,17},{... | collective-permute-start | bytes 319496 | tf_op jit(solution)/shard_map/ppermute | solution.py:42
  27.7 6.7 %collective-permute-start.10 = (bf16[416,128]{1,0:T(8,128)(2,1)S(1)}, bf16[416,128]{1,0:T(8,128)(2,1)S(1)}, u32[]{:S(2)}, u32[]{:S(2)}) collective-permute-start(bf16[416,128]{1,0:T(8,128)(2,1)S(1)} %get-tuple-element.53), channel_id=1, source_target_pairs={{0,8},{4,12},{8,0},{12,4},{16,24},{20,28},{24,16},{28,20},{1,9},{5... | collective-permute-start | bytes 319496 | tf_op jit(solution)/shard_map/ppermute | solution.py:42
  30.0 6.6 %collective-permute-start.7 = (bf16[416,128]{1,0:T(8,128)(2,1)S(1)}, bf16[416,128]{1,0:T(8,128)(2,1)S(1)}, u32[]{:S(2)}, u32[]{:S(2)}) collective-permute-start(bf16[416,128]{1,0:T(8,128)(2,1)S(1)} %get-tuple-element.50), channel_id=1, source_target_pairs={{0,20},{4,16},{8,28},{12,24},{16,4},{20,0},{24,12},{28,8},{1,21},{... | collective-permute-start | bytes 319496 | tf_op jit(solution)/shard_map/ppermute | solution.py:42
  30.0 6.6 %collective-permute-start.8 = (bf16[416,128]{1,0:T(8,128)(2,1)S(1)}, bf16[416,128]{1,0:T(8,128)(2,1)S(1)}, u32[]{:S(2)}, u32[]{:S(2)}) collective-permute-start(bf16[416,128]{1,0:T(8,128)(2,1)S(1)} %get-tuple-element.51), channel_id=1, source_target_pairs={{0,12},{4,8},{8,4},{12,0},{16,28},{20,24},{24,20},{28,16},{1,13},{... | collective-permute-start | bytes 319496 | tf_op jit(solution)/shard_map/ppermute | solution.py:42

commit v16 on v12

--- a/solution.py
+++ b/solution.py
@@ -16,6 +16,7 @@
 TILE = 16
 PAD = 8
 CHUNK = 32
+ROWS = 8
 RIM = 2
 PIECES = 2
 MIB = 1024 * 1024
@@ -247,7 +248,7 @@
         lanes = slice(at * LANES, (at + 1) * LANES)
         for r, pair in enumerate(inverse_mix(mixed)):
             for rows, part in zip((real, imag), pair):
-                products[r, rows, lanes] = part.astype(BF16)
+                products[r, rows, lanes] = part
 
     for chunk in chunks:
         rows = rows_of(chunk)
@@ -269,9 +270,9 @@
             signals[r, rows, 2 * LANES :] = (cot_now[r] * query_now[r]).astype(BF16)
     for r in range(PHASES):
         spectra[r, :, 2 * LANES :] = transform(forward[r], signals[r, :, 2 * LANES :])
-    for step in range(size // TILE):
-        real = slice(step * TILE, (step + 1) * TILE)
-        imag = slice(size + step * TILE, size + (step + 1) * TILE)
+    for step in range(size // ROWS):
+        real = slice(step * ROWS, (step + 1) * ROWS)
+        imag = slice(size + step * ROWS, size + (step + 1) * ROWS)
         prod, filt = spectrum(0, real, imag), spectrum(1, real, imag)
         for at, mixed in enumerate((prod, filt)):
             lanes = slice(at * LANES, (at + 1) * LANES)
@@ -279,18 +280,18 @@
                 spectra[q, real, lanes], spectra[q, imag, lanes] = pair
         keep(0, real, imag, times(prod, filt))
     for r in range(PHASES):
-        result = transform(backward[r], products[r, :, :LANES])
+        result = transform(backward[r], products[r, :, :LANES].astype(BF16))
         conv[pl.ds(PAD + r, size, stride=PHASES), :] = result.astype(BF16).astype(F32)
-    for step in range(size // TILE):
-        real = slice(step * TILE, (step + 1) * TILE)
-        imag = slice(size + step * TILE, size + (step + 1) * TILE)
+    for step in range(size // ROWS):
+        real = slice(step * ROWS, (step + 1) * ROWS)
+        imag = slice(size + step * ROWS, size + (step + 1) * ROWS)
         grad = spectrum(2, real, imag)
         for at in range(2):
             lanes = slice(at * LANES, (at + 1) * LANES)
             known = [(spectra[q, real, lanes], spectra[q, imag, lanes]) for q in range(PHASES)]
             keep(2 - at, real, imag, conj_times(known, grad))
     for r in range(PHASES):
-        result = transform(backward[r], products[r, :, LANES:])
+        result = transform(backward[r], products[r, :, LANES:].astype(BF16))
         conv_grad[pl.ds(PAD + r, size, stride=PHASES), :] = (
             result[:, :LANES].astype(BF16).astype(F32)
         )
@@ -364,7 +365,7 @@
             phases,
             pltpu.VMEM((PHASES, size, 3 * LANES), BF16),
             pltpu.VMEM((PHASES, 2 * size, 3 * LANES), F32),
-            pltpu.VMEM((PHASES, 2 * size, 3 * LANES), BF16),
+            pltpu.VMEM((PHASES, 2 * size, 3 * LANES), F32),
             pltpu.VMEM((extra, LANES), F32),
         ],
         compiler_params=pltpu.CompilerParams(vmem_limit_bytes=VMEM_LIMIT),

time: 37.9 us -> 37.8 us (level)
  no operation moved by 1% of the time
where the time goes in v16:
time: 37.8 us; the launch traced here: 37.7 us
  starting transfers between devices  15.8 us (42%)
  waiting for transfers between devices  11.7 us (31%)
  Pallas kernels  8.08 us (21%)
  local copies, waits for them, and re-layouts  1.25 us (3%)
  between operations  0.74 us (2%)
    ppermute x14, starting transfers between devices, exchange(): lax.ppermute(block, 'ctx', [(i, i ^ step) for i in range(peers)])  15.8 us
    ppermute x14, waiting for transfers between devices, exchange(): lax.ppermute(block, 'ctx', [(i, i ^ step) for i in range(peers)])  11.7 us
    pallas_call x3, Pallas kernels, token_step(): pl.pallas_call(functools.partial(token_kernel, steps, extra_rows(short_we...  3.46 us
    pallas_call x1, Pallas kernels, channel_step(): pl.pallas_call(functools.partial(channel_kernel, tokens, heard, told, 1.0...  2.64 us
    pallas_call x1, Pallas kernels, pack(): pl.pallas_call(functools.partial(pack_kernel, count, steps), in_specs=[pl...  1.56 us
    unnamed x14, local copies, waits for them, and re-layouts  1.25 us
  transfers between devices with their start and end apart: 14, of which 7 were waited for; matrix products, arithmetic and copies ran while one was open for 0% of the time, Pallas kernels for 8%

profile of v16, /device:TPU:0, one launch (start us, length us, event | category | flops | bytes accessed | tf_op | source)
XLA Modules:
  0.0 37.7 jit_solution(944261741168876218)
XLA Ops:
  0.6 0.0 copy-start.4
  0.7 1.6 %pack_inputs.1 = (bf16[640,128]{1,0:T(8,128)(2,1)S(1)}, bf16[640,128]{1,0:T(8,128)(2,1)S(1)}, bf16[640,128]{1,0:T(8,128)(2,1)S(1)}, bf16[640,128]{1,0:T(8,128)(2...) custom-call(bf16[128,1024]{1,0:T(8,128)(2,1)} %refs_2_.6, ...), custom_call_target="tpu_custom_call" | custom-call | bytes 8388608 | tf_op jit(solution)/shard_map/pack_inputs/pallas_call | solution.py:76
  2.2 3.0 %collective-permute-start = (bf16[640,128]{1,0:T(8,128)(2,1)S(1)}, bf16[640,128]{1,0:T(8,128)(2,1)S(1)}, u32[]{:S(2)}, u32[]{:S(2)}) collective-permute-start(bf16[640,128]{1,0:T(8,128)(2,1)S(1)} %get-tuple-element.39), channel_id=1, source_target_pairs={{0,16},{4,20},{8,24},{12,28},{16,0},{20,4},{24,8},{28,12},{1,17},{... | collective-permute-start | bytes 491528 | tf_op jit(solution)/shard_map/ppermute | solution.py:43
  5.3 1.5 %collective-permute-start.1 = (bf16[640,128]{1,0:T(8,128)(2,1)S(1)}, bf16[640,128]{1,0:T(8,128)(2,1)S(1)}, u32[]{:S(2)}, u32[]{:S(2)}) collective-permute-start(bf16[640,128]{1,0:T(8,128)(2,1)S(1)} %get-tuple-element.41), channel_id=1, source_target_pairs={{0,8},{4,12},{8,0},{12,4},{16,24},{20,28},{24,16},{28,20},{1,9},{5... | collective-permute-start | bytes 491528 | tf_op jit(solution)/shard_map/ppermute | solution.py:43
  6.7 0.0 collective-permute-start.2
  6.8 1.5 %collective-permute-start.3 = (bf16[640,128]{1,0:T(8,128)(2,1)S(1)}, bf16[640,128]{1,0:T(8,128)(2,1)S(1)}, u32[]{:S(2)}, u32[]{:S(2)}) collective-permute-start(bf16[640,128]{1,0:T(8,128)(2,1)S(1)} %get-tuple-element.43), channel_id=1, source_target_pairs={{0,28},{4,24},{8,20},{12,16},{16,12},{20,8},{24,4},{28,0},{1,29},{... | collective-permute-start | bytes 491528 | tf_op jit(solution)/shard_map/ppermute | solution.py:43
  8.3 1.6 %collective-permute-start.4 = (bf16[640,128]{1,0:T(8,128)(2,1)S(1)}, bf16[640,128]{1,0:T(8,128)(2,1)S(1)}, u32[]{:S(2)}, u32[]{:S(2)}) collective-permute-start(bf16[640,128]{1,0:T(8,128)(2,1)S(1)} %get-tuple-element.44), channel_id=1, source_target_pairs={{0,20},{4,16},{8,28},{12,24},{16,4},{20,0},{24,12},{28,8},{1,21},{... | collective-permute-start | bytes 491528 | tf_op jit(solution)/shard_map/ppermute | solution.py:43
  9.9 0.0 collective-permute-done.refs_4_.refs_1_
  9.9 0.1 collective-permute-start.5
  10.0 2.4 %collective-permute-done.1.refs_2_ = bf16[640,128]{1,0:T(8,128)(2,1)S(1)} collective-permute-done((bf16[640,128]{1,0:T(8,128)(2,1)S(1)}, bf16[640,128]{1,0:T(8,128)(2,1)S(1)}, u32[]{:S(2)}, u32[]{:S(2)}) %collective-permute-start.1) | collective-permute-done | bytes 163872 | tf_op jit(solution)/shard_map/ppermute | solution.py:43
  12.4 0.0 copy-start.5
  12.4 1.2 %copy-done.5 = bf16[4,512,256]{2,1,0:T(8,128)(2,1)S(1)} copy-done((bf16[4,512,256]{2,1,0:T(8,128)(2,1)S(1)}, bf16[4,512,256]{2,1,0:T(8,128)(2,1)}, u32[]{:S(2)}) %copy-start.5) | copy-done | bytes 1048600
  13.6 0.4 %stage_tables.1 = (bf16[640,128]{1,0:T(8,128)(2,1)S(1)}, f32[3,3,1024]{2,1,0:T(4,128)S(1)}, bf16[4,512,256]{2,1,0:T(8,128)(2,1)S(1)}, bf16[4,256,512]{2,1,0:T(8,128)(2,1)S(1)}) custom-call(bf16[640,128]{1,0:T(8,128)(2,1)S(1)} %get-tuple-element.38.refs_0_, f32[3,3,1024]{2,1,0:T(4,128)S(1)} %copy-done.6, bf16[4,512,256]{2,1,0:T(8,128)(2,1)S(1)} %copy-done.5, ...), custom_call_target="tpu_custom_call" | custom-call | bytes 8388608 | tf_op jit(solution)/shard_map/stage_tables/pallas_call | solution.py:181
  14.0 1.4 %collective-permute-done.2.refs_3_ = bf16[640,128]{1,0:T(8,128)(2,1)S(1)} collective-permute-done((bf16[640,128]{1,0:T(8,128)(2,1)S(1)}, bf16[640,128]{1,0:T(8,128)(2,1)S(1)}, u32[]{:S(2)}, u32[]{:S(2)}) %collective-permute-start.2) | collective-permute-done | bytes 163872 | tf_op jit(solution)/shard_map/ppermute | solution.py:43
  15.5 3.0 %collective-permute-done.3.refs_4_ = bf16[640,128]{1,0:T(8,128)(2,1)S(1)} collective-permute-done((bf16[640,128]{1,0:T(8,128)(2,1)S(1)}, bf16[640,128]{1,0:T(8,128)(2,1)S(1)}, u32[]{:S(2)}, u32[]{:S(2)}) %collective-permute-start.3) | collective-permute-done | bytes 163872 | tf_op jit(solution)/shard_map/ppermute | solution.py:43
  18.5 2.0 %collective-permute-done.4.refs_5_ = bf16[640,128]{1,0:T(8,128)(2,1)S(1)} collective-permute-done((bf16[640,128]{1,0:T(8,128)(2,1)S(1)}, bf16[640,128]{1,0:T(8,128)(2,1)S(1)}, u32[]{:S(2)}, u32[]{:S(2)}) %collective-permute-start.4) | collective-permute-done | bytes 163872 | tf_op jit(solution)/shard_map/ppermute | solution.py:43
  20.5 0.0 collective-permute-done.5.refs_6_
  20.5 0.0 collective-permute-done.6.refs_7_
  20.5 0.0 copy-start.3
  20.5 2.6 %channel_operator.1 = (bf16[416,128]{1,0:T(8,128)(2,1)S(1)}, bf16[416,128]{1,0:T(8,128)(2,1)S(1)}, bf16[416,128]{1,0:T(8,128)(2,1)S(1)}, bf16[416,128]{1,0:T(8,1...) custom-call(bf16[640,128]{1,0:T(8,128)(2,1)S(1)} %get-tuple-element., ...), custom_call_target="tpu_custom_call" | custom-call | tf_op jit(solution)/shard_map/channel_operator/pallas_call | solution.py:355
  23.2 2.2 %collective-permute-start.11 = (bf16[416,128]{1,0:T(8,128)(2,1)S(1)}, bf16[416,128]{1,0:T(8,128)(2,1)S(1)}, u32[]{:S(2)}, u32[]{:S(2)}) collective-permute-start(bf16[416,128]{1,0:T(8,128)(2,1)S(1)} %get-tuple-element.55), channel_id=1, source_target_pairs={{0,24},{4,28},{8,16},{12,20},{16,8},{20,12},{24,0},{28,4},{1,25},{... | collective-permute-start | bytes 319496 | tf_op jit(solution)/shard_map/ppermute | solution.py:43
  25.4 0.0 collective-permute-start.12
  25.4 0.9 %collective-permute-start.13 = (bf16[416,128]{1,0:T(8,128)(2,1)S(1)}, bf16[416,128]{1,0:T(8,128)(2,1)S(1)}, u32[]{:S(2)}, u32[]{:S(2)}) collective-permute-start(bf16[416,128]{1,0:T(8,128)(2,1)S(1)} %get-tuple-element.57), channel_id=1, source_target_pairs={{0,28},{4,24},{8,20},{12,16},{16,12},{20,8},{24,4},{28,0},{1,29},{... | collective-permute-start | bytes 319496 | tf_op jit(solution)/shard_map/ppermute | solution.py:43
  26.3 1.5 %collective-permute-start.9 = (bf16[416,128]{1,0:T(8,128)(2,1)S(1)}, bf16[416,128]{1,0:T(8,128)(2,1)S(1)}, u32[]{:S(2)}, u32[]{:S(2)}) collective-permute-start(bf16[416,128]{1,0:T(8,128)(2,1)S(1)} %get-tuple-element.52), channel_id=1, source_target_pairs={{0,16},{4,20},{8,24},{12,28},{16,0},{20,4},{24,8},{28,12},{1,17},{... | collective-permute-start | bytes 319496 | tf_op jit(solution)/shard_map/ppermute | solution.py:43
  27.8 1.2 %collective-permute-start.10 = (bf16[416,128]{1,0:T(8,128)(2,1)S(1)}, bf16[416,128]{1,0:T(8,128)(2,1)S(1)}, u32[]{:S(2)}, u32[]{:S(2)}) collective-permute-start(bf16[416,128]{1,0:T(8,128)(2,1)S(1)} %get-tuple-element.53), channel_id=1, source_target_pairs={{0,8},{4,12},{8,0},{12,4},{16,24},{20,28},{24,16},{28,20},{1,9},{5... | collective-permute-start | bytes 319496 | tf_op jit(solution)/shard_map/ppermute | solution.py:43
  29.0 1.1 %collective-permute-done.11.refs_1_ = bf16[416,128]{1,0:T(8,128)(2,1)S(1)} collective-permute-done((bf16[416,128]{1,0:T(8,128)(2,1)S(1)}, bf16[416,128]{1,0:T(8,128)(2,1)S(1)}, u32[]{:S(2)}, u32[]{:S(2)}) %collective-permute-start.11) | collective-permute-done | bytes 106528 | tf_op jit(solution)/shard_map/ppermute | solution.py:43
  30.1 2.3 %collective-permute-start.8 = (bf16[416,128]{1,0:T(8,128)(2,1)S(1)}, bf16[416,128]{1,0:T(8,128)(2,1)S(1)}, u32[]{:S(2)}, u32[]{:S(2)}) collective-permute-start(bf16[416,128]{1,0:T(8,128)(2,1)S(1)} %get-tuple-element.51), channel_id=1, source_target_pairs={{0,12},{4,8},{8,4},{12,0},{16,28},{20,24},{24,20},{28,16},{1,13},{... | collective-permute-start | bytes 319496 | tf_op jit(solution)/shard_map/ppermute | solution.py:43
  32.4 1.4 %token_outputs.3 = (bf16[128,1024]{1,0:T(8,128)(2,1)}, bf16[128,1024]{1,0:T(8,128)(2,1)}, bf16[128,1024]{1,0:T(8,128)(2,1)}, bf16[128,1024]{1,0:T(8,128)(2,1)}, ...) custom-call(bf16[416,128]{1,0:T(8,128)(2,1)S(1)} %get-tuple-element.54.refs_0_, ...), custom_call_target="tpu_custom_call" | custom-call | bytes 4194304 | tf_op jit(solution)/shard_map/token_outputs/pallas_call | solution.py:446
  33.8 0.6 %collective-permute-done.9.refs_0_ = bf16[416,128]{1,0:T(8,128)(2,1)S(1)} collective-permute-done((bf16[416,128]{1,0:T(8,128)(2,1)S(1)}, bf16[416,128]{1,0:T(8,128)(2,1)S(1)}, u32[]{:S(2)}, u32[]{:S(2)}) %collective-permute-start.9) | collective-permute-done | bytes 106528 | tf_op jit(solution)/shard_map/ppermute | solution.py:43
  34.4 1.0 %token_outputs.4 = (bf16[128,1024]{1,0:T(8,128)(2,1)}, bf16[128,1024]{1,0:T(8,128)(2,1)}, bf16[128,1024]{1,0:T(8,128)(2,1)}, bf16[128,1024]{1,0:T(8,128)(2,1)}, ...) custom-call(bf16[416,128]{1,0:T(8,128)(2,1)S(1)} %collective-permute, ...), custom_call_target="tpu_custom_call", output_to_operand_aliasing={{0}: (7, {}), {1}: (8, {}), {2}: (9, {}), {3}: (10, {}), {4... | custom-call | bytes 4194304 | tf_op jit(solution)/shard_map/token_outputs/pallas_call | solution.py:446
  35.5 1.2 %collective-permute-done.7.refs_0_ = bf16[416,128]{1,0:T(8,128)(2,1)S(1)} collective-permute-done((bf16[416,128]{1,0:T(8,128)(2,1)S(1)}, bf16[416,128]{1,0:T(8,128)(2,1)S(1)}, u32[]{:S(2)}, u32[]{:S(2)}) %collective-permute-start.7) | collective-permute-done | bytes 106528 | tf_op jit(solution)/shard_map/ppermute | solution.py:43
  36.6 1.0 %token_outputs.5 = (bf16[128,1024]{1,0:T(8,128)(2,1)}, bf16[128,1024]{1,0:T(8,128)(2,1)}, bf16[128,1024]{1,0:T(8,128)(2,1)}, bf16[128,1024]{1,0:T(8,128)(2,1)}, ...) custom-call(bf16[416,128]{1,0:T(8,128)(2,1)S(1)} %collective-permute, ...), custom_call_target="tpu_custom_call", output_to_operand_aliasing={{0}: (7, {}), {1}: (8, {}), {2}: (9, {}), {3}: (10, {}), {4... | custom-call | bytes 4194304 | tf_op jit(solution)/shard_map/token_outputs/pallas_call | solution.py:446
  (16 shorter events, 0.0 us)
Async XLA Ops:
  0.6 11.8 %copy-start.4 = (bf16[4,256,512]{2,1,0:T(8,128)(2,1)S(1)}, bf16[4,256,512]{2,1,0:T(8,128)(2,1)}, u32[]{:S(2)}) copy-start(bf16[4,256,512]{2,1,0:T(8,128)(2,1)} %constant.5.clone.refs_3_) | copy-start | bytes 3145732
  0.6 11.7 %copy-start.6 = (f32[3,3,1024]{2,1,0:T(4,128)S(1)}, f32[3,3,1024]{2,1,0:T(4,128)}, u32[]{:S(2)}) copy-start(f32[3,3,1024]{2,1,0:T(4,128)} %refs_6_.5) | copy-start | bytes 110596
  2.2 7.7 %collective-permute-start = (bf16[640,128]{1,0:T(8,128)(2,1)S(1)}, bf16[640,128]{1,0:T(8,128)(2,1)S(1)}, u32[]{:S(2)}, u32[]{:S(2)}) collective-permute-start(bf16[640,128]{1,0:T(8,128)(2,1)S(1)} %get-tuple-element.39), channel_id=1, source_target_pairs={{0,16},{4,20},{8,24},{12,28},{16,0},{20,4},{24,8},{28,12},{1,17},{... | collective-permute-start | bytes 491528 | tf_op jit(solution)/shard_map/ppermute | solution.py:43
  5.3 7.1 %collective-permute-start.1 = (bf16[640,128]{1,0:T(8,128)(2,1)S(1)}, bf16[640,128]{1,0:T(8,128)(2,1)S(1)}, u32[]{:S(2)}, u32[]{:S(2)}) collective-permute-start(bf16[640,128]{1,0:T(8,128)(2,1)S(1)} %get-tuple-element.41), channel_id=1, source_target_pairs={{0,8},{4,12},{8,0},{12,4},{16,24},{20,28},{24,16},{28,20},{1,9},{5... | collective-permute-start | bytes 491528 | tf_op jit(solution)/shard_map/ppermute | solution.py:43
  6.7 8.7 %collective-permute-start.2 = (bf16[640,128]{1,0:T(8,128)(2,1)S(1)}, bf16[640,128]{1,0:T(8,128)(2,1)S(1)}, u32[]{:S(2)}, u32[]{:S(2)}) collective-permute-start(bf16[640,128]{1,0:T(8,128)(2,1)S(1)} %get-tuple-element.42), channel_id=1, source_target_pairs={{0,24},{4,28},{8,16},{12,20},{16,8},{20,12},{24,0},{28,4},{1,25},{... | collective-permute-start | bytes 491528 | tf_op jit(solution)/shard_map/ppermute | solution.py:43
  6.8 11.7 %collective-permute-start.3 = (bf16[640,128]{1,0:T(8,128)(2,1)S(1)}, bf16[640,128]{1,0:T(8,128)(2,1)S(1)}, u32[]{:S(2)}, u32[]{:S(2)}) collective-permute-start(bf16[640,128]{1,0:T(8,128)(2,1)S(1)} %get-tuple-element.43), channel_id=1, source_target_pairs={{0,28},{4,24},{8,20},{12,16},{16,12},{20,8},{24,4},{28,0},{1,29},{... | collective-permute-start | bytes 491528 | tf_op jit(solution)/shard_map/ppermute | solution.py:43
  8.3 12.2 %collective-permute-start.4 = (bf16[640,128]{1,0:T(8,128)(2,1)S(1)}, bf16[640,128]{1,0:T(8,128)(2,1)S(1)}, u32[]{:S(2)}, u32[]{:S(2)}) collective-permute-start(bf16[640,128]{1,0:T(8,128)(2,1)S(1)} %get-tuple-element.44), channel_id=1, source_target_pairs={{0,20},{4,16},{8,28},{12,24},{16,4},{20,0},{24,12},{28,8},{1,21},{... | collective-permute-start | bytes 491528 | tf_op jit(solution)/shard_map/ppermute | solution.py:43
  9.9 10.6 %collective-permute-start.5 = (bf16[640,128]{1,0:T(8,128)(2,1)S(1)}, bf16[640,128]{1,0:T(8,128)(2,1)S(1)}, u32[]{:S(2)}, u32[]{:S(2)}) collective-permute-start(bf16[640,128]{1,0:T(8,128)(2,1)S(1)} %get-tuple-element.45), channel_id=1, source_target_pairs={{0,12},{4,8},{8,4},{12,0},{16,28},{20,24},{24,20},{28,16},{1,13},{... | collective-permute-start | bytes 491528 | tf_op jit(solution)/shard_map/ppermute | solution.py:43
  12.4 8.1 %collective-permute-start.6 = (bf16[640,128]{1,0:T(8,128)(2,1)S(1)}, bf16[640,128]{1,0:T(8,128)(2,1)S(1)}, u32[]{:S(2)}, u32[]{:S(2)}) collective-permute-start(bf16[640,128]{1,0:T(8,128)(2,1)S(1)} %get-tuple-element.46), channel_id=1, source_target_pairs={{0,4},{4,0},{8,12},{12,8},{16,20},{20,16},{24,28},{28,24},{1,5},{5... | collective-permute-start | bytes 491528 | tf_op jit(solution)/shard_map/ppermute | solution.py:43
  12.4 1.2 %copy-start.5 = (bf16[4,512,256]{2,1,0:T(8,128)(2,1)S(1)}, bf16[4,512,256]{2,1,0:T(8,128)(2,1)}, u32[]{:S(2)}) copy-start(bf16[4,512,256]{2,1,0:T(8,128)(2,1)} %constant.4.clone.refs_2_) | copy-start | bytes 3145732
  20.5 11.9 %copy-start = (bf16[128,1024]{1,0:T(8,128)(2,1)S(1)}, bf16[128,1024]{1,0:T(8,128)(2,1)}, u32[]{:S(2)}) copy-start(bf16[128,1024]{1,0:T(8,128)(2,1)} %refs_2_.6) | copy-start | bytes 786436
  20.5 11.9 %copy-start.1 = (bf16[128,1024]{1,0:T(8,128)(2,1)S(1)}, bf16[128,1024]{1,0:T(8,128)(2,1)}, u32[]{:S(2)}) copy-start(bf16[128,1024]{1,0:T(8,128)(2,1)} %refs_3_.6) | copy-start | bytes 786436
  20.5 11.9 %copy-start.2 = (bf16[128,1024]{1,0:T(8,128)(2,1)S(1)}, bf16[128,1024]{1,0:T(8,128)(2,1)}, u32[]{:S(2)}) copy-start(bf16[128,1024]{1,0:T(8,128)(2,1)} %refs_4_.7) | copy-start | bytes 786436
  20.5 11.9 %copy-start.3 = (bf16[128,1024]{1,0:T(8,128)(2,1)S(1)}, bf16[128,1024]{1,0:T(8,128)(2,1)}, u32[]{:S(2)}) copy-start(bf16[128,1024]{1,0:T(8,128)(2,1)} %refs_5_.5) | copy-start | bytes 786436
  23.2 6.9 %collective-permute-start.11 = (bf16[416,128]{1,0:T(8,128)(2,1)S(1)}, bf16[416,128]{1,0:T(8,128)(2,1)S(1)}, u32[]{:S(2)}, u32[]{:S(2)}) collective-permute-start(bf16[416,128]{1,0:T(8,128)(2,1)S(1)} %get-tuple-element.55), channel_id=1, source_target_pairs={{0,24},{4,28},{8,16},{12,20},{16,8},{20,12},{24,0},{28,4},{1,25},{... | collective-permute-start | bytes 319496 | tf_op jit(solution)/shard_map/ppermute | solution.py:43
  25.4 4.7 %collective-permute-start.12 = (bf16[416,128]{1,0:T(8,128)(2,1)S(1)}, bf16[416,128]{1,0:T(8,128)(2,1)S(1)}, u32[]{:S(2)}, u32[]{:S(2)}) collective-permute-start(bf16[416,128]{1,0:T(8,128)(2,1)S(1)} %get-tuple-element.56), channel_id=1, source_target_pairs={{0,4},{4,0},{8,12},{12,8},{16,20},{20,16},{24,28},{28,24},{1,5},{5... | collective-permute-start | bytes 319496 | tf_op jit(solution)/shard_map/ppermute | solution.py:43
  25.4 7.0 %collective-permute-start.13 = (bf16[416,128]{1,0:T(8,128)(2,1)S(1)}, bf16[416,128]{1,0:T(8,128)(2,1)S(1)}, u32[]{:S(2)}, u32[]{:S(2)}) collective-permute-start(bf16[416,128]{1,0:T(8,128)(2,1)S(1)} %get-tuple-element.57), channel_id=1, source_target_pairs={{0,28},{4,24},{8,20},{12,16},{16,12},{20,8},{24,4},{28,0},{1,29},{... | collective-permute-start | bytes 319496 | tf_op jit(solution)/shard_map/ppermute | solution.py:43
  26.3 8.1 %collective-permute-start.9 = (bf16[416,128]{1,0:T(8,128)(2,1)S(1)}, bf16[416,128]{1,0:T(8,128)(2,1)S(1)}, u32[]{:S(2)}, u32[]{:S(2)}) collective-permute-start(bf16[416,128]{1,0:T(8,128)(2,1)S(1)} %get-tuple-element.52), channel_id=1, source_target_pairs={{0,16},{4,20},{8,24},{12,28},{16,0},{20,4},{24,8},{28,12},{1,17},{... | collective-permute-start | bytes 319496 | tf_op jit(solution)/shard_map/ppermute | solution.py:43
  27.8 6.7 %collective-permute-start.10 = (bf16[416,128]{1,0:T(8,128)(2,1)S(1)}, bf16[416,128]{1,0:T(8,128)(2,1)S(1)}, u32[]{:S(2)}, u32[]{:S(2)}) collective-permute-start(bf16[416,128]{1,0:T(8,128)(2,1)S(1)} %get-tuple-element.53), channel_id=1, source_target_pairs={{0,8},{4,12},{8,0},{12,4},{16,24},{20,28},{24,16},{28,20},{1,9},{5... | collective-permute-start | bytes 319496 | tf_op jit(solution)/shard_map/ppermute | solution.py:43
  30.0 6.6 %collective-permute-start.7 = (bf16[416,128]{1,0:T(8,128)(2,1)S(1)}, bf16[416,128]{1,0:T(8,128)(2,1)S(1)}, u32[]{:S(2)}, u32[]{:S(2)}) collective-permute-start(bf16[416,128]{1,0:T(8,128)(2,1)S(1)} %get-tuple-element.50), channel_id=1, source_target_pairs={{0,20},{4,16},{8,28},{12,24},{16,4},{20,0},{24,12},{28,8},{1,21},{... | collective-permute-start | bytes 319496 | tf_op jit(solution)/shard_map/ppermute | solution.py:43
  30.1 6.6 %collective-permute-start.8 = (bf16[416,128]{1,0:T(8,128)(2,1)S(1)}, bf16[416,128]{1,0:T(8,128)(2,1)S(1)}, u32[]{:S(2)}, u32[]{:S(2)}) collective-permute-start(bf16[416,128]{1,0:T(8,128)(2,1)S(1)} %get-tuple-element.51), channel_id=1, source_target_pairs={{0,12},{4,8},{8,4},{12,0},{16,28},{20,24},{24,20},{28,16},{1,13},{... | collective-permute-start | bytes 319496 | tf_op jit(solution)/shard_map/ppermute | solution.py:43

commit v17 on v16

--- a/solution.py
+++ b/solution.py
@@ -274,28 +274,17 @@
         real = slice(step * ROWS, (step + 1) * ROWS)
         imag = slice(size + step * ROWS, size + (step + 1) * ROWS)
         prod, filt = spectrum(0, real, imag), spectrum(1, real, imag)
-        for at, mixed in enumerate((prod, filt)):
-            lanes = slice(at * LANES, (at + 1) * LANES)
-            for q, pair in enumerate(mixed):
-                spectra[q, real, lanes], spectra[q, imag, lanes] = pair
         keep(0, real, imag, times(prod, filt))
+        grad = spectrum(2, real, imag)
+        keep(1, real, imag, conj_times(filt, grad))
+        keep(2, real, imag, conj_times(prod, grad))
     for r in range(PHASES):
-        result = transform(backward[r], products[r, :, :LANES].astype(BF16))
-        conv[pl.ds(PAD + r, size, stride=PHASES), :] = result.astype(BF16).astype(F32)
-    for step in range(size // ROWS):
-        real = slice(step * ROWS, (step + 1) * ROWS)
-        imag = slice(size + step * ROWS, size + (step + 1) * ROWS)
-        grad = spectrum(2, real, imag)
-        for at in range(2):
-            lanes = slice(at * LANES, (at + 1) * LANES)
-            known = [(spectra[q, real, lanes], spectra[q, imag, lanes]) for q in range(PHASES)]
-            keep(2 - at, real, imag, conj_times(known, grad))
-    for r in range(PHASES):
-        result = transform(backward[r], products[r, :, LANES:].astype(BF16))
-        conv_grad[pl.ds(PAD + r, size, stride=PHASES), :] = (
-            result[:, :LANES].astype(BF16).astype(F32)
-        )
-        filter_grad[pl.ds(r, size, stride=PHASES), :] = result[:, LANES:] * grad_scale
+        result = transform(backward[r], products[r].astype(BF16))
+        for at, ref in enumerate((conv, conv_grad)):
+            ref[pl.ds(PAD + r, size, stride=PHASES), :] = (
+                result[:, at * LANES : (at + 1) * LANES].astype(BF16).astype(F32)
+            )
+        filter_grad[pl.ds(r, size, stride=PHASES), :] = result[:, 2 * LANES :] * grad_scale
 
     totals = [[None] * tap_count for _ in range(3)]
 

time: 37.8 us -> 38.1 us (level)
  no operation moved by 1% of the time
where the time goes in v17:
time: 38.1 us; the launch traced here: 37.9 us
  starting transfers between devices  15.9 us (42%)
  waiting for transfers between devices  11.7 us (31%)
  Pallas kernels  8.3 us (22%)
  local copies, waits for them, and re-layouts  1.25 us (3%)
  between operations  0.74 us (2%)
    ppermute x14, starting transfers between devices, exchange(): lax.ppermute(block, 'ctx', [(i, i ^ step) for i in range(peers)])  15.9 us
    ppermute x14, waiting for transfers between devices, exchange(): lax.ppermute(block, 'ctx', [(i, i ^ step) for i in range(peers)])  11.7 us
    pallas_call x3, Pallas kernels, token_step(): pl.pallas_call(functools.partial(token_kernel, steps, extra_rows(short_we...  3.46 us
    pallas_call x1, Pallas kernels, channel_step(): pl.pallas_call(functools.partial(channel_kernel, tokens, heard, told, 1.0...  2.86 us
    pallas_call x1, Pallas kernels, pack(): pl.pallas_call(functools.partial(pack_kernel, count, steps), in_specs=[pl...  1.56 us
    unnamed x14, local copies, waits for them, and re-layouts  1.25 us
  transfers between devices with their start and end apart: 14, of which 7 were waited for; matrix products, arithmetic and copies ran while one was open for 0% of the time, Pallas kernels for 8%

profile of v17, /device:TPU:0, one launch (start us, length us, event | category | flops | bytes accessed | tf_op | source)
XLA Modules:
  0.0 37.9 jit_solution(5127297951893948076)
XLA Ops:
  0.6 0.0 copy-start.4
  0.7 1.6 %pack_inputs.1 = (bf16[640,128]{1,0:T(8,128)(2,1)S(1)}, bf16[640,128]{1,0:T(8,128)(2,1)S(1)}, bf16[640,128]{1,0:T(8,128)(2,1)S(1)}, bf16[640,128]{1,0:T(8,128)(2...) custom-call(bf16[128,1024]{1,0:T(8,128)(2,1)} %refs_2_.6, ...), custom_call_target="tpu_custom_call" | custom-call | bytes 8388608 | tf_op jit(solution)/shard_map/pack_inputs/pallas_call | solution.py:76
  2.2 3.0 %collective-permute-start = (bf16[640,128]{1,0:T(8,128)(2,1)S(1)}, bf16[640,128]{1,0:T(8,128)(2,1)S(1)}, u32[]{:S(2)}, u32[]{:S(2)}) collective-permute-start(bf16[640,128]{1,0:T(8,128)(2,1)S(1)} %get-tuple-element.39), channel_id=1, source_target_pairs={{0,16},{4,20},{8,24},{12,28},{16,0},{20,4},{24,8},{28,12},{1,17},{... | collective-permute-start | bytes 491528 | tf_op jit(solution)/shard_map/ppermute | solution.py:43
  5.3 1.5 %collective-permute-start.1 = (bf16[640,128]{1,0:T(8,128)(2,1)S(1)}, bf16[640,128]{1,0:T(8,128)(2,1)S(1)}, u32[]{:S(2)}, u32[]{:S(2)}) collective-permute-start(bf16[640,128]{1,0:T(8,128)(2,1)S(1)} %get-tuple-element.41), channel_id=1, source_target_pairs={{0,8},{4,12},{8,0},{12,4},{16,24},{20,28},{24,16},{28,20},{1,9},{5... | collective-permute-start | bytes 491528 | tf_op jit(solution)/shard_map/ppermute | solution.py:43
  6.7 0.0 collective-permute-start.2
  6.8 1.5 %collective-permute-start.3 = (bf16[640,128]{1,0:T(8,128)(2,1)S(1)}, bf16[640,128]{1,0:T(8,128)(2,1)S(1)}, u32[]{:S(2)}, u32[]{:S(2)}) collective-permute-start(bf16[640,128]{1,0:T(8,128)(2,1)S(1)} %get-tuple-element.43), channel_id=1, source_target_pairs={{0,28},{4,24},{8,20},{12,16},{16,12},{20,8},{24,4},{28,0},{1,29},{... | collective-permute-start | bytes 491528 | tf_op jit(solution)/shard_map/ppermute | solution.py:43
  8.3 1.6 %collective-permute-start.4 = (bf16[640,128]{1,0:T(8,128)(2,1)S(1)}, bf16[640,128]{1,0:T(8,128)(2,1)S(1)}, u32[]{:S(2)}, u32[]{:S(2)}) collective-permute-start(bf16[640,128]{1,0:T(8,128)(2,1)S(1)} %get-tuple-element.44), channel_id=1, source_target_pairs={{0,20},{4,16},{8,28},{12,24},{16,4},{20,0},{24,12},{28,8},{1,21},{... | collective-permute-start | bytes 491528 | tf_op jit(solution)/shard_map/ppermute | solution.py:43
  9.9 0.0 collective-permute-done.refs_4_.refs_1_
  9.9 0.1 collective-permute-start.5
  10.0 2.4 %collective-permute-done.1.refs_2_ = bf16[640,128]{1,0:T(8,128)(2,1)S(1)} collective-permute-done((bf16[640,128]{1,0:T(8,128)(2,1)S(1)}, bf16[640,128]{1,0:T(8,128)(2,1)S(1)}, u32[]{:S(2)}, u32[]{:S(2)}) %collective-permute-start.1) | collective-permute-done | bytes 163872 | tf_op jit(solution)/shard_map/ppermute | solution.py:43
  12.4 0.0 copy-start.5
  12.4 1.2 %copy-done.5 = bf16[4,512,256]{2,1,0:T(8,128)(2,1)S(1)} copy-done((bf16[4,512,256]{2,1,0:T(8,128)(2,1)S(1)}, bf16[4,512,256]{2,1,0:T(8,128)(2,1)}, u32[]{:S(2)}) %copy-start.5) | copy-done | bytes 1048600
  13.6 0.4 %stage_tables.1 = (bf16[640,128]{1,0:T(8,128)(2,1)S(1)}, f32[3,3,1024]{2,1,0:T(4,128)S(1)}, bf16[4,512,256]{2,1,0:T(8,128)(2,1)S(1)}, bf16[4,256,512]{2,1,0:T(8,128)(2,1)S(1)}) custom-call(bf16[640,128]{1,0:T(8,128)(2,1)S(1)} %get-tuple-element.38.refs_0_, f32[3,3,1024]{2,1,0:T(4,128)S(1)} %copy-done.6, bf16[4,512,256]{2,1,0:T(8,128)(2,1)S(1)} %copy-done.5, ...), custom_call_target="tpu_custom_call" | custom-call | bytes 8388608 | tf_op jit(solution)/shard_map/stage_tables/pallas_call | solution.py:181
  14.0 1.4 %collective-permute-done.2.refs_3_ = bf16[640,128]{1,0:T(8,128)(2,1)S(1)} collective-permute-done((bf16[640,128]{1,0:T(8,128)(2,1)S(1)}, bf16[640,128]{1,0:T(8,128)(2,1)S(1)}, u32[]{:S(2)}, u32[]{:S(2)}) %collective-permute-start.2) | collective-permute-done | bytes 163872 | tf_op jit(solution)/shard_map/ppermute | solution.py:43
  15.5 3.0 %collective-permute-done.3.refs_4_ = bf16[640,128]{1,0:T(8,128)(2,1)S(1)} collective-permute-done((bf16[640,128]{1,0:T(8,128)(2,1)S(1)}, bf16[640,128]{1,0:T(8,128)(2,1)S(1)}, u32[]{:S(2)}, u32[]{:S(2)}) %collective-permute-start.3) | collective-permute-done | bytes 163872 | tf_op jit(solution)/shard_map/ppermute | solution.py:43
  18.5 2.0 %collective-permute-done.4.refs_5_ = bf16[640,128]{1,0:T(8,128)(2,1)S(1)} collective-permute-done((bf16[640,128]{1,0:T(8,128)(2,1)S(1)}, bf16[640,128]{1,0:T(8,128)(2,1)S(1)}, u32[]{:S(2)}, u32[]{:S(2)}) %collective-permute-start.4) | collective-permute-done | bytes 163872 | tf_op jit(solution)/shard_map/ppermute | solution.py:43
  20.5 0.0 collective-permute-done.5.refs_6_
  20.5 0.0 collective-permute-done.6.refs_7_
  20.5 0.0 copy-start.3
  20.5 2.9 %channel_operator.1 = (bf16[416,128]{1,0:T(8,128)(2,1)S(1)}, bf16[416,128]{1,0:T(8,128)(2,1)S(1)}, bf16[416,128]{1,0:T(8,128)(2,1)S(1)}, bf16[416,128]{1,0:T(8,1...) custom-call(bf16[640,128]{1,0:T(8,128)(2,1)S(1)} %get-tuple-element., ...), custom_call_target="tpu_custom_call" | custom-call | tf_op jit(solution)/shard_map/channel_operator/pallas_call | solution.py:344
  23.4 2.2 %collective-permute-start.11 = (bf16[416,128]{1,0:T(8,128)(2,1)S(1)}, bf16[416,128]{1,0:T(8,128)(2,1)S(1)}, u32[]{:S(2)}, u32[]{:S(2)}) collective-permute-start(bf16[416,128]{1,0:T(8,128)(2,1)S(1)} %get-tuple-element.55), channel_id=1, source_target_pairs={{0,24},{4,28},{8,16},{12,20},{16,8},{20,12},{24,0},{28,4},{1,25},{... | collective-permute-start | bytes 319496 | tf_op jit(solution)/shard_map/ppermute | solution.py:43
  25.6 0.9 %collective-permute-start.13 = (bf16[416,128]{1,0:T(8,128)(2,1)S(1)}, bf16[416,128]{1,0:T(8,128)(2,1)S(1)}, u32[]{:S(2)}, u32[]{:S(2)}) collective-permute-start(bf16[416,128]{1,0:T(8,128)(2,1)S(1)} %get-tuple-element.57), channel_id=1, source_target_pairs={{0,28},{4,24},{8,20},{12,16},{16,12},{20,8},{24,4},{28,0},{1,29},{... | collective-permute-start | bytes 319496 | tf_op jit(solution)/shard_map/ppermute | solution.py:43
  26.5 1.4 %collective-permute-start.9 = (bf16[416,128]{1,0:T(8,128)(2,1)S(1)}, bf16[416,128]{1,0:T(8,128)(2,1)S(1)}, u32[]{:S(2)}, u32[]{:S(2)}) collective-permute-start(bf16[416,128]{1,0:T(8,128)(2,1)S(1)} %get-tuple-element.52), channel_id=1, source_target_pairs={{0,16},{4,20},{8,24},{12,28},{16,0},{20,4},{24,8},{28,12},{1,17},{... | collective-permute-start | bytes 319496 | tf_op jit(solution)/shard_map/ppermute | solution.py:43
  28.0 1.2 %collective-permute-start.10 = (bf16[416,128]{1,0:T(8,128)(2,1)S(1)}, bf16[416,128]{1,0:T(8,128)(2,1)S(1)}, u32[]{:S(2)}, u32[]{:S(2)}) collective-permute-start(bf16[416,128]{1,0:T(8,128)(2,1)S(1)} %get-tuple-element.53), channel_id=1, source_target_pairs={{0,8},{4,12},{8,0},{12,4},{16,24},{20,28},{24,16},{28,20},{1,9},{5... | collective-permute-start | bytes 319496 | tf_op jit(solution)/shard_map/ppermute | solution.py:43
  29.2 1.1 %collective-permute-done.11.refs_1_ = bf16[416,128]{1,0:T(8,128)(2,1)S(1)} collective-permute-done((bf16[416,128]{1,0:T(8,128)(2,1)S(1)}, bf16[416,128]{1,0:T(8,128)(2,1)S(1)}, u32[]{:S(2)}, u32[]{:S(2)}) %collective-permute-start.11) | collective-permute-done | bytes 106528 | tf_op jit(solution)/shard_map/ppermute | solution.py:43
  30.3 2.3 %collective-permute-start.8 = (bf16[416,128]{1,0:T(8,128)(2,1)S(1)}, bf16[416,128]{1,0:T(8,128)(2,1)S(1)}, u32[]{:S(2)}, u32[]{:S(2)}) collective-permute-start(bf16[416,128]{1,0:T(8,128)(2,1)S(1)} %get-tuple-element.51), channel_id=1, source_target_pairs={{0,12},{4,8},{8,4},{12,0},{16,28},{20,24},{24,20},{28,16},{1,13},{... | collective-permute-start | bytes 319496 | tf_op jit(solution)/shard_map/ppermute | solution.py:43
  32.6 0.0 collective-permute-done.13.refs_3_
  32.6 1.4 %token_outputs.3 = (bf16[128,1024]{1,0:T(8,128)(2,1)}, bf16[128,1024]{1,0:T(8,128)(2,1)}, bf16[128,1024]{1,0:T(8,128)(2,1)}, bf16[128,1024]{1,0:T(8,128)(2,1)}, ...) custom-call(bf16[416,128]{1,0:T(8,128)(2,1)S(1)} %get-tuple-element.54.refs_0_, ...), custom_call_target="tpu_custom_call" | custom-call | bytes 4194304 | tf_op jit(solution)/shard_map/token_outputs/pallas_call | solution.py:435
  34.0 0.6 %collective-permute-done.9.refs_0_ = bf16[416,128]{1,0:T(8,128)(2,1)S(1)} collective-permute-done((bf16[416,128]{1,0:T(8,128)(2,1)S(1)}, bf16[416,128]{1,0:T(8,128)(2,1)S(1)}, u32[]{:S(2)}, u32[]{:S(2)}) %collective-permute-start.9) | collective-permute-done | bytes 106528 | tf_op jit(solution)/shard_map/ppermute | solution.py:43
  34.7 1.0 %token_outputs.4 = (bf16[128,1024]{1,0:T(8,128)(2,1)}, bf16[128,1024]{1,0:T(8,128)(2,1)}, bf16[128,1024]{1,0:T(8,128)(2,1)}, bf16[128,1024]{1,0:T(8,128)(2,1)}, ...) custom-call(bf16[416,128]{1,0:T(8,128)(2,1)S(1)} %collective-permute, ...), custom_call_target="tpu_custom_call", output_to_operand_aliasing={{0}: (7, {}), {1}: (8, {}), {2}: (9, {}), {3}: (10, {}), {4... | custom-call | bytes 4194304 | tf_op jit(solution)/shard_map/token_outputs/pallas_call | solution.py:435
  35.7 1.2 %collective-permute-done.7.refs_0_ = bf16[416,128]{1,0:T(8,128)(2,1)S(1)} collective-permute-done((bf16[416,128]{1,0:T(8,128)(2,1)S(1)}, bf16[416,128]{1,0:T(8,128)(2,1)S(1)}, u32[]{:S(2)}, u32[]{:S(2)}) %collective-permute-start.7) | collective-permute-done | bytes 106528 | tf_op jit(solution)/shard_map/ppermute | solution.py:43
  36.9 1.0 %token_outputs.5 = (bf16[128,1024]{1,0:T(8,128)(2,1)}, bf16[128,1024]{1,0:T(8,128)(2,1)}, bf16[128,1024]{1,0:T(8,128)(2,1)}, bf16[128,1024]{1,0:T(8,128)(2,1)}, ...) custom-call(bf16[416,128]{1,0:T(8,128)(2,1)S(1)} %collective-permute, ...), custom_call_target="tpu_custom_call", output_to_operand_aliasing={{0}: (7, {}), {1}: (8, {}), {2}: (9, {}), {3}: (10, {}), {4... | custom-call | bytes 4194304 | tf_op jit(solution)/shard_map/token_outputs/pallas_call | solution.py:435
  (16 shorter events, 0.0 us)
Async XLA Ops:
  0.6 11.8 %copy-start.4 = (bf16[4,256,512]{2,1,0:T(8,128)(2,1)S(1)}, bf16[4,256,512]{2,1,0:T(8,128)(2,1)}, u32[]{:S(2)}) copy-start(bf16[4,256,512]{2,1,0:T(8,128)(2,1)} %constant.5.clone.refs_3_) | copy-start | bytes 3145732
  0.6 11.7 %copy-start.6 = (f32[3,3,1024]{2,1,0:T(4,128)S(1)}, f32[3,3,1024]{2,1,0:T(4,128)}, u32[]{:S(2)}) copy-start(f32[3,3,1024]{2,1,0:T(4,128)} %refs_6_.5) | copy-start | bytes 110596
  2.2 7.7 %collective-permute-start = (bf16[640,128]{1,0:T(8,128)(2,1)S(1)}, bf16[640,128]{1,0:T(8,128)(2,1)S(1)}, u32[]{:S(2)}, u32[]{:S(2)}) collective-permute-start(bf16[640,128]{1,0:T(8,128)(2,1)S(1)} %get-tuple-element.39), channel_id=1, source_target_pairs={{0,16},{4,20},{8,24},{12,28},{16,0},{20,4},{24,8},{28,12},{1,17},{... | collective-permute-start | bytes 491528 | tf_op jit(solution)/shard_map/ppermute | solution.py:43
  5.3 7.1 %collective-permute-start.1 = (bf16[640,128]{1,0:T(8,128)(2,1)S(1)}, bf16[640,128]{1,0:T(8,128)(2,1)S(1)}, u32[]{:S(2)}, u32[]{:S(2)}) collective-permute-start(bf16[640,128]{1,0:T(8,128)(2,1)S(1)} %get-tuple-element.41), channel_id=1, source_target_pairs={{0,8},{4,12},{8,0},{12,4},{16,24},{20,28},{24,16},{28,20},{1,9},{5... | collective-permute-start | bytes 491528 | tf_op jit(solution)/shard_map/ppermute | solution.py:43
  6.7 8.7 %collective-permute-start.2 = (bf16[640,128]{1,0:T(8,128)(2,1)S(1)}, bf16[640,128]{1,0:T(8,128)(2,1)S(1)}, u32[]{:S(2)}, u32[]{:S(2)}) collective-permute-start(bf16[640,128]{1,0:T(8,128)(2,1)S(1)} %get-tuple-element.42), channel_id=1, source_target_pairs={{0,24},{4,28},{8,16},{12,20},{16,8},{20,12},{24,0},{28,4},{1,25},{... | collective-permute-start | bytes 491528 | tf_op jit(solution)/shard_map/ppermute | solution.py:43
  6.8 11.7 %collective-permute-start.3 = (bf16[640,128]{1,0:T(8,128)(2,1)S(1)}, bf16[640,128]{1,0:T(8,128)(2,1)S(1)}, u32[]{:S(2)}, u32[]{:S(2)}) collective-permute-start(bf16[640,128]{1,0:T(8,128)(2,1)S(1)} %get-tuple-element.43), channel_id=1, source_target_pairs={{0,28},{4,24},{8,20},{12,16},{16,12},{20,8},{24,4},{28,0},{1,29},{... | collective-permute-start | bytes 491528 | tf_op jit(solution)/shard_map/ppermute | solution.py:43
  8.3 12.2 %collective-permute-start.4 = (bf16[640,128]{1,0:T(8,128)(2,1)S(1)}, bf16[640,128]{1,0:T(8,128)(2,1)S(1)}, u32[]{:S(2)}, u32[]{:S(2)}) collective-permute-start(bf16[640,128]{1,0:T(8,128)(2,1)S(1)} %get-tuple-element.44), channel_id=1, source_target_pairs={{0,20},{4,16},{8,28},{12,24},{16,4},{20,0},{24,12},{28,8},{1,21},{... | collective-permute-start | bytes 491528 | tf_op jit(solution)/shard_map/ppermute | solution.py:43
  9.9 10.6 %collective-permute-start.5 = (bf16[640,128]{1,0:T(8,128)(2,1)S(1)}, bf16[640,128]{1,0:T(8,128)(2,1)S(1)}, u32[]{:S(2)}, u32[]{:S(2)}) collective-permute-start(bf16[640,128]{1,0:T(8,128)(2,1)S(1)} %get-tuple-element.45), channel_id=1, source_target_pairs={{0,12},{4,8},{8,4},{12,0},{16,28},{20,24},{24,20},{28,16},{1,13},{... | collective-permute-start | bytes 491528 | tf_op jit(solution)/shard_map/ppermute | solution.py:43
  12.4 8.1 %collective-permute-start.6 = (bf16[640,128]{1,0:T(8,128)(2,1)S(1)}, bf16[640,128]{1,0:T(8,128)(2,1)S(1)}, u32[]{:S(2)}, u32[]{:S(2)}) collective-permute-start(bf16[640,128]{1,0:T(8,128)(2,1)S(1)} %get-tuple-element.46), channel_id=1, source_target_pairs={{0,4},{4,0},{8,12},{12,8},{16,20},{20,16},{24,28},{28,24},{1,5},{5... | collective-permute-start | bytes 491528 | tf_op jit(solution)/shard_map/ppermute | solution.py:43
  12.4 1.2 %copy-start.5 = (bf16[4,512,256]{2,1,0:T(8,128)(2,1)S(1)}, bf16[4,512,256]{2,1,0:T(8,128)(2,1)}, u32[]{:S(2)}) copy-start(bf16[4,512,256]{2,1,0:T(8,128)(2,1)} %constant.4.clone.refs_2_) | copy-start | bytes 3145732
  20.5 12.1 %copy-start = (bf16[128,1024]{1,0:T(8,128)(2,1)S(1)}, bf16[128,1024]{1,0:T(8,128)(2,1)}, u32[]{:S(2)}) copy-start(bf16[128,1024]{1,0:T(8,128)(2,1)} %refs_2_.6) | copy-start | bytes 786436
  20.5 12.1 %copy-start.1 = (bf16[128,1024]{1,0:T(8,128)(2,1)S(1)}, bf16[128,1024]{1,0:T(8,128)(2,1)}, u32[]{:S(2)}) copy-start(bf16[128,1024]{1,0:T(8,128)(2,1)} %refs_3_.6) | copy-start | bytes 786436
  20.5 12.1 %copy-start.2 = (bf16[128,1024]{1,0:T(8,128)(2,1)S(1)}, bf16[128,1024]{1,0:T(8,128)(2,1)}, u32[]{:S(2)}) copy-start(bf16[128,1024]{1,0:T(8,128)(2,1)} %refs_4_.7) | copy-start | bytes 786436
  20.5 12.1 %copy-start.3 = (bf16[128,1024]{1,0:T(8,128)(2,1)S(1)}, bf16[128,1024]{1,0:T(8,128)(2,1)}, u32[]{:S(2)}) copy-start(bf16[128,1024]{1,0:T(8,128)(2,1)} %refs_5_.5) | copy-start | bytes 786436
  23.4 6.9 %collective-permute-start.11 = (bf16[416,128]{1,0:T(8,128)(2,1)S(1)}, bf16[416,128]{1,0:T(8,128)(2,1)S(1)}, u32[]{:S(2)}, u32[]{:S(2)}) collective-permute-start(bf16[416,128]{1,0:T(8,128)(2,1)S(1)} %get-tuple-element.55), channel_id=1, source_target_pairs={{0,24},{4,28},{8,16},{12,20},{16,8},{20,12},{24,0},{28,4},{1,25},{... | collective-permute-start | bytes 319496 | tf_op jit(solution)/shard_map/ppermute | solution.py:43
  25.6 4.7 %collective-permute-start.12 = (bf16[416,128]{1,0:T(8,128)(2,1)S(1)}, bf16[416,128]{1,0:T(8,128)(2,1)S(1)}, u32[]{:S(2)}, u32[]{:S(2)}) collective-permute-start(bf16[416,128]{1,0:T(8,128)(2,1)S(1)} %get-tuple-element.56), channel_id=1, source_target_pairs={{0,4},{4,0},{8,12},{12,8},{16,20},{20,16},{24,28},{28,24},{1,5},{5... | collective-permute-start | bytes 319496 | tf_op jit(solution)/shard_map/ppermute | solution.py:43
  25.6 7.0 %collective-permute-start.13 = (bf16[416,128]{1,0:T(8,128)(2,1)S(1)}, bf16[416,128]{1,0:T(8,128)(2,1)S(1)}, u32[]{:S(2)}, u32[]{:S(2)}) collective-permute-start(bf16[416,128]{1,0:T(8,128)(2,1)S(1)} %get-tuple-element.57), channel_id=1, source_target_pairs={{0,28},{4,24},{8,20},{12,16},{16,12},{20,8},{24,4},{28,0},{1,29},{... | collective-permute-start | bytes 319496 | tf_op jit(solution)/shard_map/ppermute | solution.py:43
  26.5 8.1 %collective-permute-start.9 = (bf16[416,128]{1,0:T(8,128)(2,1)S(1)}, bf16[416,128]{1,0:T(8,128)(2,1)S(1)}, u32[]{:S(2)}, u32[]{:S(2)}) collective-permute-start(bf16[416,128]{1,0:T(8,128)(2,1)S(1)} %get-tuple-element.52), channel_id=1, source_target_pairs={{0,16},{4,20},{8,24},{12,28},{16,0},{20,4},{24,8},{28,12},{1,17},{... | collective-permute-start | bytes 319496 | tf_op jit(solution)/shard_map/ppermute | solution.py:43
  28.0 6.7 %collective-permute-start.10 = (bf16[416,128]{1,0:T(8,128)(2,1)S(1)}, bf16[416,128]{1,0:T(8,128)(2,1)S(1)}, u32[]{:S(2)}, u32[]{:S(2)}) collective-permute-start(bf16[416,128]{1,0:T(8,128)(2,1)S(1)} %get-tuple-element.53), channel_id=1, source_target_pairs={{0,8},{4,12},{8,0},{12,4},{16,24},{20,28},{24,16},{28,20},{1,9},{5... | collective-permute-start | bytes 319496 | tf_op jit(solution)/shard_map/ppermute | solution.py:43
  30.3 6.6 %collective-permute-start.7 = (bf16[416,128]{1,0:T(8,128)(2,1)S(1)}, bf16[416,128]{1,0:T(8,128)(2,1)S(1)}, u32[]{:S(2)}, u32[]{:S(2)}) collective-permute-start(bf16[416,128]{1,0:T(8,128)(2,1)S(1)} %get-tuple-element.50), channel_id=1, source_target_pairs={{0,20},{4,16},{8,28},{12,24},{16,4},{20,0},{24,12},{28,8},{1,21},{... | collective-permute-start | bytes 319496 | tf_op jit(solution)/shard_map/ppermute | solution.py:43
  30.3 6.6 %collective-permute-start.8 = (bf16[416,128]{1,0:T(8,128)(2,1)S(1)}, bf16[416,128]{1,0:T(8,128)(2,1)S(1)}, u32[]{:S(2)}, u32[]{:S(2)}) collective-permute-start(bf16[416,128]{1,0:T(8,128)(2,1)S(1)} %get-tuple-element.51), channel_id=1, source_target_pairs={{0,12},{4,8},{8,4},{12,0},{16,28},{20,24},{24,20},{28,16},{1,13},{... | collective-permute-start | bytes 319496 | tf_op jit(solution)/shard_map/ppermute | solution.py:43

commit v18 on v16

--- a/solution.py
+++ b/solution.py
@@ -244,6 +244,10 @@
             [(spectra[r, real, lanes], spectra[r, imag, lanes]) for r in range(PHASES)]
         )
 
+    def mixed_spectrum(at, real, imag):
+        lanes = slice(at * LANES, (at + 1) * LANES)
+        return [(spectra[q, real, lanes], spectra[q, imag, lanes]) for q in range(PHASES)]
+
     def keep(at, real, imag, mixed):
         lanes = slice(at * LANES, (at + 1) * LANES)
         for r, pair in enumerate(inverse_mix(mixed)):
@@ -286,16 +290,20 @@
         real = slice(step * ROWS, (step + 1) * ROWS)
         imag = slice(size + step * ROWS, size + (step + 1) * ROWS)
         grad = spectrum(2, real, imag)
-        for at in range(2):
-            lanes = slice(at * LANES, (at + 1) * LANES)
-            known = [(spectra[q, real, lanes], spectra[q, imag, lanes]) for q in range(PHASES)]
-            keep(2 - at, real, imag, conj_times(known, grad))
+        for q, pair in enumerate(grad):
+            spectra[q, real, 2 * LANES :], spectra[q, imag, 2 * LANES :] = pair
+        keep(1, real, imag, conj_times(mixed_spectrum(1, real, imag), grad))
     for r in range(PHASES):
-        result = transform(backward[r], products[r, :, LANES:].astype(BF16))
-        conv_grad[pl.ds(PAD + r, size, stride=PHASES), :] = (
-            result[:, :LANES].astype(BF16).astype(F32)
-        )
-        filter_grad[pl.ds(r, size, stride=PHASES), :] = result[:, LANES:] * grad_scale
+        result = transform(backward[r], products[r, :, LANES : 2 * LANES].astype(BF16))
+        conv_grad[pl.ds(PAD + r, size, stride=PHASES), :] = result.astype(BF16).astype(F32)
+    for step in range(size // ROWS):
+        real = slice(step * ROWS, (step + 1) * ROWS)
+        imag = slice(size + step * ROWS, size + (step + 1) * ROWS)
+        known = (mixed_spectrum(at, real, imag) for at in (0, 2))
+        keep(2, real, imag, conj_times(*known))
+    for r in range(PHASES):
+        result = transform(backward[r], products[r, :, 2 * LANES :].astype(BF16))
+        filter_grad[pl.ds(r, size, stride=PHASES), :] = result * grad_scale
 
     totals = [[None] * tap_count for _ in range(3)]
 

time: 37.8 us -> 38.3 us (1.013)
  Pallas kernels: 8.08 us -> 8.52 us
    pallas_call x1, Pallas kernels: 2.64 us -> 3.08 us  [channel_step(): pl.pallas_call(functools.partial(channel_kernel, tokens, heard, told, 1.0...]
  transfers between devices with their start and end apart: 14 -> 14, of which waited for: 7 -> 7; matrix products, arithmetic and copies ran while one was open for 0% -> 0% of each run, Pallas kernels for 8% -> 7%
where the time goes in v18:
time: 38.3 us; the launch traced here: 38.1 us
  starting transfers between devices  15.9 us (42%)
  waiting for transfers between devices  11.7 us (31%)
  Pallas kernels  8.52 us (22%)
  local copies, waits for them, and re-layouts  1.25 us (3%)
  between operations  0.75 us (2%)
    ppermute x14, starting transfers between devices, exchange(): lax.ppermute(block, 'ctx', [(i, i ^ step) for i in range(peers)])  15.9 us
    ppermute x14, waiting for transfers between devices, exchange(): lax.ppermute(block, 'ctx', [(i, i ^ step) for i in range(peers)])  11.7 us
    pallas_call x3, Pallas kernels, token_step(): pl.pallas_call(functools.partial(token_kernel, steps, extra_rows(short_we...  3.46 us
    pallas_call x1, Pallas kernels, channel_step(): pl.pallas_call(functools.partial(channel_kernel, tokens, heard, told, 1.0...  3.08 us
    pallas_call x1, Pallas kernels, pack(): pl.pallas_call(functools.partial(pack_kernel, count, steps), in_specs=[pl...  1.56 us
    unnamed x14, local copies, waits for them, and re-layouts  1.25 us
  transfers between devices with their start and end apart: 14, of which 7 were waited for; matrix products, arithmetic and copies ran while one was open for 0% of the time, Pallas kernels for 7%

profile of v18, /device:TPU:0, one launch (start us, length us, event | category | flops | bytes accessed | tf_op | source)
XLA Modules:
  0.0 38.1 jit_solution(7517398395537125130)
XLA Ops:
  0.6 0.0 copy-start.4
  0.7 1.6 %pack_inputs.1 = (bf16[640,128]{1,0:T(8,128)(2,1)S(1)}, bf16[640,128]{1,0:T(8,128)(2,1)S(1)}, bf16[640,128]{1,0:T(8,128)(2,1)S(1)}, bf16[640,128]{1,0:T(8,128)(2...) custom-call(bf16[128,1024]{1,0:T(8,128)(2,1)} %refs_2_.6, ...), custom_call_target="tpu_custom_call" | custom-call | bytes 8388608 | tf_op jit(solution)/shard_map/pack_inputs/pallas_call | solution.py:76
  2.2 3.0 %collective-permute-start = (bf16[640,128]{1,0:T(8,128)(2,1)S(1)}, bf16[640,128]{1,0:T(8,128)(2,1)S(1)}, u32[]{:S(2)}, u32[]{:S(2)}) collective-permute-start(bf16[640,128]{1,0:T(8,128)(2,1)S(1)} %get-tuple-element.39), channel_id=1, source_target_pairs={{0,16},{4,20},{8,24},{12,28},{16,0},{20,4},{24,8},{28,12},{1,17},{... | collective-permute-start | bytes 491528 | tf_op jit(solution)/shard_map/ppermute | solution.py:43
  5.3 1.5 %collective-permute-start.1 = (bf16[640,128]{1,0:T(8,128)(2,1)S(1)}, bf16[640,128]{1,0:T(8,128)(2,1)S(1)}, u32[]{:S(2)}, u32[]{:S(2)}) collective-permute-start(bf16[640,128]{1,0:T(8,128)(2,1)S(1)} %get-tuple-element.41), channel_id=1, source_target_pairs={{0,8},{4,12},{8,0},{12,4},{16,24},{20,28},{24,16},{28,20},{1,9},{5... | collective-permute-start | bytes 491528 | tf_op jit(solution)/shard_map/ppermute | solution.py:43
  6.7 0.0 collective-permute-start.2
  6.8 1.5 %collective-permute-start.3 = (bf16[640,128]{1,0:T(8,128)(2,1)S(1)}, bf16[640,128]{1,0:T(8,128)(2,1)S(1)}, u32[]{:S(2)}, u32[]{:S(2)}) collective-permute-start(bf16[640,128]{1,0:T(8,128)(2,1)S(1)} %get-tuple-element.43), channel_id=1, source_target_pairs={{0,28},{4,24},{8,20},{12,16},{16,12},{20,8},{24,4},{28,0},{1,29},{... | collective-permute-start | bytes 491528 | tf_op jit(solution)/shard_map/ppermute | solution.py:43
  8.3 1.6 %collective-permute-start.4 = (bf16[640,128]{1,0:T(8,128)(2,1)S(1)}, bf16[640,128]{1,0:T(8,128)(2,1)S(1)}, u32[]{:S(2)}, u32[]{:S(2)}) collective-permute-start(bf16[640,128]{1,0:T(8,128)(2,1)S(1)} %get-tuple-element.44), channel_id=1, source_target_pairs={{0,20},{4,16},{8,28},{12,24},{16,4},{20,0},{24,12},{28,8},{1,21},{... | collective-permute-start | bytes 491528 | tf_op jit(solution)/shard_map/ppermute | solution.py:43
  9.9 0.1 collective-permute-start.5
  10.0 2.4 %collective-permute-done.1.refs_2_ = bf16[640,128]{1,0:T(8,128)(2,1)S(1)} collective-permute-done((bf16[640,128]{1,0:T(8,128)(2,1)S(1)}, bf16[640,128]{1,0:T(8,128)(2,1)S(1)}, u32[]{:S(2)}, u32[]{:S(2)}) %collective-permute-start.1) | collective-permute-done | bytes 163872 | tf_op jit(solution)/shard_map/ppermute | solution.py:43
  12.4 0.0 copy-start.5
  12.4 1.2 %copy-done.5 = bf16[4,512,256]{2,1,0:T(8,128)(2,1)S(1)} copy-done((bf16[4,512,256]{2,1,0:T(8,128)(2,1)S(1)}, bf16[4,512,256]{2,1,0:T(8,128)(2,1)}, u32[]{:S(2)}) %copy-start.5) | copy-done | bytes 1048600
  13.6 0.4 %stage_tables.1 = (bf16[640,128]{1,0:T(8,128)(2,1)S(1)}, f32[3,3,1024]{2,1,0:T(4,128)S(1)}, bf16[4,512,256]{2,1,0:T(8,128)(2,1)S(1)}, bf16[4,256,512]{2,1,0:T(8,128)(2,1)S(1)}) custom-call(bf16[640,128]{1,0:T(8,128)(2,1)S(1)} %get-tuple-element.38.refs_0_, f32[3,3,1024]{2,1,0:T(4,128)S(1)} %copy-done.6, bf16[4,512,256]{2,1,0:T(8,128)(2,1)S(1)} %copy-done.5, ...), custom_call_target="tpu_custom_call" | custom-call | bytes 8388608 | tf_op jit(solution)/shard_map/stage_tables/pallas_call | solution.py:181
  14.0 1.4 %collective-permute-done.2.refs_3_ = bf16[640,128]{1,0:T(8,128)(2,1)S(1)} collective-permute-done((bf16[640,128]{1,0:T(8,128)(2,1)S(1)}, bf16[640,128]{1,0:T(8,128)(2,1)S(1)}, u32[]{:S(2)}, u32[]{:S(2)}) %collective-permute-start.2) | collective-permute-done | bytes 163872 | tf_op jit(solution)/shard_map/ppermute | solution.py:43
  15.5 3.0 %collective-permute-done.3.refs_4_ = bf16[640,128]{1,0:T(8,128)(2,1)S(1)} collective-permute-done((bf16[640,128]{1,0:T(8,128)(2,1)S(1)}, bf16[640,128]{1,0:T(8,128)(2,1)S(1)}, u32[]{:S(2)}, u32[]{:S(2)}) %collective-permute-start.3) | collective-permute-done | bytes 163872 | tf_op jit(solution)/shard_map/ppermute | solution.py:43
  18.5 2.0 %collective-permute-done.4.refs_5_ = bf16[640,128]{1,0:T(8,128)(2,1)S(1)} collective-permute-done((bf16[640,128]{1,0:T(8,128)(2,1)S(1)}, bf16[640,128]{1,0:T(8,128)(2,1)S(1)}, u32[]{:S(2)}, u32[]{:S(2)}) %collective-permute-start.4) | collective-permute-done | bytes 163872 | tf_op jit(solution)/shard_map/ppermute | solution.py:43
  20.5 0.0 collective-permute-done.5.refs_6_
  20.5 0.0 copy-start.3
  20.5 3.1 %channel_operator.1 = (bf16[416,128]{1,0:T(8,128)(2,1)S(1)}, bf16[416,128]{1,0:T(8,128)(2,1)S(1)}, bf16[416,128]{1,0:T(8,128)(2,1)S(1)}, bf16[416,128]{1,0:T(8,1...) custom-call(bf16[640,128]{1,0:T(8,128)(2,1)S(1)} %get-tuple-element., ...), custom_call_target="tpu_custom_call" | custom-call | tf_op jit(solution)/shard_map/channel_operator/pallas_call | solution.py:363
  23.6 2.2 %collective-permute-start.11 = (bf16[416,128]{1,0:T(8,128)(2,1)S(1)}, bf16[416,128]{1,0:T(8,128)(2,1)S(1)}, u32[]{:S(2)}, u32[]{:S(2)}) collective-permute-start(bf16[416,128]{1,0:T(8,128)(2,1)S(1)} %get-tuple-element.55), channel_id=1, source_target_pairs={{0,24},{4,28},{8,16},{12,20},{16,8},{20,12},{24,0},{28,4},{1,25},{... | collective-permute-start | bytes 319496 | tf_op jit(solution)/shard_map/ppermute | solution.py:43
  25.8 0.9 %collective-permute-start.13 = (bf16[416,128]{1,0:T(8,128)(2,1)S(1)}, bf16[416,128]{1,0:T(8,128)(2,1)S(1)}, u32[]{:S(2)}, u32[]{:S(2)}) collective-permute-start(bf16[416,128]{1,0:T(8,128)(2,1)S(1)} %get-tuple-element.57), channel_id=1, source_target_pairs={{0,28},{4,24},{8,20},{12,16},{16,12},{20,8},{24,4},{28,0},{1,29},{... | collective-permute-start | bytes 319496 | tf_op jit(solution)/shard_map/ppermute | solution.py:43
  26.7 1.4 %collective-permute-start.9 = (bf16[416,128]{1,0:T(8,128)(2,1)S(1)}, bf16[416,128]{1,0:T(8,128)(2,1)S(1)}, u32[]{:S(2)}, u32[]{:S(2)}) collective-permute-start(bf16[416,128]{1,0:T(8,128)(2,1)S(1)} %get-tuple-element.52), channel_id=1, source_target_pairs={{0,16},{4,20},{8,24},{12,28},{16,0},{20,4},{24,8},{28,12},{1,17},{... | collective-permute-start | bytes 319496 | tf_op jit(solution)/shard_map/ppermute | solution.py:43
  28.2 1.2 %collective-permute-start.10 = (bf16[416,128]{1,0:T(8,128)(2,1)S(1)}, bf16[416,128]{1,0:T(8,128)(2,1)S(1)}, u32[]{:S(2)}, u32[]{:S(2)}) collective-permute-start(bf16[416,128]{1,0:T(8,128)(2,1)S(1)} %get-tuple-element.53), channel_id=1, source_target_pairs={{0,8},{4,12},{8,0},{12,4},{16,24},{20,28},{24,16},{28,20},{1,9},{5... | collective-permute-start | bytes 319496 | tf_op jit(solution)/shard_map/ppermute | solution.py:43
  29.4 1.1 %collective-permute-done.11.refs_1_ = bf16[416,128]{1,0:T(8,128)(2,1)S(1)} collective-permute-done((bf16[416,128]{1,0:T(8,128)(2,1)S(1)}, bf16[416,128]{1,0:T(8,128)(2,1)S(1)}, u32[]{:S(2)}, u32[]{:S(2)}) %collective-permute-start.11) | collective-permute-done | bytes 106528 | tf_op jit(solution)/shard_map/ppermute | solution.py:43
  30.5 0.0 collective-permute-start.7
  30.5 0.0 collective-permute-done.12.refs_2_
  30.5 2.3 %collective-permute-start.8 = (bf16[416,128]{1,0:T(8,128)(2,1)S(1)}, bf16[416,128]{1,0:T(8,128)(2,1)S(1)}, u32[]{:S(2)}, u32[]{:S(2)}) collective-permute-start(bf16[416,128]{1,0:T(8,128)(2,1)S(1)} %get-tuple-element.51), channel_id=1, source_target_pairs={{0,12},{4,8},{8,4},{12,0},{16,28},{20,24},{24,20},{28,16},{1,13},{... | collective-permute-start | bytes 319496 | tf_op jit(solution)/shard_map/ppermute | solution.py:43
  32.8 0.0 collective-permute-done.13.refs_3_
  32.8 1.4 %token_outputs.3 = (bf16[128,1024]{1,0:T(8,128)(2,1)}, bf16[128,1024]{1,0:T(8,128)(2,1)}, bf16[128,1024]{1,0:T(8,128)(2,1)}, bf16[128,1024]{1,0:T(8,128)(2,1)}, ...) custom-call(bf16[416,128]{1,0:T(8,128)(2,1)S(1)} %get-tuple-element.54.refs_0_, ...), custom_call_target="tpu_custom_call" | custom-call | bytes 4194304 | tf_op jit(solution)/shard_map/token_outputs/pallas_call | solution.py:454
  34.3 0.6 %collective-permute-done.9.refs_0_ = bf16[416,128]{1,0:T(8,128)(2,1)S(1)} collective-permute-done((bf16[416,128]{1,0:T(8,128)(2,1)S(1)}, bf16[416,128]{1,0:T(8,128)(2,1)S(1)}, u32[]{:S(2)}, u32[]{:S(2)}) %collective-permute-start.9) | collective-permute-done | bytes 106528 | tf_op jit(solution)/shard_map/ppermute | solution.py:43
  34.9 1.0 %token_outputs.4 = (bf16[128,1024]{1,0:T(8,128)(2,1)}, bf16[128,1024]{1,0:T(8,128)(2,1)}, bf16[128,1024]{1,0:T(8,128)(2,1)}, bf16[128,1024]{1,0:T(8,128)(2,1)}, ...) custom-call(bf16[416,128]{1,0:T(8,128)(2,1)S(1)} %collective-permute, ...), custom_call_target="tpu_custom_call", output_to_operand_aliasing={{0}: (7, {}), {1}: (8, {}), {2}: (9, {}), {3}: (10, {}), {4... | custom-call | bytes 4194304 | tf_op jit(solution)/shard_map/token_outputs/pallas_call | solution.py:454
  35.9 1.2 %collective-permute-done.7.refs_0_ = bf16[416,128]{1,0:T(8,128)(2,1)S(1)} collective-permute-done((bf16[416,128]{1,0:T(8,128)(2,1)S(1)}, bf16[416,128]{1,0:T(8,128)(2,1)S(1)}, u32[]{:S(2)}, u32[]{:S(2)}) %collective-permute-start.7) | collective-permute-done | bytes 106528 | tf_op jit(solution)/shard_map/ppermute | solution.py:43
  37.1 1.0 %token_outputs.5 = (bf16[128,1024]{1,0:T(8,128)(2,1)}, bf16[128,1024]{1,0:T(8,128)(2,1)}, bf16[128,1024]{1,0:T(8,128)(2,1)}, bf16[128,1024]{1,0:T(8,128)(2,1)}, ...) custom-call(bf16[416,128]{1,0:T(8,128)(2,1)S(1)} %collective-permute, ...), custom_call_target="tpu_custom_call", output_to_operand_aliasing={{0}: (7, {}), {1}: (8, {}), {2}: (9, {}), {3}: (10, {}), {4... | custom-call | bytes 4194304 | tf_op jit(solution)/shard_map/token_outputs/pallas_call | solution.py:454
  (16 shorter events, 0.0 us)
Async XLA Ops:
  0.6 11.8 %copy-start.4 = (bf16[4,256,512]{2,1,0:T(8,128)(2,1)S(1)}, bf16[4,256,512]{2,1,0:T(8,128)(2,1)}, u32[]{:S(2)}) copy-start(bf16[4,256,512]{2,1,0:T(8,128)(2,1)} %constant.5.clone.refs_3_) | copy-start | bytes 3145732
  0.6 11.7 %copy-start.6 = (f32[3,3,1024]{2,1,0:T(4,128)S(1)}, f32[3,3,1024]{2,1,0:T(4,128)}, u32[]{:S(2)}) copy-start(f32[3,3,1024]{2,1,0:T(4,128)} %refs_6_.5) | copy-start | bytes 110596
  2.2 7.7 %collective-permute-start = (bf16[640,128]{1,0:T(8,128)(2,1)S(1)}, bf16[640,128]{1,0:T(8,128)(2,1)S(1)}, u32[]{:S(2)}, u32[]{:S(2)}) collective-permute-start(bf16[640,128]{1,0:T(8,128)(2,1)S(1)} %get-tuple-element.39), channel_id=1, source_target_pairs={{0,16},{4,20},{8,24},{12,28},{16,0},{20,4},{24,8},{28,12},{1,17},{... | collective-permute-start | bytes 491528 | tf_op jit(solution)/shard_map/ppermute | solution.py:43
  5.3 7.1 %collective-permute-start.1 = (bf16[640,128]{1,0:T(8,128)(2,1)S(1)}, bf16[640,128]{1,0:T(8,128)(2,1)S(1)}, u32[]{:S(2)}, u32[]{:S(2)}) collective-permute-start(bf16[640,128]{1,0:T(8,128)(2,1)S(1)} %get-tuple-element.41), channel_id=1, source_target_pairs={{0,8},{4,12},{8,0},{12,4},{16,24},{20,28},{24,16},{28,20},{1,9},{5... | collective-permute-start | bytes 491528 | tf_op jit(solution)/shard_map/ppermute | solution.py:43
  6.7 8.7 %collective-permute-start.2 = (bf16[640,128]{1,0:T(8,128)(2,1)S(1)}, bf16[640,128]{1,0:T(8,128)(2,1)S(1)}, u32[]{:S(2)}, u32[]{:S(2)}) collective-permute-start(bf16[640,128]{1,0:T(8,128)(2,1)S(1)} %get-tuple-element.42), channel_id=1, source_target_pairs={{0,24},{4,28},{8,16},{12,20},{16,8},{20,12},{24,0},{28,4},{1,25},{... | collective-permute-start | bytes 491528 | tf_op jit(solution)/shard_map/ppermute | solution.py:43
  6.8 11.7 %collective-permute-start.3 = (bf16[640,128]{1,0:T(8,128)(2,1)S(1)}, bf16[640,128]{1,0:T(8,128)(2,1)S(1)}, u32[]{:S(2)}, u32[]{:S(2)}) collective-permute-start(bf16[640,128]{1,0:T(8,128)(2,1)S(1)} %get-tuple-element.43), channel_id=1, source_target_pairs={{0,28},{4,24},{8,20},{12,16},{16,12},{20,8},{24,4},{28,0},{1,29},{... | collective-permute-start | bytes 491528 | tf_op jit(solution)/shard_map/ppermute | solution.py:43
  8.3 12.2 %collective-permute-start.4 = (bf16[640,128]{1,0:T(8,128)(2,1)S(1)}, bf16[640,128]{1,0:T(8,128)(2,1)S(1)}, u32[]{:S(2)}, u32[]{:S(2)}) collective-permute-start(bf16[640,128]{1,0:T(8,128)(2,1)S(1)} %get-tuple-element.44), channel_id=1, source_target_pairs={{0,20},{4,16},{8,28},{12,24},{16,4},{20,0},{24,12},{28,8},{1,21},{... | collective-permute-start | bytes 491528 | tf_op jit(solution)/shard_map/ppermute | solution.py:43
  9.9 10.6 %collective-permute-start.5 = (bf16[640,128]{1,0:T(8,128)(2,1)S(1)}, bf16[640,128]{1,0:T(8,128)(2,1)S(1)}, u32[]{:S(2)}, u32[]{:S(2)}) collective-permute-start(bf16[640,128]{1,0:T(8,128)(2,1)S(1)} %get-tuple-element.45), channel_id=1, source_target_pairs={{0,12},{4,8},{8,4},{12,0},{16,28},{20,24},{24,20},{28,16},{1,13},{... | collective-permute-start | bytes 491528 | tf_op jit(solution)/shard_map/ppermute | solution.py:43
  12.4 8.1 %collective-permute-start.6 = (bf16[640,128]{1,0:T(8,128)(2,1)S(1)}, bf16[640,128]{1,0:T(8,128)(2,1)S(1)}, u32[]{:S(2)}, u32[]{:S(2)}) collective-permute-start(bf16[640,128]{1,0:T(8,128)(2,1)S(1)} %get-tuple-element.46), channel_id=1, source_target_pairs={{0,4},{4,0},{8,12},{12,8},{16,20},{20,16},{24,28},{28,24},{1,5},{5... | collective-permute-start | bytes 491528 | tf_op jit(solution)/shard_map/ppermute | solution.py:43
  12.4 1.2 %copy-start.5 = (bf16[4,512,256]{2,1,0:T(8,128)(2,1)S(1)}, bf16[4,512,256]{2,1,0:T(8,128)(2,1)}, u32[]{:S(2)}) copy-start(bf16[4,512,256]{2,1,0:T(8,128)(2,1)} %constant.4.clone.refs_2_) | copy-start | bytes 3145732
  20.5 12.3 %copy-start = (bf16[128,1024]{1,0:T(8,128)(2,1)S(1)}, bf16[128,1024]{1,0:T(8,128)(2,1)}, u32[]{:S(2)}) copy-start(bf16[128,1024]{1,0:T(8,128)(2,1)} %refs_2_.6) | copy-start | bytes 786436
  20.5 12.3 %copy-start.1 = (bf16[128,1024]{1,0:T(8,128)(2,1)S(1)}, bf16[128,1024]{1,0:T(8,128)(2,1)}, u32[]{:S(2)}) copy-start(bf16[128,1024]{1,0:T(8,128)(2,1)} %refs_3_.6) | copy-start | bytes 786436
  20.5 12.3 %copy-start.2 = (bf16[128,1024]{1,0:T(8,128)(2,1)S(1)}, bf16[128,1024]{1,0:T(8,128)(2,1)}, u32[]{:S(2)}) copy-start(bf16[128,1024]{1,0:T(8,128)(2,1)} %refs_4_.7) | copy-start | bytes 786436
  20.5 12.3 %copy-start.3 = (bf16[128,1024]{1,0:T(8,128)(2,1)S(1)}, bf16[128,1024]{1,0:T(8,128)(2,1)}, u32[]{:S(2)}) copy-start(bf16[128,1024]{1,0:T(8,128)(2,1)} %refs_5_.5) | copy-start | bytes 786436
  23.6 6.9 %collective-permute-start.11 = (bf16[416,128]{1,0:T(8,128)(2,1)S(1)}, bf16[416,128]{1,0:T(8,128)(2,1)S(1)}, u32[]{:S(2)}, u32[]{:S(2)}) collective-permute-start(bf16[416,128]{1,0:T(8,128)(2,1)S(1)} %get-tuple-element.55), channel_id=1, source_target_pairs={{0,24},{4,28},{8,16},{12,20},{16,8},{20,12},{24,0},{28,4},{1,25},{... | collective-permute-start | bytes 319496 | tf_op jit(solution)/shard_map/ppermute | solution.py:43
  25.8 4.7 %collective-permute-start.12 = (bf16[416,128]{1,0:T(8,128)(2,1)S(1)}, bf16[416,128]{1,0:T(8,128)(2,1)S(1)}, u32[]{:S(2)}, u32[]{:S(2)}) collective-permute-start(bf16[416,128]{1,0:T(8,128)(2,1)S(1)} %get-tuple-element.56), channel_id=1, source_target_pairs={{0,4},{4,0},{8,12},{12,8},{16,20},{20,16},{24,28},{28,24},{1,5},{5... | collective-permute-start | bytes 319496 | tf_op jit(solution)/shard_map/ppermute | solution.py:43
  25.8 7.0 %collective-permute-start.13 = (bf16[416,128]{1,0:T(8,128)(2,1)S(1)}, bf16[416,128]{1,0:T(8,128)(2,1)S(1)}, u32[]{:S(2)}, u32[]{:S(2)}) collective-permute-start(bf16[416,128]{1,0:T(8,128)(2,1)S(1)} %get-tuple-element.57), channel_id=1, source_target_pairs={{0,28},{4,24},{8,20},{12,16},{16,12},{20,8},{24,4},{28,0},{1,29},{... | collective-permute-start | bytes 319496 | tf_op jit(solution)/shard_map/ppermute | solution.py:43
  26.7 8.1 %collective-permute-start.9 = (bf16[416,128]{1,0:T(8,128)(2,1)S(1)}, bf16[416,128]{1,0:T(8,128)(2,1)S(1)}, u32[]{:S(2)}, u32[]{:S(2)}) collective-permute-start(bf16[416,128]{1,0:T(8,128)(2,1)S(1)} %get-tuple-element.52), channel_id=1, source_target_pairs={{0,16},{4,20},{8,24},{12,28},{16,0},{20,4},{24,8},{28,12},{1,17},{... | collective-permute-start | bytes 319496 | tf_op jit(solution)/shard_map/ppermute | solution.py:43
  28.2 6.7 %collective-permute-start.10 = (bf16[416,128]{1,0:T(8,128)(2,1)S(1)}, bf16[416,128]{1,0:T(8,128)(2,1)S(1)}, u32[]{:S(2)}, u32[]{:S(2)}) collective-permute-start(bf16[416,128]{1,0:T(8,128)(2,1)S(1)} %get-tuple-element.53), channel_id=1, source_target_pairs={{0,8},{4,12},{8,0},{12,4},{16,24},{20,28},{24,16},{28,20},{1,9},{5... | collective-permute-start | bytes 319496 | tf_op jit(solution)/shard_map/ppermute | solution.py:43
  30.5 6.6 %collective-permute-start.7 = (bf16[416,128]{1,0:T(8,128)(2,1)S(1)}, bf16[416,128]{1,0:T(8,128)(2,1)S(1)}, u32[]{:S(2)}, u32[]{:S(2)}) collective-permute-start(bf16[416,128]{1,0:T(8,128)(2,1)S(1)} %get-tuple-element.50), channel_id=1, source_target_pairs={{0,20},{4,16},{8,28},{12,24},{16,4},{20,0},{24,12},{28,8},{1,21},{... | collective-permute-start | bytes 319496 | tf_op jit(solution)/shard_map/ppermute | solution.py:43
  30.5 6.6 %collective-permute-start.8 = (bf16[416,128]{1,0:T(8,128)(2,1)S(1)}, bf16[416,128]{1,0:T(8,128)(2,1)S(1)}, u32[]{:S(2)}, u32[]{:S(2)}) collective-permute-start(bf16[416,128]{1,0:T(8,128)(2,1)S(1)} %get-tuple-element.51), channel_id=1, source_target_pairs={{0,12},{4,8},{8,4},{12,0},{16,28},{20,24},{24,20},{28,16},{1,13},{... | collective-permute-start | bytes 319496 | tf_op jit(solution)/shard_map/ppermute | solution.py:43

commit v19 on v16

--- a/solution.py
+++ b/solution.py
@@ -30,7 +30,8 @@
         if links == 0:
             return (1 if diagonal_first else 5, 0)
         if links == 1:
-            return (4 if other_core else 3, -step)
+            first = diagonal_first and step == peers // 2
+            return (4 if other_core else 3 - 4 * first, -step)
         return (2 * other_core if diagonal_first else 3.5, other_core)
 
     return [0] + sorted(range(1, peers), key=rank)

time: 37.8 us -> 39.8 us (1.053)
  waiting for transfers between devices: 11.7 us -> 14.3 us
  starting transfers between devices: 15.8 us -> 15.3 us
    ppermute x14, waiting for transfers between devices: 11.7 us -> 14.3 us  [exchange(): lax.ppermute(block, 'ctx', [(i, i ^ step) for i in range(peers)])]
    ppermute x14, starting transfers between devices: 15.8 us -> 15.3 us  [exchange(): lax.ppermute(block, 'ctx', [(i, i ^ step) for i in range(peers)])]
  transfers between devices with their start and end apart: 14 -> 14, of which waited for: 7 -> 6; matrix products, arithmetic and copies ran while one was open for 0% -> 0% of each run, Pallas kernels for 8% -> 7%
where the time goes in v19:
time: 39.8 us; the launch traced here: 39.7 us
  starting transfers between devices  15.3 us (38%)
  waiting for transfers between devices  14.3 us (36%)
  Pallas kernels  8.1 us (20%)
  local copies, waits for them, and re-layouts  1.25 us (3%)
  between operations  0.76 us (2%)
    ppermute x14, starting transfers between devices, exchange(): lax.ppermute(block, 'ctx', [(i, i ^ step) for i in range(peers)])  15.3 us
    ppermute x14, waiting for transfers between devices, exchange(): lax.ppermute(block, 'ctx', [(i, i ^ step) for i in range(peers)])  14.3 us
    pallas_call x3, Pallas kernels, token_step(): pl.pallas_call(functools.partial(token_kernel, steps, extra_rows(short_we...  3.47 us
    pallas_call x1, Pallas kernels, channel_step(): pl.pallas_call(functools.partial(channel_kernel, tokens, heard, told, 1.0...  2.64 us
    pallas_call x1, Pallas kernels, pack(): pl.pallas_call(functools.partial(pack_kernel, count, steps), in_specs=[pl...  1.56 us
    unnamed x14, local copies, waits for them, and re-layouts  1.25 us
  transfers between devices with their start and end apart: 14, of which 6 were waited for; matrix products, arithmetic and copies ran while one was open for 0% of the time, Pallas kernels for 7%

profile of v19, /device:TPU:0, one launch (start us, length us, event | category | flops | bytes accessed | tf_op | source)
XLA Modules:
  0.0 39.7 jit_solution(17621234593914848418)
XLA Ops:
  0.6 0.0 copy-start.4
  0.7 1.6 %pack_inputs.1 = (bf16[640,128]{1,0:T(8,128)(2,1)S(1)}, bf16[640,128]{1,0:T(8,128)(2,1)S(1)}, bf16[640,128]{1,0:T(8,128)(2,1)S(1)}, bf16[640,128]{1,0:T(8,128)(2...) custom-call(bf16[128,1024]{1,0:T(8,128)(2,1)} %refs_2_.6, ...), custom_call_target="tpu_custom_call" | custom-call | bytes 8388608 | tf_op jit(solution)/shard_map/pack_inputs/pallas_call | solution.py:77
  2.2 3.0 %collective-permute-start = (bf16[640,128]{1,0:T(8,128)(2,1)S(1)}, bf16[640,128]{1,0:T(8,128)(2,1)S(1)}, u32[]{:S(2)}, u32[]{:S(2)}) collective-permute-start(bf16[640,128]{1,0:T(8,128)(2,1)S(1)} %get-tuple-element.39), channel_id=1, source_target_pairs={{0,16},{4,20},{8,24},{12,28},{16,0},{20,4},{24,8},{28,12},{1,17},{... | collective-permute-start | bytes 491528 | tf_op jit(solution)/shard_map/ppermute | solution.py:44
  5.3 1.5 %collective-permute-start.1 = (bf16[640,128]{1,0:T(8,128)(2,1)S(1)}, bf16[640,128]{1,0:T(8,128)(2,1)S(1)}, u32[]{:S(2)}, u32[]{:S(2)}) collective-permute-start(bf16[640,128]{1,0:T(8,128)(2,1)S(1)} %get-tuple-element.41), channel_id=1, source_target_pairs={{0,8},{4,12},{8,0},{12,4},{16,24},{20,28},{24,16},{28,20},{1,9},{5... | collective-permute-start | bytes 491528 | tf_op jit(solution)/shard_map/ppermute | solution.py:44
  6.7 0.0 collective-permute-start.2
  6.8 1.5 %collective-permute-start.3 = (bf16[640,128]{1,0:T(8,128)(2,1)S(1)}, bf16[640,128]{1,0:T(8,128)(2,1)S(1)}, u32[]{:S(2)}, u32[]{:S(2)}) collective-permute-start(bf16[640,128]{1,0:T(8,128)(2,1)S(1)} %get-tuple-element.43), channel_id=1, source_target_pairs={{0,28},{4,24},{8,20},{12,16},{16,12},{20,8},{24,4},{28,0},{1,29},{... | collective-permute-start | bytes 491528 | tf_op jit(solution)/shard_map/ppermute | solution.py:44
  8.3 1.6 %collective-permute-start.4 = (bf16[640,128]{1,0:T(8,128)(2,1)S(1)}, bf16[640,128]{1,0:T(8,128)(2,1)S(1)}, u32[]{:S(2)}, u32[]{:S(2)}) collective-permute-start(bf16[640,128]{1,0:T(8,128)(2,1)S(1)} %get-tuple-element.44), channel_id=1, source_target_pairs={{0,20},{4,16},{8,28},{12,24},{16,4},{20,0},{24,12},{28,8},{1,21},{... | collective-permute-start | bytes 491528 | tf_op jit(solution)/shard_map/ppermute | solution.py:44
  9.9 0.1 collective-permute-start.5
  10.0 2.4 %collective-permute-done.1.refs_2_ = bf16[640,128]{1,0:T(8,128)(2,1)S(1)} collective-permute-done((bf16[640,128]{1,0:T(8,128)(2,1)S(1)}, bf16[640,128]{1,0:T(8,128)(2,1)S(1)}, u32[]{:S(2)}, u32[]{:S(2)}) %collective-permute-start.1) | collective-permute-done | bytes 163872 | tf_op jit(solution)/shard_map/ppermute | solution.py:44
  12.4 0.0 collective-permute-start.6
  12.4 0.0 copy-start.5
  12.4 1.2 %copy-done.5 = bf16[4,512,256]{2,1,0:T(8,128)(2,1)S(1)} copy-done((bf16[4,512,256]{2,1,0:T(8,128)(2,1)S(1)}, bf16[4,512,256]{2,1,0:T(8,128)(2,1)}, u32[]{:S(2)}) %copy-start.5) | copy-done | bytes 1048600
  13.6 0.4 %stage_tables.1 = (bf16[640,128]{1,0:T(8,128)(2,1)S(1)}, f32[3,3,1024]{2,1,0:T(4,128)S(1)}, bf16[4,512,256]{2,1,0:T(8,128)(2,1)S(1)}, bf16[4,256,512]{2,1,0:T(8,128)(2,1)S(1)}) custom-call(bf16[640,128]{1,0:T(8,128)(2,1)S(1)} %get-tuple-element.38.refs_0_, f32[3,3,1024]{2,1,0:T(4,128)S(1)} %copy-done.6, bf16[4,512,256]{2,1,0:T(8,128)(2,1)S(1)} %copy-done.5, ...), custom_call_target="tpu_custom_call" | custom-call | bytes 8388608 | tf_op jit(solution)/shard_map/stage_tables/pallas_call | solution.py:182
  14.0 1.4 %collective-permute-done.2.refs_3_ = bf16[640,128]{1,0:T(8,128)(2,1)S(1)} collective-permute-done((bf16[640,128]{1,0:T(8,128)(2,1)S(1)}, bf16[640,128]{1,0:T(8,128)(2,1)S(1)}, u32[]{:S(2)}, u32[]{:S(2)}) %collective-permute-start.2) | collective-permute-done | bytes 163872 | tf_op jit(solution)/shard_map/ppermute | solution.py:44
  15.5 3.0 %collective-permute-done.3.refs_4_ = bf16[640,128]{1,0:T(8,128)(2,1)S(1)} collective-permute-done((bf16[640,128]{1,0:T(8,128)(2,1)S(1)}, bf16[640,128]{1,0:T(8,128)(2,1)S(1)}, u32[]{:S(2)}, u32[]{:S(2)}) %collective-permute-start.3) | collective-permute-done | bytes 163872 | tf_op jit(solution)/shard_map/ppermute | solution.py:44
  18.5 2.0 %collective-permute-done.4.refs_5_ = bf16[640,128]{1,0:T(8,128)(2,1)S(1)} collective-permute-done((bf16[640,128]{1,0:T(8,128)(2,1)S(1)}, bf16[640,128]{1,0:T(8,128)(2,1)S(1)}, u32[]{:S(2)}, u32[]{:S(2)}) %collective-permute-start.4) | collective-permute-done | bytes 163872 | tf_op jit(solution)/shard_map/ppermute | solution.py:44
  20.5 0.0 collective-permute-done.5.refs_6_
  20.5 0.0 copy-start.3
  20.5 2.6 %channel_operator.1 = (bf16[416,128]{1,0:T(8,128)(2,1)S(1)}, bf16[416,128]{1,0:T(8,128)(2,1)S(1)}, bf16[416,128]{1,0:T(8,128)(2,1)S(1)}, bf16[416,128]{1,0:T(8,1...) custom-call(bf16[640,128]{1,0:T(8,128)(2,1)S(1)} %get-tuple-element., ...), custom_call_target="tpu_custom_call" | custom-call | tf_op jit(solution)/shard_map/channel_operator/pallas_call | solution.py:356
  23.2 1.5 %collective-permute-start.11 = (bf16[416,128]{1,0:T(8,128)(2,1)S(1)}, bf16[416,128]{1,0:T(8,128)(2,1)S(1)}, u32[]{:S(2)}, u32[]{:S(2)}) collective-permute-start(bf16[416,128]{1,0:T(8,128)(2,1)S(1)} %get-tuple-element.55), channel_id=1, source_target_pairs={{0,16},{4,20},{8,24},{12,28},{16,0},{20,4},{24,8},{28,12},{1,17},{... | collective-permute-start | bytes 319496 | tf_op jit(solution)/shard_map/ppermute | solution.py:44
  24.7 1.0 %collective-permute-start.12 = (bf16[416,128]{1,0:T(8,128)(2,1)S(1)}, bf16[416,128]{1,0:T(8,128)(2,1)S(1)}, u32[]{:S(2)}, u32[]{:S(2)}) collective-permute-start(bf16[416,128]{1,0:T(8,128)(2,1)S(1)} %get-tuple-element.56), channel_id=1, source_target_pairs={{0,24},{4,28},{8,16},{12,20},{16,8},{20,12},{24,0},{28,4},{1,25},{... | collective-permute-start | bytes 319496 | tf_op jit(solution)/shard_map/ppermute | solution.py:44
  25.7 0.7 %collective-permute-start.13 = (bf16[416,128]{1,0:T(8,128)(2,1)S(1)}, bf16[416,128]{1,0:T(8,128)(2,1)S(1)}, u32[]{:S(2)}, u32[]{:S(2)}) collective-permute-start(bf16[416,128]{1,0:T(8,128)(2,1)S(1)} %get-tuple-element.57), channel_id=1, source_target_pairs={{0,4},{4,0},{8,12},{12,8},{16,20},{20,16},{24,28},{28,24},{1,5},{5... | collective-permute-start | bytes 319496 | tf_op jit(solution)/shard_map/ppermute | solution.py:44
  26.4 1.3 %collective-permute-start.9 = (bf16[416,128]{1,0:T(8,128)(2,1)S(1)}, bf16[416,128]{1,0:T(8,128)(2,1)S(1)}, u32[]{:S(2)}, u32[]{:S(2)}) collective-permute-start(bf16[416,128]{1,0:T(8,128)(2,1)S(1)} %get-tuple-element.52), channel_id=1, source_target_pairs={{0,28},{4,24},{8,20},{12,16},{16,12},{20,8},{24,4},{28,0},{1,29},{... | collective-permute-start | bytes 319496 | tf_op jit(solution)/shard_map/ppermute | solution.py:44
  27.8 1.2 %collective-permute-start.10 = (bf16[416,128]{1,0:T(8,128)(2,1)S(1)}, bf16[416,128]{1,0:T(8,128)(2,1)S(1)}, u32[]{:S(2)}, u32[]{:S(2)}) collective-permute-start(bf16[416,128]{1,0:T(8,128)(2,1)S(1)} %get-tuple-element.53), channel_id=1, source_target_pairs={{0,8},{4,12},{8,0},{12,4},{16,24},{20,28},{24,16},{28,20},{1,9},{5... | collective-permute-start | bytes 319496 | tf_op jit(solution)/shard_map/ppermute | solution.py:44
  29.0 4.5 %collective-permute-done.11.refs_1_ = bf16[416,128]{1,0:T(8,128)(2,1)S(1)} collective-permute-done((bf16[416,128]{1,0:T(8,128)(2,1)S(1)}, bf16[416,128]{1,0:T(8,128)(2,1)S(1)}, u32[]{:S(2)}, u32[]{:S(2)}) %collective-permute-start.11) | collective-permute-done | bytes 106528 | tf_op jit(solution)/shard_map/ppermute | solution.py:44
  33.5 0.0 collective-permute-start.7
  33.5 1.7 %collective-permute-start.8 = (bf16[416,128]{1,0:T(8,128)(2,1)S(1)}, bf16[416,128]{1,0:T(8,128)(2,1)S(1)}, u32[]{:S(2)}, u32[]{:S(2)}) collective-permute-start(bf16[416,128]{1,0:T(8,128)(2,1)S(1)} %get-tuple-element.51), channel_id=1, source_target_pairs={{0,12},{4,8},{8,4},{12,0},{16,28},{20,24},{24,20},{28,16},{1,13},{... | collective-permute-start | bytes 319496 | tf_op jit(solution)/shard_map/ppermute | solution.py:44
  35.2 0.0 collective-permute-done.13.refs_3_
  35.2 1.4 %token_outputs.3 = (bf16[128,1024]{1,0:T(8,128)(2,1)}, bf16[128,1024]{1,0:T(8,128)(2,1)}, bf16[128,1024]{1,0:T(8,128)(2,1)}, bf16[128,1024]{1,0:T(8,128)(2,1)}, ...) custom-call(bf16[416,128]{1,0:T(8,128)(2,1)S(1)} %get-tuple-element.54.refs_0_, ...), custom_call_target="tpu_custom_call" | custom-call | bytes 4194304 | tf_op jit(solution)/shard_map/token_outputs/pallas_call | solution.py:447
  36.7 1.0 %token_outputs.4 = (bf16[128,1024]{1,0:T(8,128)(2,1)}, bf16[128,1024]{1,0:T(8,128)(2,1)}, bf16[128,1024]{1,0:T(8,128)(2,1)}, bf16[128,1024]{1,0:T(8,128)(2,1)}, ...) custom-call(bf16[416,128]{1,0:T(8,128)(2,1)S(1)} %collective-permute, ...), custom_call_target="tpu_custom_call", output_to_operand_aliasing={{0}: (7, {}), {1}: (8, {}), {2}: (9, {}), {3}: (10, {}), {4... | custom-call | bytes 4194304 | tf_op jit(solution)/shard_map/token_outputs/pallas_call | solution.py:447
  37.7 0.9 %collective-permute-done.7.refs_0_ = bf16[416,128]{1,0:T(8,128)(2,1)S(1)} collective-permute-done((bf16[416,128]{1,0:T(8,128)(2,1)S(1)}, bf16[416,128]{1,0:T(8,128)(2,1)S(1)}, u32[]{:S(2)}, u32[]{:S(2)}) %collective-permute-start.7) | collective-permute-done | bytes 106528 | tf_op jit(solution)/shard_map/ppermute | solution.py:44
  38.6 1.0 %token_outputs.5 = (bf16[128,1024]{1,0:T(8,128)(2,1)}, bf16[128,1024]{1,0:T(8,128)(2,1)}, bf16[128,1024]{1,0:T(8,128)(2,1)}, bf16[128,1024]{1,0:T(8,128)(2,1)}, ...) custom-call(bf16[416,128]{1,0:T(8,128)(2,1)S(1)} %collective-permute, ...), custom_call_target="tpu_custom_call", output_to_operand_aliasing={{0}: (7, {}), {1}: (8, {}), {2}: (9, {}), {3}: (10, {}), {4... | custom-call | bytes 4194304 | tf_op jit(solution)/shard_map/token_outputs/pallas_call | solution.py:447
  (16 shorter events, 0.0 us)
Async XLA Ops:
  0.6 11.8 %copy-start.4 = (bf16[4,256,512]{2,1,0:T(8,128)(2,1)S(1)}, bf16[4,256,512]{2,1,0:T(8,128)(2,1)}, u32[]{:S(2)}) copy-start(bf16[4,256,512]{2,1,0:T(8,128)(2,1)} %constant.5.clone.refs_3_) | copy-start | bytes 3145732
  0.6 11.7 %copy-start.6 = (f32[3,3,1024]{2,1,0:T(4,128)S(1)}, f32[3,3,1024]{2,1,0:T(4,128)}, u32[]{:S(2)}) copy-start(f32[3,3,1024]{2,1,0:T(4,128)} %refs_6_.5) | copy-start | bytes 110596
  2.2 7.7 %collective-permute-start = (bf16[640,128]{1,0:T(8,128)(2,1)S(1)}, bf16[640,128]{1,0:T(8,128)(2,1)S(1)}, u32[]{:S(2)}, u32[]{:S(2)}) collective-permute-start(bf16[640,128]{1,0:T(8,128)(2,1)S(1)} %get-tuple-element.39), channel_id=1, source_target_pairs={{0,16},{4,20},{8,24},{12,28},{16,0},{20,4},{24,8},{28,12},{1,17},{... | collective-permute-start | bytes 491528 | tf_op jit(solution)/shard_map/ppermute | solution.py:44
  5.3 7.1 %collective-permute-start.1 = (bf16[640,128]{1,0:T(8,128)(2,1)S(1)}, bf16[640,128]{1,0:T(8,128)(2,1)S(1)}, u32[]{:S(2)}, u32[]{:S(2)}) collective-permute-start(bf16[640,128]{1,0:T(8,128)(2,1)S(1)} %get-tuple-element.41), channel_id=1, source_target_pairs={{0,8},{4,12},{8,0},{12,4},{16,24},{20,28},{24,16},{28,20},{1,9},{5... | collective-permute-start | bytes 491528 | tf_op jit(solution)/shard_map/ppermute | solution.py:44
  6.7 8.7 %collective-permute-start.2 = (bf16[640,128]{1,0:T(8,128)(2,1)S(1)}, bf16[640,128]{1,0:T(8,128)(2,1)S(1)}, u32[]{:S(2)}, u32[]{:S(2)}) collective-permute-start(bf16[640,128]{1,0:T(8,128)(2,1)S(1)} %get-tuple-element.42), channel_id=1, source_target_pairs={{0,24},{4,28},{8,16},{12,20},{16,8},{20,12},{24,0},{28,4},{1,25},{... | collective-permute-start | bytes 491528 | tf_op jit(solution)/shard_map/ppermute | solution.py:44
  6.8 11.7 %collective-permute-start.3 = (bf16[640,128]{1,0:T(8,128)(2,1)S(1)}, bf16[640,128]{1,0:T(8,128)(2,1)S(1)}, u32[]{:S(2)}, u32[]{:S(2)}) collective-permute-start(bf16[640,128]{1,0:T(8,128)(2,1)S(1)} %get-tuple-element.43), channel_id=1, source_target_pairs={{0,28},{4,24},{8,20},{12,16},{16,12},{20,8},{24,4},{28,0},{1,29},{... | collective-permute-start | bytes 491528 | tf_op jit(solution)/shard_map/ppermute | solution.py:44
  8.3 12.2 %collective-permute-start.4 = (bf16[640,128]{1,0:T(8,128)(2,1)S(1)}, bf16[640,128]{1,0:T(8,128)(2,1)S(1)}, u32[]{:S(2)}, u32[]{:S(2)}) collective-permute-start(bf16[640,128]{1,0:T(8,128)(2,1)S(1)} %get-tuple-element.44), channel_id=1, source_target_pairs={{0,20},{4,16},{8,28},{12,24},{16,4},{20,0},{24,12},{28,8},{1,21},{... | collective-permute-start | bytes 491528 | tf_op jit(solution)/shard_map/ppermute | solution.py:44
  9.9 10.6 %collective-permute-start.5 = (bf16[640,128]{1,0:T(8,128)(2,1)S(1)}, bf16[640,128]{1,0:T(8,128)(2,1)S(1)}, u32[]{:S(2)}, u32[]{:S(2)}) collective-permute-start(bf16[640,128]{1,0:T(8,128)(2,1)S(1)} %get-tuple-element.45), channel_id=1, source_target_pairs={{0,12},{4,8},{8,4},{12,0},{16,28},{20,24},{24,20},{28,16},{1,13},{... | collective-permute-start | bytes 491528 | tf_op jit(solution)/shard_map/ppermute | solution.py:44
  12.4 8.1 %collective-permute-start.6 = (bf16[640,128]{1,0:T(8,128)(2,1)S(1)}, bf16[640,128]{1,0:T(8,128)(2,1)S(1)}, u32[]{:S(2)}, u32[]{:S(2)}) collective-permute-start(bf16[640,128]{1,0:T(8,128)(2,1)S(1)} %get-tuple-element.46), channel_id=1, source_target_pairs={{0,4},{4,0},{8,12},{12,8},{16,20},{20,16},{24,28},{28,24},{1,5},{5... | collective-permute-start | bytes 491528 | tf_op jit(solution)/shard_map/ppermute | solution.py:44
  12.4 1.2 %copy-start.5 = (bf16[4,512,256]{2,1,0:T(8,128)(2,1)S(1)}, bf16[4,512,256]{2,1,0:T(8,128)(2,1)}, u32[]{:S(2)}) copy-start(bf16[4,512,256]{2,1,0:T(8,128)(2,1)} %constant.4.clone.refs_2_) | copy-start | bytes 3145732
  20.5 14.7 %copy-start = (bf16[128,1024]{1,0:T(8,128)(2,1)S(1)}, bf16[128,1024]{1,0:T(8,128)(2,1)}, u32[]{:S(2)}) copy-start(bf16[128,1024]{1,0:T(8,128)(2,1)} %refs_2_.6) | copy-start | bytes 786436
  20.5 14.7 %copy-start.1 = (bf16[128,1024]{1,0:T(8,128)(2,1)S(1)}, bf16[128,1024]{1,0:T(8,128)(2,1)}, u32[]{:S(2)}) copy-start(bf16[128,1024]{1,0:T(8,128)(2,1)} %refs_3_.6) | copy-start | bytes 786436
  20.5 14.7 %copy-start.2 = (bf16[128,1024]{1,0:T(8,128)(2,1)S(1)}, bf16[128,1024]{1,0:T(8,128)(2,1)}, u32[]{:S(2)}) copy-start(bf16[128,1024]{1,0:T(8,128)(2,1)} %refs_4_.7) | copy-start | bytes 786436
  20.5 14.7 %copy-start.3 = (bf16[128,1024]{1,0:T(8,128)(2,1)S(1)}, bf16[128,1024]{1,0:T(8,128)(2,1)}, u32[]{:S(2)}) copy-start(bf16[128,1024]{1,0:T(8,128)(2,1)} %refs_5_.5) | copy-start | bytes 786436
  23.2 10.3 %collective-permute-start.11 = (bf16[416,128]{1,0:T(8,128)(2,1)S(1)}, bf16[416,128]{1,0:T(8,128)(2,1)S(1)}, u32[]{:S(2)}, u32[]{:S(2)}) collective-permute-start(bf16[416,128]{1,0:T(8,128)(2,1)S(1)} %get-tuple-element.55), channel_id=1, source_target_pairs={{0,16},{4,20},{8,24},{12,28},{16,0},{20,4},{24,8},{28,12},{1,17},{... | collective-permute-start | bytes 319496 | tf_op jit(solution)/shard_map/ppermute | solution.py:44
  24.7 8.8 %collective-permute-start.12 = (bf16[416,128]{1,0:T(8,128)(2,1)S(1)}, bf16[416,128]{1,0:T(8,128)(2,1)S(1)}, u32[]{:S(2)}, u32[]{:S(2)}) collective-permute-start(bf16[416,128]{1,0:T(8,128)(2,1)S(1)} %get-tuple-element.56), channel_id=1, source_target_pairs={{0,24},{4,28},{8,16},{12,20},{16,8},{20,12},{24,0},{28,4},{1,25},{... | collective-permute-start | bytes 319496 | tf_op jit(solution)/shard_map/ppermute | solution.py:44
  25.7 9.5 %collective-permute-start.13 = (bf16[416,128]{1,0:T(8,128)(2,1)S(1)}, bf16[416,128]{1,0:T(8,128)(2,1)S(1)}, u32[]{:S(2)}, u32[]{:S(2)}) collective-permute-start(bf16[416,128]{1,0:T(8,128)(2,1)S(1)} %get-tuple-element.57), channel_id=1, source_target_pairs={{0,4},{4,0},{8,12},{12,8},{16,20},{20,16},{24,28},{28,24},{1,5},{5... | collective-permute-start | bytes 319496 | tf_op jit(solution)/shard_map/ppermute | solution.py:44
  26.4 10.2 %collective-permute-start.9 = (bf16[416,128]{1,0:T(8,128)(2,1)S(1)}, bf16[416,128]{1,0:T(8,128)(2,1)S(1)}, u32[]{:S(2)}, u32[]{:S(2)}) collective-permute-start(bf16[416,128]{1,0:T(8,128)(2,1)S(1)} %get-tuple-element.52), channel_id=1, source_target_pairs={{0,28},{4,24},{8,20},{12,16},{16,12},{20,8},{24,4},{28,0},{1,29},{... | collective-permute-start | bytes 319496 | tf_op jit(solution)/shard_map/ppermute | solution.py:44
  27.8 8.9 %collective-permute-start.10 = (bf16[416,128]{1,0:T(8,128)(2,1)S(1)}, bf16[416,128]{1,0:T(8,128)(2,1)S(1)}, u32[]{:S(2)}, u32[]{:S(2)}) collective-permute-start(bf16[416,128]{1,0:T(8,128)(2,1)S(1)} %get-tuple-element.53), channel_id=1, source_target_pairs={{0,8},{4,12},{8,0},{12,4},{16,24},{20,28},{24,16},{28,20},{1,9},{5... | collective-permute-start | bytes 319496 | tf_op jit(solution)/shard_map/ppermute | solution.py:44
  33.5 5.1 %collective-permute-start.7 = (bf16[416,128]{1,0:T(8,128)(2,1)S(1)}, bf16[416,128]{1,0:T(8,128)(2,1)S(1)}, u32[]{:S(2)}, u32[]{:S(2)}) collective-permute-start(bf16[416,128]{1,0:T(8,128)(2,1)S(1)} %get-tuple-element.50), channel_id=1, source_target_pairs={{0,20},{4,16},{8,28},{12,24},{16,4},{20,0},{24,12},{28,8},{1,21},{... | collective-permute-start | bytes 319496 | tf_op jit(solution)/shard_map/ppermute | solution.py:44
  33.5 5.1 %collective-permute-start.8 = (bf16[416,128]{1,0:T(8,128)(2,1)S(1)}, bf16[416,128]{1,0:T(8,128)(2,1)S(1)}, u32[]{:S(2)}, u32[]{:S(2)}) collective-permute-start(bf16[416,128]{1,0:T(8,128)(2,1)S(1)} %get-tuple-element.51), channel_id=1, source_target_pairs={{0,12},{4,8},{8,4},{12,0},{16,28},{20,24},{24,20},{28,16},{1,13},{... | collective-permute-start | bytes 319496 | tf_op jit(solution)/shard_map/ppermute | solution.py:44

commit v20 on v15

--- a/solution.py
+++ b/solution.py
@@ -16,6 +16,7 @@
 TILE = 16
 PAD = 8
 CHUNK = 16
+ROWS = 8
 RIM = 2
 PIECES = 2
 MIB = 1024 * 1024
@@ -248,7 +249,7 @@
         lanes = slice(at * LANES, (at + 1) * LANES)
         for r, pair in enumerate(inverse_mix(mixed)):
             for rows, part in zip((real, imag), pair):
-                products[r, rows, lanes] = part.astype(BF16)
+                products[r, rows, lanes] = part
 
     for chunk in chunks:
         rows = rows_of(chunk)
@@ -270,9 +271,9 @@
             signals[r, rows, 2 * LANES :] = (cot_now[r] * query_now[r]).astype(BF16)
     for r in range(PHASES):
         spectra[r, :, 2 * LANES :] = transform(forward[r], signals[r, :, 2 * LANES :])
-    for step in range(size // TILE):
-        real = slice(step * TILE, (step + 1) * TILE)
-        imag = slice(size + step * TILE, size + (step + 1) * TILE)
+    for step in range(size // ROWS):
+        real = slice(step * ROWS, (step + 1) * ROWS)
+        imag = slice(size + step * ROWS, size + (step + 1) * ROWS)
         prod, filt = spectrum(0, real, imag), spectrum(1, real, imag)
         for at, mixed in enumerate((prod, filt)):
             lanes = slice(at * LANES, (at + 1) * LANES)
@@ -280,18 +281,18 @@
                 spectra[q, real, lanes], spectra[q, imag, lanes] = pair
         keep(0, real, imag, times(prod, filt))
     for r in range(PHASES):
-        result = transform(backward[r], products[r, :, :LANES])
+        result = transform(backward[r], products[r, :, :LANES].astype(BF16))
         conv[r, :size, :] = result.astype(BF16).astype(F32)
-    for step in range(size // TILE):
-        real = slice(step * TILE, (step + 1) * TILE)
-        imag = slice(size + step * TILE, size + (step + 1) * TILE)
+    for step in range(size // ROWS):
+        real = slice(step * ROWS, (step + 1) * ROWS)
+        imag = slice(size + step * ROWS, size + (step + 1) * ROWS)
         grad = spectrum(2, real, imag)
         for at in range(2):
             lanes = slice(at * LANES, (at + 1) * LANES)
             known = [(spectra[q, real, lanes], spectra[q, imag, lanes]) for q in range(PHASES)]
             keep(2 - at, real, imag, conj_times(known, grad))
     for r in range(PHASES):
-        result = transform(backward[r], products[r, :, LANES:])
+        result = transform(backward[r], products[r, :, LANES:].astype(BF16))
         conv_grad[r, :size, :] = result[:, :LANES].astype(BF16).astype(F32)
         filter_grad[r] = (result[:, LANES:] * grad_scale).astype(BF16)
 
@@ -372,7 +373,7 @@
             phases,
             pltpu.VMEM((PHASES, size, 3 * LANES), BF16),
             pltpu.VMEM((PHASES, 2 * size, 3 * LANES), F32),
-            pltpu.VMEM((PHASES, 2 * size, 3 * LANES), BF16),
+            pltpu.VMEM((PHASES, 2 * size, 3 * LANES), F32),
             pltpu.VMEM((extra, LANES), F32),
         ],
         compiler_params=pltpu.CompilerParams(vmem_limit_bytes=VMEM_LIMIT),

time: 37.8 us -> 37.8 us (level)
  no operation moved by 1% of the time
where the time goes in v20:
time: 37.8 us; the launch traced here: 37.6 us
  starting transfers between devices  15.9 us (42%)
  waiting for transfers between devices  11.8 us (31%)
  Pallas kernels  8 us (21%)
  local copies, waits for them, and re-layouts  1.25 us (3%)
  between operations  0.74 us (2%)
    ppermute x14, starting transfers between devices, exchange(): lax.ppermute(block, 'ctx', [(i, i ^ step) for i in range(peers)])  15.9 us
    ppermute x14, waiting for transfers between devices, exchange(): lax.ppermute(block, 'ctx', [(i, i ^ step) for i in range(peers)])  11.8 us
    pallas_call x3, Pallas kernels, token_step(): pl.pallas_call(functools.partial(token_kernel, steps, extra_rows(short_we...  3.43 us
    pallas_call x1, Pallas kernels, channel_step(): pl.pallas_call(functools.partial(channel_kernel, tokens, heard, told, 1.0...  2.59 us
    pallas_call x1, Pallas kernels, pack(): pl.pallas_call(functools.partial(pack_kernel, count, steps), in_specs=[pl...  1.56 us
    unnamed x14, local copies, waits for them, and re-layouts  1.25 us
  transfers between devices with their start and end apart: 14, of which 7 were waited for; matrix products, arithmetic and copies ran while one was open for 0% of the time, Pallas kernels for 8%

profile of v20, /device:TPU:0, one launch (start us, length us, event | category | flops | bytes accessed | tf_op | source)
XLA Modules:
  0.0 37.6 jit_solution(1024892214413287051)
XLA Ops:
  0.6 0.0 copy-start.4
  0.7 1.6 %pack_inputs.1 = (bf16[640,128]{1,0:T(8,128)(2,1)S(1)}, bf16[640,128]{1,0:T(8,128)(2,1)S(1)}, bf16[640,128]{1,0:T(8,128)(2,1)S(1)}, bf16[640,128]{1,0:T(8,128)(2...) custom-call(bf16[128,1024]{1,0:T(8,128)(2,1)} %refs_2_.6, ...), custom_call_target="tpu_custom_call" | custom-call | bytes 8388608 | tf_op jit(solution)/shard_map/pack_inputs/pallas_call | solution.py:76
  2.2 3.0 %collective-permute-start = (bf16[640,128]{1,0:T(8,128)(2,1)S(1)}, bf16[640,128]{1,0:T(8,128)(2,1)S(1)}, u32[]{:S(2)}, u32[]{:S(2)}) collective-permute-start(bf16[640,128]{1,0:T(8,128)(2,1)S(1)} %get-tuple-element.39), channel_id=1, source_target_pairs={{0,16},{4,20},{8,24},{12,28},{16,0},{20,4},{24,8},{28,12},{1,17},{... | collective-permute-start | bytes 491528 | tf_op jit(solution)/shard_map/ppermute | solution.py:43
  5.3 1.5 %collective-permute-start.1 = (bf16[640,128]{1,0:T(8,128)(2,1)S(1)}, bf16[640,128]{1,0:T(8,128)(2,1)S(1)}, u32[]{:S(2)}, u32[]{:S(2)}) collective-permute-start(bf16[640,128]{1,0:T(8,128)(2,1)S(1)} %get-tuple-element.41), channel_id=1, source_target_pairs={{0,8},{4,12},{8,0},{12,4},{16,24},{20,28},{24,16},{28,20},{1,9},{5... | collective-permute-start | bytes 491528 | tf_op jit(solution)/shard_map/ppermute | solution.py:43
  6.7 0.0 collective-permute-start.2
  6.8 1.5 %collective-permute-start.3 = (bf16[640,128]{1,0:T(8,128)(2,1)S(1)}, bf16[640,128]{1,0:T(8,128)(2,1)S(1)}, u32[]{:S(2)}, u32[]{:S(2)}) collective-permute-start(bf16[640,128]{1,0:T(8,128)(2,1)S(1)} %get-tuple-element.43), channel_id=1, source_target_pairs={{0,28},{4,24},{8,20},{12,16},{16,12},{20,8},{24,4},{28,0},{1,29},{... | collective-permute-start | bytes 491528 | tf_op jit(solution)/shard_map/ppermute | solution.py:43
  8.3 1.6 %collective-permute-start.4 = (bf16[640,128]{1,0:T(8,128)(2,1)S(1)}, bf16[640,128]{1,0:T(8,128)(2,1)S(1)}, u32[]{:S(2)}, u32[]{:S(2)}) collective-permute-start(bf16[640,128]{1,0:T(8,128)(2,1)S(1)} %get-tuple-element.44), channel_id=1, source_target_pairs={{0,20},{4,16},{8,28},{12,24},{16,4},{20,0},{24,12},{28,8},{1,21},{... | collective-permute-start | bytes 491528 | tf_op jit(solution)/shard_map/ppermute | solution.py:43
  9.9 0.0 collective-permute-done.refs_4_.refs_1_
  9.9 0.1 collective-permute-start.5
  10.0 2.4 %collective-permute-done.1.refs_2_ = bf16[640,128]{1,0:T(8,128)(2,1)S(1)} collective-permute-done((bf16[640,128]{1,0:T(8,128)(2,1)S(1)}, bf16[640,128]{1,0:T(8,128)(2,1)S(1)}, u32[]{:S(2)}, u32[]{:S(2)}) %collective-permute-start.1) | collective-permute-done | bytes 163872 | tf_op jit(solution)/shard_map/ppermute | solution.py:43
  12.4 0.0 collective-permute-start.6
  12.4 0.0 copy-start.5
  12.4 1.2 %copy-done.5 = bf16[4,512,256]{2,1,0:T(8,128)(2,1)S(1)} copy-done((bf16[4,512,256]{2,1,0:T(8,128)(2,1)S(1)}, bf16[4,512,256]{2,1,0:T(8,128)(2,1)}, u32[]{:S(2)}) %copy-start.5) | copy-done | bytes 1048600
  13.6 0.4 %stage_tables.1 = (bf16[640,128]{1,0:T(8,128)(2,1)S(1)}, f32[3,3,1024]{2,1,0:T(4,128)S(1)}, bf16[4,512,256]{2,1,0:T(8,128)(2,1)S(1)}, bf16[4,256,512]{2,1,0:T(8,128)(2,1)S(1)}) custom-call(bf16[640,128]{1,0:T(8,128)(2,1)S(1)} %get-tuple-element.38.refs_0_, f32[3,3,1024]{2,1,0:T(4,128)S(1)} %copy-done.6, bf16[4,512,256]{2,1,0:T(8,128)(2,1)S(1)} %copy-done.5, ...), custom_call_target="tpu_custom_call" | custom-call | bytes 8388608 | tf_op jit(solution)/shard_map/stage_tables/pallas_call | solution.py:181
  14.0 1.4 %collective-permute-done.2.refs_3_ = bf16[640,128]{1,0:T(8,128)(2,1)S(1)} collective-permute-done((bf16[640,128]{1,0:T(8,128)(2,1)S(1)}, bf16[640,128]{1,0:T(8,128)(2,1)S(1)}, u32[]{:S(2)}, u32[]{:S(2)}) %collective-permute-start.2) | collective-permute-done | bytes 163872 | tf_op jit(solution)/shard_map/ppermute | solution.py:43
  15.5 3.0 %collective-permute-done.3.refs_4_ = bf16[640,128]{1,0:T(8,128)(2,1)S(1)} collective-permute-done((bf16[640,128]{1,0:T(8,128)(2,1)S(1)}, bf16[640,128]{1,0:T(8,128)(2,1)S(1)}, u32[]{:S(2)}, u32[]{:S(2)}) %collective-permute-start.3) | collective-permute-done | bytes 163872 | tf_op jit(solution)/shard_map/ppermute | solution.py:43
  18.5 2.0 %collective-permute-done.4.refs_5_ = bf16[640,128]{1,0:T(8,128)(2,1)S(1)} collective-permute-done((bf16[640,128]{1,0:T(8,128)(2,1)S(1)}, bf16[640,128]{1,0:T(8,128)(2,1)S(1)}, u32[]{:S(2)}, u32[]{:S(2)}) %collective-permute-start.4) | collective-permute-done | bytes 163872 | tf_op jit(solution)/shard_map/ppermute | solution.py:43
  20.5 0.0 collective-permute-done.5.refs_6_
  20.5 0.0 collective-permute-done.6.refs_7_
  20.5 0.0 copy-start.3
  20.5 2.6 %channel_operator.1 = (bf16[416,128]{1,0:T(8,128)(2,1)S(1)}, bf16[416,128]{1,0:T(8,128)(2,1)S(1)}, bf16[416,128]{1,0:T(8,128)(2,1)S(1)}, bf16[416,128]{1,0:T(8,1...) custom-call(bf16[640,128]{1,0:T(8,128)(2,1)S(1)} %get-tuple-element., ...), custom_call_target="tpu_custom_call" | custom-call | tf_op jit(solution)/shard_map/channel_operator/pallas_call | solution.py:361
  23.1 2.2 %collective-permute-start.11 = (bf16[416,128]{1,0:T(8,128)(2,1)S(1)}, bf16[416,128]{1,0:T(8,128)(2,1)S(1)}, u32[]{:S(2)}, u32[]{:S(2)}) collective-permute-start(bf16[416,128]{1,0:T(8,128)(2,1)S(1)} %get-tuple-element.55), channel_id=1, source_target_pairs={{0,24},{4,28},{8,16},{12,20},{16,8},{20,12},{24,0},{28,4},{1,25},{... | collective-permute-start | bytes 319496 | tf_op jit(solution)/shard_map/ppermute | solution.py:43
  25.3 0.9 %collective-permute-start.13 = (bf16[416,128]{1,0:T(8,128)(2,1)S(1)}, bf16[416,128]{1,0:T(8,128)(2,1)S(1)}, u32[]{:S(2)}, u32[]{:S(2)}) collective-permute-start(bf16[416,128]{1,0:T(8,128)(2,1)S(1)} %get-tuple-element.57), channel_id=1, source_target_pairs={{0,28},{4,24},{8,20},{12,16},{16,12},{20,8},{24,4},{28,0},{1,29},{... | collective-permute-start | bytes 319496 | tf_op jit(solution)/shard_map/ppermute | solution.py:43
  26.3 1.4 %collective-permute-start.9 = (bf16[416,128]{1,0:T(8,128)(2,1)S(1)}, bf16[416,128]{1,0:T(8,128)(2,1)S(1)}, u32[]{:S(2)}, u32[]{:S(2)}) collective-permute-start(bf16[416,128]{1,0:T(8,128)(2,1)S(1)} %get-tuple-element.52), channel_id=1, source_target_pairs={{0,16},{4,20},{8,24},{12,28},{16,0},{20,4},{24,8},{28,12},{1,17},{... | collective-permute-start | bytes 319496 | tf_op jit(solution)/shard_map/ppermute | solution.py:43
  27.7 1.2 %collective-permute-start.10 = (bf16[416,128]{1,0:T(8,128)(2,1)S(1)}, bf16[416,128]{1,0:T(8,128)(2,1)S(1)}, u32[]{:S(2)}, u32[]{:S(2)}) collective-permute-start(bf16[416,128]{1,0:T(8,128)(2,1)S(1)} %get-tuple-element.53), channel_id=1, source_target_pairs={{0,8},{4,12},{8,0},{12,4},{16,24},{20,28},{24,16},{28,20},{1,9},{5... | collective-permute-start | bytes 319496 | tf_op jit(solution)/shard_map/ppermute | solution.py:43
  28.9 1.1 %collective-permute-done.11.refs_1_ = bf16[416,128]{1,0:T(8,128)(2,1)S(1)} collective-permute-done((bf16[416,128]{1,0:T(8,128)(2,1)S(1)}, bf16[416,128]{1,0:T(8,128)(2,1)S(1)}, u32[]{:S(2)}, u32[]{:S(2)}) %collective-permute-start.11) | collective-permute-done | bytes 106528 | tf_op jit(solution)/shard_map/ppermute | solution.py:43
  30.0 2.3 %collective-permute-start.8 = (bf16[416,128]{1,0:T(8,128)(2,1)S(1)}, bf16[416,128]{1,0:T(8,128)(2,1)S(1)}, u32[]{:S(2)}, u32[]{:S(2)}) collective-permute-start(bf16[416,128]{1,0:T(8,128)(2,1)S(1)} %get-tuple-element.51), channel_id=1, source_target_pairs={{0,12},{4,8},{8,4},{12,0},{16,28},{20,24},{24,20},{28,16},{1,13},{... | collective-permute-start | bytes 319496 | tf_op jit(solution)/shard_map/ppermute | solution.py:43
  32.3 1.4 %token_outputs.3 = (bf16[128,1024]{1,0:T(8,128)(2,1)}, bf16[128,1024]{1,0:T(8,128)(2,1)}, bf16[128,1024]{1,0:T(8,128)(2,1)}, bf16[128,1024]{1,0:T(8,128)(2,1)}, ...) custom-call(bf16[416,128]{1,0:T(8,128)(2,1)S(1)} %get-tuple-element.54.refs_0_, ...), custom_call_target="tpu_custom_call" | custom-call | bytes 4194304 | tf_op jit(solution)/shard_map/token_outputs/pallas_call | solution.py:462
  33.7 0.6 %collective-permute-done.9.refs_0_ = bf16[416,128]{1,0:T(8,128)(2,1)S(1)} collective-permute-done((bf16[416,128]{1,0:T(8,128)(2,1)S(1)}, bf16[416,128]{1,0:T(8,128)(2,1)S(1)}, u32[]{:S(2)}, u32[]{:S(2)}) %collective-permute-start.9) | collective-permute-done | bytes 106528 | tf_op jit(solution)/shard_map/ppermute | solution.py:43
  34.4 1.0 %token_outputs.4 = (bf16[128,1024]{1,0:T(8,128)(2,1)}, bf16[128,1024]{1,0:T(8,128)(2,1)}, bf16[128,1024]{1,0:T(8,128)(2,1)}, bf16[128,1024]{1,0:T(8,128)(2,1)}, ...) custom-call(bf16[416,128]{1,0:T(8,128)(2,1)S(1)} %collective-permute, ...), custom_call_target="tpu_custom_call", output_to_operand_aliasing={{0}: (7, {}), {1}: (8, {}), {2}: (9, {}), {3}: (10, {}), {4... | custom-call | bytes 4194304 | tf_op jit(solution)/shard_map/token_outputs/pallas_call | solution.py:462
  35.4 1.2 %collective-permute-done.7.refs_0_ = bf16[416,128]{1,0:T(8,128)(2,1)S(1)} collective-permute-done((bf16[416,128]{1,0:T(8,128)(2,1)S(1)}, bf16[416,128]{1,0:T(8,128)(2,1)S(1)}, u32[]{:S(2)}, u32[]{:S(2)}) %collective-permute-start.7) | collective-permute-done | bytes 106528 | tf_op jit(solution)/shard_map/ppermute | solution.py:43
  36.6 1.0 %token_outputs.5 = (bf16[128,1024]{1,0:T(8,128)(2,1)}, bf16[128,1024]{1,0:T(8,128)(2,1)}, bf16[128,1024]{1,0:T(8,128)(2,1)}, bf16[128,1024]{1,0:T(8,128)(2,1)}, ...) custom-call(bf16[416,128]{1,0:T(8,128)(2,1)S(1)} %collective-permute, ...), custom_call_target="tpu_custom_call", output_to_operand_aliasing={{0}: (7, {}), {1}: (8, {}), {2}: (9, {}), {3}: (10, {}), {4... | custom-call | bytes 4194304 | tf_op jit(solution)/shard_map/token_outputs/pallas_call | solution.py:462
  (16 shorter events, 0.0 us)
Async XLA Ops:
  0.6 11.8 %copy-start.4 = (bf16[4,256,512]{2,1,0:T(8,128)(2,1)S(1)}, bf16[4,256,512]{2,1,0:T(8,128)(2,1)}, u32[]{:S(2)}) copy-start(bf16[4,256,512]{2,1,0:T(8,128)(2,1)} %constant.5.clone.refs_3_) | copy-start | bytes 3145732
  0.6 11.7 %copy-start.6 = (f32[3,3,1024]{2,1,0:T(4,128)S(1)}, f32[3,3,1024]{2,1,0:T(4,128)}, u32[]{:S(2)}) copy-start(f32[3,3,1024]{2,1,0:T(4,128)} %refs_6_.5) | copy-start | bytes 110596
  2.2 7.7 %collective-permute-start = (bf16[640,128]{1,0:T(8,128)(2,1)S(1)}, bf16[640,128]{1,0:T(8,128)(2,1)S(1)}, u32[]{:S(2)}, u32[]{:S(2)}) collective-permute-start(bf16[640,128]{1,0:T(8,128)(2,1)S(1)} %get-tuple-element.39), channel_id=1, source_target_pairs={{0,16},{4,20},{8,24},{12,28},{16,0},{20,4},{24,8},{28,12},{1,17},{... | collective-permute-start | bytes 491528 | tf_op jit(solution)/shard_map/ppermute | solution.py:43
  5.3 7.1 %collective-permute-start.1 = (bf16[640,128]{1,0:T(8,128)(2,1)S(1)}, bf16[640,128]{1,0:T(8,128)(2,1)S(1)}, u32[]{:S(2)}, u32[]{:S(2)}) collective-permute-start(bf16[640,128]{1,0:T(8,128)(2,1)S(1)} %get-tuple-element.41), channel_id=1, source_target_pairs={{0,8},{4,12},{8,0},{12,4},{16,24},{20,28},{24,16},{28,20},{1,9},{5... | collective-permute-start | bytes 491528 | tf_op jit(solution)/shard_map/ppermute | solution.py:43
  6.7 8.7 %collective-permute-start.2 = (bf16[640,128]{1,0:T(8,128)(2,1)S(1)}, bf16[640,128]{1,0:T(8,128)(2,1)S(1)}, u32[]{:S(2)}, u32[]{:S(2)}) collective-permute-start(bf16[640,128]{1,0:T(8,128)(2,1)S(1)} %get-tuple-element.42), channel_id=1, source_target_pairs={{0,24},{4,28},{8,16},{12,20},{16,8},{20,12},{24,0},{28,4},{1,25},{... | collective-permute-start | bytes 491528 | tf_op jit(solution)/shard_map/ppermute | solution.py:43
  6.8 11.7 %collective-permute-start.3 = (bf16[640,128]{1,0:T(8,128)(2,1)S(1)}, bf16[640,128]{1,0:T(8,128)(2,1)S(1)}, u32[]{:S(2)}, u32[]{:S(2)}) collective-permute-start(bf16[640,128]{1,0:T(8,128)(2,1)S(1)} %get-tuple-element.43), channel_id=1, source_target_pairs={{0,28},{4,24},{8,20},{12,16},{16,12},{20,8},{24,4},{28,0},{1,29},{... | collective-permute-start | bytes 491528 | tf_op jit(solution)/shard_map/ppermute | solution.py:43
  8.3 12.2 %collective-permute-start.4 = (bf16[640,128]{1,0:T(8,128)(2,1)S(1)}, bf16[640,128]{1,0:T(8,128)(2,1)S(1)}, u32[]{:S(2)}, u32[]{:S(2)}) collective-permute-start(bf16[640,128]{1,0:T(8,128)(2,1)S(1)} %get-tuple-element.44), channel_id=1, source_target_pairs={{0,20},{4,16},{8,28},{12,24},{16,4},{20,0},{24,12},{28,8},{1,21},{... | collective-permute-start | bytes 491528 | tf_op jit(solution)/shard_map/ppermute | solution.py:43
  9.9 10.6 %collective-permute-start.5 = (bf16[640,128]{1,0:T(8,128)(2,1)S(1)}, bf16[640,128]{1,0:T(8,128)(2,1)S(1)}, u32[]{:S(2)}, u32[]{:S(2)}) collective-permute-start(bf16[640,128]{1,0:T(8,128)(2,1)S(1)} %get-tuple-element.45), channel_id=1, source_target_pairs={{0,12},{4,8},{8,4},{12,0},{16,28},{20,24},{24,20},{28,16},{1,13},{... | collective-permute-start | bytes 491528 | tf_op jit(solution)/shard_map/ppermute | solution.py:43
  12.4 8.1 %collective-permute-start.6 = (bf16[640,128]{1,0:T(8,128)(2,1)S(1)}, bf16[640,128]{1,0:T(8,128)(2,1)S(1)}, u32[]{:S(2)}, u32[]{:S(2)}) collective-permute-start(bf16[640,128]{1,0:T(8,128)(2,1)S(1)} %get-tuple-element.46), channel_id=1, source_target_pairs={{0,4},{4,0},{8,12},{12,8},{16,20},{20,16},{24,28},{28,24},{1,5},{5... | collective-permute-start | bytes 491528 | tf_op jit(solution)/shard_map/ppermute | solution.py:43
  12.4 1.2 %copy-start.5 = (bf16[4,512,256]{2,1,0:T(8,128)(2,1)S(1)}, bf16[4,512,256]{2,1,0:T(8,128)(2,1)}, u32[]{:S(2)}) copy-start(bf16[4,512,256]{2,1,0:T(8,128)(2,1)} %constant.4.clone.refs_2_) | copy-start | bytes 3145732
  20.5 11.8 %copy-start = (bf16[128,1024]{1,0:T(8,128)(2,1)S(1)}, bf16[128,1024]{1,0:T(8,128)(2,1)}, u32[]{:S(2)}) copy-start(bf16[128,1024]{1,0:T(8,128)(2,1)} %refs_2_.6) | copy-start | bytes 786436
  20.5 11.8 %copy-start.1 = (bf16[128,1024]{1,0:T(8,128)(2,1)S(1)}, bf16[128,1024]{1,0:T(8,128)(2,1)}, u32[]{:S(2)}) copy-start(bf16[128,1024]{1,0:T(8,128)(2,1)} %refs_3_.6) | copy-start | bytes 786436
  20.5 11.8 %copy-start.2 = (bf16[128,1024]{1,0:T(8,128)(2,1)S(1)}, bf16[128,1024]{1,0:T(8,128)(2,1)}, u32[]{:S(2)}) copy-start(bf16[128,1024]{1,0:T(8,128)(2,1)} %refs_4_.7) | copy-start | bytes 786436
  20.5 11.8 %copy-start.3 = (bf16[128,1024]{1,0:T(8,128)(2,1)S(1)}, bf16[128,1024]{1,0:T(8,128)(2,1)}, u32[]{:S(2)}) copy-start(bf16[128,1024]{1,0:T(8,128)(2,1)} %refs_5_.5) | copy-start | bytes 786436
  23.1 6.9 %collective-permute-start.11 = (bf16[416,128]{1,0:T(8,128)(2,1)S(1)}, bf16[416,128]{1,0:T(8,128)(2,1)S(1)}, u32[]{:S(2)}, u32[]{:S(2)}) collective-permute-start(bf16[416,128]{1,0:T(8,128)(2,1)S(1)} %get-tuple-element.55), channel_id=1, source_target_pairs={{0,24},{4,28},{8,16},{12,20},{16,8},{20,12},{24,0},{28,4},{1,25},{... | collective-permute-start | bytes 319496 | tf_op jit(solution)/shard_map/ppermute | solution.py:43
  25.3 4.7 %collective-permute-start.12 = (bf16[416,128]{1,0:T(8,128)(2,1)S(1)}, bf16[416,128]{1,0:T(8,128)(2,1)S(1)}, u32[]{:S(2)}, u32[]{:S(2)}) collective-permute-start(bf16[416,128]{1,0:T(8,128)(2,1)S(1)} %get-tuple-element.56), channel_id=1, source_target_pairs={{0,4},{4,0},{8,12},{12,8},{16,20},{20,16},{24,28},{28,24},{1,5},{5... | collective-permute-start | bytes 319496 | tf_op jit(solution)/shard_map/ppermute | solution.py:43
  25.3 7.0 %collective-permute-start.13 = (bf16[416,128]{1,0:T(8,128)(2,1)S(1)}, bf16[416,128]{1,0:T(8,128)(2,1)S(1)}, u32[]{:S(2)}, u32[]{:S(2)}) collective-permute-start(bf16[416,128]{1,0:T(8,128)(2,1)S(1)} %get-tuple-element.57), channel_id=1, source_target_pairs={{0,28},{4,24},{8,20},{12,16},{16,12},{20,8},{24,4},{28,0},{1,29},{... | collective-permute-start | bytes 319496 | tf_op jit(solution)/shard_map/ppermute | solution.py:43
  26.3 8.1 %collective-permute-start.9 = (bf16[416,128]{1,0:T(8,128)(2,1)S(1)}, bf16[416,128]{1,0:T(8,128)(2,1)S(1)}, u32[]{:S(2)}, u32[]{:S(2)}) collective-permute-start(bf16[416,128]{1,0:T(8,128)(2,1)S(1)} %get-tuple-element.52), channel_id=1, source_target_pairs={{0,16},{4,20},{8,24},{12,28},{16,0},{20,4},{24,8},{28,12},{1,17},{... | collective-permute-start | bytes 319496 | tf_op jit(solution)/shard_map/ppermute | solution.py:43
  27.7 6.7 %collective-permute-start.10 = (bf16[416,128]{1,0:T(8,128)(2,1)S(1)}, bf16[416,128]{1,0:T(8,128)(2,1)S(1)}, u32[]{:S(2)}, u32[]{:S(2)}) collective-permute-start(bf16[416,128]{1,0:T(8,128)(2,1)S(1)} %get-tuple-element.53), channel_id=1, source_target_pairs={{0,8},{4,12},{8,0},{12,4},{16,24},{20,28},{24,16},{28,20},{1,9},{5... | collective-permute-start | bytes 319496 | tf_op jit(solution)/shard_map/ppermute | solution.py:43
  30.0 6.6 %collective-permute-start.7 = (bf16[416,128]{1,0:T(8,128)(2,1)S(1)}, bf16[416,128]{1,0:T(8,128)(2,1)S(1)}, u32[]{:S(2)}, u32[]{:S(2)}) collective-permute-start(bf16[416,128]{1,0:T(8,128)(2,1)S(1)} %get-tuple-element.50), channel_id=1, source_target_pairs={{0,20},{4,16},{8,28},{12,24},{16,4},{20,0},{24,12},{28,8},{1,21},{... | collective-permute-start | bytes 319496 | tf_op jit(solution)/shard_map/ppermute | solution.py:43
  30.0 6.6 %collective-permute-start.8 = (bf16[416,128]{1,0:T(8,128)(2,1)S(1)}, bf16[416,128]{1,0:T(8,128)(2,1)S(1)}, u32[]{:S(2)}, u32[]{:S(2)}) collective-permute-start(bf16[416,128]{1,0:T(8,128)(2,1)S(1)} %get-tuple-element.51), channel_id=1, source_target_pairs={{0,12},{4,8},{8,4},{12,0},{16,28},{20,24},{24,20},{28,16},{1,13},{... | collective-permute-start | bytes 319496 | tf_op jit(solution)/shard_map/ppermute | solution.py:43

commit v21 on v16

--- a/solution.py
+++ b/solution.py
@@ -61,9 +61,11 @@
         pltpu.make_async_copy(source, target, sems.at[at])
         for at, (source, target) in enumerate(zip(sources, held))
     ]
-    for copy in arriving:
-        copy.start()
-    for at, source in enumerate(held):
+    order = [count - 1, *range(count - 1)]
+    for at in order:
+        arriving[at].start()
+    for at in order:
+        source = held[at]
         arriving[at].wait()
         rows = slice(at * tokens, (at + 1) * tokens)
         for step, target in zip(steps, packed):

time: 37.8 us -> 37.8 us (level)
  no operation moved by 1% of the time
where the time goes in v21:
time: 37.8 us; the launch traced here: 37.6 us
  starting transfers between devices  15.9 us (42%)
  waiting for transfers between devices  11.7 us (31%)
  Pallas kernels  8.07 us (21%)
  local copies, waits for them, and re-layouts  1.25 us (3%)
  between operations  0.74 us (2%)
    ppermute x14, starting transfers between devices, exchange(): lax.ppermute(block, 'ctx', [(i, i ^ step) for i in range(peers)])  15.9 us
    ppermute x14, waiting for transfers between devices, exchange(): lax.ppermute(block, 'ctx', [(i, i ^ step) for i in range(peers)])  11.7 us
    pallas_call x3, Pallas kernels, token_step(): pl.pallas_call(functools.partial(token_kernel, steps, extra_rows(short_we...  3.46 us
    pallas_call x1, Pallas kernels, channel_step(): pl.pallas_call(functools.partial(channel_kernel, tokens, heard, told, 1.0...  2.65 us
    pallas_call x1, Pallas kernels, pack(): pl.pallas_call(functools.partial(pack_kernel, count, steps), in_specs=[pl...  1.54 us
    unnamed x14, local copies, waits for them, and re-layouts  1.25 us
  transfers between devices with their start and end apart: 14, of which 7 were waited for; matrix products, arithmetic and copies ran while one was open for 0% of the time, Pallas kernels for 8%

profile of v21, /device:TPU:0, one launch (start us, length us, event | category | flops | bytes accessed | tf_op | source)
XLA Modules:
  0.0 37.6 jit_solution(4917054197309609509)
XLA Ops:
  0.6 0.0 copy-start.4
  0.7 1.5 %pack_inputs.1 = (bf16[640,128]{1,0:T(8,128)(2,1)S(1)}, bf16[640,128]{1,0:T(8,128)(2,1)S(1)}, bf16[640,128]{1,0:T(8,128)(2,1)S(1)}, bf16[640,128]{1,0:T(8,128)(2...) custom-call(bf16[128,1024]{1,0:T(8,128)(2,1)} %refs_2_.6, ...), custom_call_target="tpu_custom_call" | custom-call | bytes 8388608 | tf_op jit(solution)/shard_map/pack_inputs/pallas_call | solution.py:78
  2.2 3.0 %collective-permute-start = (bf16[640,128]{1,0:T(8,128)(2,1)S(1)}, bf16[640,128]{1,0:T(8,128)(2,1)S(1)}, u32[]{:S(2)}, u32[]{:S(2)}) collective-permute-start(bf16[640,128]{1,0:T(8,128)(2,1)S(1)} %get-tuple-element.39), channel_id=1, source_target_pairs={{0,16},{4,20},{8,24},{12,28},{16,0},{20,4},{24,8},{28,12},{1,17},{... | collective-permute-start | bytes 491528 | tf_op jit(solution)/shard_map/ppermute | solution.py:43
  5.2 1.5 %collective-permute-start.1 = (bf16[640,128]{1,0:T(8,128)(2,1)S(1)}, bf16[640,128]{1,0:T(8,128)(2,1)S(1)}, u32[]{:S(2)}, u32[]{:S(2)}) collective-permute-start(bf16[640,128]{1,0:T(8,128)(2,1)S(1)} %get-tuple-element.41), channel_id=1, source_target_pairs={{0,8},{4,12},{8,0},{12,4},{16,24},{20,28},{24,16},{28,20},{1,9},{5... | collective-permute-start | bytes 491528 | tf_op jit(solution)/shard_map/ppermute | solution.py:43
  6.7 0.0 collective-permute-start.2
  6.8 1.5 %collective-permute-start.3 = (bf16[640,128]{1,0:T(8,128)(2,1)S(1)}, bf16[640,128]{1,0:T(8,128)(2,1)S(1)}, u32[]{:S(2)}, u32[]{:S(2)}) collective-permute-start(bf16[640,128]{1,0:T(8,128)(2,1)S(1)} %get-tuple-element.43), channel_id=1, source_target_pairs={{0,28},{4,24},{8,20},{12,16},{16,12},{20,8},{24,4},{28,0},{1,29},{... | collective-permute-start | bytes 491528 | tf_op jit(solution)/shard_map/ppermute | solution.py:43
  8.3 1.6 %collective-permute-start.4 = (bf16[640,128]{1,0:T(8,128)(2,1)S(1)}, bf16[640,128]{1,0:T(8,128)(2,1)S(1)}, u32[]{:S(2)}, u32[]{:S(2)}) collective-permute-start(bf16[640,128]{1,0:T(8,128)(2,1)S(1)} %get-tuple-element.44), channel_id=1, source_target_pairs={{0,20},{4,16},{8,28},{12,24},{16,4},{20,0},{24,12},{28,8},{1,21},{... | collective-permute-start | bytes 491528 | tf_op jit(solution)/shard_map/ppermute | solution.py:43
  9.9 0.0 collective-permute-done.refs_4_.refs_1_
  9.9 0.1 collective-permute-start.5
  9.9 2.4 %collective-permute-done.1.refs_2_ = bf16[640,128]{1,0:T(8,128)(2,1)S(1)} collective-permute-done((bf16[640,128]{1,0:T(8,128)(2,1)S(1)}, bf16[640,128]{1,0:T(8,128)(2,1)S(1)}, u32[]{:S(2)}, u32[]{:S(2)}) %collective-permute-start.1) | collective-permute-done | bytes 163872 | tf_op jit(solution)/shard_map/ppermute | solution.py:43
  12.4 0.0 collective-permute-start.6
  12.4 0.0 copy-start.5
  12.4 1.2 %copy-done.5 = bf16[4,512,256]{2,1,0:T(8,128)(2,1)S(1)} copy-done((bf16[4,512,256]{2,1,0:T(8,128)(2,1)S(1)}, bf16[4,512,256]{2,1,0:T(8,128)(2,1)}, u32[]{:S(2)}) %copy-start.5) | copy-done | bytes 1048600
  13.6 0.4 %stage_tables.1 = (bf16[640,128]{1,0:T(8,128)(2,1)S(1)}, f32[3,3,1024]{2,1,0:T(4,128)S(1)}, bf16[4,512,256]{2,1,0:T(8,128)(2,1)S(1)}, bf16[4,256,512]{2,1,0:T(8,128)(2,1)S(1)}) custom-call(bf16[640,128]{1,0:T(8,128)(2,1)S(1)} %get-tuple-element.38.refs_0_, f32[3,3,1024]{2,1,0:T(4,128)S(1)} %copy-done.6, bf16[4,512,256]{2,1,0:T(8,128)(2,1)S(1)} %copy-done.5, ...), custom_call_target="tpu_custom_call" | custom-call | bytes 8388608 | tf_op jit(solution)/shard_map/stage_tables/pallas_call | solution.py:183
  14.0 1.4 %collective-permute-done.2.refs_3_ = bf16[640,128]{1,0:T(8,128)(2,1)S(1)} collective-permute-done((bf16[640,128]{1,0:T(8,128)(2,1)S(1)}, bf16[640,128]{1,0:T(8,128)(2,1)S(1)}, u32[]{:S(2)}, u32[]{:S(2)}) %collective-permute-start.2) | collective-permute-done | bytes 163872 | tf_op jit(solution)/shard_map/ppermute | solution.py:43
  15.5 3.0 %collective-permute-done.3.refs_4_ = bf16[640,128]{1,0:T(8,128)(2,1)S(1)} collective-permute-done((bf16[640,128]{1,0:T(8,128)(2,1)S(1)}, bf16[640,128]{1,0:T(8,128)(2,1)S(1)}, u32[]{:S(2)}, u32[]{:S(2)}) %collective-permute-start.3) | collective-permute-done | bytes 163872 | tf_op jit(solution)/shard_map/ppermute | solution.py:43
  18.4 2.0 %collective-permute-done.4.refs_5_ = bf16[640,128]{1,0:T(8,128)(2,1)S(1)} collective-permute-done((bf16[640,128]{1,0:T(8,128)(2,1)S(1)}, bf16[640,128]{1,0:T(8,128)(2,1)S(1)}, u32[]{:S(2)}, u32[]{:S(2)}) %collective-permute-start.4) | collective-permute-done | bytes 163872 | tf_op jit(solution)/shard_map/ppermute | solution.py:43
  20.5 0.0 collective-permute-done.5.refs_6_
  20.5 0.0 copy-start.3
  20.5 2.6 %channel_operator.1 = (bf16[416,128]{1,0:T(8,128)(2,1)S(1)}, bf16[416,128]{1,0:T(8,128)(2,1)S(1)}, bf16[416,128]{1,0:T(8,128)(2,1)S(1)}, bf16[416,128]{1,0:T(8,1...) custom-call(bf16[640,128]{1,0:T(8,128)(2,1)S(1)} %get-tuple-element., ...), custom_call_target="tpu_custom_call" | custom-call | tf_op jit(solution)/shard_map/channel_operator/pallas_call | solution.py:357
  23.2 2.2 %collective-permute-start.11 = (bf16[416,128]{1,0:T(8,128)(2,1)S(1)}, bf16[416,128]{1,0:T(8,128)(2,1)S(1)}, u32[]{:S(2)}, u32[]{:S(2)}) collective-permute-start(bf16[416,128]{1,0:T(8,128)(2,1)S(1)} %get-tuple-element.55), channel_id=1, source_target_pairs={{0,24},{4,28},{8,16},{12,20},{16,8},{20,12},{24,0},{28,4},{1,25},{... | collective-permute-start | bytes 319496 | tf_op jit(solution)/shard_map/ppermute | solution.py:43
  25.4 0.9 %collective-permute-start.13 = (bf16[416,128]{1,0:T(8,128)(2,1)S(1)}, bf16[416,128]{1,0:T(8,128)(2,1)S(1)}, u32[]{:S(2)}, u32[]{:S(2)}) collective-permute-start(bf16[416,128]{1,0:T(8,128)(2,1)S(1)} %get-tuple-element.57), channel_id=1, source_target_pairs={{0,28},{4,24},{8,20},{12,16},{16,12},{20,8},{24,4},{28,0},{1,29},{... | collective-permute-start | bytes 319496 | tf_op jit(solution)/shard_map/ppermute | solution.py:43
  26.3 1.5 %collective-permute-start.9 = (bf16[416,128]{1,0:T(8,128)(2,1)S(1)}, bf16[416,128]{1,0:T(8,128)(2,1)S(1)}, u32[]{:S(2)}, u32[]{:S(2)}) collective-permute-start(bf16[416,128]{1,0:T(8,128)(2,1)S(1)} %get-tuple-element.52), channel_id=1, source_target_pairs={{0,16},{4,20},{8,24},{12,28},{16,0},{20,4},{24,8},{28,12},{1,17},{... | collective-permute-start | bytes 319496 | tf_op jit(solution)/shard_map/ppermute | solution.py:43
  27.7 1.2 %collective-permute-start.10 = (bf16[416,128]{1,0:T(8,128)(2,1)S(1)}, bf16[416,128]{1,0:T(8,128)(2,1)S(1)}, u32[]{:S(2)}, u32[]{:S(2)}) collective-permute-start(bf16[416,128]{1,0:T(8,128)(2,1)S(1)} %get-tuple-element.53), channel_id=1, source_target_pairs={{0,8},{4,12},{8,0},{12,4},{16,24},{20,28},{24,16},{28,20},{1,9},{5... | collective-permute-start | bytes 319496 | tf_op jit(solution)/shard_map/ppermute | solution.py:43
  29.0 1.1 %collective-permute-done.11.refs_1_ = bf16[416,128]{1,0:T(8,128)(2,1)S(1)} collective-permute-done((bf16[416,128]{1,0:T(8,128)(2,1)S(1)}, bf16[416,128]{1,0:T(8,128)(2,1)S(1)}, u32[]{:S(2)}, u32[]{:S(2)}) %collective-permute-start.11) | collective-permute-done | bytes 106528 | tf_op jit(solution)/shard_map/ppermute | solution.py:43
  30.0 2.3 %collective-permute-start.8 = (bf16[416,128]{1,0:T(8,128)(2,1)S(1)}, bf16[416,128]{1,0:T(8,128)(2,1)S(1)}, u32[]{:S(2)}, u32[]{:S(2)}) collective-permute-start(bf16[416,128]{1,0:T(8,128)(2,1)S(1)} %get-tuple-element.51), channel_id=1, source_target_pairs={{0,12},{4,8},{8,4},{12,0},{16,28},{20,24},{24,20},{28,16},{1,13},{... | collective-permute-start | bytes 319496 | tf_op jit(solution)/shard_map/ppermute | solution.py:43
  32.4 0.0 collective-permute-done.13.refs_3_
  32.4 1.4 %token_outputs.3 = (bf16[128,1024]{1,0:T(8,128)(2,1)}, bf16[128,1024]{1,0:T(8,128)(2,1)}, bf16[128,1024]{1,0:T(8,128)(2,1)}, bf16[128,1024]{1,0:T(8,128)(2,1)}, ...) custom-call(bf16[416,128]{1,0:T(8,128)(2,1)S(1)} %get-tuple-element.54.refs_0_, ...), custom_call_target="tpu_custom_call" | custom-call | bytes 4194304 | tf_op jit(solution)/shard_map/token_outputs/pallas_call | solution.py:448
  33.8 0.6 %collective-permute-done.9.refs_0_ = bf16[416,128]{1,0:T(8,128)(2,1)S(1)} collective-permute-done((bf16[416,128]{1,0:T(8,128)(2,1)S(1)}, bf16[416,128]{1,0:T(8,128)(2,1)S(1)}, u32[]{:S(2)}, u32[]{:S(2)}) %collective-permute-start.9) | collective-permute-done | bytes 106528 | tf_op jit(solution)/shard_map/ppermute | solution.py:43
  34.4 1.0 %token_outputs.4 = (bf16[128,1024]{1,0:T(8,128)(2,1)}, bf16[128,1024]{1,0:T(8,128)(2,1)}, bf16[128,1024]{1,0:T(8,128)(2,1)}, bf16[128,1024]{1,0:T(8,128)(2,1)}, ...) custom-call(bf16[416,128]{1,0:T(8,128)(2,1)S(1)} %collective-permute, ...), custom_call_target="tpu_custom_call", output_to_operand_aliasing={{0}: (7, {}), {1}: (8, {}), {2}: (9, {}), {3}: (10, {}), {4... | custom-call | bytes 4194304 | tf_op jit(solution)/shard_map/token_outputs/pallas_call | solution.py:448
  35.4 1.2 %collective-permute-done.7.refs_0_ = bf16[416,128]{1,0:T(8,128)(2,1)S(1)} collective-permute-done((bf16[416,128]{1,0:T(8,128)(2,1)S(1)}, bf16[416,128]{1,0:T(8,128)(2,1)S(1)}, u32[]{:S(2)}, u32[]{:S(2)}) %collective-permute-start.7) | collective-permute-done | bytes 106528 | tf_op jit(solution)/shard_map/ppermute | solution.py:43
  36.6 1.0 %token_outputs.5 = (bf16[128,1024]{1,0:T(8,128)(2,1)}, bf16[128,1024]{1,0:T(8,128)(2,1)}, bf16[128,1024]{1,0:T(8,128)(2,1)}, bf16[128,1024]{1,0:T(8,128)(2,1)}, ...) custom-call(bf16[416,128]{1,0:T(8,128)(2,1)S(1)} %collective-permute, ...), custom_call_target="tpu_custom_call", output_to_operand_aliasing={{0}: (7, {}), {1}: (8, {}), {2}: (9, {}), {3}: (10, {}), {4... | custom-call | bytes 4194304 | tf_op jit(solution)/shard_map/token_outputs/pallas_call | solution.py:448
  (16 shorter events, 0.0 us)
Async XLA Ops:
  0.6 11.7 %copy-start.4 = (bf16[4,256,512]{2,1,0:T(8,128)(2,1)S(1)}, bf16[4,256,512]{2,1,0:T(8,128)(2,1)}, u32[]{:S(2)}) copy-start(bf16[4,256,512]{2,1,0:T(8,128)(2,1)} %constant.5.clone.refs_3_) | copy-start | bytes 3145732
  0.6 11.7 %copy-start.6 = (f32[3,3,1024]{2,1,0:T(4,128)S(1)}, f32[3,3,1024]{2,1,0:T(4,128)}, u32[]{:S(2)}) copy-start(f32[3,3,1024]{2,1,0:T(4,128)} %refs_6_.5) | copy-start | bytes 110596
  2.2 7.7 %collective-permute-start = (bf16[640,128]{1,0:T(8,128)(2,1)S(1)}, bf16[640,128]{1,0:T(8,128)(2,1)S(1)}, u32[]{:S(2)}, u32[]{:S(2)}) collective-permute-start(bf16[640,128]{1,0:T(8,128)(2,1)S(1)} %get-tuple-element.39), channel_id=1, source_target_pairs={{0,16},{4,20},{8,24},{12,28},{16,0},{20,4},{24,8},{28,12},{1,17},{... | collective-permute-start | bytes 491528 | tf_op jit(solution)/shard_map/ppermute | solution.py:43
  5.2 7.1 %collective-permute-start.1 = (bf16[640,128]{1,0:T(8,128)(2,1)S(1)}, bf16[640,128]{1,0:T(8,128)(2,1)S(1)}, u32[]{:S(2)}, u32[]{:S(2)}) collective-permute-start(bf16[640,128]{1,0:T(8,128)(2,1)S(1)} %get-tuple-element.41), channel_id=1, source_target_pairs={{0,8},{4,12},{8,0},{12,4},{16,24},{20,28},{24,16},{28,20},{1,9},{5... | collective-permute-start | bytes 491528 | tf_op jit(solution)/shard_map/ppermute | solution.py:43
  6.7 8.7 %collective-permute-start.2 = (bf16[640,128]{1,0:T(8,128)(2,1)S(1)}, bf16[640,128]{1,0:T(8,128)(2,1)S(1)}, u32[]{:S(2)}, u32[]{:S(2)}) collective-permute-start(bf16[640,128]{1,0:T(8,128)(2,1)S(1)} %get-tuple-element.42), channel_id=1, source_target_pairs={{0,24},{4,28},{8,16},{12,20},{16,8},{20,12},{24,0},{28,4},{1,25},{... | collective-permute-start | bytes 491528 | tf_op jit(solution)/shard_map/ppermute | solution.py:43
  6.8 11.7 %collective-permute-start.3 = (bf16[640,128]{1,0:T(8,128)(2,1)S(1)}, bf16[640,128]{1,0:T(8,128)(2,1)S(1)}, u32[]{:S(2)}, u32[]{:S(2)}) collective-permute-start(bf16[640,128]{1,0:T(8,128)(2,1)S(1)} %get-tuple-element.43), channel_id=1, source_target_pairs={{0,28},{4,24},{8,20},{12,16},{16,12},{20,8},{24,4},{28,0},{1,29},{... | collective-permute-start | bytes 491528 | tf_op jit(solution)/shard_map/ppermute | solution.py:43
  8.3 12.2 %collective-permute-start.4 = (bf16[640,128]{1,0:T(8,128)(2,1)S(1)}, bf16[640,128]{1,0:T(8,128)(2,1)S(1)}, u32[]{:S(2)}, u32[]{:S(2)}) collective-permute-start(bf16[640,128]{1,0:T(8,128)(2,1)S(1)} %get-tuple-element.44), channel_id=1, source_target_pairs={{0,20},{4,16},{8,28},{12,24},{16,4},{20,0},{24,12},{28,8},{1,21},{... | collective-permute-start | bytes 491528 | tf_op jit(solution)/shard_map/ppermute | solution.py:43
  9.9 10.6 %collective-permute-start.5 = (bf16[640,128]{1,0:T(8,128)(2,1)S(1)}, bf16[640,128]{1,0:T(8,128)(2,1)S(1)}, u32[]{:S(2)}, u32[]{:S(2)}) collective-permute-start(bf16[640,128]{1,0:T(8,128)(2,1)S(1)} %get-tuple-element.45), channel_id=1, source_target_pairs={{0,12},{4,8},{8,4},{12,0},{16,28},{20,24},{24,20},{28,16},{1,13},{... | collective-permute-start | bytes 491528 | tf_op jit(solution)/shard_map/ppermute | solution.py:43
  12.4 8.1 %collective-permute-start.6 = (bf16[640,128]{1,0:T(8,128)(2,1)S(1)}, bf16[640,128]{1,0:T(8,128)(2,1)S(1)}, u32[]{:S(2)}, u32[]{:S(2)}) collective-permute-start(bf16[640,128]{1,0:T(8,128)(2,1)S(1)} %get-tuple-element.46), channel_id=1, source_target_pairs={{0,4},{4,0},{8,12},{12,8},{16,20},{20,16},{24,28},{28,24},{1,5},{5... | collective-permute-start | bytes 491528 | tf_op jit(solution)/shard_map/ppermute | solution.py:43
  12.4 1.2 %copy-start.5 = (bf16[4,512,256]{2,1,0:T(8,128)(2,1)S(1)}, bf16[4,512,256]{2,1,0:T(8,128)(2,1)}, u32[]{:S(2)}) copy-start(bf16[4,512,256]{2,1,0:T(8,128)(2,1)} %constant.4.clone.refs_2_) | copy-start | bytes 3145732
  20.5 11.9 %copy-start = (bf16[128,1024]{1,0:T(8,128)(2,1)S(1)}, bf16[128,1024]{1,0:T(8,128)(2,1)}, u32[]{:S(2)}) copy-start(bf16[128,1024]{1,0:T(8,128)(2,1)} %refs_2_.6) | copy-start | bytes 786436
  20.5 11.9 %copy-start.1 = (bf16[128,1024]{1,0:T(8,128)(2,1)S(1)}, bf16[128,1024]{1,0:T(8,128)(2,1)}, u32[]{:S(2)}) copy-start(bf16[128,1024]{1,0:T(8,128)(2,1)} %refs_3_.6) | copy-start | bytes 786436
  20.5 11.9 %copy-start.2 = (bf16[128,1024]{1,0:T(8,128)(2,1)S(1)}, bf16[128,1024]{1,0:T(8,128)(2,1)}, u32[]{:S(2)}) copy-start(bf16[128,1024]{1,0:T(8,128)(2,1)} %refs_4_.7) | copy-start | bytes 786436
  20.5 11.9 %copy-start.3 = (bf16[128,1024]{1,0:T(8,128)(2,1)S(1)}, bf16[128,1024]{1,0:T(8,128)(2,1)}, u32[]{:S(2)}) copy-start(bf16[128,1024]{1,0:T(8,128)(2,1)} %refs_5_.5) | copy-start | bytes 786436
  23.2 6.9 %collective-permute-start.11 = (bf16[416,128]{1,0:T(8,128)(2,1)S(1)}, bf16[416,128]{1,0:T(8,128)(2,1)S(1)}, u32[]{:S(2)}, u32[]{:S(2)}) collective-permute-start(bf16[416,128]{1,0:T(8,128)(2,1)S(1)} %get-tuple-element.55), channel_id=1, source_target_pairs={{0,24},{4,28},{8,16},{12,20},{16,8},{20,12},{24,0},{28,4},{1,25},{... | collective-permute-start | bytes 319496 | tf_op jit(solution)/shard_map/ppermute | solution.py:43
  25.4 4.7 %collective-permute-start.12 = (bf16[416,128]{1,0:T(8,128)(2,1)S(1)}, bf16[416,128]{1,0:T(8,128)(2,1)S(1)}, u32[]{:S(2)}, u32[]{:S(2)}) collective-permute-start(bf16[416,128]{1,0:T(8,128)(2,1)S(1)} %get-tuple-element.56), channel_id=1, source_target_pairs={{0,4},{4,0},{8,12},{12,8},{16,20},{20,16},{24,28},{28,24},{1,5},{5... | collective-permute-start | bytes 319496 | tf_op jit(solution)/shard_map/ppermute | solution.py:43
  25.4 7.0 %collective-permute-start.13 = (bf16[416,128]{1,0:T(8,128)(2,1)S(1)}, bf16[416,128]{1,0:T(8,128)(2,1)S(1)}, u32[]{:S(2)}, u32[]{:S(2)}) collective-permute-start(bf16[416,128]{1,0:T(8,128)(2,1)S(1)} %get-tuple-element.57), channel_id=1, source_target_pairs={{0,28},{4,24},{8,20},{12,16},{16,12},{20,8},{24,4},{28,0},{1,29},{... | collective-permute-start | bytes 319496 | tf_op jit(solution)/shard_map/ppermute | solution.py:43
  26.3 8.1 %collective-permute-start.9 = (bf16[416,128]{1,0:T(8,128)(2,1)S(1)}, bf16[416,128]{1,0:T(8,128)(2,1)S(1)}, u32[]{:S(2)}, u32[]{:S(2)}) collective-permute-start(bf16[416,128]{1,0:T(8,128)(2,1)S(1)} %get-tuple-element.52), channel_id=1, source_target_pairs={{0,16},{4,20},{8,24},{12,28},{16,0},{20,4},{24,8},{28,12},{1,17},{... | collective-permute-start | bytes 319496 | tf_op jit(solution)/shard_map/ppermute | solution.py:43
  27.7 6.7 %collective-permute-start.10 = (bf16[416,128]{1,0:T(8,128)(2,1)S(1)}, bf16[416,128]{1,0:T(8,128)(2,1)S(1)}, u32[]{:S(2)}, u32[]{:S(2)}) collective-permute-start(bf16[416,128]{1,0:T(8,128)(2,1)S(1)} %get-tuple-element.53), channel_id=1, source_target_pairs={{0,8},{4,12},{8,0},{12,4},{16,24},{20,28},{24,16},{28,20},{1,9},{5... | collective-permute-start | bytes 319496 | tf_op jit(solution)/shard_map/ppermute | solution.py:43
  30.0 6.6 %collective-permute-start.7 = (bf16[416,128]{1,0:T(8,128)(2,1)S(1)}, bf16[416,128]{1,0:T(8,128)(2,1)S(1)}, u32[]{:S(2)}, u32[]{:S(2)}) collective-permute-start(bf16[416,128]{1,0:T(8,128)(2,1)S(1)} %get-tuple-element.50), channel_id=1, source_target_pairs={{0,20},{4,16},{8,28},{12,24},{16,4},{20,0},{24,12},{28,8},{1,21},{... | collective-permute-start | bytes 319496 | tf_op jit(solution)/shard_map/ppermute | solution.py:43
  30.0 6.6 %collective-permute-start.8 = (bf16[416,128]{1,0:T(8,128)(2,1)S(1)}, bf16[416,128]{1,0:T(8,128)(2,1)S(1)}, u32[]{:S(2)}, u32[]{:S(2)}) collective-permute-start(bf16[416,128]{1,0:T(8,128)(2,1)S(1)} %get-tuple-element.51), channel_id=1, source_target_pairs={{0,12},{4,8},{8,4},{12,0},{16,28},{20,24},{24,20},{28,16},{1,13},{... | collective-permute-start | bytes 319496 | tf_op jit(solution)/shard_map/ppermute | solution.py:43
